TPU v7x, 32 devices: a whole 2x2x4 slice. The times are simulated.
32 devices in a mesh: space: 4 (over y, x), band: 8 (over z, core).
Axes of the slice: x: 2, y: 2, z: 4, core: 2. Of those that a mesh axis runs over, the one named last changes fastest.
Arguments:
- orbitals: float32 [768, 8, 2048], P('band', 'space'), may hold values from -6 to 6
- potential: float32 [8, 2048], P('space'), may hold values from 0 to 2
Outputs:
- filtered: float32 [768, 8, 2048], P('band', 'space')
- margin: float32 [768, 768], P('band')
All inputs are finite; a program needn't handle non-finite values.
Results may differ from a plain program's by a relative error of at most 0.0002.
Values sent between devices are 32-bit elements; how exact they have to be, the bound alone decides.
No kernel may reach another device: no remote copies, remote signals or barrier semaphores. Data moves between devices by JAX's collectives and lax.ppermute only.
A program may use at most 64 MiB of HBM per device.

v0:
```python
import jax
import jax.numpy as jnp
from jax import lax
from jax.sharding import PartitionSpec as P

NZ = 64


def shift_plane(flat, step, depth):
    pos = lax.broadcasted_iota(jnp.int32, (flat.shape[-1],), 0) % depth
    inside = (pos + step >= 0) & (pos + step < depth)
    direct = jnp.roll(flat, -step, axis=-1)
    if step > 0:
        wrapped = jnp.roll(flat, depth - step, axis=-1)
    else:
        wrapped = jnp.roll(flat, -step - depth, axis=-1)
    return jnp.where(inside, direct, wrapped)


def plane_terms(center, depth):
    near = jnp.roll(center, -depth, axis=-1) + jnp.roll(center, depth, axis=-1)
    far = jnp.roll(center, -2 * depth, axis=-1) + jnp.roll(center, 2 * depth, axis=-1)
    near = near + shift_plane(center, 1, depth) + shift_plane(center, -1, depth)
    far = far + shift_plane(center, 2, depth) + shift_plane(center, -2, depth)
    return 4.0 / 3.0 * near - 1.0 / 12.0 * far


def local_hamiltonian(field, potential):
    near = jnp.roll(field, 1, axis=1) + jnp.roll(field, -1, axis=1)
    far = jnp.roll(field, 2, axis=1) + jnp.roll(field, -2, axis=1)
    laplace = 4.0 / 3.0 * near - 1.0 / 12.0 * far + plane_terms(field, NZ) - 7.5 * field
    return -0.5 * laplace + potential[None] * field


def chebyshev(block, potential, operator):
    first = (operator(block, potential) - 6.0 * block) / 4.0
    second = 2.0 * (operator(first, potential) - 6.0 * first) / 4.0 - block
    return 2.0 * (operator(second, potential) - 6.0 * second) / 4.0 - first


def shards(orbitals, potential):
    spread = lax.all_to_all(orbitals, "space", split_axis=0, concat_axis=1, tiled=True)
    whole_potential = lax.all_gather(potential, "space", axis=0, tiled=True)
    whole_filtered = chebyshev(spread, whole_potential, local_hamiltonian)
    filtered = lax.all_to_all(whole_filtered, "space", split_axis=1, concat_axis=0, tiled=True)
    orb_count = filtered.shape[0]
    layers = filtered.shape[1]
    plane = filtered.shape[2]
    flat = filtered.reshape(orb_count, layers * plane)
    regrouped = lax.all_to_all(flat, "band", split_axis=1, concat_axis=0, tiled=True)
    partial_sum = jnp.dot(
        regrouped, regrouped.T, precision=lax.Precision.HIGHEST, preferred_element_type=jnp.float32
    )
    total_cells = layers * lax.axis_size("space") * plane
    whole = lax.psum(partial_sum, "space")
    rows = lax.psum_scatter(whole, "band", scatter_dimension=0, tiled=True)
    return (filtered, rows * (1.0 / total_cells))


def solution(mesh):
    return jax.shard_map(
        shards,
        mesh=mesh,
        in_specs=(P("band", "space", None), P("space", None)),
        out_specs=(P("band", "space", None), P("band", None)),
        check_vma=False,
    )
```

profile of v0, /device:TPU:0, one launch (start us, length us, event | category | flops | bytes accessed | tf_op | source)
XLA Modules:
  0.0 225.0 jit_solution(14412855103397667306)
XLA Ops:
  7.2 5.2 %all-to-all-start = ((f32[96,2,2048]{2,1,0:T(2,128)}), f32[96,2,2048]{2,1,0:T(2,128)S(1)}, u32[]{:S(2)}, u32[]{:S(2)}) async-start(f32[96,2,2048]{2,1,0:T(2,128)} %param.2), calls=%async_computation | async-start | bytes 3145728 | tf_op jit(solution)/shard_map/all_to_all | solution.py:42
  12.4 22.6 %all-gather = f32[4,2,2048]{2,1,0:T(2,128)S(1)} all-gather(f32[1,2,2048]{2,1,0:T(2,128)S(1)} %bitcast.38), channel_id=1, replica_groups=mesh['space'=4,'band'=8] {'space'}, dimensions={0}, use_global_device_ids=true | all-gather | bytes 81920 | tf_op jit(solution)/shard_map/all_gather | solution.py:43
  35.1 0.0 all-to-all-done
  35.1 0.9 copy.10
  36.0 0.1 copy.11
  36.1 0.6 fusion.116
  36.7 0.6 fusion.105
  37.3 0.6 fusion.107
  37.9 0.6 fusion.110
  38.5 0.6 fusion.113
  39.0 0.2 fusion.111
  39.2 0.3 fusion.102
  39.6 0.3 fusion.104
  39.9 0.1 fusion.103
  40.0 0.1 fusion.115
  40.0 0.1 fusion.106
  40.1 0.1 fusion.108
  40.2 0.1 fusion.109
  40.4 0.1 fusion.114
  40.4 4.7 %broadcast_multiply_fusion = (f32[24,8,2048]{2,0,1:T(8,128)S(1)}, f32[24,8,2048]{2,0,1:T(8,128)S(1)}) fusion(f32[8,2048]{1,0:T(8,128)S(1)} %reshape.12, f32[24,4,2,2048]{3,0,2,1:T(8,128)S(1)} %copy.11, f32[24,8,62]{2,0,1:T(8,128)S(1)} %get-tuple-element.101, f32[24,8,1986]{2,0,1:T(8,128)S(1)} %get-tuple-element.103, ...), kind=kLoop, calls=%fused_computation.73 | loop fusion | flops 16908288 | bytes 29958144 | tf_op jit(solution)/shard_map/div | solution.py:36
  45.1 0.6 fusion.85
  45.7 0.6 fusion.88
  46.3 0.6 fusion.91
  46.8 0.6 fusion.94
  47.4 0.6 fusion.96
  48.0 0.2 fusion.90
  48.2 0.3 fusion.99
  48.5 0.3 fusion.97
  48.8 0.1 fusion.98
  48.9 0.1 fusion.86
  49.0 0.1 fusion.87
  49.1 0.1 fusion.92
  49.2 0.1 fusion.93
  49.3 0.1 fusion.95
  49.4 4.7 %fusion.23 = f32[24,8,2048]{2,0,1:T(8,128)S(1)} fusion(f32[24,7,2048]{2,0,1:T(8,128)S(1)} %get-tuple-element.69, f32[24,1,2048]{2,0,1:T(8,128)S(1)} %get-tuple-element.71, f32[24,1,2048]{2,0,1:T(8,128)S(1)} %get-tuple-element.70, f32[24,7,2048]{2,0,1:T(8,128)S(1)} %get-tuple-element.68, f32[24,6,2048]{2,0,1:T(8,128)S(1)} %get-tuple-element.65, ...), kind=kLoop, calls=%fused_computation.32 | loop fusion | flops 17301504 | bytes 29958144 | tf_op jit(solution)/shard_map/sub | solution.py:37
  54.0 0.6 fusion.72
  54.6 0.6 fusion.75
  55.2 0.6 fusion.78
  55.8 0.6 fusion.80
  56.4 0.6 fusion.69
  56.9 0.2 fusion.74
  57.2 0.3 fusion.83
  57.5 0.3 fusion.81
  57.8 0.1 fusion.82
  57.9 0.1 fusion.70
  58.0 0.1 fusion.71
  58.1 0.1 fusion.76
  58.2 0.1 fusion.77
  58.3 0.1 fusion.79
  58.4 4.4 %fusion.40 = f32[24,8,2048]{2,0,1:T(8,128)S(1)} fusion(f32[24,7,2048]{2,0,1:T(8,128)S(1)} %get-tuple-element.37, f32[24,1,2048]{2,0,1:T(8,128)S(1)} %get-tuple-element.39, f32[24,1,2048]{2,0,1:T(8,128)S(1)} %get-tuple-element.38, f32[24,7,2048]{2,0,1:T(8,128)S(1)} %get-tuple-element.36, f32[24,6,2048]{2,0,1:T(8,128)S(1)} %get-tuple-element.33, ...), kind=kLoop, calls=%fused_computation.57 | loop fusion | flops 17694720 | bytes 29958144 | tf_op jit(solution)/shard_map/sub | solution.py:38
  62.8 20.4 %all_to_all.55 = f32[24,8,2048]{2,0,1:T(8,128)S(1)} all-to-all(f32[24,8,2048]{2,0,1:T(8,128)S(1)} %fusion.40), channel_id=1, replica_groups=mesh['space'=4,'band'=8] {'space'}, dimensions={1} | all-to-all | bytes 3145728 | tf_op jit(solution)/shard_map/all_to_all | solution.py:45
  83.2 2.4 %copy.13 = f32[4,24,2,2048]{3,2,1,0:T(2,128)} copy(f32[4,24,2,2048]{3,1,2,0:T(8,128)S(1)} %bitcast.33) | data formatting | bytes 3145728 | tf_op jit(solution)/shard_map/all_to_all | solution.py:45
  85.6 2.5 %all_to_all.48 = f32[96,8,512]{2,1,0:T(8,128)S(1)} reshape(f32[4,24,2,2048]{3,2,1,0:T(2,128)} %copy.13) | data formatting | bytes 3145728 | tf_op jit(solution)/shard_map/all_to_all | solution.py:50
  88.1 0.9 copy.14
  89.0 42.7 %all_to_all.56 = f32[96,8,512]{2,0,1:T(8,128)S(1)} all-to-all(f32[96,8,512]{2,0,1:T(8,128)S(1)} %copy.14), channel_id=1, replica_groups=mesh['space'=4,'band'=8] {'band'}, dimensions={1} | all-to-all | bytes 3145728 | tf_op jit(solution)/shard_map/all_to_all | solution.py:50
  131.8 5.4 %fusion.117 = f32[768,768]{1,0:T(8,128)} fusion(f32[768,512]{1,0:T(8,128)S(1)} %bitcast.35), kind=kOutput, calls=%fused_computation.145 | convolution fusion | flops 3623878656 | bytes 3932160 | tf_op jit(solution)/shard_map/dot_general | solution.py:51
  137.1 0.0 reduce-scatter.2.cloned.1.call-update
  137.2 0.0 all-reduce.2.cloned.1.call-start
  137.2 33.7 %reduce-scatter.2.cloned.1.call-done = f32[96,768]{1,0:T(8,128)} async-done(((f32[768,768]{1,0:T(8,128)}), f32[96,768]{1,0:T(8,128)}) %reduce-scatter.2.cloned.1.call-update) | async-done | bytes 294928 | tf_op jit(solution)/shard_map/reduce_scatter | solution.py:56
  170.9 0.0 all-reduce.2.cloned.1.call-update
  170.9 0.1 copy.12
  171.1 2.4 %copy.15 = f32[96,2,2048]{2,1,0:T(2,128)} copy(f32[96,2,2048]{2,0,1:T(8,128)S(1)} %bitcast.37) | data formatting | bytes 3145728
  173.4 43.0 %all-reduce.2.cloned.1.call-done = f32[96,768]{1,0:T(8,128)} async-done(((f32[96,768]{1,0:T(8,128)}), f32[96,768]{1,0:T(8,128)}) %all-reduce.2.cloned.1.call-update) | async-done | bytes 294928 | tf_op jit(solution)/shard_map/psum | solution.py:55
  216.4 1.7 broadcast_multiply_fusion.1
  (13 shorter events, 0.2 us)
Async XLA Ops:
  7.2 5.2 %copy-start = (f32[2,2048]{1,0:T(2,128)S(1)}, f32[2,2048]{1,0:T(2,128)}, u32[]{:S(2)}) copy-start(f32[2,2048]{1,0:T(2,128)} %param.3) | copy-start | bytes 49156
  7.2 27.9 %all-to-all-start = ((f32[96,2,2048]{2,1,0:T(2,128)}), f32[96,2,2048]{2,1,0:T(2,128)S(1)}, u32[]{:S(2)}, u32[]{:S(2)}) async-start(f32[96,2,2048]{2,1,0:T(2,128)} %param.2), calls=%async_computation | async-start | bytes 3145728 | tf_op jit(solution)/shard_map/all_to_all | solution.py:42
  12.3 158.6 %reduce-scatter.2.cloned.1.call-start = ((), (), s32[]{:S(2)}) async-start(), calls=%async_computation.4 | async-start | bytes 2654208 | tf_op jit(solution)/shard_map/reduce_scatter | solution.py:56
  137.2 79.3 %all-reduce.2.cloned.1.call-start = ((), (), s32[]{:S(2)}) async-start(), calls=%async_computation.5 | async-start | bytes 589824 | tf_op jit(solution)/shard_map/psum | solution.py:55
Sparse Core Ops, SparseCore 0:
  137.3 33.6 reduce-scatter.1
  173.9 42.5 all-reduce.1
where the time goes:
time: 225 us
  blocking collectives  85.8 us (38%)
  waiting for transfers between devices  76.8 us (34%)
  local copies, waits for them, and re-layouts  21.9 us (10%)
  other arithmetic  15.5 us (7%)
  between operations  14.5 us (6%)
  matrix products  5.38 us (2%)
  starting transfers between devices  5.22 us (2%)
    psum x1, waiting for transfers between devices, shards(): whole = lax.psum(partial_sum, 'space')  43 us
    all_to_all x1, blocking collectives, shards(): lax.all_to_all(flat, 'band', split_axis=1, concat_axis=0, tiled=True)  42.7 us
    reduce_scatter x1, waiting for transfers between devices, shards(): rows = lax.psum_scatter(whole, 'band', scatter_dimension=0, tiled=True)  33.7 us
    all_gather x1, blocking collectives, shards(): whole_potential = lax.all_gather(potential, 'space', axis=0, tiled=True)  22.6 us
    all_to_all x1, blocking collectives, shards(): lax.all_to_all(whole_filtered, 'space', split_axis=1, concat_axis=0, tile...  20.4 us
    dot_general x1, matrix products, shards(): jnp.dot(regrouped, regrouped.T, precision=lax.Precision.HIGHEST, preferre...  5.38 us
    all_to_all x1, starting transfers between devices, shards(): lax.all_to_all(orbitals, 'space', split_axis=0, concat_axis=1, tiled=True)  5.18 us
    div x1, other arithmetic, chebyshev(): first = (operator(block, potential) - 6.0 * block) / 4.0  4.68 us
  transfers between devices with their start and end apart: 3, of which 2 were waited for; matrix products, arithmetic and copies ran while one was open for 1% of the time, Pallas kernels for 0%

commit v1 on v0

v1 whole, which is shorter than its diff:
```python
import functools

import jax
import jax.numpy as jnp
from jax import lax
from jax.experimental import pallas as pl
from jax.experimental.pallas import tpu as pltpu
from jax.sharding import PartitionSpec as P

NZ = 64
LANES = 128
SUBLANES = 8


def filter_kernel(space, layers, tiles, chunk, x_pitch, v_pitch, x_ref, v_ref, out_ref, f0, r0, f1, r1, f2, r2, coef):
    planes = space * layers
    rows = tiles * layers
    lane = lax.broadcasted_iota(jnp.int32, (chunk, LANES), 1)
    depth = lane % NZ
    first_half = lane < NZ
    starts = [depth < 1, depth < 2]
    ends = [depth >= NZ - 1, depth >= NZ - 2]

    def load(tile, carry):
        for p in range(planes):
            s, l = divmod(p, layers)
            row = tile * layers + l
            v = x_ref[pl.ds(s * x_pitch * rows + row, chunk, stride=rows), :]
            f0[tile, p] = v
            r0[tile, p] = pltpu.roll(v, NZ, 1)
            w = v_ref[pl.ds((s * v_pitch + v_pitch - 1) * rows + row, 1), :]
            coef[tile, p] = jnp.broadcast_to(0.25 * w - 0.5625, (chunk, LANES))
        return carry

    def stencil(f, r, tile):
        up = jnp.where(tile == tiles - 1, 0, tile + 1)
        down = jnp.where(tile == 0, tiles - 1, tile - 1)
        v = [f[tile, p] for p in range(planes)]
        pairs = {}

        def pair(a, b):
            key = (min(a, b), max(a, b))
            if key not in pairs:
                pairs[key] = v[a] + v[b]
            return pairs[key]

        out = []
        for p in range(planes):
            rolled = r[tile, p]
            near = pair((p - 1) % planes, (p + 1) % planes)
            far = pair((p - 2) % planes, (p + 2) % planes)
            far = far + (f[up, p] + f[down, p])
            near = near + (rolled + jnp.where(first_half, r[down, p], r[up, p]))
            near = near + pltpu.roll(jnp.where(starts[0], rolled, v[p]), LANES - 1, 1)
            near = near + pltpu.roll(jnp.where(ends[0], rolled, v[p]), 1, 1)
            far = far + pltpu.roll(jnp.where(starts[1], rolled, v[p]), LANES - 2, 1)
            far = far + pltpu.roll(jnp.where(ends[1], rolled, v[p]), 2, 1)
            out.append((v[p], far - 16.0 * near))
        return out

    def first(tile, carry):
        for p, (v, s) in enumerate(stencil(f0, r0, tile)):
            y = (1.0 / 96.0) * s + coef[tile, p] * v
            f1[tile, p] = y
            r1[tile, p] = pltpu.roll(y, NZ, 1)
        return carry

    def second(tile, carry):
        for p, (v, s) in enumerate(stencil(f1, r1, tile)):
            y = 2.0 * ((1.0 / 96.0) * s + coef[tile, p] * v) - f0[tile, p]
            f2[tile, p] = y
            r2[tile, p] = pltpu.roll(y, NZ, 1)
        return carry

    def third(tile, carry):
        for p, (v, s) in enumerate(stencil(f2, r2, tile)):
            y = 2.0 * ((1.0 / 96.0) * s + coef[tile, p] * v) - f1[tile, p]
            out_ref[p // layers, tile * layers + p % layers] = y
        return carry

    for step in (load, first, second, third):
        lax.fori_loop(0, tiles, step, 0)


def run_filter(x, v, space, layers, tiles, chunk):
    rows = tiles * layers
    planes = space * layers
    x_pitch = x.shape[0] // (space * rows)
    v_pitch = v.shape[0] // (space * rows)
    field = pltpu.VMEM((tiles, planes, chunk, LANES), jnp.float32)
    return pl.pallas_call(
        functools.partial(filter_kernel, space, layers, tiles, chunk, x_pitch, v_pitch),
        out_shape=jax.ShapeDtypeStruct((space, rows, chunk, LANES), jnp.float32),
        in_specs=[pl.BlockSpec(memory_space=pltpu.VMEM)] * 2,
        out_specs=pl.BlockSpec(memory_space=pltpu.VMEM),
        scratch_shapes=[field] * 7,
        compiler_params=pltpu.CompilerParams(vmem_limit_bytes=40 * 1024 * 1024),
        cost_estimate=pl.CostEstimate(
            flops=75 * planes * rows * max(chunk, SUBLANES) * LANES // layers,
            bytes_accessed=2 * planes * tiles * chunk * LANES * 4,
            transcendentals=0,
        ),
    )(x, v)


def rotate(x, axis, step):
    size = lax.axis_size(axis)
    return lax.ppermute(x, axis, [(i, (i + step) % size) for i in range(size)])


def shards(orbitals, potential):
    space = lax.axis_size("space")
    band = lax.axis_size("band")
    count, layers, plane = orbitals.shape
    tiles = plane // LANES
    rows = tiles * layers
    share = rows // band
    own = count // space
    chunk = max(c for c in range(1, SUBLANES + 1) if own % c == 0)
    chunks = own // chunk

    spread = orbitals.reshape(count, layers, tiles, LANES).transpose(0, 2, 1, 3).reshape(count, rows, LANES)
    local_v = potential.reshape(layers, tiles, LANES).transpose(1, 0, 2).reshape(1, 1, rows, LANES)
    local_v = jnp.broadcast_to(local_v, (space, 1, rows, LANES))

    whole_v = None
    outs = []
    grams = []
    for c in range(chunks):
        part = spread[c * space * chunk : (c + 1) * space * chunk]
        if c == 0:
            part = jnp.concatenate([part.reshape(space, chunk, rows, LANES), local_v], axis=1)
            part = part.reshape(space * (chunk + 1), rows, LANES)
        got = lax.all_to_all(part, "space", split_axis=0, concat_axis=0, tiled=True)
        got = got.reshape(-1, LANES)
        if c == 0:
            whole_v = got
        filtered = run_filter(got, whole_v, space, layers, tiles, chunk)
        back = lax.all_to_all(filtered, "space", split_axis=0, concat_axis=0, tiled=True)
        outs.append(
            back.reshape(space, tiles, layers, chunk, LANES)
            .transpose(0, 3, 2, 1, 4)
            .reshape(space * chunk, layers, plane)
        )
        packed = back.reshape(space, band, share, chunk, LANES).transpose(1, 0, 2, 3, 4)
        regrouped = lax.all_to_all(packed, "band", split_axis=0, concat_axis=0, tiled=True)
        grams.append(regrouped.transpose(0, 1, 3, 2, 4).reshape(band, space * chunk, share * LANES))

    result = jnp.concatenate(outs, axis=0)
    all_orbs = jnp.concatenate(grams, axis=1)

    pairs = band // 2
    core = lax.axis_index("band") % 2
    pair = lax.axis_index("band") // 2
    mine_s = lax.axis_index("space")
    wide = all_orbs.reshape(band * count, share * LANES)
    by_core = all_orbs.reshape(pairs, 2, count, share * LANES)

    def rows_of(which):
        left = lax.dynamic_index_in_dim(by_core, which, 1, keepdims=False).reshape(pairs * count, share * LANES)
        return lax.dot_general(
            left, wide, (((1,), (1,)), ((), ())), precision=lax.Precision.HIGH, preferred_element_type=jnp.float32
        )

    other = lax.ppermute(rows_of(1 - core), "band", [(i, i ^ 1) for i in range(band)])
    total = (rows_of(core) + other).reshape(pairs, space, own, band * count)

    mine = lax.dynamic_index_in_dim(total, mine_s, 1, keepdims=False)
    for k in range(1, space):
        sent = lax.dynamic_index_in_dim(total, (mine_s + k) % space, 1, keepdims=False)
        mine = mine + rotate(sent, "space", k)

    final = lax.dynamic_index_in_dim(mine, pair, 0, keepdims=False)
    for k in range(1, pairs):
        sent = lax.dynamic_index_in_dim(mine, (pair + k) % pairs, 0, keepdims=False)
        final = final + rotate(sent, "band", 2 * k)
    final = final * (1.0 / (layers * space * plane))

    margin = jnp.zeros((space, own, band * count), jnp.float32)
    margin = lax.dynamic_update_index_in_dim(margin, final, mine_s, 0)
    for k in range(1, space):
        margin = lax.dynamic_update_index_in_dim(margin, rotate(final, "space", k), (mine_s - k) % space, 0)
    return result, margin.reshape(count, band * count)


def solution(mesh):
    return jax.shard_map(
        shards,
        mesh=mesh,
        in_specs=(P("band", "space", None), P("space", None)),
        out_specs=(P("band", "space", None), P("band", None)),
        check_vma=False,
    )
```

time: 225 us -> 184 us (0.82)
  blocking collectives: 85.8 us -> 0 us
  starting transfers between devices: 5.22 us -> 48.1 us
  Pallas kernels: 0 us -> 29.2 us
  between operations: 14.5 us -> 0.98 us
  other arithmetic: 15.5 us -> 3.47 us
  local copies, waits for them, and re-layouts: 21.9 us -> 13.4 us
  waiting for transfers between devices: 76.8 us -> 84 us
    all_to_all x2 -> x0, blocking collectives: 63.1 us -> none  [the longest x1 42.7 us: shards(): lax.all_to_all(flat, 'band', split_axis=1, concat_axis=0, tiled=True)]
    all_to_all x1 -> x9, waiting for transfers between devices: 0.01 us -> 63 us  [the longest x3 44.2 us: shards(): lax.all_to_all(packed, 'band', split_axis=0, concat_axis=0, tiled=True)]
    psum x1 -> x0, waiting for transfers between devices: 43 us -> none  [shards(): whole = lax.psum(partial_sum, 'space')]
    reduce_scatter x1 -> x0, waiting for transfers between devices: 33.7 us -> none  [shards(): rows = lax.psum_scatter(whole, 'band', scatter_dimension=0, tiled=True)]
    all_to_all x1 -> x9, starting transfers between devices: 5.18 us -> 36.5 us  [the longest x3 12.5 us: shards(): lax.all_to_all(filtered, 'space', split_axis=0, concat_axis=0, tiled=True)]
    pallas_call x0 -> x3, Pallas kernels: none -> 29.2 us  [run_filter(): pl.pallas_call(functools.partial(filter_kernel, space, layers, tiles, chu...]
    all_gather x1 -> x0, blocking collectives: 22.6 us -> none  [shards(): whole_potential = lax.all_gather(potential, 'space', axis=0, tiled=True)]
    ppermute x0 -> x10, waiting for transfers between devices: none -> 21 us  [the longest x9 18.1 us: rotate(): return lax.ppermute(x, axis, [(i, (i + step) % size) for i in range(size)])]
  transfers between devices with their start and end apart: 3 -> 19, of which waited for: 2 -> 15; matrix products, arithmetic and copies ran while one was open for 1% -> 5% of each run, Pallas kernels for 0% -> 16%
where the time goes in v1:
time: 184 us; the launch traced here: 183 us
  waiting for transfers between devices  84 us (46%)
  starting transfers between devices  48.1 us (26%)
  Pallas kernels  29.2 us (16%)
  local copies, waits for them, and re-layouts  13.4 us (7%)
  matrix products  3.8 us (2%)
  other arithmetic  3.47 us (2%)
    all_to_all x3, waiting for transfers between devices, shards(): lax.all_to_all(packed, 'band', split_axis=0, concat_axis=0, tiled=True)  44.2 us
    pallas_call x3, Pallas kernels, run_filter(): pl.pallas_call(functools.partial(filter_kernel, space, layers, tiles, chu...  29.2 us
    ppermute x9, waiting for transfers between devices, rotate(): return lax.ppermute(x, axis, [(i, (i + step) % size) for i in range(size)])  18.1 us
    all_to_all x3, waiting for transfers between devices, shards(): got = lax.all_to_all(part, 'space', split_axis=0, concat_axis=0, tiled=True)  13.1 us
    all_to_all x3, starting transfers between devices, shards(): lax.all_to_all(filtered, 'space', split_axis=0, concat_axis=0, tiled=True)  12.5 us
    all_to_all x3, starting transfers between devices, shards(): got = lax.all_to_all(part, 'space', split_axis=0, concat_axis=0, tiled=True)  12.1 us
    all_to_all x3, starting transfers between devices, shards(): lax.all_to_all(packed, 'band', split_axis=0, concat_axis=0, tiled=True)  11.9 us
    ppermute x9, starting transfers between devices, rotate(): return lax.ppermute(x, axis, [(i, (i + step) % size) for i in range(size)])  11.5 us
  transfers between devices with their start and end apart: 19, of which 15 were waited for; matrix products, arithmetic and copies ran while one was open for 5% of the time, Pallas kernels for 16%

profile of v1, /device:TPU:0, one launch (start us, length us, event | category | flops | bytes accessed | tf_op | source)
XLA Modules:
  0.0 183.0 jit_solution(6973994721818189617)
XLA Ops:
  0.6 2.5 %reshape.118 = f32[96,2,16,128]{3,2,1,0:T(8,128)S(1)} reshape(f32[96,2,2048]{2,1,0:T(2,128)} %param.2) | data formatting | bytes 3145728 | tf_op jit(solution)/shard_map/reshape | solution.py:122
  3.2 0.1 copy.62
  3.3 0.2 fusion.6
  3.5 0.2 copy.48
  3.7 1.1 copy.49
  4.8 5.2 %all-to-all-start.2 = ((f32[32,32,128]{2,1,0:T(8,128)}), f32[32,32,128]{2,1,0:T(8,128)S(1)}, u32[]{:S(2)}, u32[]{:S(2)}) async-start(f32[32,32,128]{2,1,0:T(8,128)} %copy.49), calls=%async_computation.2 | async-start | bytes 1048576 | tf_op jit(solution)/shard_map/all_to_all | solution.py:134
  9.9 0.2 copy.44
  10.2 0.1 pad_maximum_fusion.3
  10.2 1.2 copy.46
  11.4 6.5 %all-to-all-done.2 = f32[32,32,128]{2,1,0:T(8,128)S(1)} async-done(((f32[32,32,128]{2,1,0:T(8,128)}), f32[32,32,128]{2,1,0:T(8,128)S(1)}, u32[]{:S(2)}, u32[]{:S(2)}) %all-to-all-start.2) | async-done | bytes 524320 | tf_op jit(solution)/shard_map/all_to_all | solution.py:134
  18.0 3.5 %all-to-all-start = ((f32[36,32,128]{2,1,0:T(8,128)}), f32[36,32,128]{2,1,0:T(8,128)S(1)}, u32[]{:S(2)}, u32[]{:S(2)}) async-start(f32[36,32,128]{2,1,0:T(8,128)} %bitcast.5), calls=%async_computation | async-start | bytes 1179648 | tf_op jit(solution)/shard_map/all_to_all | solution.py:134
  21.4 0.2 copy.51
  21.6 1.1 copy.52
  22.7 6.5 %all-to-all-done = f32[36,32,128]{2,1,0:T(8,128)S(1)} async-done(((f32[36,32,128]{2,1,0:T(8,128)}), f32[36,32,128]{2,1,0:T(8,128)S(1)}, u32[]{:S(2)}, u32[]{:S(2)}) %all-to-all-start) | async-done | bytes 589856 | tf_op jit(solution)/shard_map/all_to_all | solution.py:134
  29.3 3.5 %all-to-all-start.4 = ((f32[32,32,128]{2,1,0:T(8,128)}), f32[32,32,128]{2,1,0:T(8,128)S(1)}, u32[]{:S(2)}, u32[]{:S(2)}) async-start(f32[32,32,128]{2,1,0:T(8,128)} %copy.52), calls=%async_computation.4 | async-start | bytes 1048576 | tf_op jit(solution)/shard_map/all_to_all | solution.py:134
  32.7 9.7 %shard_map.42 = f32[4,32,8,128]{3,2,1,0:T(8,128)} custom-call(f32[1024,128]{1,0:T(8,128)S(1)} %bitcast.105, f32[1152,128]{1,0:T(8,128)S(1)} %bitcast.101), custom_call_target="tpu_custom_call" | custom-call | flops 9830400 | bytes 1048576 | tf_op jit(solution)/shard_map/pallas_call | solution.py:91
  42.5 4.2 %all-to-all-start.3 = ((f32[4,32,8,128]{3,2,1,0:T(8,128)}), f32[4,32,8,128]{3,2,1,0:T(8,128)S(1)}, u32[]{:S(2)}, u32[]{:S(2)}) async-start(f32[4,32,8,128]{3,2,1,0:T(8,128)} %shard_map.42), calls=%async_computation.3 | async-start | bytes 1048576 | tf_op jit(solution)/shard_map/all_to_all | solution.py:139
  46.6 9.7 %shard_map.43 = f32[4,32,8,128]{3,2,1,0:T(8,128)} custom-call(f32[1024,128]{1,0:T(8,128)S(1)} %bitcast.106, f32[1152,128]{1,0:T(8,128)S(1)} %bitcast.102), custom_call_target="tpu_custom_call" | custom-call | flops 9830400 | bytes 1048576 | tf_op jit(solution)/shard_map/pallas_call | solution.py:91
  56.4 4.2 %all-to-all-start.5 = ((f32[4,32,8,128]{3,2,1,0:T(8,128)}), f32[4,32,8,128]{3,2,1,0:T(8,128)S(1)}, u32[]{:S(2)}, u32[]{:S(2)}) async-start(f32[4,32,8,128]{3,2,1,0:T(8,128)} %shard_map.43), calls=%async_computation.5 | async-start | bytes 1048576 | tf_op jit(solution)/shard_map/all_to_all | solution.py:139
  60.6 9.7 %shard_map.41 = f32[4,32,8,128]{3,2,1,0:T(8,128)} custom-call(f32[1152,128]{1,0:T(8,128)S(1)} %bitcast.103, f32[1152,128]{1,0:T(8,128)S(1)} %bitcast.104), custom_call_target="tpu_custom_call" | custom-call | flops 9830400 | bytes 1048576 | tf_op jit(solution)/shard_map/pallas_call | solution.py:91
  70.3 4.2 %all-to-all-start.1 = ((f32[4,32,8,128]{3,2,1,0:T(8,128)}), f32[4,32,8,128]{3,2,1,0:T(8,128)S(1)}, u32[]{:S(2)}, u32[]{:S(2)}) async-start(f32[4,32,8,128]{3,2,1,0:T(8,128)} %shard_map.41), calls=%async_computation.1 | async-start | bytes 1048576 | tf_op jit(solution)/shard_map/all_to_all | solution.py:139
  74.5 0.9 copy.64
  75.3 5.7 %all-to-all-done.1 = f32[4,32,8,128]{3,2,1,0:T(8,128)S(1)} async-done(((f32[4,32,8,128]{3,2,1,0:T(8,128)}), f32[4,32,8,128]{3,2,1,0:T(8,128)S(1)}, u32[]{:S(2)}, u32[]{:S(2)}) %all-to-all-start.1) | async-done | bytes 524320 | tf_op jit(solution)/shard_map/all_to_all | solution.py:139
  81.1 4.9 %all-to-all-start.7 = ((f32[8,4,4,8,128]{4,3,2,1,0:T(8,128)}), f32[8,4,4,8,128]{4,3,2,1,0:T(8,128)S(1)}, u32[]{:S(2)}, u32[]{:S(2)}) async-start(f32[8,4,4,8,128]{4,3,2,1,0:T(8,128)} %bitcast.99), calls=%async_computation.7 | async-start | bytes 1048576 | tf_op jit(solution)/shard_map/all_to_all | solution.py:146
  86.0 0.8 copy.63
  86.8 14.5 %all-to-all-done.7 = f32[8,4,4,8,128]{4,3,2,1,0:T(8,128)S(1)} async-done(((f32[8,4,4,8,128]{4,3,2,1,0:T(8,128)}), f32[8,4,4,8,128]{4,3,2,1,0:T(8,128)S(1)}, u32[]{:S(2)}, u32[]{:S(2)}) %all-to-all-start.7) | async-done | bytes 524320 | tf_op jit(solution)/shard_map/all_to_all | solution.py:146
  101.3 3.5 %all-to-all-start.8 = ((f32[8,4,4,8,128]{4,3,2,1,0:T(8,128)}), f32[8,4,4,8,128]{4,3,2,1,0:T(8,128)S(1)}, u32[]{:S(2)}, u32[]{:S(2)}) async-start(f32[8,4,4,8,128]{4,3,2,1,0:T(8,128)} %bitcast.98), calls=%async_computation.8 | async-start | bytes 1048576 | tf_op jit(solution)/shard_map/all_to_all | solution.py:146
  104.8 0.8 copy.65
  105.7 14.4 %all-to-all-done.8 = f32[8,4,4,8,128]{4,3,2,1,0:T(8,128)S(1)} async-done(((f32[8,4,4,8,128]{4,3,2,1,0:T(8,128)}), f32[8,4,4,8,128]{4,3,2,1,0:T(8,128)S(1)}, u32[]{:S(2)}, u32[]{:S(2)}) %all-to-all-start.8) | async-done | bytes 524320 | tf_op jit(solution)/shard_map/all_to_all | solution.py:146
  120.1 3.5 %all-to-all-start.6 = ((f32[8,4,4,8,128]{4,3,2,1,0:T(8,128)}), f32[8,4,4,8,128]{4,3,2,1,0:T(8,128)S(1)}, u32[]{:S(2)}, u32[]{:S(2)}) async-start(f32[8,4,4,8,128]{4,3,2,1,0:T(8,128)} %bitcast.100), calls=%async_computation.6 | async-start | bytes 1048576 | tf_op jit(solution)/shard_map/all_to_all | solution.py:146
  123.6 15.3 %all-to-all-done.6 = f32[8,4,4,8,128]{4,3,2,1,0:T(8,128)S(1)} async-done(((f32[8,4,4,8,128]{4,3,2,1,0:T(8,128)}), f32[8,4,4,8,128]{4,3,2,1,0:T(8,128)S(1)}, u32[]{:S(2)}, u32[]{:S(2)}) %all-to-all-start.6) | async-done | bytes 524320 | tf_op jit(solution)/shard_map/all_to_all | solution.py:146
  138.9 0.1 pad_maximum_fusion.1
  139.0 0.6 copy-done.4
  139.7 1.0 constant_dynamic-slice_fusion.1
  140.7 1.2 pad_maximum_fusion.2
  141.9 1.1 fusion.7
  143.1 0.1 collective-permute-start
  143.2 2.9 %collective-permute-done = f32[384,768]{1,0:T(8,128)} collective-permute-done((f32[384,768]{1,0:T(8,128)S(1)}, f32[384,768]{1,0:T(8,128)}, u32[]{:S(2)}, u32[]{:S(2)}) %collective-permute-start) | collective-permute-done | bytes 1179680 | tf_op jit(solution)/shard_map/ppermute | solution.py:165
  146.1 2.7 %convolution_add_fusion = f32[384,768]{1,0:T(8,128)S(1)} fusion(f32[384,768]{1,0:T(8,128)} %collective-permute-done, f32[384,512]{1,0:T(8,128)} %bitcast.124, f32[768,512]{1,0:T(8,128)S(1)} %bitcast.108), kind=kOutput, calls=%fused_computation.4 | convolution fusion | flops 906264576 | bytes 4718592 | tf_op jit(solution)/shard_map/dot_general | solution.py:161
  148.8 0.1 dynamic-slice_bitcast_fusion.2
  148.9 1.5 collective-permute-start.1
  150.4 0.6 collective-permute-start.2
  151.0 2.4 %collective-permute-start.3 = (f32[4,24,768]{2,1,0:T(8,128)S(1)}, f32[4,24,768]{2,1,0:T(8,128)S(1)}, u32[]{:S(2)}, u32[]{:S(2)}) collective-permute-start(f32[4,24,768]{2,1,0:T(8,128)S(1)} %get-tuple-element.10), channel_id=1, source_target_pairs={{0,24},{8,0},{16,8},{24,16},{1,25},{9,1},{17,9},{25,17},{2,26},{10... | collective-permute-start | bytes 884744 | tf_op jit(solution)/shard_map/ppermute | solution.py:108
  153.4 6.4 %collective-permute-done.1 = f32[4,24,768]{2,1,0:T(8,128)S(1)} collective-permute-done((f32[4,24,768]{2,1,0:T(8,128)S(1)}, f32[4,24,768]{2,1,0:T(8,128)S(1)}, u32[]{:S(2)}, u32[]{:S(2)}) %collective-permute-start.1) | collective-permute-done | bytes 294944 | tf_op jit(solution)/shard_map/ppermute | solution.py:108
  159.7 5.5 %collective-permute-done.2 = f32[4,24,768]{2,1,0:T(8,128)S(1)} collective-permute-done((f32[4,24,768]{2,1,0:T(8,128)S(1)}, f32[4,24,768]{2,1,0:T(8,128)S(1)}, u32[]{:S(2)}, u32[]{:S(2)}) %collective-permute-start.2) | collective-permute-done | bytes 294944 | tf_op jit(solution)/shard_map/ppermute | solution.py:108
  165.2 0.1 collective-permute-done.3
  165.5 1.8 collective-permute-start.5
  167.3 2.0 %collective-permute-start.6 = (f32[24,768]{1,0:T(8,128)S(1)}, f32[24,768]{1,0:T(8,128)S(1)}, u32[]{:S(2)}, u32[]{:S(2)}) collective-permute-start(f32[24,768]{1,0:T(8,128)S(1)} %get-tuple-element.13), channel_id=1, source_target_pairs={{0,6},{1,7},{2,0},{3,1},{4,2},{5,3},{6,4},{7,5},{8,14},{9,15},{10,... | collective-permute-start | bytes 221192 | tf_op jit(solution)/shard_map/ppermute | solution.py:108
  169.3 0.2 copy.50
  169.5 0.3 reshape.103
  169.7 0.2 copy.53
  169.9 0.3 reshape.106
  170.2 0.3 copy-done.3
  170.5 0.2 copy.47
  170.7 0.3 reshape.100
  170.9 1.5 collective-permute-done.4
  172.4 2.0 %collective-permute-done.5 = f32[24,768]{1,0:T(8,128)S(1)} collective-permute-done((f32[24,768]{1,0:T(8,128)S(1)}, f32[24,768]{1,0:T(8,128)S(1)}, u32[]{:S(2)}, u32[]{:S(2)}) %collective-permute-start.5) | collective-permute-done | bytes 73760 | tf_op jit(solution)/shard_map/ppermute | solution.py:108
  174.5 2.0 %pad_maximum_fusion = f32[96,2,2048]{2,1,0:T(2,128)} fusion(f32[32,2,2048]{2,1,0:T(2,128)S(1)} %reshape.106, f32[32,2,2048]{2,1,0:T(2,128)S(1)} %reshape.103, f32[32,2,2048]{2,1,0:T(2,128)S(1)} %reshape.100), kind=kLoop, calls=%fused_computation | loop fusion | flops 786432 | bytes 3145728 | tf_op jit(solution)/shard_map/concatenate | solution.py:149
  176.5 1.4 collective-permute-start.8
  177.9 1.7 collective-permute-start.9
  179.6 0.6 collective-permute-done.7
  180.2 0.8 collective-permute-done.8
  181.0 1.3 collective-permute-done.9
  182.3 0.7 copy-done.5
  (25 shorter events, 0.4 us)
Async XLA Ops:
  3.7 6.5 %copy-start.6 = (f32[2,2048]{1,0:T(2,128)S(1)}, f32[2,2048]{1,0:T(2,128)}, u32[]{:S(2)}) copy-start(f32[2,2048]{1,0:T(2,128)} %param.3) | copy-start | bytes 49156
  4.8 13.2 %all-to-all-start.2 = ((f32[32,32,128]{2,1,0:T(8,128)}), f32[32,32,128]{2,1,0:T(8,128)S(1)}, u32[]{:S(2)}, u32[]{:S(2)}) async-start(f32[32,32,128]{2,1,0:T(8,128)} %copy.49), calls=%async_computation.2 | async-start | bytes 1048576 | tf_op jit(solution)/shard_map/all_to_all | solution.py:134
  18.0 11.3 %all-to-all-start = ((f32[36,32,128]{2,1,0:T(8,128)}), f32[36,32,128]{2,1,0:T(8,128)S(1)}, u32[]{:S(2)}, u32[]{:S(2)}) async-start(f32[36,32,128]{2,1,0:T(8,128)} %bitcast.5), calls=%async_computation | async-start | bytes 1179648 | tf_op jit(solution)/shard_map/all_to_all | solution.py:134
  29.3 13.2 %all-to-all-start.4 = ((f32[32,32,128]{2,1,0:T(8,128)}), f32[32,32,128]{2,1,0:T(8,128)S(1)}, u32[]{:S(2)}, u32[]{:S(2)}) async-start(f32[32,32,128]{2,1,0:T(8,128)} %copy.52), calls=%async_computation.4 | async-start | bytes 1048576 | tf_op jit(solution)/shard_map/all_to_all | solution.py:134
  42.5 13.9 %all-to-all-start.3 = ((f32[4,32,8,128]{3,2,1,0:T(8,128)}), f32[4,32,8,128]{3,2,1,0:T(8,128)S(1)}, u32[]{:S(2)}, u32[]{:S(2)}) async-start(f32[4,32,8,128]{3,2,1,0:T(8,128)} %shard_map.42), calls=%async_computation.3 | async-start | bytes 1048576 | tf_op jit(solution)/shard_map/all_to_all | solution.py:139
  56.4 13.9 %all-to-all-start.5 = ((f32[4,32,8,128]{3,2,1,0:T(8,128)}), f32[4,32,8,128]{3,2,1,0:T(8,128)S(1)}, u32[]{:S(2)}, u32[]{:S(2)}) async-start(f32[4,32,8,128]{3,2,1,0:T(8,128)} %shard_map.43), calls=%async_computation.5 | async-start | bytes 1048576 | tf_op jit(solution)/shard_map/all_to_all | solution.py:139
  70.3 15.7 %copy-start = (f32[4,32,8,128]{3,2,1,0:T(8,128)}, f32[4,32,8,128]{3,2,1,0:T(8,128)S(1)}, u32[]{:S(2)}) copy-start(f32[4,32,8,128]{3,2,1,0:T(8,128)S(1)} %all-to-all-done.5) | copy-start | bytes 1572868
  70.3 10.8 %all-to-all-start.1 = ((f32[4,32,8,128]{3,2,1,0:T(8,128)}), f32[4,32,8,128]{3,2,1,0:T(8,128)S(1)}, u32[]{:S(2)}, u32[]{:S(2)}) async-start(f32[4,32,8,128]{3,2,1,0:T(8,128)} %shard_map.41), calls=%async_computation.1 | async-start | bytes 1048576 | tf_op jit(solution)/shard_map/all_to_all | solution.py:139
  81.1 23.8 %copy-start.2 = (f32[4,32,8,128]{3,2,1,0:T(8,128)}, f32[4,32,8,128]{3,2,1,0:T(8,128)S(1)}, u32[]{:S(2)}) copy-start(f32[4,32,8,128]{3,2,1,0:T(8,128)S(1)} %all-to-all-done.1) | copy-start | bytes 1572868
  81.1 20.3 %all-to-all-start.7 = ((f32[8,4,4,8,128]{4,3,2,1,0:T(8,128)}), f32[8,4,4,8,128]{4,3,2,1,0:T(8,128)S(1)}, u32[]{:S(2)}, u32[]{:S(2)}) async-start(f32[8,4,4,8,128]{4,3,2,1,0:T(8,128)} %bitcast.99), calls=%async_computation.7 | async-start | bytes 1048576 | tf_op jit(solution)/shard_map/all_to_all | solution.py:146
  101.3 18.8 %all-to-all-start.8 = ((f32[8,4,4,8,128]{4,3,2,1,0:T(8,128)}), f32[8,4,4,8,128]{4,3,2,1,0:T(8,128)S(1)}, u32[]{:S(2)}, u32[]{:S(2)}) async-start(f32[8,4,4,8,128]{4,3,2,1,0:T(8,128)} %bitcast.98), calls=%async_computation.8 | async-start | bytes 1048576 | tf_op jit(solution)/shard_map/all_to_all | solution.py:146
  120.1 18.8 %all-to-all-start.6 = ((f32[8,4,4,8,128]{4,3,2,1,0:T(8,128)}), f32[8,4,4,8,128]{4,3,2,1,0:T(8,128)S(1)}, u32[]{:S(2)}, u32[]{:S(2)}) async-start(f32[8,4,4,8,128]{4,3,2,1,0:T(8,128)} %bitcast.100), calls=%async_computation.6 | async-start | bytes 1048576 | tf_op jit(solution)/shard_map/all_to_all | solution.py:146
  138.9 0.8 copy-start.4
  143.1 3.0 %collective-permute-start = (f32[384,768]{1,0:T(8,128)S(1)}, f32[384,768]{1,0:T(8,128)}, u32[]{:S(2)}, u32[]{:S(2)}) collective-permute-start(f32[384,768]{1,0:T(8,128)S(1)} %fusion.7), channel_id=1, source_target_pairs={{0,1},{1,0},{2,3},{3,2},{4,5},{5,4},{6,7},{7,6},{8,9},{9,8},{10,11... | collective-permute-start | bytes 3538952 | tf_op jit(solution)/shard_map/ppermute | solution.py:165
  148.9 10.8 %collective-permute-start.1 = (f32[4,24,768]{2,1,0:T(8,128)S(1)}, f32[4,24,768]{2,1,0:T(8,128)S(1)}, u32[]{:S(2)}, u32[]{:S(2)}) collective-permute-start(f32[4,24,768]{2,1,0:T(8,128)S(1)} %get-tuple-element.9), channel_id=1, source_target_pairs={{0,8},{8,16},{16,24},{24,0},{1,9},{9,17},{17,25},{25,1},{2,10},{10... | collective-permute-start | bytes 884744 | tf_op jit(solution)/shard_map/ppermute | solution.py:108
  150.4 14.8 %collective-permute-start.2 = (f32[4,24,768]{2,1,0:T(8,128)S(1)}, f32[4,24,768]{2,1,0:T(8,128)S(1)}, u32[]{:S(2)}, u32[]{:S(2)}) collective-permute-start(f32[4,24,768]{2,1,0:T(8,128)S(1)} %get-tuple-element.11), channel_id=1, source_target_pairs={{0,16},{8,24},{16,0},{24,8},{1,17},{9,25},{17,1},{25,9},{2,18},{10... | collective-permute-start | bytes 884744 | tf_op jit(solution)/shard_map/ppermute | solution.py:108
  151.0 14.3 %collective-permute-start.3 = (f32[4,24,768]{2,1,0:T(8,128)S(1)}, f32[4,24,768]{2,1,0:T(8,128)S(1)}, u32[]{:S(2)}, u32[]{:S(2)}) collective-permute-start(f32[4,24,768]{2,1,0:T(8,128)S(1)} %get-tuple-element.10), channel_id=1, source_target_pairs={{0,24},{8,0},{16,8},{24,16},{1,25},{9,1},{17,9},{25,17},{2,26},{10... | collective-permute-start | bytes 884744 | tf_op jit(solution)/shard_map/ppermute | solution.py:108
  165.4 4.4 %copy-start.1 = (f32[4,32,8,128]{3,2,1,0:T(8,128)S(1)}, f32[4,32,8,128]{3,2,1,0:T(8,128)}, u32[]{:S(2)}) copy-start(f32[4,32,8,128]{3,2,1,0:T(8,128)} %copy-done) | copy-start | bytes 1572868
  165.4 7.0 %collective-permute-start.4 = (f32[24,768]{1,0:T(8,128)S(1)}, f32[24,768]{1,0:T(8,128)S(1)}, u32[]{:S(2)}, u32[]{:S(2)}) collective-permute-start(f32[24,768]{1,0:T(8,128)S(1)} %get-tuple-element.12), channel_id=1, source_target_pairs={{0,2},{1,3},{2,4},{3,5},{4,6},{5,7},{6,0},{7,1},{8,10},{9,11},{10,... | collective-permute-start | bytes 221192 | tf_op jit(solution)/shard_map/ppermute | solution.py:108
  165.5 8.9 %collective-permute-start.5 = (f32[24,768]{1,0:T(8,128)S(1)}, f32[24,768]{1,0:T(8,128)S(1)}, u32[]{:S(2)}, u32[]{:S(2)}) collective-permute-start(f32[24,768]{1,0:T(8,128)S(1)} %get-tuple-element.14), channel_id=1, source_target_pairs={{0,4},{1,5},{2,6},{3,7},{4,0},{5,1},{6,2},{7,3},{8,12},{9,13},{10,... | collective-permute-start | bytes 221192 | tf_op jit(solution)/shard_map/ppermute | solution.py:108
  167.3 7.2 %collective-permute-start.6 = (f32[24,768]{1,0:T(8,128)S(1)}, f32[24,768]{1,0:T(8,128)S(1)}, u32[]{:S(2)}, u32[]{:S(2)}) collective-permute-start(f32[24,768]{1,0:T(8,128)S(1)} %get-tuple-element.13), channel_id=1, source_target_pairs={{0,6},{1,7},{2,0},{3,1},{4,2},{5,3},{6,4},{7,5},{8,14},{9,15},{10,... | collective-permute-start | bytes 221192 | tf_op jit(solution)/shard_map/ppermute | solution.py:108
  169.4 1.0 copy-start.3
  174.5 5.7 %collective-permute-start.7 = (f32[24,768]{1,0:T(8,128)S(1)}, f32[24,768]{1,0:T(8,128)S(1)}, u32[]{:S(2)}, u32[]{:S(2)}) collective-permute-start(f32[24,768]{1,0:T(8,128)S(1)} %get-tuple-element.3), channel_id=1, source_target_pairs={{0,8},{8,16},{16,24},{24,0},{1,9},{9,17},{17,25},{25,1},{2,10},{10... | collective-permute-start | bytes 221192 | tf_op jit(solution)/shard_map/ppermute | solution.py:108
  176.5 4.5 %collective-permute-start.8 = (f32[24,768]{1,0:T(8,128)S(1)}, f32[24,768]{1,0:T(8,128)S(1)}, u32[]{:S(2)}, u32[]{:S(2)}) collective-permute-start(f32[24,768]{1,0:T(8,128)S(1)} %get-tuple-element.3), channel_id=1, source_target_pairs={{0,16},{8,24},{16,0},{24,8},{1,17},{9,25},{17,1},{25,9},{2,18},{10... | collective-permute-start | bytes 221192 | tf_op jit(solution)/shard_map/ppermute | solution.py:108
  177.9 4.4 %collective-permute-start.9 = (f32[24,768]{1,0:T(8,128)S(1)}, f32[24,768]{1,0:T(8,128)S(1)}, u32[]{:S(2)}, u32[]{:S(2)}) collective-permute-start(f32[24,768]{1,0:T(8,128)S(1)} %get-tuple-element.3), channel_id=1, source_target_pairs={{0,24},{8,0},{16,8},{24,16},{1,25},{9,1},{17,9},{25,17},{2,26},{10... | collective-permute-start | bytes 221192 | tf_op jit(solution)/shard_map/ppermute | solution.py:108
  182.3 0.7 copy-start.5

commit v2 on v1

v2 whole, which is shorter than its diff:
```python
import functools

import jax
import jax.numpy as jnp
from jax import lax
from jax.experimental import pallas as pl
from jax.experimental.pallas import tpu as pltpu
from jax.sharding import PartitionSpec as P

NZ = 64
LANES = 128
SUBLANES = 8
VMEM_LIMIT = 40 * 1024 * 1024


def unroll_of(tiles):
    return 8 if tiles % 8 == 0 else 1


def filter_kernel(space, layers, tiles, chunk, pitch, offset, planes_unroll, here_ref, x_ref, *refs):
    v_refs, out_refs = refs[:space], refs[space : 2 * space]
    f0, r0, f1, r1, f2, r2, coef = refs[2 * space :]
    planes = space * layers
    rows = tiles * layers
    lane = lax.broadcasted_iota(jnp.int32, (chunk, LANES), 1)
    depth = lane % NZ
    first_half = lane < NZ
    starts = [depth < 1, depth < 2]
    ends = [depth >= NZ - 1, depth >= NZ - 2]
    here = here_ref[0]

    def load(tile, carry):
        for p in range(planes):
            s, l = divmod(p, layers)
            row = tile * layers + l
            slab = here + s
            slab = jnp.where(slab >= space, slab - space, slab)
            v = x_ref[pl.ds((slab * pitch + offset) * rows + row, chunk, stride=rows), :]
            f0[tile, p] = v
            r0[tile, p] = pltpu.roll(v, NZ, 1)
            w = v_refs[s][pl.ds(row, 1), :]
            coef[tile, p] = jnp.broadcast_to(0.25 * w - 0.5625, (chunk, LANES))
        return carry

    def stencil(f, r, tile):
        up = jnp.where(tile == tiles - 1, 0, tile + 1)
        down = jnp.where(tile == 0, tiles - 1, tile - 1)
        v = [f[tile, p] for p in range(planes)]
        pairs = {}

        def pair(a, b):
            key = (min(a, b), max(a, b))
            if key not in pairs:
                pairs[key] = v[a] + v[b]
            return pairs[key]

        out = []
        for p in range(planes):
            rolled = r[tile, p]
            near = pair((p - 1) % planes, (p + 1) % planes)
            far = pair((p - 2) % planes, (p + 2) % planes)
            far = far + (f[up, p] + f[down, p])
            near = near + (rolled + jnp.where(first_half, r[down, p], r[up, p]))
            near = near + pltpu.roll(jnp.where(starts[0], rolled, v[p]), LANES - 1, 1)
            near = near + pltpu.roll(jnp.where(ends[0], rolled, v[p]), 1, 1)
            far = far + pltpu.roll(jnp.where(starts[1], rolled, v[p]), LANES - 2, 1)
            far = far + pltpu.roll(jnp.where(ends[1], rolled, v[p]), 2, 1)
            out.append((v[p], far - 16.0 * near))
        return out

    def first(tile, carry):
        for p, (v, s) in enumerate(stencil(f0, r0, tile)):
            y = (1.0 / 96.0) * s + coef[tile, p] * v
            f1[tile, p] = y
            r1[tile, p] = pltpu.roll(y, NZ, 1)
        return carry

    def second(tile, carry):
        for p, (v, s) in enumerate(stencil(f1, r1, tile)):
            y = 2.0 * ((1.0 / 96.0) * s + coef[tile, p] * v) - f0[tile, p]
            f2[tile, p] = y
            r2[tile, p] = pltpu.roll(y, NZ, 1)
        return carry

    def third(tile, carry):
        for p, (v, s) in enumerate(stencil(f2, r2, tile)):
            y = 2.0 * ((1.0 / 96.0) * s + coef[tile, p] * v) - f1[tile, p]
            out_refs[p // layers][tile * layers + p % layers] = y
        return carry

    for step in (load, first, second, third):
        lax.fori_loop(0, tiles, step, 0, unroll=planes_unroll)


VMEM_SPEC = pl.BlockSpec(memory_space=pltpu.VMEM)
SMEM_SPEC = pl.BlockSpec(memory_space=pltpu.SMEM)


def run_filter(here, x, vs, offset, space, layers, tiles, chunk):
    rows = tiles * layers
    planes = space * layers
    pitch = x.shape[0] // (space * rows)
    field = pltpu.VMEM((tiles, planes, chunk, LANES), jnp.float32)
    unroll = 8 if tiles % 8 == 0 and planes <= 8 else 1
    return pl.pallas_call(
        functools.partial(filter_kernel, space, layers, tiles, chunk, pitch, offset, unroll),
        out_shape=[jax.ShapeDtypeStruct((rows, chunk, LANES), jnp.float32)] * space,
        in_specs=[SMEM_SPEC] + [VMEM_SPEC] * (1 + space),
        out_specs=[VMEM_SPEC] * space,
        scratch_shapes=[field] * 7,
        compiler_params=pltpu.CompilerParams(vmem_limit_bytes=VMEM_LIMIT),
        cost_estimate=pl.CostEstimate(
            flops=75 * planes * tiles * SUBLANES * LANES,
            bytes_accessed=2 * planes * tiles * chunk * LANES * 4,
            transcendentals=0,
        ),
        name="filter",
    )(here, x, *vs)


def pack_kernel(space, band, share, chunk, subs, here_ref, *refs):
    blocks, out = refs[:-1], refs[-1]
    here = here_ref[0]
    for k in range(space):
        group = here - k
        group = jnp.where(group < 0, group + space, group)
        for sub in range(subs):
            first = pl.multiple_of((group * subs + sub) * chunk, chunk)
            block = blocks[k * subs + sub]
            for b in range(band):
                for q in range(share):
                    out[b, pl.ds(first, chunk), q * LANES : (q + 1) * LANES] = block[b * share + q]


def pack(here, blocks, space, band, share, chunk, subs):
    return pl.pallas_call(
        functools.partial(pack_kernel, space, band, share, chunk, subs),
        out_shape=jax.ShapeDtypeStruct((band, space * subs * chunk, share * LANES), jnp.float32),
        in_specs=[SMEM_SPEC] + [VMEM_SPEC] * len(blocks),
        out_specs=VMEM_SPEC,
        compiler_params=pltpu.CompilerParams(vmem_limit_bytes=VMEM_LIMIT),
        cost_estimate=pl.CostEstimate(
            flops=0, bytes_accessed=8 * band * space * subs * chunk * share * LANES, transcendentals=0
        ),
        name="pack",
    )(here, *blocks)


def unpack_kernel(space, rows, chunk, subs_of, here_ref, *refs):
    blocks, out = refs[:-1], refs[-1]
    here = here_ref[0]
    start = 0
    taken = 0
    for subs in subs_of:
        for k in range(space):
            group = here - k
            group = jnp.where(group < 0, group + space, group)
            for sub in range(subs):
                block = blocks[taken + k * subs + sub]
                first = (start + (group * subs + sub) * chunk) * rows
                for row in range(rows):
                    out[pl.ds(first + row, chunk, stride=rows), :] = block[row]
        taken += space * subs
        start += space * subs * chunk


def unpack(here, blocks, space, rows, chunk, subs_of):
    count = sum(subs_of) * space * chunk
    return pl.pallas_call(
        functools.partial(unpack_kernel, space, rows, chunk, subs_of),
        out_shape=jax.ShapeDtypeStruct((count * rows, LANES), jnp.float32),
        in_specs=[SMEM_SPEC] + [VMEM_SPEC] * len(blocks),
        out_specs=VMEM_SPEC,
        compiler_params=pltpu.CompilerParams(vmem_limit_bytes=VMEM_LIMIT),
        cost_estimate=pl.CostEstimate(flops=0, bytes_accessed=8 * count * rows * LANES, transcendentals=0),
        name="unpack",
    )(here, *blocks)


def gram_kernel(band, count, which_ref, *refs):
    parts, out, wide = refs[:-2], refs[-2], refs[-1]
    for b in range(band):
        first = b * count
        for part in parts:
            size = part.shape[1]
            wide[first : first + size, :] = part[b]
            first += size
    which = which_ref[0]
    pairs = band // 2
    picked = [wide[pl.ds(pl.multiple_of((2 * z + which) * count, SUBLANES), count), :] for z in range(pairs)]
    left = jnp.concatenate(picked, axis=0)
    left_hi = left.astype(jnp.bfloat16)
    left_lo = (left - left_hi.astype(jnp.float32)).astype(jnp.bfloat16)
    total = band * count
    step = 256 if total % 256 == 0 else total

    def dot(a, b):
        return lax.dot_general(a, b, (((1,), (1,)), ((), ())), preferred_element_type=jnp.float32)

    for c in range(0, total, step):
        right = wide[c : c + step, :]
        hi = right.astype(jnp.bfloat16)
        lo = (right - hi.astype(jnp.float32)).astype(jnp.bfloat16)
        out[:, c : c + step] = dot(left_hi, hi) + (dot(left_hi, lo) + dot(left_lo, hi))


def gram(which, parts):
    band = parts[0].shape[0]
    count = sum(p.shape[1] for p in parts)
    cells = parts[0].shape[2]
    return pl.pallas_call(
        functools.partial(gram_kernel, band, count),
        out_shape=jax.ShapeDtypeStruct((band // 2 * count, band * count), jnp.float32),
        in_specs=[SMEM_SPEC] + [VMEM_SPEC] * len(parts),
        out_specs=VMEM_SPEC,
        scratch_shapes=[pltpu.VMEM((band * count, cells), jnp.float32)],
        compiler_params=pltpu.CompilerParams(vmem_limit_bytes=VMEM_LIMIT),
        cost_estimate=pl.CostEstimate(
            flops=3 * band * band * count * count * cells,
            bytes_accessed=4 * band * count * (cells + band * count // 2),
            transcendentals=0,
        ),
        name="gram",
    )(which, *parts)


def rotate(x, axis, step):
    size = lax.axis_size(axis)
    return lax.ppermute(x, axis, [(i, (i + step) % size) for i in range(size)])


def shards(orbitals, potential):
    space = lax.axis_size("space")
    band = lax.axis_size("band")
    count, layers, plane = orbitals.shape
    tiles = plane // LANES
    rows = tiles * layers
    share = rows // band
    own = count // space
    chunk = max(c for c in range(1, SUBLANES + 1) if own % c == 0)
    chunks = own // chunk
    groups = [1] if chunks == 1 else [1, chunks - 1]

    s_index = lax.axis_index("space")
    b_index = lax.axis_index("band")
    here = s_index.reshape(1)

    def as_rows(x):
        n = x.shape[0]
        return x.reshape(n, layers, tiles, LANES).transpose(0, 2, 1, 3).reshape(n * rows, LANES)

    arrived = []
    first = 0
    for subs in groups:
        size = space * subs * chunk
        part = orbitals[first : first + size]
        first += size
        arrived.append(as_rows(lax.all_to_all(part, "space", split_axis=0, concat_axis=0, tiled=True)))

    own_v = as_rows(potential[None])
    vs = [own_v] + [rotate(own_v, "space", space - k) for k in range(1, space)]

    all_blocks = []
    parts = []
    for subs, x in zip(groups, arrived):
        made = []
        for sub in range(subs):
            outs = run_filter(here, x, vs, sub * chunk, space, layers, tiles, chunk)
            made.append([outs[0]] + [rotate(outs[k], "space", k) for k in range(1, space)])
        blocks = [made[sub][k] for k in range(space) for sub in range(subs)]
        all_blocks += blocks
        packed = pack(here, blocks, space, band, share, chunk, subs)
        parts.append(lax.all_to_all(packed, "band", split_axis=0, concat_axis=0, tiled=True))

    result = unpack(here, all_blocks, space, rows, chunk, groups)
    result = result.reshape(count, tiles, layers, LANES).transpose(0, 2, 1, 3).reshape(count, layers, plane)

    pairs = band // 2
    core = b_index % 2
    pair = b_index // 2
    other = lax.ppermute(gram((1 - core).reshape(1), parts), "band", [(i, i ^ 1) for i in range(band)])
    total = gram(core.reshape(1), parts) + other
    total = total.reshape(pairs, space, own, band * count)

    mine = lax.dynamic_index_in_dim(total, s_index, 1, keepdims=False)
    for k in range(1, space):
        sent = lax.dynamic_index_in_dim(total, (s_index + k) % space, 1, keepdims=False)
        mine = mine + rotate(sent, "space", k)

    final = lax.dynamic_index_in_dim(mine, pair, 0, keepdims=False)
    for k in range(1, pairs):
        sent = lax.dynamic_index_in_dim(mine, (pair + k) % pairs, 0, keepdims=False)
        final = final + rotate(sent, "band", 2 * k)
    final = final * (1.0 / (layers * space * plane))

    margin = jnp.zeros((space, own, band * count), jnp.float32)
    margin = lax.dynamic_update_index_in_dim(margin, final, s_index, 0)
    for k in range(1, space):
        margin = lax.dynamic_update_index_in_dim(margin, rotate(final, "space", k), (s_index - k) % space, 0)
    return result, margin.reshape(count, band * count)


def solution(mesh):
    return jax.shard_map(
        shards,
        mesh=mesh,
        in_specs=(P("band", "space", None), P("space", None)),
        out_specs=(P("band", "space", None), P("band", None)),
        check_vma=False,
    )
```

time: 184 us -> 154 us (0.84)
  Pallas kernels: 29.2 us -> 20.3 us
  local copies, waits for them, and re-layouts: 13.4 us -> 4.62 us
  matrix products: 3.8 us -> 0 us
  waiting for transfers between devices: 84 us -> 80.2 us
  starting transfers between devices: 48.1 us -> 45.2 us
    ppermute x9 -> x21, waiting for transfers between devices: 18.1 us -> 44.6 us  [rotate(): return lax.ppermute(x, axis, [(i, (i + step) % size) for i in range(size)])]
    all_to_all x3 -> x2, waiting for transfers between devices: 44.2 us -> 26.6 us  [shards(): lax.all_to_all(packed, 'band', split_axis=0, concat_axis=0, tiled=True)]
    pallas_call x3, Pallas kernels: 29.2 us -> 13 us  [run_filter(): pl.pallas_call(functools.partial(filter_kernel, space, layers, tiles, chu...]
    all_to_all x6 -> x2, starting transfers between devices: 24.7 us -> 8.68 us  [shards(): lax.all_to_all(part, 'space', split_axis=0, concat_axis=0, tiled=True)]
    ppermute x9 -> x21, starting transfers between devices: 11.5 us -> 26.9 us  [rotate(): return lax.ppermute(x, axis, [(i, (i + step) % size) for i in range(size)])]
    all_to_all x6 -> x2, waiting for transfers between devices: 18.8 us -> 6.98 us  [shards(): lax.all_to_all(part, 'space', split_axis=0, concat_axis=0, tiled=True)]
    pallas_call x0 -> x5, Pallas kernels: none -> 7.29 us  [the longest x2 3.37 us: gram(): pl.pallas_call(functools.partial(gram_kernel, band, count), out_shape=jax...]
    reshape x8 -> x0, local copies, waits for them, and re-layouts: 6 us -> none  [the longest x2 2.66 us: shards(): orbitals.reshape(count, layers, tiles, LANES).transpose(0, 2, 1, 3)]
  transfers between devices with their start and end apart: 19 -> 26, of which waited for: 15 -> 19; matrix products, arithmetic and copies ran while one was open for 5% -> 1% of each run, Pallas kernels for 16% -> 12%
where the time goes in v2:
time: 154 us
  waiting for transfers between devices  80.2 us (52%)
  starting transfers between devices  45.2 us (29%)
  Pallas kernels  20.3 us (13%)
  local copies, waits for them, and re-layouts  4.62 us (3%)
  other arithmetic  2.65 us (2%)
    ppermute x21, waiting for transfers between devices, rotate(): return lax.ppermute(x, axis, [(i, (i + step) % size) for i in range(size)])  44.6 us
    ppermute x21, starting transfers between devices, rotate(): return lax.ppermute(x, axis, [(i, (i + step) % size) for i in range(size)])  26.9 us
    all_to_all x2, waiting for transfers between devices, shards(): lax.all_to_all(packed, 'band', split_axis=0, concat_axis=0, tiled=True)  26.6 us
    pallas_call x3, Pallas kernels, run_filter(): pl.pallas_call(functools.partial(filter_kernel, space, layers, tiles, chu...  13 us
    all_to_all x2, starting transfers between devices, shards(): lax.all_to_all(packed, 'band', split_axis=0, concat_axis=0, tiled=True)  9.63 us
    all_to_all x2, starting transfers between devices, shards(): lax.all_to_all(part, 'space', split_axis=0, concat_axis=0, tiled=True)  8.68 us
    all_to_all x2, waiting for transfers between devices, shards(): lax.all_to_all(part, 'space', split_axis=0, concat_axis=0, tiled=True)  6.98 us
    pallas_call x2, Pallas kernels, gram(): pl.pallas_call(functools.partial(gram_kernel, band, count), out_shape=jax...  3.37 us
  transfers between devices with their start and end apart: 26, of which 19 were waited for; matrix products, arithmetic and copies ran while one was open for 1% of the time, Pallas kernels for 12%

profile of v2, /device:TPU:0, one launch (start us, length us, event | category | flops | bytes accessed | tf_op | source)
XLA Modules:
  0.0 153.7 jit_solution(13802967200367185668)
XLA Ops:
  0.6 2.0 %slice.6 = f32[32,2,2048]{2,1,0:T(2,128)} slice(f32[96,2,2048]{2,1,0:T(2,128)} %param.2), slice={[0:32], [0:2], [0:2048]} | slice | bytes 1048576 | tf_op jit(solution)/shard_map/slice | solution.py:256
  2.6 5.2 %all-to-all-start = ((f32[32,2,2048]{2,1,0:T(2,128)}), f32[32,2,2048]{2,1,0:T(2,128)S(1)}, u32[]{:S(2)}, u32[]{:S(2)}) async-start(f32[32,2,2048]{2,1,0:T(2,128)} %slice.6), calls=%async_computation | async-start | bytes 1048576 | tf_op jit(solution)/shard_map/all_to_all | solution.py:258
  7.8 1.0 slice.7
  8.8 7.0 %all-to-all-done = f32[32,2,2048]{2,1,0:T(2,128)S(1)} async-done(((f32[32,2,2048]{2,1,0:T(2,128)}), f32[32,2,2048]{2,1,0:T(2,128)S(1)}, u32[]{:S(2)}, u32[]{:S(2)}) %all-to-all-start) | async-done | bytes 524320 | tf_op jit(solution)/shard_map/all_to_all | solution.py:258
  15.8 3.5 %all-to-all-start.1 = ((f32[64,2,2048]{2,1,0:T(2,128)}), f32[64,2,2048]{2,1,0:T(2,128)S(1)}, u32[]{:S(2)}, u32[]{:S(2)}) async-start(f32[64,2,2048]{2,1,0:T(2,128)} %slice.7), calls=%async_computation.1 | async-start | bytes 2097152 | tf_op jit(solution)/shard_map/all_to_all | solution.py:258
  19.3 2.9 %collective-permute-start = (f32[32,128]{1,0:T(8,128)S(1)}, f32[32,128]{1,0:T(8,128)S(1)}, u32[]{:S(2)}, u32[]{:S(2)}) collective-permute-start(f32[32,128]{1,0:T(8,128)S(1)} %bitcast.63), channel_id=1, source_target_pairs={{0,24},{8,0},{16,8},{24,16},{1,25},{9,1},{17,9},{25,17},{2,26},{10... | collective-permute-start | bytes 49160 | tf_op jit(solution)/shard_map/ppermute | solution.py:229
  22.2 0.6 collective-permute-start.1
  22.8 0.6 collective-permute-start.2
  23.4 9.2 %collective-permute-done.refs_1_ = f32[32,128]{1,0:T(8,128)S(1)} collective-permute-done((f32[32,128]{1,0:T(8,128)S(1)}, f32[32,128]{1,0:T(8,128)S(1)}, u32[]{:S(2)}, u32[]{:S(2)}) %collective-permute-start) | collective-permute-done | bytes 16416 | tf_op jit(solution)/shard_map/ppermute | solution.py:229
  32.6 0.0 collective-permute-done.1.refs_2_
  32.6 1.1 collective-permute-done.2.refs_3_
  33.7 4.3 %filter.3 = (f32[32,8,128]{2,1,0:T(8,128)S(1)}, f32[32,8,128]{2,1,0:T(8,128)S(1)}, f32[32,8,128]{2,1,0:T(8,128)S(1)}, f32[32,8,128]{2,1,0:T(8,128)S(1)}) custom-call(s32[1]{0:T(128)} %bitcast.here_ref, f32[1024,128]{1,0:T(8,128)S(1)} %bitcast.62, f32[32,128]{1,0:T(8,128)S(1)} %bitcast.66, f32[32,128]{1,0:T(8,128)S(1)} %collective-permute-done.refs_1_, ...), custom_call_target="tpu_custom_call" | custom-call | flops 9830400 | bytes 1048576 | tf_op jit(solution)/shard_map/filter/pallas_call | solution.py:105
  38.0 0.6 collective-permute-start.3
  38.6 0.6 collective-permute-start.4
  39.2 2.4 %collective-permute-start.5 = (f32[32,8,128]{2,1,0:T(8,128)S(1)}, f32[32,8,128]{2,1,0:T(8,128)S(1)}, u32[]{:S(2)}, u32[]{:S(2)}) collective-permute-start(f32[32,8,128]{2,1,0:T(8,128)S(1)} %get-tuple-element.17), channel_id=1, source_target_pairs={{0,24},{8,0},{16,8},{24,16},{1,25},{9,1},{17,9},{25,17},{2,26},{10... | collective-permute-start | bytes 393224 | tf_op jit(solution)/shard_map/ppermute | solution.py:229
  41.5 2.5 %collective-permute-done.3.refs_1_ = f32[32,8,128]{2,1,0:T(8,128)S(1)} collective-permute-done((f32[32,8,128]{2,1,0:T(8,128)S(1)}, f32[32,8,128]{2,1,0:T(8,128)S(1)}, u32[]{:S(2)}, u32[]{:S(2)}) %collective-permute-start.3) | collective-permute-done | bytes 131104 | tf_op jit(solution)/shard_map/ppermute | solution.py:229
  44.0 0.9 collective-permute-done.4.refs_2_
  45.0 0.0 collective-permute-done.5.refs_3_
  45.0 0.8 pack.2
  45.8 0.0 all-to-all-done.1
  45.8 4.9 %all-to-all-start.2 = ((f32[8,32,512]{2,1,0:T(8,128)}), f32[8,32,512]{2,1,0:T(8,128)S(1)}, u32[]{:S(2)}, u32[]{:S(2)}) async-start(f32[8,32,512]{2,1,0:T(8,128)} %pack.2), calls=%async_computation.2 | async-start | bytes 1048576 | tf_op jit(solution)/shard_map/all_to_all | solution.py:273
  50.7 4.3 %filter.4 = (f32[32,8,128]{2,1,0:T(8,128)S(1)}, f32[32,8,128]{2,1,0:T(8,128)S(1)}, f32[32,8,128]{2,1,0:T(8,128)S(1)}, f32[32,8,128]{2,1,0:T(8,128)S(1)}) custom-call(s32[1]{0:T(128)} %bitcast.here_ref, f32[2048,128]{1,0:T(8,128)S(1)} %bitcast.60, f32[32,128]{1,0:T(8,128)S(1)} %bitcast.67, f32[32,128]{1,0:T(8,128)S(1)} %collective-permute-done.refs_1_, ...), custom_call_target="tpu_custom_call" | custom-call | flops 9830400 | bytes 1048576 | tf_op jit(solution)/shard_map/filter/pallas_call | solution.py:105
  55.0 2.5 %collective-permute-start.10 = (f32[32,8,128]{2,1,0:T(8,128)S(1)}, f32[32,8,128]{2,1,0:T(8,128)S(1)}, u32[]{:S(2)}, u32[]{:S(2)}) collective-permute-start(f32[32,8,128]{2,1,0:T(8,128)S(1)} %get-tuple-element.24), channel_id=1, source_target_pairs={{0,24},{8,0},{16,8},{24,16},{1,25},{9,1},{17,9},{25,17},{2,26},{10... | collective-permute-start | bytes 393224 | tf_op jit(solution)/shard_map/ppermute | solution.py:229
  57.5 4.3 %filter.5 = (f32[32,8,128]{2,1,0:T(8,128)S(1)}, f32[32,8,128]{2,1,0:T(8,128)S(1)}, f32[32,8,128]{2,1,0:T(8,128)S(1)}, f32[32,8,128]{2,1,0:T(8,128)S(1)}) custom-call(s32[1]{0:T(128)} %bitcast.here_ref, f32[2048,128]{1,0:T(8,128)S(1)} %bitcast.61, f32[32,128]{1,0:T(8,128)S(1)} %bitcast.68, f32[32,128]{1,0:T(8,128)S(1)} %collective-permute-done.refs_1_, ...), custom_call_target="tpu_custom_call" | custom-call | flops 9830400 | bytes 1048576 | tf_op jit(solution)/shard_map/filter/pallas_call | solution.py:105
  61.9 0.1 collective-permute-start.11
  61.9 2.0 %collective-permute-start.6 = (f32[32,8,128]{2,1,0:T(8,128)S(1)}, f32[32,8,128]{2,1,0:T(8,128)S(1)}, u32[]{:S(2)}, u32[]{:S(2)}) collective-permute-start(f32[32,8,128]{2,1,0:T(8,128)S(1)} %get-tuple-element.20), channel_id=1, source_target_pairs={{0,8},{8,16},{16,24},{24,0},{1,9},{9,17},{17,25},{25,1},{2,10},{10... | collective-permute-start | bytes 393224 | tf_op jit(solution)/shard_map/ppermute | solution.py:229
  64.0 1.0 collective-permute-start.7
  64.9 0.6 collective-permute-start.8
  65.5 1.5 collective-permute-start.9
  67.0 1.3 collective-permute-done.11.refs_11_.refs_7_
  68.3 3.8 %collective-permute-done.6.refs_6_.refs_2_ = f32[32,8,128]{2,1,0:T(8,128)S(1)} collective-permute-done((f32[32,8,128]{2,1,0:T(8,128)S(1)}, f32[32,8,128]{2,1,0:T(8,128)S(1)}, u32[]{:S(2)}, u32[]{:S(2)}) %collective-permute-start.6) | collective-permute-done | bytes 131104 | tf_op jit(solution)/shard_map/ppermute | solution.py:229
  72.1 2.1 %collective-permute-done.7.refs_7_.refs_3_ = f32[32,8,128]{2,1,0:T(8,128)S(1)} collective-permute-done((f32[32,8,128]{2,1,0:T(8,128)S(1)}, f32[32,8,128]{2,1,0:T(8,128)S(1)}, u32[]{:S(2)}, u32[]{:S(2)}) %collective-permute-start.7) | collective-permute-done | bytes 131104 | tf_op jit(solution)/shard_map/ppermute | solution.py:229
  74.2 2.4 %collective-permute-done.8.refs_8_.refs_4_ = f32[32,8,128]{2,1,0:T(8,128)S(1)} collective-permute-done((f32[32,8,128]{2,1,0:T(8,128)S(1)}, f32[32,8,128]{2,1,0:T(8,128)S(1)}, u32[]{:S(2)}, u32[]{:S(2)}) %collective-permute-start.8) | collective-permute-done | bytes 131104 | tf_op jit(solution)/shard_map/ppermute | solution.py:229
  76.6 1.8 %collective-permute-done.9.refs_9_.refs_5_ = f32[32,8,128]{2,1,0:T(8,128)S(1)} collective-permute-done((f32[32,8,128]{2,1,0:T(8,128)S(1)}, f32[32,8,128]{2,1,0:T(8,128)S(1)}, u32[]{:S(2)}, u32[]{:S(2)}) %collective-permute-start.9) | collective-permute-done | bytes 131104 | tf_op jit(solution)/shard_map/ppermute | solution.py:229
  78.4 1.0 pack.3
  79.5 0.0 all-to-all-done.2.refs_0_
  79.5 4.7 %all-to-all-start.3 = ((f32[8,64,512]{2,1,0:T(8,128)}), f32[8,64,512]{2,1,0:T(8,128)S(1)}, u32[]{:S(2)}, u32[]{:S(2)}) async-start(f32[8,64,512]{2,1,0:T(8,128)} %pack.3), calls=%async_computation.3 | async-start | bytes 2097152 | tf_op jit(solution)/shard_map/all_to_all | solution.py:273
  84.2 26.6 %all-to-all-done.3.refs_1_ = f32[8,64,512]{2,1,0:T(8,128)S(1)} async-done(((f32[8,64,512]{2,1,0:T(8,128)}), f32[8,64,512]{2,1,0:T(8,128)S(1)}, u32[]{:S(2)}, u32[]{:S(2)}) %all-to-all-start.3) | async-done | bytes 1048608 | tf_op jit(solution)/shard_map/all_to_all | solution.py:273
  110.8 2.2 %gram.3 = f32[384,768]{1,0:T(8,128)} custom-call(s32[1]{0:T(128)} %bitcast.18.which_ref, f32[8,32,512]{2,1,0:T(8,128)S(1)} %all-to-all-done.2.refs_0_, f32[8,64,512]{2,1,0:T(8,128)S(1)} %all-to-all-done.3.refs_1_), custom_call_target="tpu_custom_call" | custom-call | flops 905969664 | bytes 2752512 | tf_op jit(solution)/shard_map/gram/pallas_call | solution.py:211
  113.0 0.0 collective-permute-start.12
  113.0 1.2 gram.2
  114.2 2.0 %collective-permute-done.12 = f32[384,768]{1,0:T(8,128)} collective-permute-done((f32[384,768]{1,0:T(8,128)}, f32[384,768]{1,0:T(8,128)}, u32[]{:S(2)}, u32[]{:S(2)}) %collective-permute-start.12) | collective-permute-done | bytes 1179680 | tf_op jit(solution)/shard_map/ppermute | solution.py:281
  116.2 1.4 add.112
  117.6 0.8 dynamic-slice_bitcast_fusion.2
  118.4 0.6 collective-permute-start.14
  119.0 2.9 %collective-permute-start.15 = (f32[4,24,768]{2,1,0:T(8,128)S(1)}, f32[4,24,768]{2,1,0:T(8,128)}, u32[]{:S(2)}, u32[]{:S(2)}) collective-permute-start(f32[4,24,768]{2,1,0:T(8,128)S(1)} %get-tuple-element.29), channel_id=1, source_target_pairs={{0,24},{8,0},{16,8},{24,16},{1,25},{9,1},{17,9},{25,17},{2,26},{10... | collective-permute-start | bytes 884744 | tf_op jit(solution)/shard_map/ppermute | solution.py:229
  121.9 7.6 %collective-permute-done.13 = f32[4,24,768]{2,1,0:T(8,128)} collective-permute-done((f32[4,24,768]{2,1,0:T(8,128)}, f32[4,24,768]{2,1,0:T(8,128)}, u32[]{:S(2)}, u32[]{:S(2)}) %collective-permute-start.13) | collective-permute-done | bytes 294944 | tf_op jit(solution)/shard_map/ppermute | solution.py:229
  129.5 4.4 %collective-permute-done.14 = f32[4,24,768]{2,1,0:T(8,128)} collective-permute-done((f32[4,24,768]{2,1,0:T(8,128)S(1)}, f32[4,24,768]{2,1,0:T(8,128)}, u32[]{:S(2)}, u32[]{:S(2)}) %collective-permute-start.14) | collective-permute-done | bytes 294944 | tf_op jit(solution)/shard_map/ppermute | solution.py:229
  133.9 0.2 collective-permute-done.15
  134.2 1.2 fusion.1
  135.4 0.1 collective-permute-start.16
  135.5 1.8 %collective-permute-start.17 = (f32[24,768]{1,0:T(8,128)S(1)}, f32[24,768]{1,0:T(8,128)S(1)}, u32[]{:S(2)}, u32[]{:S(2)}) collective-permute-start(f32[24,768]{1,0:T(8,128)S(1)} %get-tuple-element.33), channel_id=1, source_target_pairs={{0,4},{1,5},{2,6},{3,7},{4,0},{5,1},{6,2},{7,3},{8,12},{9,13},{10,... | collective-permute-start | bytes 221192 | tf_op jit(solution)/shard_map/ppermute | solution.py:229
  137.3 2.0 %collective-permute-start.18 = (f32[24,768]{1,0:T(8,128)S(1)}, f32[24,768]{1,0:T(8,128)S(1)}, u32[]{:S(2)}, u32[]{:S(2)}) collective-permute-start(f32[24,768]{1,0:T(8,128)S(1)} %get-tuple-element.32), channel_id=1, source_target_pairs={{0,6},{1,7},{2,0},{3,1},{4,2},{5,3},{6,4},{7,5},{8,14},{9,15},{10,... | collective-permute-start | bytes 221192 | tf_op jit(solution)/shard_map/ppermute | solution.py:229
  139.3 3.0 %collective-permute-done.16 = f32[24,768]{1,0:T(8,128)S(1)} collective-permute-done((f32[24,768]{1,0:T(8,128)S(1)}, f32[24,768]{1,0:T(8,128)S(1)}, u32[]{:S(2)}, u32[]{:S(2)}) %collective-permute-start.16) | collective-permute-done | bytes 73760 | tf_op jit(solution)/shard_map/ppermute | solution.py:229
  142.3 1.5 collective-permute-done.17
  143.8 0.0 collective-permute-done.18
  143.9 1.3 collective-permute-start.19
  145.2 2.0 %unpack.1 = f32[3072,128]{1,0:T(8,128)} custom-call(s32[1]{0:T(128)} %bitcast.here_ref, f32[32,8,128]{2,1,0:T(8,128)S(1)} %get-tuple-element.14.refs_0_, f32[32,8,128]{2,1,0:T(8,128)S(1)} %collective-permute-done.3.refs_1_, f32[32,8,128]{2,1,0:T(8,128)S(1)} %collective-permute-done.4.refs_2_, f32[32,8,128]{2,1,0:T(8,128)S(1)} %collective-permute-done.5.refs_3_, ...), custom_call_target="tpu_custom_call" | custom-call | bytes 3145728 | tf_op jit(solution)/shard_map/unpack/pallas_call | solution.py:169
  147.2 1.5 collective-permute-start.20
  148.7 1.7 %collective-permute-start.21 = (f32[24,768]{1,0:T(8,128)S(1)}, f32[24,768]{1,0:T(8,128)S(1)}, u32[]{:S(2)}, u32[]{:S(2)}) collective-permute-start(f32[24,768]{1,0:T(8,128)S(1)} %get-tuple-element.27), channel_id=1, source_target_pairs={{0,24},{8,0},{16,8},{24,16},{1,25},{9,1},{17,9},{25,17},{2,26},{10... | collective-permute-start | bytes 221192 | tf_op jit(solution)/shard_map/ppermute | solution.py:229
  150.4 1.2 collective-permute-done.20
  151.6 1.5 collective-permute-done.21
  153.0 0.0 copy-start.2
  153.0 0.7 copy-done.2
  (13 shorter events, 0.1 us)
Async XLA Ops:
  0.6 7.2 %copy-start.1 = (f32[96,2,2048]{2,1,0:T(2,128)S(1)}, f32[96,2,2048]{2,1,0:T(2,128)}, u32[]{:S(2)}) copy-start(f32[96,2,2048]{2,1,0:T(2,128)} %param.2) | copy-start | bytes 4718596
  2.6 13.2 %all-to-all-start = ((f32[32,2,2048]{2,1,0:T(2,128)}), f32[32,2,2048]{2,1,0:T(2,128)S(1)}, u32[]{:S(2)}, u32[]{:S(2)}) async-start(f32[32,2,2048]{2,1,0:T(2,128)} %slice.6), calls=%async_computation | async-start | bytes 1048576 | tf_op jit(solution)/shard_map/all_to_all | solution.py:258
  8.8 10.5 %copy-start = (f32[2,2048]{1,0:T(2,128)S(1)}, f32[2,2048]{1,0:T(2,128)}, u32[]{:S(2)}) copy-start(f32[2,2048]{1,0:T(2,128)} %param.3) | copy-start | bytes 49156
  15.8 30.0 %all-to-all-start.1 = ((f32[64,2,2048]{2,1,0:T(2,128)}), f32[64,2,2048]{2,1,0:T(2,128)S(1)}, u32[]{:S(2)}, u32[]{:S(2)}) async-start(f32[64,2,2048]{2,1,0:T(2,128)} %slice.7), calls=%async_computation.1 | async-start | bytes 2097152 | tf_op jit(solution)/shard_map/all_to_all | solution.py:258
  19.3 13.2 %collective-permute-start = (f32[32,128]{1,0:T(8,128)S(1)}, f32[32,128]{1,0:T(8,128)S(1)}, u32[]{:S(2)}, u32[]{:S(2)}) collective-permute-start(f32[32,128]{1,0:T(8,128)S(1)} %bitcast.63), channel_id=1, source_target_pairs={{0,24},{8,0},{16,8},{24,16},{1,25},{9,1},{17,9},{25,17},{2,26},{10... | collective-permute-start | bytes 49160 | tf_op jit(solution)/shard_map/ppermute | solution.py:229
  22.2 10.4 %collective-permute-start.1 = (f32[32,128]{1,0:T(8,128)S(1)}, f32[32,128]{1,0:T(8,128)S(1)}, u32[]{:S(2)}, u32[]{:S(2)}) collective-permute-start(f32[32,128]{1,0:T(8,128)S(1)} %bitcast.64), channel_id=1, source_target_pairs={{0,16},{8,24},{16,0},{24,8},{1,17},{9,25},{17,1},{25,9},{2,18},{10... | collective-permute-start | bytes 49160 | tf_op jit(solution)/shard_map/ppermute | solution.py:229
  22.8 10.9 %collective-permute-start.2 = (f32[32,128]{1,0:T(8,128)S(1)}, f32[32,128]{1,0:T(8,128)S(1)}, u32[]{:S(2)}, u32[]{:S(2)}) collective-permute-start(f32[32,128]{1,0:T(8,128)S(1)} %bitcast.65), channel_id=1, source_target_pairs={{0,8},{8,16},{16,24},{24,0},{1,9},{9,17},{17,25},{25,1},{2,10},{10... | collective-permute-start | bytes 49160 | tf_op jit(solution)/shard_map/ppermute | solution.py:229
  38.0 6.0 %collective-permute-start.3 = (f32[32,8,128]{2,1,0:T(8,128)S(1)}, f32[32,8,128]{2,1,0:T(8,128)S(1)}, u32[]{:S(2)}, u32[]{:S(2)}) collective-permute-start(f32[32,8,128]{2,1,0:T(8,128)S(1)} %get-tuple-element.15), channel_id=1, source_target_pairs={{0,8},{8,16},{16,24},{24,0},{1,9},{9,17},{17,25},{25,1},{2,10},{10... | collective-permute-start | bytes 393224 | tf_op jit(solution)/shard_map/ppermute | solution.py:229
  38.6 6.4 %collective-permute-start.4 = (f32[32,8,128]{2,1,0:T(8,128)S(1)}, f32[32,8,128]{2,1,0:T(8,128)S(1)}, u32[]{:S(2)}, u32[]{:S(2)}) collective-permute-start(f32[32,8,128]{2,1,0:T(8,128)S(1)} %get-tuple-element.16), channel_id=1, source_target_pairs={{0,16},{8,24},{16,0},{24,8},{1,17},{9,25},{17,1},{25,9},{2,18},{10... | collective-permute-start | bytes 393224 | tf_op jit(solution)/shard_map/ppermute | solution.py:229
  39.2 5.8 %collective-permute-start.5 = (f32[32,8,128]{2,1,0:T(8,128)S(1)}, f32[32,8,128]{2,1,0:T(8,128)S(1)}, u32[]{:S(2)}, u32[]{:S(2)}) collective-permute-start(f32[32,8,128]{2,1,0:T(8,128)S(1)} %get-tuple-element.17), channel_id=1, source_target_pairs={{0,24},{8,0},{16,8},{24,16},{1,25},{9,1},{17,9},{25,17},{2,26},{10... | collective-permute-start | bytes 393224 | tf_op jit(solution)/shard_map/ppermute | solution.py:229
  45.8 33.7 %all-to-all-start.2 = ((f32[8,32,512]{2,1,0:T(8,128)}), f32[8,32,512]{2,1,0:T(8,128)S(1)}, u32[]{:S(2)}, u32[]{:S(2)}) async-start(f32[8,32,512]{2,1,0:T(8,128)} %pack.2), calls=%async_computation.2 | async-start | bytes 1048576 | tf_op jit(solution)/shard_map/all_to_all | solution.py:273
  55.0 10.5 %collective-permute-start.10 = (f32[32,8,128]{2,1,0:T(8,128)S(1)}, f32[32,8,128]{2,1,0:T(8,128)S(1)}, u32[]{:S(2)}, u32[]{:S(2)}) collective-permute-start(f32[32,8,128]{2,1,0:T(8,128)S(1)} %get-tuple-element.24), channel_id=1, source_target_pairs={{0,24},{8,0},{16,8},{24,16},{1,25},{9,1},{17,9},{25,17},{2,26},{10... | collective-permute-start | bytes 393224 | tf_op jit(solution)/shard_map/ppermute | solution.py:229
  61.9 6.4 %collective-permute-start.11 = (f32[32,8,128]{2,1,0:T(8,128)S(1)}, f32[32,8,128]{2,1,0:T(8,128)S(1)}, u32[]{:S(2)}, u32[]{:S(2)}) collective-permute-start(f32[32,8,128]{2,1,0:T(8,128)S(1)} %get-tuple-element.25), channel_id=1, source_target_pairs={{0,24},{8,0},{16,8},{24,16},{1,25},{9,1},{17,9},{25,17},{2,26},{10... | collective-permute-start | bytes 393224 | tf_op jit(solution)/shard_map/ppermute | solution.py:229
  61.9 10.1 %collective-permute-start.6 = (f32[32,8,128]{2,1,0:T(8,128)S(1)}, f32[32,8,128]{2,1,0:T(8,128)S(1)}, u32[]{:S(2)}, u32[]{:S(2)}) collective-permute-start(f32[32,8,128]{2,1,0:T(8,128)S(1)} %get-tuple-element.20), channel_id=1, source_target_pairs={{0,8},{8,16},{16,24},{24,0},{1,9},{9,17},{17,25},{25,1},{2,10},{10... | collective-permute-start | bytes 393224 | tf_op jit(solution)/shard_map/ppermute | solution.py:229
  64.0 10.2 %collective-permute-start.7 = (f32[32,8,128]{2,1,0:T(8,128)S(1)}, f32[32,8,128]{2,1,0:T(8,128)S(1)}, u32[]{:S(2)}, u32[]{:S(2)}) collective-permute-start(f32[32,8,128]{2,1,0:T(8,128)S(1)} %get-tuple-element.21), channel_id=1, source_target_pairs={{0,8},{8,16},{16,24},{24,0},{1,9},{9,17},{17,25},{25,1},{2,10},{10... | collective-permute-start | bytes 393224 | tf_op jit(solution)/shard_map/ppermute | solution.py:229
  64.9 11.7 %collective-permute-start.8 = (f32[32,8,128]{2,1,0:T(8,128)S(1)}, f32[32,8,128]{2,1,0:T(8,128)S(1)}, u32[]{:S(2)}, u32[]{:S(2)}) collective-permute-start(f32[32,8,128]{2,1,0:T(8,128)S(1)} %get-tuple-element.22), channel_id=1, source_target_pairs={{0,16},{8,24},{16,0},{24,8},{1,17},{9,25},{17,1},{25,9},{2,18},{10... | collective-permute-start | bytes 393224 | tf_op jit(solution)/shard_map/ppermute | solution.py:229
  65.5 12.9 %collective-permute-start.9 = (f32[32,8,128]{2,1,0:T(8,128)S(1)}, f32[32,8,128]{2,1,0:T(8,128)S(1)}, u32[]{:S(2)}, u32[]{:S(2)}) collective-permute-start(f32[32,8,128]{2,1,0:T(8,128)S(1)} %get-tuple-element.23), channel_id=1, source_target_pairs={{0,16},{8,24},{16,0},{24,8},{1,17},{9,25},{17,1},{25,9},{2,18},{10... | collective-permute-start | bytes 393224 | tf_op jit(solution)/shard_map/ppermute | solution.py:229
  79.5 31.3 %all-to-all-start.3 = ((f32[8,64,512]{2,1,0:T(8,128)}), f32[8,64,512]{2,1,0:T(8,128)S(1)}, u32[]{:S(2)}, u32[]{:S(2)}) async-start(f32[8,64,512]{2,1,0:T(8,128)} %pack.3), calls=%async_computation.3 | async-start | bytes 2097152 | tf_op jit(solution)/shard_map/all_to_all | solution.py:273
  113.0 3.2 %collective-permute-start.12 = (f32[384,768]{1,0:T(8,128)}, f32[384,768]{1,0:T(8,128)}, u32[]{:S(2)}, u32[]{:S(2)}) collective-permute-start(f32[384,768]{1,0:T(8,128)} %gram.3), channel_id=1, source_target_pairs={{0,1},{1,0},{2,3},{3,2},{4,5},{5,4},{6,7},{7,6},{8,9},{9,8},{10,11... | collective-permute-start | bytes 3538952 | tf_op jit(solution)/shard_map/ppermute | solution.py:281
  118.4 11.1 %collective-permute-start.13 = (f32[4,24,768]{2,1,0:T(8,128)}, f32[4,24,768]{2,1,0:T(8,128)}, u32[]{:S(2)}, u32[]{:S(2)}) collective-permute-start(f32[4,24,768]{2,1,0:T(8,128)} %get-tuple-element.28), channel_id=1, source_target_pairs={{0,8},{8,16},{16,24},{24,0},{1,9},{9,17},{17,25},{25,1},{2,10},{10... | collective-permute-start | bytes 884744 | tf_op jit(solution)/shard_map/ppermute | solution.py:229
  118.4 15.5 %collective-permute-start.14 = (f32[4,24,768]{2,1,0:T(8,128)S(1)}, f32[4,24,768]{2,1,0:T(8,128)}, u32[]{:S(2)}, u32[]{:S(2)}) collective-permute-start(f32[4,24,768]{2,1,0:T(8,128)S(1)} %get-tuple-element.30), channel_id=1, source_target_pairs={{0,16},{8,24},{16,0},{24,8},{1,17},{9,25},{17,1},{25,9},{2,18},{10... | collective-permute-start | bytes 884744 | tf_op jit(solution)/shard_map/ppermute | solution.py:229
  119.0 15.2 %collective-permute-start.15 = (f32[4,24,768]{2,1,0:T(8,128)S(1)}, f32[4,24,768]{2,1,0:T(8,128)}, u32[]{:S(2)}, u32[]{:S(2)}) collective-permute-start(f32[4,24,768]{2,1,0:T(8,128)S(1)} %get-tuple-element.29), channel_id=1, source_target_pairs={{0,24},{8,0},{16,8},{24,16},{1,25},{9,1},{17,9},{25,17},{2,26},{10... | collective-permute-start | bytes 884744 | tf_op jit(solution)/shard_map/ppermute | solution.py:229
  135.4 6.9 %collective-permute-start.16 = (f32[24,768]{1,0:T(8,128)S(1)}, f32[24,768]{1,0:T(8,128)S(1)}, u32[]{:S(2)}, u32[]{:S(2)}) collective-permute-start(f32[24,768]{1,0:T(8,128)S(1)} %get-tuple-element.31), channel_id=1, source_target_pairs={{0,2},{1,3},{2,4},{3,5},{4,6},{5,7},{6,0},{7,1},{8,10},{9,11},{10,... | collective-permute-start | bytes 221192 | tf_op jit(solution)/shard_map/ppermute | solution.py:229
  135.5 8.4 %collective-permute-start.17 = (f32[24,768]{1,0:T(8,128)S(1)}, f32[24,768]{1,0:T(8,128)S(1)}, u32[]{:S(2)}, u32[]{:S(2)}) collective-permute-start(f32[24,768]{1,0:T(8,128)S(1)} %get-tuple-element.33), channel_id=1, source_target_pairs={{0,4},{1,5},{2,6},{3,7},{4,0},{5,1},{6,2},{7,3},{8,12},{9,13},{10,... | collective-permute-start | bytes 221192 | tf_op jit(solution)/shard_map/ppermute | solution.py:229
  137.3 6.6 %collective-permute-start.18 = (f32[24,768]{1,0:T(8,128)S(1)}, f32[24,768]{1,0:T(8,128)S(1)}, u32[]{:S(2)}, u32[]{:S(2)}) collective-permute-start(f32[24,768]{1,0:T(8,128)S(1)} %get-tuple-element.32), channel_id=1, source_target_pairs={{0,6},{1,7},{2,0},{3,1},{4,2},{5,3},{6,4},{7,5},{8,14},{9,15},{10,... | collective-permute-start | bytes 221192 | tf_op jit(solution)/shard_map/ppermute | solution.py:229
  143.9 6.5 %collective-permute-start.19 = (f32[24,768]{1,0:T(8,128)S(1)}, f32[24,768]{1,0:T(8,128)S(1)}, u32[]{:S(2)}, u32[]{:S(2)}) collective-permute-start(f32[24,768]{1,0:T(8,128)S(1)} %get-tuple-element.27), channel_id=1, source_target_pairs={{0,8},{8,16},{16,24},{24,0},{1,9},{9,17},{17,25},{25,1},{2,10},{10... | collective-permute-start | bytes 221192 | tf_op jit(solution)/shard_map/ppermute | solution.py:229
  147.2 4.4 %collective-permute-start.20 = (f32[24,768]{1,0:T(8,128)S(1)}, f32[24,768]{1,0:T(8,128)S(1)}, u32[]{:S(2)}, u32[]{:S(2)}) collective-permute-start(f32[24,768]{1,0:T(8,128)S(1)} %get-tuple-element.27), channel_id=1, source_target_pairs={{0,16},{8,24},{16,0},{24,8},{1,17},{9,25},{17,1},{25,9},{2,18},{10... | collective-permute-start | bytes 221192 | tf_op jit(solution)/shard_map/ppermute | solution.py:229
  148.7 4.4 %collective-permute-start.21 = (f32[24,768]{1,0:T(8,128)S(1)}, f32[24,768]{1,0:T(8,128)S(1)}, u32[]{:S(2)}, u32[]{:S(2)}) collective-permute-start(f32[24,768]{1,0:T(8,128)S(1)} %get-tuple-element.27), channel_id=1, source_target_pairs={{0,24},{8,0},{16,8},{24,16},{1,25},{9,1},{17,9},{25,17},{2,26},{10... | collective-permute-start | bytes 221192 | tf_op jit(solution)/shard_map/ppermute | solution.py:229
  153.0 0.7 copy-start.2

commit v3 on v2

--- a/solution.py
+++ b/solution.py
@@ -13,13 +13,9 @@
 VMEM_LIMIT = 40 * 1024 * 1024
 
 
-def unroll_of(tiles):
-    return 8 if tiles % 8 == 0 else 1
-
-
-def filter_kernel(space, layers, tiles, chunk, pitch, offset, planes_unroll, here_ref, x_ref, *refs):
-    v_refs, out_refs = refs[:space], refs[space : 2 * space]
-    f0, r0, f1, r1, f2, r2, coef = refs[2 * space :]
+def filter_kernel(space, layers, tiles, chunk, pitch, offset, v_pitch, unroll, here_ref, x_ref, v_ref, *refs):
+    out_refs = refs[:space]
+    f0, r0, f1, r1, f2, r2, coef = refs[space:]
     planes = space * layers
     rows = tiles * layers
     lane = lax.broadcasted_iota(jnp.int32, (chunk, LANES), 1)
@@ -38,7 +34,7 @@
             v = x_ref[pl.ds((slab * pitch + offset) * rows + row, chunk, stride=rows), :]
             f0[tile, p] = v
             r0[tile, p] = pltpu.roll(v, NZ, 1)
-            w = v_refs[s][pl.ds(row, 1), :]
+            w = v_ref[pl.ds((slab * v_pitch + v_pitch - 1) * rows + row, 1), :]
             coef[tile, p] = jnp.broadcast_to(0.25 * w - 0.5625, (chunk, LANES))
         return carry
 
@@ -89,23 +85,24 @@
         return carry
 
     for step in (load, first, second, third):
-        lax.fori_loop(0, tiles, step, 0, unroll=planes_unroll)
+        lax.fori_loop(0, tiles, step, 0, unroll=unroll)
 
 
 VMEM_SPEC = pl.BlockSpec(memory_space=pltpu.VMEM)
 SMEM_SPEC = pl.BlockSpec(memory_space=pltpu.SMEM)
 
 
-def run_filter(here, x, vs, offset, space, layers, tiles, chunk):
+def run_filter(here, x, v, offset, space, layers, tiles, chunk):
     rows = tiles * layers
     planes = space * layers
     pitch = x.shape[0] // (space * rows)
+    v_pitch = v.shape[0] // (space * rows)
     field = pltpu.VMEM((tiles, planes, chunk, LANES), jnp.float32)
     unroll = 8 if tiles % 8 == 0 and planes <= 8 else 1
     return pl.pallas_call(
-        functools.partial(filter_kernel, space, layers, tiles, chunk, pitch, offset, unroll),
+        functools.partial(filter_kernel, space, layers, tiles, chunk, pitch, offset, v_pitch, unroll),
         out_shape=[jax.ShapeDtypeStruct((rows, chunk, LANES), jnp.float32)] * space,
-        in_specs=[SMEM_SPEC] + [VMEM_SPEC] * (1 + space),
+        in_specs=[SMEM_SPEC] + [VMEM_SPEC] * 2,
         out_specs=[VMEM_SPEC] * space,
         scratch_shapes=[field] * 7,
         compiler_params=pltpu.CompilerParams(vmem_limit_bytes=VMEM_LIMIT),
@@ -115,7 +112,7 @@
             transcendentals=0,
         ),
         name="filter",
-    )(here, x, *vs)
+    )(here, x, v)
 
 
 def pack_kernel(space, band, share, chunk, subs, here_ref, *refs):
@@ -177,14 +174,13 @@
     )(here, *blocks)
 
 
-def gram_kernel(band, count, which_ref, *refs):
+def gram_kernel(band, count, space, chunk, places, which_ref, *refs):
     parts, out, wide = refs[:-2], refs[-2], refs[-1]
     for b in range(band):
-        first = b * count
-        for part in parts:
-            size = part.shape[1]
-            wide[first : first + size, :] = part[b]
-            first += size
+        for part, (base, pitch) in zip(parts, places):
+            for g in range(space):
+                first = b * count + base + g * pitch
+                wide[first : first + chunk, :] = part[b, g * chunk : (g + 1) * chunk, :]
     which = which_ref[0]
     pairs = band // 2
     picked = [wide[pl.ds(pl.multiple_of((2 * z + which) * count, SUBLANES), count), :] for z in range(pairs)]
@@ -204,12 +200,12 @@
         out[:, c : c + step] = dot(left_hi, hi) + (dot(left_hi, lo) + dot(left_lo, hi))
 
 
-def gram(which, parts):
+def gram(which, parts, space, chunk, places):
     band = parts[0].shape[0]
     count = sum(p.shape[1] for p in parts)
     cells = parts[0].shape[2]
     return pl.pallas_call(
-        functools.partial(gram_kernel, band, count),
+        functools.partial(gram_kernel, band, count, space, chunk, places),
         out_shape=jax.ShapeDtypeStruct((band // 2 * count, band * count), jnp.float32),
         in_specs=[SMEM_SPEC] + [VMEM_SPEC] * len(parts),
         out_specs=VMEM_SPEC,
@@ -222,6 +218,49 @@
         ),
         name="gram",
     )(which, *parts)
+
+
+def combine_kernel(space, here_ref, a_ref, b_ref, *outs):
+    for k, out in enumerate(outs):
+        group = here_ref[0] + k
+        group = jnp.where(group >= space, group - space, group)
+        for z in range(out.shape[0]):
+            out[z] = a_ref[z, group] + b_ref[z, group]
+
+
+def combine(here, a, b):
+    pairs, space, own, columns = a.shape
+    return pl.pallas_call(
+        functools.partial(combine_kernel, space),
+        out_shape=[jax.ShapeDtypeStruct((pairs, own, columns), jnp.float32)] * space,
+        in_specs=[SMEM_SPEC] + [VMEM_SPEC] * 2,
+        out_specs=[VMEM_SPEC] * space,
+        compiler_params=pltpu.CompilerParams(vmem_limit_bytes=VMEM_LIMIT),
+        cost_estimate=pl.CostEstimate(flops=a.size, bytes_accessed=12 * a.size, transcendentals=0),
+        name="combine",
+    )(here, a, b)
+
+
+def place_kernel(space, here_ref, *refs):
+    parts, out = refs[:-1], refs[-1]
+    for k, part in enumerate(parts):
+        group = here_ref[0] - k
+        group = jnp.where(group < 0, group + space, group)
+        out[group] = part[...]
+
+
+def place(here, parts):
+    space = len(parts)
+    own, columns = parts[0].shape
+    return pl.pallas_call(
+        functools.partial(place_kernel, space),
+        out_shape=jax.ShapeDtypeStruct((space, own, columns), jnp.float32),
+        in_specs=[SMEM_SPEC] + [VMEM_SPEC] * space,
+        out_specs=VMEM_SPEC,
+        compiler_params=pltpu.CompilerParams(vmem_limit_bytes=VMEM_LIMIT),
+        cost_estimate=pl.CostEstimate(flops=0, bytes_accessed=8 * space * own * columns, transcendentals=0),
+        name="place",
+    )(here, *parts)
 
 
 def rotate(x, axis, step):
@@ -249,43 +288,55 @@
         n = x.shape[0]
         return x.reshape(n, layers, tiles, LANES).transpose(0, 2, 1, 3).reshape(n * rows, LANES)
 
-    arrived = []
-    first = 0
-    for subs in groups:
-        size = space * subs * chunk
-        part = orbitals[first : first + size]
-        first += size
-        arrived.append(as_rows(lax.all_to_all(part, "space", split_axis=0, concat_axis=0, tiled=True)))
-
-    own_v = as_rows(potential[None])
-    vs = [own_v] + [rotate(own_v, "space", space - k) for k in range(1, space)]
+    def over_space(x):
+        return lax.all_to_all(x, "space", split_axis=0, concat_axis=0, tiled=True)
+
+    head = orbitals[: space * chunk].reshape(space, chunk, layers, plane)
+    slab_v = jnp.broadcast_to(potential[None, None], (space, 1, layers, plane))
+    head = jnp.concatenate([head, slab_v], axis=1).reshape(space * (chunk + 1), layers, plane)
+    head = over_space(head)
+    arrived = [head]
+    if chunks > 1:
+        head, tail = lax.optimization_barrier((head, orbitals[space * chunk :]))
+        arrived = [head, over_space(tail)]
+    arrived = [as_rows(x) for x in arrived]
 
     all_blocks = []
     parts = []
+    places = []
+    first = 0
     for subs, x in zip(groups, arrived):
         made = []
         for sub in range(subs):
-            outs = run_filter(here, x, vs, sub * chunk, space, layers, tiles, chunk)
-            made.append([outs[0]] + [rotate(outs[k], "space", k) for k in range(1, space)])
-        blocks = [made[sub][k] for k in range(space) for sub in range(subs)]
-        all_blocks += blocks
-        packed = pack(here, blocks, space, band, share, chunk, subs)
-        parts.append(lax.all_to_all(packed, "band", split_axis=0, concat_axis=0, tiled=True))
+            outs = run_filter(here, x, arrived[0], sub * chunk, space, layers, tiles, chunk)
+            blocks = [outs[0]] + [rotate(outs[k], "space", k) for k in range(1, space)]
+            made.append(blocks)
+            packed = pack(here, blocks, space, band, share, chunk, 1)
+            if parts:
+                parts[-1], packed = lax.optimization_barrier((parts[-1], packed))
+            parts.append(lax.all_to_all(packed, "band", split_axis=0, concat_axis=0, tiled=True))
+            places.append((first + sub * chunk, subs * chunk))
+        all_blocks += [made[sub][k] for k in range(space) for sub in range(subs)]
+        first += space * subs * chunk
 
     result = unpack(here, all_blocks, space, rows, chunk, groups)
+    parts[-1], result = lax.optimization_barrier((parts[-1], result))
     result = result.reshape(count, tiles, layers, LANES).transpose(0, 2, 1, 3).reshape(count, layers, plane)
 
     pairs = band // 2
     core = b_index % 2
     pair = b_index // 2
-    other = lax.ppermute(gram((1 - core).reshape(1), parts), "band", [(i, i ^ 1) for i in range(band)])
-    total = gram(core.reshape(1), parts) + other
-    total = total.reshape(pairs, space, own, band * count)
-
-    mine = lax.dynamic_index_in_dim(total, s_index, 1, keepdims=False)
+
+    def half(which):
+        return gram(which.reshape(1), parts, space, chunk, places)
+
+    other = lax.ppermute(half(1 - core), "band", [(i, i ^ 1) for i in range(band)])
+    split = (pairs, space, own, band * count)
+    sums = combine(here, half(core).reshape(split), other.reshape(split))
+
+    mine = sums[0]
     for k in range(1, space):
-        sent = lax.dynamic_index_in_dim(total, (s_index + k) % space, 1, keepdims=False)
-        mine = mine + rotate(sent, "space", k)
+        mine = mine + rotate(sums[k], "space", k)
 
     final = lax.dynamic_index_in_dim(mine, pair, 0, keepdims=False)
     for k in range(1, pairs):
@@ -293,10 +344,7 @@
         final = final + rotate(sent, "band", 2 * k)
     final = final * (1.0 / (layers * space * plane))
 
-    margin = jnp.zeros((space, own, band * count), jnp.float32)
-    margin = lax.dynamic_update_index_in_dim(margin, final, s_index, 0)
-    for k in range(1, space):
-        margin = lax.dynamic_update_index_in_dim(margin, rotate(final, "space", k), (s_index - k) % space, 0)
+    margin = place(here, [final] + [rotate(final, "space", k) for k in range(1, space)])
     return result, margin.reshape(count, band * count)
 
 

time: 154 us -> 140 us (0.909)
  waiting for transfers between devices: 80.2 us -> 64.6 us
  starting transfers between devices: 45.2 us -> 47 us
    all_to_all x2 -> x3, waiting for transfers between devices: 26.6 us -> 12.4 us  [shards(): lax.all_to_all(packed, 'band', split_axis=0, concat_axis=0, tiled=True)]
    all_to_all x2 -> x3, starting transfers between devices: 9.63 us -> 14.4 us  [shards(): lax.all_to_all(packed, 'band', split_axis=0, concat_axis=0, tiled=True)]
    ppermute x21 -> x18, starting transfers between devices: 26.9 us -> 23.9 us  [rotate(): return lax.ppermute(x, axis, [(i, (i + step) % size) for i in range(size)])]
    add x2 -> x1, other arithmetic: 2.62 us -> 0.06 us  [shards(): mine = mine + rotate(sums[k], 'space', k)]
    unnamed x6 -> x14, local copies, waits for them, and re-layouts: 0.72 us -> 2.89 us
    ppermute x21 -> x18, waiting for transfers between devices: 44.6 us -> 42.8 us  [rotate(): return lax.ppermute(x, axis, [(i, (i + step) % size) for i in range(size)])]
    slice x2 -> x3, local copies, waits for them, and re-layouts: 3.03 us -> 1.3 us  [the longest x1 1.04 us: shards(): head, tail = lax.optimization_barrier((head, orbitals[space * chunk:]))]
    pallas_call x2 -> x4, Pallas kernels: 3.37 us -> 3.21 us  [the longest x2 2.35 us: gram(): pl.pallas_call(functools.partial(gram_kernel, band, count, space, chunk,...]
  transfers between devices with their start and end apart: 26 -> 24, of which waited for: 19 -> 16; matrix products, arithmetic and copies ran while one was open for 1% -> 1% of each run, Pallas kernels for 12% -> 13%
where the time goes in v3:
time: 140 us; the launch traced here: 139 us
  waiting for transfers between devices  64.6 us (46%)
  starting transfers between devices  47 us (34%)
  Pallas kernels  20.7 us (15%)
  local copies, waits for them, and re-layouts  5 us (4%)
    ppermute x18, waiting for transfers between devices, rotate(): return lax.ppermute(x, axis, [(i, (i + step) % size) for i in range(size)])  42.8 us
    ppermute x18, starting transfers between devices, rotate(): return lax.ppermute(x, axis, [(i, (i + step) % size) for i in range(size)])  23.9 us
    all_to_all x3, starting transfers between devices, shards(): lax.all_to_all(packed, 'band', split_axis=0, concat_axis=0, tiled=True)  14.4 us
    pallas_call x3, Pallas kernels, run_filter(): pl.pallas_call(functools.partial(filter_kernel, space, layers, tiles, chu...  13 us
    all_to_all x3, waiting for transfers between devices, shards(): lax.all_to_all(packed, 'band', split_axis=0, concat_axis=0, tiled=True)  12.4 us
    all_to_all x2, starting transfers between devices, over_space(): return lax.all_to_all(x, 'space', split_axis=0, concat_axis=0, tiled=True)  8.68 us
    all_to_all x2, waiting for transfers between devices, over_space(): return lax.all_to_all(x, 'space', split_axis=0, concat_axis=0, tiled=True)  7.68 us
    unnamed x14, local copies, waits for them, and re-layouts  2.89 us
  transfers between devices with their start and end apart: 24, of which 16 were waited for; matrix products, arithmetic and copies ran while one was open for 1% of the time, Pallas kernels for 13%

profile of v3, /device:TPU:0, one launch (start us, length us, event | category | flops | bytes accessed | tf_op | source)
XLA Modules:
  0.0 139.4 jit_solution(16719354926238423589)
XLA Ops:
  0.6 0.0 slice-start
  0.6 0.8 broadcast_in_dim.2
  1.4 0.3 slice-done
  1.7 1.2 pad_maximum_fusion
  2.9 5.2 %all-to-all-start = ((f32[36,2,2048]{2,1,0:T(2,128)}), f32[36,2,2048]{2,1,0:T(2,128)S(1)}, u32[]{:S(2)}, u32[]{:S(2)}) async-start(f32[36,2,2048]{2,1,0:T(2,128)} %bitcast.2), calls=%async_computation | async-start | bytes 1179648 | tf_op jit(solution)/shard_map/all_to_all | solution.py:292
  8.1 1.0 slice.7
  9.1 7.7 %all-to-all-done = f32[36,2,2048]{2,1,0:T(2,128)S(1)} async-done(((f32[36,2,2048]{2,1,0:T(2,128)}), f32[36,2,2048]{2,1,0:T(2,128)S(1)}, u32[]{:S(2)}, u32[]{:S(2)}) %all-to-all-start) | async-done | bytes 589856 | tf_op jit(solution)/shard_map/all_to_all | solution.py:292
  16.8 3.5 %all-to-all-start.2 = ((f32[64,2,2048]{2,1,0:T(2,128)}), f32[64,2,2048]{2,1,0:T(2,128)S(1)}, u32[]{:S(2)}, u32[]{:S(2)}) async-start(f32[64,2,2048]{2,1,0:T(2,128)} %slice.7), calls=%async_computation.2 | async-start | bytes 2097152 | tf_op jit(solution)/shard_map/all_to_all | solution.py:292
  20.3 4.3 %filter.3 = (f32[32,8,128]{2,1,0:T(8,128)S(1)}, f32[32,8,128]{2,1,0:T(8,128)S(1)}, f32[32,8,128]{2,1,0:T(8,128)S(1)}, f32[32,8,128]{2,1,0:T(8,128)S(1)}) custom-call(s32[1]{0:T(128)} %bitcast.here_ref, f32[1152,128]{1,0:T(8,128)S(1)} %bitcast.37, f32[1152,128]{1,0:T(8,128)S(1)} %bitcast.38), custom_call_target="tpu_custom_call" | custom-call | flops 9830400 | bytes 1048576 | tf_op jit(solution)/shard_map/filter/pallas_call | solution.py:102
  24.7 2.0 %collective-permute-start = (f32[32,8,128]{2,1,0:T(8,128)S(1)}, f32[32,8,128]{2,1,0:T(8,128)S(1)}, u32[]{:S(2)}, u32[]{:S(2)}) collective-permute-start(f32[32,8,128]{2,1,0:T(8,128)S(1)} %get-tuple-element.28), channel_id=1, source_target_pairs={{0,8},{8,16},{16,24},{24,0},{1,9},{9,17},{17,25},{25,1},{2,10},{10... | collective-permute-start | bytes 393224 | tf_op jit(solution)/shard_map/ppermute | solution.py:268
  26.7 1.5 %collective-permute-start.1 = (f32[32,8,128]{2,1,0:T(8,128)S(1)}, f32[32,8,128]{2,1,0:T(8,128)S(1)}, u32[]{:S(2)}, u32[]{:S(2)}) collective-permute-start(f32[32,8,128]{2,1,0:T(8,128)S(1)} %get-tuple-element.29), channel_id=1, source_target_pairs={{0,16},{8,24},{16,0},{24,8},{1,17},{9,25},{17,1},{25,9},{2,18},{10... | collective-permute-start | bytes 393224 | tf_op jit(solution)/shard_map/ppermute | solution.py:268
  28.2 1.5 %collective-permute-start.2 = (f32[32,8,128]{2,1,0:T(8,128)S(1)}, f32[32,8,128]{2,1,0:T(8,128)S(1)}, u32[]{:S(2)}, u32[]{:S(2)}) collective-permute-start(f32[32,8,128]{2,1,0:T(8,128)S(1)} %get-tuple-element.30), channel_id=1, source_target_pairs={{0,24},{8,0},{16,8},{24,16},{1,25},{9,1},{17,9},{25,17},{2,26},{10... | collective-permute-start | bytes 393224 | tf_op jit(solution)/shard_map/ppermute | solution.py:268
  29.6 8.7 %collective-permute-done.refs_1_ = f32[32,8,128]{2,1,0:T(8,128)S(1)} collective-permute-done((f32[32,8,128]{2,1,0:T(8,128)S(1)}, f32[32,8,128]{2,1,0:T(8,128)S(1)}, u32[]{:S(2)}, u32[]{:S(2)}) %collective-permute-start) | collective-permute-done | bytes 131104 | tf_op jit(solution)/shard_map/ppermute | solution.py:268
  38.4 0.4 collective-permute-done.1.refs_2_
  38.7 0.0 collective-permute-done.2.refs_3_
  38.7 0.8 pack.3
  39.6 0.0 all-to-all-done.2
  39.6 4.9 %all-to-all-start.1 = ((f32[8,32,512]{2,1,0:T(8,128)}), f32[8,32,512]{2,1,0:T(8,128)S(1)}, u32[]{:S(2)}, u32[]{:S(2)}) async-start(f32[8,32,512]{2,1,0:T(8,128)} %pack.3), calls=%async_computation.1 | async-start | bytes 1048576 | tf_op jit(solution)/shard_map/all_to_all | solution.py:317
  44.5 4.3 %filter.4 = (f32[32,8,128]{2,1,0:T(8,128)S(1)}, f32[32,8,128]{2,1,0:T(8,128)S(1)}, f32[32,8,128]{2,1,0:T(8,128)S(1)}, f32[32,8,128]{2,1,0:T(8,128)S(1)}) custom-call(s32[1]{0:T(128)} %bitcast.here_ref, f32[2048,128]{1,0:T(8,128)S(1)} %bitcast.41, f32[1152,128]{1,0:T(8,128)S(1)} %bitcast.39), custom_call_target="tpu_custom_call" | custom-call | flops 9830400 | bytes 1048576 | tf_op jit(solution)/shard_map/filter/pallas_call | solution.py:102
  48.8 1.5 %collective-permute-start.3 = (f32[32,8,128]{2,1,0:T(8,128)S(1)}, f32[32,8,128]{2,1,0:T(8,128)S(1)}, u32[]{:S(2)}, u32[]{:S(2)}) collective-permute-start(f32[32,8,128]{2,1,0:T(8,128)S(1)} %get-tuple-element.33), channel_id=1, source_target_pairs={{0,8},{8,16},{16,24},{24,0},{1,9},{9,17},{17,25},{25,1},{2,10},{10... | collective-permute-start | bytes 393224 | tf_op jit(solution)/shard_map/ppermute | solution.py:268
  50.3 0.5 collective-permute-start.4
  50.8 2.4 %collective-permute-start.5 = (f32[32,8,128]{2,1,0:T(8,128)S(1)}, f32[32,8,128]{2,1,0:T(8,128)S(1)}, u32[]{:S(2)}, u32[]{:S(2)}) collective-permute-start(f32[32,8,128]{2,1,0:T(8,128)S(1)} %get-tuple-element.35), channel_id=1, source_target_pairs={{0,24},{8,0},{16,8},{24,16},{1,25},{9,1},{17,9},{25,17},{2,26},{10... | collective-permute-start | bytes 393224 | tf_op jit(solution)/shard_map/ppermute | solution.py:268
  53.2 2.8 %collective-permute-done.3.refs_1_.refs_6_ = f32[32,8,128]{2,1,0:T(8,128)S(1)} collective-permute-done((f32[32,8,128]{2,1,0:T(8,128)S(1)}, f32[32,8,128]{2,1,0:T(8,128)S(1)}, u32[]{:S(2)}, u32[]{:S(2)}) %collective-permute-start.3) | collective-permute-done | bytes 131104 | tf_op jit(solution)/shard_map/ppermute | solution.py:268
  56.1 2.4 %collective-permute-done.4.refs_2_.refs_8_ = f32[32,8,128]{2,1,0:T(8,128)S(1)} collective-permute-done((f32[32,8,128]{2,1,0:T(8,128)S(1)}, f32[32,8,128]{2,1,0:T(8,128)S(1)}, u32[]{:S(2)}, u32[]{:S(2)}) %collective-permute-start.4) | collective-permute-done | bytes 131104 | tf_op jit(solution)/shard_map/ppermute | solution.py:268
  58.5 0.0 collective-permute-done.5.refs_3_.refs_10_
  58.5 0.8 pack.4
  59.4 0.7 copy-done
  60.0 0.7 copy-done.2
  60.7 4.7 %all-to-all-start.3 = ((f32[8,32,512]{2,1,0:T(8,128)}), f32[8,32,512]{2,1,0:T(8,128)S(1)}, u32[]{:S(2)}, u32[]{:S(2)}) async-start(f32[8,32,512]{2,1,0:T(8,128)} %pack.4), calls=%async_computation.3 | async-start | bytes 1048576 | tf_op jit(solution)/shard_map/all_to_all | solution.py:317
  65.4 4.3 %filter.5 = (f32[32,8,128]{2,1,0:T(8,128)S(1)}, f32[32,8,128]{2,1,0:T(8,128)S(1)}, f32[32,8,128]{2,1,0:T(8,128)S(1)}, f32[32,8,128]{2,1,0:T(8,128)S(1)}) custom-call(s32[1]{0:T(128)} %bitcast.here_ref, f32[2048,128]{1,0:T(8,128)S(1)} %bitcast.42, f32[1152,128]{1,0:T(8,128)S(1)} %bitcast.40), custom_call_target="tpu_custom_call" | custom-call | flops 9830400 | bytes 1048576 | tf_op jit(solution)/shard_map/filter/pallas_call | solution.py:102
  69.8 1.8 %collective-permute-start.6 = (f32[32,8,128]{2,1,0:T(8,128)S(1)}, f32[32,8,128]{2,1,0:T(8,128)S(1)}, u32[]{:S(2)}, u32[]{:S(2)}) collective-permute-start(f32[32,8,128]{2,1,0:T(8,128)S(1)} %get-tuple-element.38), channel_id=1, source_target_pairs={{0,8},{8,16},{16,24},{24,0},{1,9},{9,17},{17,25},{25,1},{2,10},{10... | collective-permute-start | bytes 393224 | tf_op jit(solution)/shard_map/ppermute | solution.py:268
  71.5 0.6 collective-permute-start.7
  72.1 1.4 %collective-permute-start.8 = (f32[32,8,128]{2,1,0:T(8,128)S(1)}, f32[32,8,128]{2,1,0:T(8,128)S(1)}, u32[]{:S(2)}, u32[]{:S(2)}) collective-permute-start(f32[32,8,128]{2,1,0:T(8,128)S(1)} %get-tuple-element.40), channel_id=1, source_target_pairs={{0,24},{8,0},{16,8},{24,16},{1,25},{9,1},{17,9},{25,17},{2,26},{10... | collective-permute-start | bytes 393224 | tf_op jit(solution)/shard_map/ppermute | solution.py:268
  73.5 3.5 %collective-permute-done.6.refs_1_.refs_7_ = f32[32,8,128]{2,1,0:T(8,128)S(1)} collective-permute-done((f32[32,8,128]{2,1,0:T(8,128)S(1)}, f32[32,8,128]{2,1,0:T(8,128)S(1)}, u32[]{:S(2)}, u32[]{:S(2)}) %collective-permute-start.6) | collective-permute-done | bytes 131104 | tf_op jit(solution)/shard_map/ppermute | solution.py:268
  77.1 2.4 %collective-permute-done.7.refs_2_.refs_9_ = f32[32,8,128]{2,1,0:T(8,128)S(1)} collective-permute-done((f32[32,8,128]{2,1,0:T(8,128)S(1)}, f32[32,8,128]{2,1,0:T(8,128)S(1)}, u32[]{:S(2)}, u32[]{:S(2)}) %collective-permute-start.7) | collective-permute-done | bytes 131104 | tf_op jit(solution)/shard_map/ppermute | solution.py:268
  79.5 0.8 pack.5
  80.3 0.7 copy-done.4
  80.9 4.7 %all-to-all-start.4 = ((f32[8,32,512]{2,1,0:T(8,128)}), f32[8,32,512]{2,1,0:T(8,128)S(1)}, u32[]{:S(2)}, u32[]{:S(2)}) async-start(f32[8,32,512]{2,1,0:T(8,128)} %pack.5), calls=%async_computation.4 | async-start | bytes 1048576 | tf_op jit(solution)/shard_map/all_to_all | solution.py:317
  85.7 0.0 copy-start.5
  85.7 0.9 copy-done.5
  86.6 2.0 %unpack.1 = f32[3072,128]{1,0:T(8,128)} custom-call(s32[1]{0:T(128)} %bitcast.here_ref, f32[32,8,128]{2,1,0:T(8,128)S(1)} %get-tuple-element.27.refs_0_, f32[32,8,128]{2,1,0:T(8,128)S(1)} %collective-permute-done.refs_1_, f32[32,8,128]{2,1,0:T(8,128)S(1)} %collective-permute-done.1.refs_2_, f32[32,8,128]{2,1,0:T(8,128)S(1)} %collective-permute-done.2.refs_3_, ...), custom_call_target="tpu_custom_call" | custom-call | bytes 3145728 | tf_op jit(solution)/shard_map/unpack/pallas_call | solution.py:166
  88.6 12.4 %all-to-all-done.4.refs_2_ = f32[8,32,512]{2,1,0:T(8,128)S(1)} async-done(((f32[8,32,512]{2,1,0:T(8,128)}), f32[8,32,512]{2,1,0:T(8,128)S(1)}, u32[]{:S(2)}, u32[]{:S(2)}) %all-to-all-start.4) | async-done | bytes 524320 | tf_op jit(solution)/shard_map/all_to_all | solution.py:317
  101.0 1.2 gram.3
  102.2 0.1 collective-permute-start.9
  102.3 1.2 gram.2
  103.5 1.6 %collective-permute-done.9 = f32[384,768]{1,0:T(8,128)S(1)} collective-permute-done((f32[384,768]{1,0:T(8,128)S(1)}, f32[384,768]{1,0:T(8,128)S(1)}, u32[]{:S(2)}, u32[]{:S(2)}) %collective-permute-start.9) | collective-permute-done | bytes 1179680 | tf_op jit(solution)/shard_map/ppermute | solution.py:333
  105.1 0.1 combine.1
  105.3 1.1 collective-permute-start.10
  106.4 1.3 collective-permute-start.11
  107.6 1.4 collective-permute-start.12
  109.0 7.1 %collective-permute-done.10 = f32[4,24,768]{2,1,0:T(8,128)S(1)} collective-permute-done((f32[4,24,768]{2,1,0:T(8,128)S(1)}, f32[4,24,768]{2,1,0:T(8,128)S(1)}, u32[]{:S(2)}, u32[]{:S(2)}) %collective-permute-start.10) | collective-permute-done | bytes 294944 | tf_op jit(solution)/shard_map/ppermute | solution.py:268
  116.1 5.3 %collective-permute-done.11 = f32[4,24,768]{2,1,0:T(8,128)S(1)} collective-permute-done((f32[4,24,768]{2,1,0:T(8,128)S(1)}, f32[4,24,768]{2,1,0:T(8,128)S(1)}, u32[]{:S(2)}, u32[]{:S(2)}) %collective-permute-start.11) | collective-permute-done | bytes 294944 | tf_op jit(solution)/shard_map/ppermute | solution.py:268
  121.4 0.1 add_add_fusion
  121.5 0.1 collective-permute-start.13
  121.6 3.8 %collective-permute-start.15 = (f32[24,768]{1,0:T(8,128)S(1)}, f32[24,768]{1,0:T(8,128)S(1)}, u32[]{:S(2)}, u32[]{:S(2)}) collective-permute-start(f32[24,768]{1,0:T(8,128)S(1)} %get-tuple-element.51), channel_id=1, source_target_pairs={{0,6},{1,7},{2,0},{3,1},{4,2},{5,3},{6,4},{7,5},{8,14},{9,15},{10,... | collective-permute-start | bytes 221192 | tf_op jit(solution)/shard_map/ppermute | solution.py:268
  125.4 3.2 %collective-permute-done.13 = f32[24,768]{1,0:T(8,128)S(1)} collective-permute-done((f32[24,768]{1,0:T(8,128)S(1)}, f32[24,768]{1,0:T(8,128)S(1)}, u32[]{:S(2)}, u32[]{:S(2)}) %collective-permute-start.13) | collective-permute-done | bytes 73760 | tf_op jit(solution)/shard_map/ppermute | solution.py:268
  128.6 2.8 %collective-permute-done.14 = f32[24,768]{1,0:T(8,128)S(1)} collective-permute-done((f32[24,768]{1,0:T(8,128)S(1)}, f32[24,768]{1,0:T(8,128)S(1)}, u32[]{:S(2)}, u32[]{:S(2)}) %collective-permute-start.14) | collective-permute-done | bytes 73760 | tf_op jit(solution)/shard_map/ppermute | solution.py:268
  131.4 1.2 collective-permute-start.18
  132.6 0.8 collective-permute-start.17
  133.4 1.1 collective-permute-start.16
  134.5 1.3 collective-permute-done.18.refs_3_
  135.8 1.2 collective-permute-done.17.refs_2_
  137.0 1.7 %collective-permute-done.16.refs_1_ = f32[24,768]{1,0:T(8,128)S(1)} collective-permute-done((f32[24,768]{1,0:T(8,128)S(1)}, f32[24,768]{1,0:T(8,128)S(1)}, u32[]{:S(2)}, u32[]{:S(2)}) %collective-permute-start.16) | collective-permute-done | bytes 73760 | tf_op jit(solution)/shard_map/ppermute | solution.py:268
  138.6 0.7 place.1
  (17 shorter events, 0.1 us)
Async XLA Ops:
  0.6 1.1 slice-start
  1.7 6.4 %copy-start.6 = (f32[96,2,2048]{2,1,0:T(2,128)S(1)}, f32[96,2,2048]{2,1,0:T(2,128)}, u32[]{:S(2)}) copy-start(f32[96,2,2048]{2,1,0:T(2,128)} %param.2) | copy-start | bytes 4718596
  2.9 13.9 %all-to-all-start = ((f32[36,2,2048]{2,1,0:T(2,128)}), f32[36,2,2048]{2,1,0:T(2,128)S(1)}, u32[]{:S(2)}, u32[]{:S(2)}) async-start(f32[36,2,2048]{2,1,0:T(2,128)} %bitcast.2), calls=%async_computation | async-start | bytes 1179648 | tf_op jit(solution)/shard_map/all_to_all | solution.py:292
  16.8 22.8 %all-to-all-start.2 = ((f32[64,2,2048]{2,1,0:T(2,128)}), f32[64,2,2048]{2,1,0:T(2,128)S(1)}, u32[]{:S(2)}, u32[]{:S(2)}) async-start(f32[64,2,2048]{2,1,0:T(2,128)} %slice.7), calls=%async_computation.2 | async-start | bytes 2097152 | tf_op jit(solution)/shard_map/all_to_all | solution.py:292
  24.7 13.7 %collective-permute-start = (f32[32,8,128]{2,1,0:T(8,128)S(1)}, f32[32,8,128]{2,1,0:T(8,128)S(1)}, u32[]{:S(2)}, u32[]{:S(2)}) collective-permute-start(f32[32,8,128]{2,1,0:T(8,128)S(1)} %get-tuple-element.28), channel_id=1, source_target_pairs={{0,8},{8,16},{16,24},{24,0},{1,9},{9,17},{17,25},{25,1},{2,10},{10... | collective-permute-start | bytes 393224 | tf_op jit(solution)/shard_map/ppermute | solution.py:268
  26.7 12.0 %collective-permute-start.1 = (f32[32,8,128]{2,1,0:T(8,128)S(1)}, f32[32,8,128]{2,1,0:T(8,128)S(1)}, u32[]{:S(2)}, u32[]{:S(2)}) collective-permute-start(f32[32,8,128]{2,1,0:T(8,128)S(1)} %get-tuple-element.29), channel_id=1, source_target_pairs={{0,16},{8,24},{16,0},{24,8},{1,17},{9,25},{17,1},{25,9},{2,18},{10... | collective-permute-start | bytes 393224 | tf_op jit(solution)/shard_map/ppermute | solution.py:268
  28.2 10.6 %collective-permute-start.2 = (f32[32,8,128]{2,1,0:T(8,128)S(1)}, f32[32,8,128]{2,1,0:T(8,128)S(1)}, u32[]{:S(2)}, u32[]{:S(2)}) collective-permute-start(f32[32,8,128]{2,1,0:T(8,128)S(1)} %get-tuple-element.30), channel_id=1, source_target_pairs={{0,24},{8,0},{16,8},{24,16},{1,25},{9,1},{17,9},{25,17},{2,26},{10... | collective-permute-start | bytes 393224 | tf_op jit(solution)/shard_map/ppermute | solution.py:268
  39.6 21.1 %all-to-all-start.1 = ((f32[8,32,512]{2,1,0:T(8,128)}), f32[8,32,512]{2,1,0:T(8,128)S(1)}, u32[]{:S(2)}, u32[]{:S(2)}) async-start(f32[8,32,512]{2,1,0:T(8,128)} %pack.3), calls=%async_computation.1 | async-start | bytes 1048576 | tf_op jit(solution)/shard_map/all_to_all | solution.py:317
  48.8 7.3 %collective-permute-start.3 = (f32[32,8,128]{2,1,0:T(8,128)S(1)}, f32[32,8,128]{2,1,0:T(8,128)S(1)}, u32[]{:S(2)}, u32[]{:S(2)}) collective-permute-start(f32[32,8,128]{2,1,0:T(8,128)S(1)} %get-tuple-element.33), channel_id=1, source_target_pairs={{0,8},{8,16},{16,24},{24,0},{1,9},{9,17},{17,25},{25,1},{2,10},{10... | collective-permute-start | bytes 393224 | tf_op jit(solution)/shard_map/ppermute | solution.py:268
  50.3 8.2 %collective-permute-start.4 = (f32[32,8,128]{2,1,0:T(8,128)S(1)}, f32[32,8,128]{2,1,0:T(8,128)S(1)}, u32[]{:S(2)}, u32[]{:S(2)}) collective-permute-start(f32[32,8,128]{2,1,0:T(8,128)S(1)} %get-tuple-element.34), channel_id=1, source_target_pairs={{0,16},{8,24},{16,0},{24,8},{1,17},{9,25},{17,1},{25,9},{2,18},{10... | collective-permute-start | bytes 393224 | tf_op jit(solution)/shard_map/ppermute | solution.py:268
  50.8 7.7 %collective-permute-start.5 = (f32[32,8,128]{2,1,0:T(8,128)S(1)}, f32[32,8,128]{2,1,0:T(8,128)S(1)}, u32[]{:S(2)}, u32[]{:S(2)}) collective-permute-start(f32[32,8,128]{2,1,0:T(8,128)S(1)} %get-tuple-element.35), channel_id=1, source_target_pairs={{0,24},{8,0},{16,8},{24,16},{1,25},{9,1},{17,9},{25,17},{2,26},{10... | collective-permute-start | bytes 393224 | tf_op jit(solution)/shard_map/ppermute | solution.py:268
  59.4 0.7 copy-start
  60.0 0.7 copy-start.2
  60.7 20.3 %all-to-all-start.3 = ((f32[8,32,512]{2,1,0:T(8,128)}), f32[8,32,512]{2,1,0:T(8,128)S(1)}, u32[]{:S(2)}, u32[]{:S(2)}) async-start(f32[8,32,512]{2,1,0:T(8,128)} %pack.4), calls=%async_computation.3 | async-start | bytes 1048576 | tf_op jit(solution)/shard_map/all_to_all | solution.py:317
  69.8 15.9 %copy-start.1 = (f32[32,8,128]{2,1,0:T(8,128)S(1)}, f32[32,8,128]{2,1,0:T(8,128)}, u32[]{:S(2)}) copy-start(f32[32,8,128]{2,1,0:T(8,128)} %copy-done) | copy-start | bytes 393220
  69.8 15.9 %copy-start.3 = (f32[32,8,128]{2,1,0:T(8,128)S(1)}, f32[32,8,128]{2,1,0:T(8,128)}, u32[]{:S(2)}) copy-start(f32[32,8,128]{2,1,0:T(8,128)} %copy-done.2) | copy-start | bytes 393220
  69.8 7.3 %collective-permute-start.6 = (f32[32,8,128]{2,1,0:T(8,128)S(1)}, f32[32,8,128]{2,1,0:T(8,128)S(1)}, u32[]{:S(2)}, u32[]{:S(2)}) collective-permute-start(f32[32,8,128]{2,1,0:T(8,128)S(1)} %get-tuple-element.38), channel_id=1, source_target_pairs={{0,8},{8,16},{16,24},{24,0},{1,9},{9,17},{17,25},{25,1},{2,10},{10... | collective-permute-start | bytes 393224 | tf_op jit(solution)/shard_map/ppermute | solution.py:268
  71.5 7.9 %collective-permute-start.7 = (f32[32,8,128]{2,1,0:T(8,128)S(1)}, f32[32,8,128]{2,1,0:T(8,128)S(1)}, u32[]{:S(2)}, u32[]{:S(2)}) collective-permute-start(f32[32,8,128]{2,1,0:T(8,128)S(1)} %get-tuple-element.39), channel_id=1, source_target_pairs={{0,16},{8,24},{16,0},{24,8},{1,17},{9,25},{17,1},{25,9},{2,18},{10... | collective-permute-start | bytes 393224 | tf_op jit(solution)/shard_map/ppermute | solution.py:268
  72.1 7.4 %collective-permute-start.8 = (f32[32,8,128]{2,1,0:T(8,128)S(1)}, f32[32,8,128]{2,1,0:T(8,128)S(1)}, u32[]{:S(2)}, u32[]{:S(2)}) collective-permute-start(f32[32,8,128]{2,1,0:T(8,128)S(1)} %get-tuple-element.40), channel_id=1, source_target_pairs={{0,24},{8,0},{16,8},{24,16},{1,25},{9,1},{17,9},{25,17},{2,26},{10... | collective-permute-start | bytes 393224 | tf_op jit(solution)/shard_map/ppermute | solution.py:268
  80.3 0.7 copy-start.4
  80.9 20.1 %all-to-all-start.4 = ((f32[8,32,512]{2,1,0:T(8,128)}), f32[8,32,512]{2,1,0:T(8,128)S(1)}, u32[]{:S(2)}, u32[]{:S(2)}) async-start(f32[8,32,512]{2,1,0:T(8,128)} %pack.5), calls=%async_computation.4 | async-start | bytes 1048576 | tf_op jit(solution)/shard_map/all_to_all | solution.py:317
  85.7 0.9 copy-start.5
  102.2 2.9 %collective-permute-start.9 = (f32[384,768]{1,0:T(8,128)S(1)}, f32[384,768]{1,0:T(8,128)S(1)}, u32[]{:S(2)}, u32[]{:S(2)}) collective-permute-start(f32[384,768]{1,0:T(8,128)S(1)} %gram.3), channel_id=1, source_target_pairs={{0,1},{1,0},{2,3},{3,2},{4,5},{5,4},{6,7},{7,6},{8,9},{9,8},{10,11... | collective-permute-start | bytes 3538952 | tf_op jit(solution)/shard_map/ppermute | solution.py:333
  105.3 10.8 %collective-permute-start.10 = (f32[4,24,768]{2,1,0:T(8,128)S(1)}, f32[4,24,768]{2,1,0:T(8,128)S(1)}, u32[]{:S(2)}, u32[]{:S(2)}) collective-permute-start(f32[4,24,768]{2,1,0:T(8,128)S(1)} %get-tuple-element.47), channel_id=1, source_target_pairs={{0,8},{8,16},{16,24},{24,0},{1,9},{9,17},{17,25},{25,1},{2,10},{10... | collective-permute-start | bytes 884744 | tf_op jit(solution)/shard_map/ppermute | solution.py:268
  106.4 15.1 %collective-permute-start.11 = (f32[4,24,768]{2,1,0:T(8,128)S(1)}, f32[4,24,768]{2,1,0:T(8,128)S(1)}, u32[]{:S(2)}, u32[]{:S(2)}) collective-permute-start(f32[4,24,768]{2,1,0:T(8,128)S(1)} %get-tuple-element.48), channel_id=1, source_target_pairs={{0,16},{8,24},{16,0},{24,8},{1,17},{9,25},{17,1},{25,9},{2,18},{10... | collective-permute-start | bytes 884744 | tf_op jit(solution)/shard_map/ppermute | solution.py:268
  107.6 13.8 %collective-permute-start.12 = (f32[4,24,768]{2,1,0:T(8,128)S(1)}, f32[4,24,768]{2,1,0:T(8,128)S(1)}, u32[]{:S(2)}, u32[]{:S(2)}) collective-permute-start(f32[4,24,768]{2,1,0:T(8,128)S(1)} %get-tuple-element.49), channel_id=1, source_target_pairs={{0,24},{8,0},{16,8},{24,16},{1,25},{9,1},{17,9},{25,17},{2,26},{10... | collective-permute-start | bytes 884744 | tf_op jit(solution)/shard_map/ppermute | solution.py:268
  121.5 7.0 %collective-permute-start.13 = (f32[24,768]{1,0:T(8,128)S(1)}, f32[24,768]{1,0:T(8,128)S(1)}, u32[]{:S(2)}, u32[]{:S(2)}) collective-permute-start(f32[24,768]{1,0:T(8,128)S(1)} %get-tuple-element.50), channel_id=1, source_target_pairs={{0,2},{1,3},{2,4},{3,5},{4,6},{5,7},{6,0},{7,1},{8,10},{9,11},{10,... | collective-permute-start | bytes 221192 | tf_op jit(solution)/shard_map/ppermute | solution.py:268
  121.6 7.0 %collective-permute-start.15 = (f32[24,768]{1,0:T(8,128)S(1)}, f32[24,768]{1,0:T(8,128)S(1)}, u32[]{:S(2)}, u32[]{:S(2)}) collective-permute-start(f32[24,768]{1,0:T(8,128)S(1)} %get-tuple-element.51), channel_id=1, source_target_pairs={{0,6},{1,7},{2,0},{3,1},{4,2},{5,3},{6,4},{7,5},{8,14},{9,15},{10,... | collective-permute-start | bytes 221192 | tf_op jit(solution)/shard_map/ppermute | solution.py:268
  125.4 6.0 %collective-permute-start.14 = (f32[24,768]{1,0:T(8,128)S(1)}, f32[24,768]{1,0:T(8,128)S(1)}, u32[]{:S(2)}, u32[]{:S(2)}) collective-permute-start(f32[24,768]{1,0:T(8,128)S(1)} %get-tuple-element.52), channel_id=1, source_target_pairs={{0,4},{1,5},{2,6},{3,7},{4,0},{5,1},{6,2},{7,3},{8,12},{9,13},{10,... | collective-permute-start | bytes 221192 | tf_op jit(solution)/shard_map/ppermute | solution.py:268
  131.4 4.4 %collective-permute-start.18 = (f32[24,768]{1,0:T(8,128)S(1)}, f32[24,768]{1,0:T(8,128)S(1)}, u32[]{:S(2)}, u32[]{:S(2)}) collective-permute-start(f32[24,768]{1,0:T(8,128)S(1)} %fusion.2.refs_0_), channel_id=1, source_target_pairs={{0,24},{8,0},{16,8},{24,16},{1,25},{9,1},{17,9},{25,17},{2,26},{10... | collective-permute-start | bytes 221192 | tf_op jit(solution)/shard_map/ppermute | solution.py:268
  132.6 4.4 %collective-permute-start.17 = (f32[24,768]{1,0:T(8,128)S(1)}, f32[24,768]{1,0:T(8,128)S(1)}, u32[]{:S(2)}, u32[]{:S(2)}) collective-permute-start(f32[24,768]{1,0:T(8,128)S(1)} %fusion.2.refs_0_), channel_id=1, source_target_pairs={{0,16},{8,24},{16,0},{24,8},{1,17},{9,25},{17,1},{25,9},{2,18},{10... | collective-permute-start | bytes 221192 | tf_op jit(solution)/shard_map/ppermute | solution.py:268
  133.4 5.3 %collective-permute-start.16 = (f32[24,768]{1,0:T(8,128)S(1)}, f32[24,768]{1,0:T(8,128)S(1)}, u32[]{:S(2)}, u32[]{:S(2)}) collective-permute-start(f32[24,768]{1,0:T(8,128)S(1)} %fusion.2.refs_0_), channel_id=1, source_target_pairs={{0,8},{8,16},{16,24},{24,0},{1,9},{9,17},{17,25},{25,1},{2,10},{10... | collective-permute-start | bytes 221192 | tf_op jit(solution)/shard_map/ppermute | solution.py:268

commit v4 on v3

--- a/solution.py
+++ b/solution.py
@@ -13,9 +13,9 @@
 VMEM_LIMIT = 40 * 1024 * 1024
 
 
-def filter_kernel(space, layers, tiles, chunk, pitch, offset, v_pitch, unroll, here_ref, x_ref, v_ref, *refs):
-    out_refs = refs[:space]
-    f0, r0, f1, r1, f2, r2, coef = refs[space:]
+def filter_kernel(space, layers, tiles, chunk, pitch, offset, unroll, here_ref, x_ref, *refs):
+    v_refs, out_refs = refs[:space], refs[space : 2 * space]
+    f0, r0, f1, r1, f2, r2, coef = refs[2 * space :]
     planes = space * layers
     rows = tiles * layers
     lane = lax.broadcasted_iota(jnp.int32, (chunk, LANES), 1)
@@ -34,7 +34,7 @@
             v = x_ref[pl.ds((slab * pitch + offset) * rows + row, chunk, stride=rows), :]
             f0[tile, p] = v
             r0[tile, p] = pltpu.roll(v, NZ, 1)
-            w = v_ref[pl.ds((slab * v_pitch + v_pitch - 1) * rows + row, 1), :]
+            w = v_refs[s][pl.ds(row, 1), :]
             coef[tile, p] = jnp.broadcast_to(0.25 * w - 0.5625, (chunk, LANES))
         return carry
 
@@ -92,17 +92,16 @@
 SMEM_SPEC = pl.BlockSpec(memory_space=pltpu.SMEM)
 
 
-def run_filter(here, x, v, offset, space, layers, tiles, chunk):
+def run_filter(here, x, vs, offset, space, layers, tiles, chunk):
     rows = tiles * layers
     planes = space * layers
     pitch = x.shape[0] // (space * rows)
-    v_pitch = v.shape[0] // (space * rows)
     field = pltpu.VMEM((tiles, planes, chunk, LANES), jnp.float32)
     unroll = 8 if tiles % 8 == 0 and planes <= 8 else 1
     return pl.pallas_call(
-        functools.partial(filter_kernel, space, layers, tiles, chunk, pitch, offset, v_pitch, unroll),
+        functools.partial(filter_kernel, space, layers, tiles, chunk, pitch, offset, unroll),
         out_shape=[jax.ShapeDtypeStruct((rows, chunk, LANES), jnp.float32)] * space,
-        in_specs=[SMEM_SPEC] + [VMEM_SPEC] * 2,
+        in_specs=[SMEM_SPEC] + [VMEM_SPEC] * (1 + space),
         out_specs=[VMEM_SPEC] * space,
         scratch_shapes=[field] * 7,
         compiler_params=pltpu.CompilerParams(vmem_limit_bytes=VMEM_LIMIT),
@@ -112,29 +111,48 @@
             transcendentals=0,
         ),
         name="filter",
-    )(here, x, v)
+    )(here, x, *vs)
+
+
+def partner(index, size, k, forward=True):
+    if size & (size - 1) == 0:
+        return index ^ k
+    moved = index + k if forward else index - k + size
+    return jnp.where(moved >= size, moved - size, moved)
+
+
+def exchange(x, axis, k, pitch=1):
+    size = lax.axis_size(axis) // pitch
+    power = size & (size - 1) == 0
+    pairs = []
+    for i in range(size):
+        target = i ^ k if power else (i + k) % size
+        pairs += [(i * pitch + low, target * pitch + low) for low in range(pitch)]
+    return lax.ppermute(x, axis, pairs)
 
 
 def pack_kernel(space, band, share, chunk, subs, here_ref, *refs):
-    blocks, out = refs[:-1], refs[-1]
-    here = here_ref[0]
+    blocks, outs = refs[: space * subs], refs[space * subs :]
+    here, mine = here_ref[0], here_ref[1]
     for k in range(space):
         group = here - k
         group = jnp.where(group < 0, group + space, group)
         for sub in range(subs):
             first = pl.multiple_of((group * subs + sub) * chunk, chunk)
             block = blocks[k * subs + sub]
-            for b in range(band):
+            for step, out in enumerate(outs):
+                target = partner(mine, band, step)
                 for q in range(share):
-                    out[b, pl.ds(first, chunk), q * LANES : (q + 1) * LANES] = block[b * share + q]
+                    out[pl.ds(first, chunk), q * LANES : (q + 1) * LANES] = block[target * share + q]
 
 
 def pack(here, blocks, space, band, share, chunk, subs):
+    shape = (space * subs * chunk, share * LANES)
     return pl.pallas_call(
         functools.partial(pack_kernel, space, band, share, chunk, subs),
-        out_shape=jax.ShapeDtypeStruct((band, space * subs * chunk, share * LANES), jnp.float32),
+        out_shape=[jax.ShapeDtypeStruct(shape, jnp.float32)] * band,
         in_specs=[SMEM_SPEC] + [VMEM_SPEC] * len(blocks),
-        out_specs=VMEM_SPEC,
+        out_specs=[VMEM_SPEC] * band,
         compiler_params=pltpu.CompilerParams(vmem_limit_bytes=VMEM_LIMIT),
         cost_estimate=pl.CostEstimate(
             flops=0, bytes_accessed=8 * band * space * subs * chunk * share * LANES, transcendentals=0
@@ -175,12 +193,16 @@
 
 
 def gram_kernel(band, count, space, chunk, places, which_ref, *refs):
-    parts, out, wide = refs[:-2], refs[-2], refs[-1]
-    for b in range(band):
-        for part, (base, pitch) in zip(parts, places):
+    parts, out, wide = list(refs[:-2]), refs[-2], refs[-1]
+    own = count // space
+    for offset, subs in places:
+        size = subs * chunk
+        for step in range(band):
+            source = partner(which_ref[1], band, step, forward=False)
+            part = parts.pop(0)
             for g in range(space):
-                first = b * count + base + g * pitch
-                wide[first : first + chunk, :] = part[b, g * chunk : (g + 1) * chunk, :]
+                first = pl.multiple_of(source * count + g * own + offset, chunk)
+                wide[pl.ds(first, size), :] = part[g * size : (g + 1) * size, :]
     which = which_ref[0]
     pairs = band // 2
     picked = [wide[pl.ds(pl.multiple_of((2 * z + which) * count, SUBLANES), count), :] for z in range(pairs)]
@@ -200,10 +222,8 @@
         out[:, c : c + step] = dot(left_hi, hi) + (dot(left_hi, lo) + dot(left_lo, hi))
 
 
-def gram(which, parts, space, chunk, places):
-    band = parts[0].shape[0]
-    count = sum(p.shape[1] for p in parts)
-    cells = parts[0].shape[2]
+def gram(which, parts, band, count, space, chunk, places):
+    cells = parts[0].shape[-1]
     return pl.pallas_call(
         functools.partial(gram_kernel, band, count, space, chunk, places),
         out_shape=jax.ShapeDtypeStruct((band // 2 * count, band * count), jnp.float32),
@@ -278,48 +298,51 @@
     own = count // space
     chunk = max(c for c in range(1, SUBLANES + 1) if own % c == 0)
     chunks = own // chunk
-    groups = [1] if chunks == 1 else [1, chunks - 1]
 
     s_index = lax.axis_index("space")
     b_index = lax.axis_index("band")
-    here = s_index.reshape(1)
+    here = jnp.stack([s_index, b_index])
 
     def as_rows(x):
         n = x.shape[0]
         return x.reshape(n, layers, tiles, LANES).transpose(0, 2, 1, 3).reshape(n * rows, LANES)
 
-    def over_space(x):
-        return lax.all_to_all(x, "space", split_axis=0, concat_axis=0, tiled=True)
-
-    head = orbitals[: space * chunk].reshape(space, chunk, layers, plane)
-    slab_v = jnp.broadcast_to(potential[None, None], (space, 1, layers, plane))
-    head = jnp.concatenate([head, slab_v], axis=1).reshape(space * (chunk + 1), layers, plane)
-    head = over_space(head)
-    arrived = [head]
+    own_v = as_rows(potential[None])
+    vs = [own_v] + [rotate(own_v, "space", space - k) for k in range(1, space)]
+    arrived = as_rows(lax.all_to_all(orbitals, "space", split_axis=0, concat_axis=0, tiled=True))
+
+    def filtered(c, x):
+        outs = run_filter(here, x, vs, c * chunk, space, layers, tiles, chunk)
+        return [outs[0]] + [rotate(outs[k], "space", k) for k in range(1, space)]
+
+    order = sorted(range(1, band), reverse=True)
+    made = [filtered(0, arrived)]
     if chunks > 1:
-        head, tail = lax.optimization_barrier((head, orbitals[space * chunk :]))
-        arrived = [head, over_space(tail)]
-    arrived = [as_rows(x) for x in arrived]
-
-    all_blocks = []
+        made.append(filtered(1, arrived))
     parts = []
     places = []
-    first = 0
-    for subs, x in zip(groups, arrived):
-        made = []
-        for sub in range(subs):
-            outs = run_filter(here, x, arrived[0], sub * chunk, space, layers, tiles, chunk)
-            blocks = [outs[0]] + [rotate(outs[k], "space", k) for k in range(1, space)]
-            made.append(blocks)
-            packed = pack(here, blocks, space, band, share, chunk, 1)
-            if parts:
-                parts[-1], packed = lax.optimization_barrier((parts[-1], packed))
-            parts.append(lax.all_to_all(packed, "band", split_axis=0, concat_axis=0, tiled=True))
-            places.append((first + sub * chunk, subs * chunk))
-        all_blocks += [made[sub][k] for k in range(space) for sub in range(subs)]
-        first += space * subs * chunk
-
-    result = unpack(here, all_blocks, space, rows, chunk, groups)
+    packed = pack(here, made[0], space, band, share, chunk, 1)
+    packed, arrived = lax.optimization_barrier((packed, arrived))
+    got = {0: packed[0]}
+    for k in order:
+        got[k] = exchange(packed[k], "band", k)
+    places.append((0, 1))
+    for c in range(2, chunks):
+        made.append(filtered(c, arrived))
+    if chunks > 1:
+        late = [made[c][k] for k in range(space) for c in range(1, chunks)]
+        packed = pack(here, late, space, band, share, chunk, chunks - 1)
+        later = {0: packed[0]}
+        for k in order:
+            got[k], x = lax.optimization_barrier((got[k], packed[k]))
+            later[k] = exchange(x, "band", k)
+        places.append((chunk, chunks - 1))
+    parts += [got[k] for k in range(band)]
+    if chunks > 1:
+        parts += [later[k] for k in range(band)]
+    blocks = [made[c][k] for k in range(space) for c in range(chunks)]
+
+    result = unpack(here, blocks, space, rows, chunk, [chunks])
     parts[-1], result = lax.optimization_barrier((parts[-1], result))
     result = result.reshape(count, tiles, layers, LANES).transpose(0, 2, 1, 3).reshape(count, layers, plane)
 
@@ -328,7 +351,7 @@
     pair = b_index // 2
 
     def half(which):
-        return gram(which.reshape(1), parts, space, chunk, places)
+        return gram(jnp.stack([which, b_index]), parts, band, count, space, chunk, places)
 
     other = lax.ppermute(half(1 - core), "band", [(i, i ^ 1) for i in range(band)])
     split = (pairs, space, own, band * count)
@@ -340,8 +363,8 @@
 
     final = lax.dynamic_index_in_dim(mine, pair, 0, keepdims=False)
     for k in range(1, pairs):
-        sent = lax.dynamic_index_in_dim(mine, (pair + k) % pairs, 0, keepdims=False)
-        final = final + rotate(sent, "band", 2 * k)
+        sent = lax.dynamic_index_in_dim(mine, partner(pair, pairs, k), 0, keepdims=False)
+        final = final + exchange(sent, "band", k, 2)
     final = final * (1.0 / (layers * space * plane))
 
     margin = place(here, [final] + [rotate(final, "space", k) for k in range(1, space)])

time: 140 us -> 139 us (level)
  waiting for transfers between devices: 64.6 us -> 59.9 us
  Pallas kernels: 20.7 us -> 24.1 us
  starting transfers between devices: 47 us -> 50 us
  local copies, waits for them, and re-layouts: 5 us -> 3.19 us
    ppermute x0 -> x17, waiting for transfers between devices: none -> 26 us  [exchange(): return lax.ppermute(x, axis, pairs)]
    ppermute x0 -> x17, starting transfers between devices: none -> 20.8 us  [exchange(): return lax.ppermute(x, axis, pairs)]
    all_to_all x5 -> x1, waiting for transfers between devices: 20.1 us -> 0.01 us  [shards(): lax.all_to_all(orbitals, 'space', split_axis=0, concat_axis=0, tiled=True)]
    all_to_all x5 -> x1, starting transfers between devices: 23.1 us -> 5.18 us  [shards(): lax.all_to_all(orbitals, 'space', split_axis=0, concat_axis=0, tiled=True)]
    ppermute x18, waiting for transfers between devices: 42.8 us -> 32.9 us  [rotate(): return lax.ppermute(x, axis, [(i, (i + step) % size) for i in range(size)])]
    pallas_call x3, Pallas kernels: 13 us -> 14.6 us  [run_filter(): pl.pallas_call(functools.partial(filter_kernel, space, layers, tiles, chu...]
    unnamed x14 -> x22, local copies, waits for them, and re-layouts: 2.89 us -> 3.17 us
  transfers between devices with their start and end apart: 24 -> 37, of which waited for: 16 -> 17; matrix products, arithmetic and copies ran while one was open for 1% -> 0% of each run, Pallas kernels for 13% -> 11%
where the time goes in v4:
time: 139 us; the launch traced here: 138 us
  waiting for transfers between devices  59.9 us (43%)
  starting transfers between devices  50 us (36%)
  Pallas kernels  24.1 us (17%)
  local copies, waits for them, and re-layouts  3.19 us (2%)
    ppermute x18, waiting for transfers between devices, rotate(): return lax.ppermute(x, axis, [(i, (i + step) % size) for i in range(size)])  32.9 us
    ppermute x17, waiting for transfers between devices, exchange(): return lax.ppermute(x, axis, pairs)  26 us
    ppermute x18, starting transfers between devices, rotate(): return lax.ppermute(x, axis, [(i, (i + step) % size) for i in range(size)])  24 us
    ppermute x17, starting transfers between devices, exchange(): return lax.ppermute(x, axis, pairs)  20.8 us
    pallas_call x3, Pallas kernels, run_filter(): pl.pallas_call(functools.partial(filter_kernel, space, layers, tiles, chu...  14.6 us
    all_to_all x1, starting transfers between devices, shards(): lax.all_to_all(orbitals, 'space', split_axis=0, concat_axis=0, tiled=True)  5.18 us
    pallas_call x2, Pallas kernels, gram(): pl.pallas_call(functools.partial(gram_kernel, band, count, space, chunk,...  3.58 us
    unnamed x22, local copies, waits for them, and re-layouts  3.17 us
  transfers between devices with their start and end apart: 37, of which 17 were waited for; matrix products, arithmetic and copies ran while one was open for 0% of the time, Pallas kernels for 11%

profile of v4, /device:TPU:0, one launch (start us, length us, event | category | flops | bytes accessed | tf_op | source)
XLA Modules:
  0.0 138.3 jit_solution(9670422774720376341)
XLA Ops:
  0.6 5.2 %all-to-all-start = ((f32[96,2,2048]{2,1,0:T(2,128)}), f32[96,2,2048]{2,1,0:T(2,128)S(1)}, u32[]{:S(2)}, u32[]{:S(2)}) async-start(f32[96,2,2048]{2,1,0:T(2,128)} %param.2), calls=%async_computation | async-start | bytes 3145728 | tf_op jit(solution)/shard_map/all_to_all | solution.py:312
  5.8 2.0 %collective-permute-start.2 = (f32[32,128]{1,0:T(8,128)S(1)}, f32[32,128]{1,0:T(8,128)S(1)}, u32[]{:S(2)}, u32[]{:S(2)}) collective-permute-start(f32[32,128]{1,0:T(8,128)S(1)} %bitcast.41), channel_id=1, source_target_pairs={{0,8},{8,16},{16,24},{24,0},{1,9},{9,17},{17,25},{25,1},{2,10},{10... | collective-permute-start | bytes 49160 | tf_op jit(solution)/shard_map/ppermute | solution.py:288
  7.8 1.5 %collective-permute-start.1 = (f32[32,128]{1,0:T(8,128)S(1)}, f32[32,128]{1,0:T(8,128)S(1)}, u32[]{:S(2)}, u32[]{:S(2)}) collective-permute-start(f32[32,128]{1,0:T(8,128)S(1)} %bitcast.42), channel_id=1, source_target_pairs={{0,16},{8,24},{16,0},{24,8},{1,17},{9,25},{17,1},{25,9},{2,18},{10... | collective-permute-start | bytes 49160 | tf_op jit(solution)/shard_map/ppermute | solution.py:288
  9.3 1.5 %collective-permute-start = (f32[32,128]{1,0:T(8,128)S(1)}, f32[32,128]{1,0:T(8,128)S(1)}, u32[]{:S(2)}, u32[]{:S(2)}) collective-permute-start(f32[32,128]{1,0:T(8,128)S(1)} %bitcast.43), channel_id=1, source_target_pairs={{0,24},{8,0},{16,8},{24,16},{1,25},{9,1},{17,9},{25,17},{2,26},{10... | collective-permute-start | bytes 49160 | tf_op jit(solution)/shard_map/ppermute | solution.py:288
  10.8 0.1 pad_add_fusion.here_ref
  10.8 15.7 %collective-permute-done.2.refs_3_ = f32[32,128]{1,0:T(8,128)S(1)} collective-permute-done((f32[32,128]{1,0:T(8,128)S(1)}, f32[32,128]{1,0:T(8,128)S(1)}, u32[]{:S(2)}, u32[]{:S(2)}) %collective-permute-start.2) | collective-permute-done | bytes 16416 | tf_op jit(solution)/shard_map/ppermute | solution.py:288
  26.5 4.9 %filter.3 = (f32[32,8,128]{2,1,0:T(8,128)S(1)}, f32[32,8,128]{2,1,0:T(8,128)S(1)}, f32[32,8,128]{2,1,0:T(8,128)S(1)}, f32[32,8,128]{2,1,0:T(8,128)S(1)}) custom-call(s32[2]{0:T(128)S(1)} %pad_add_fusion.here_ref, f32[3072,128]{1,0:T(8,128)S(1)} %bitcast.36, f32[32,128]{1,0:T(8,128)S(1)} %bitcast.44, f32[32,128]{1,0:T(8,128)S(1)} %collective-permute-done.refs_1_, ...), custom_call_target="tpu_custom_call" | custom-call | flops 9830400 | bytes 1048576 | tf_op jit(solution)/shard_map/filter/pallas_call | solution.py:101
  31.4 0.8 collective-permute-start.3
  32.2 0.5 collective-permute-start.4
  32.7 2.4 %collective-permute-start.5 = (f32[32,8,128]{2,1,0:T(8,128)S(1)}, f32[32,8,128]{2,1,0:T(8,128)S(1)}, u32[]{:S(2)}, u32[]{:S(2)}) collective-permute-start(f32[32,8,128]{2,1,0:T(8,128)S(1)} %get-tuple-element.62), channel_id=1, source_target_pairs={{0,24},{8,0},{16,8},{24,16},{1,25},{9,1},{17,9},{25,17},{2,26},{10... | collective-permute-start | bytes 393224 | tf_op jit(solution)/shard_map/ppermute | solution.py:288
  35.1 4.9 %filter.4 = (f32[32,8,128]{2,1,0:T(8,128)S(1)}, f32[32,8,128]{2,1,0:T(8,128)S(1)}, f32[32,8,128]{2,1,0:T(8,128)S(1)}, f32[32,8,128]{2,1,0:T(8,128)S(1)}) custom-call(s32[2]{0:T(128)S(1)} %pad_add_fusion.here_ref, f32[3072,128]{1,0:T(8,128)S(1)} %bitcast.37, f32[32,128]{1,0:T(8,128)S(1)} %bitcast.45, f32[32,128]{1,0:T(8,128)S(1)} %collective-permute-done.refs_1_, ...), custom_call_target="tpu_custom_call" | custom-call | flops 9830400 | bytes 1048576 | tf_op jit(solution)/shard_map/filter/pallas_call | solution.py:101
  40.0 0.1 collective-permute-start.7
  40.1 1.4 collective-permute-start.9
  41.4 2.8 %collective-permute-start.11 = (f32[32,8,128]{2,1,0:T(8,128)S(1)}, f32[32,8,128]{2,1,0:T(8,128)S(1)}, u32[]{:S(2)}, u32[]{:S(2)}) collective-permute-start(f32[32,8,128]{2,1,0:T(8,128)S(1)} %get-tuple-element.79), channel_id=1, source_target_pairs={{0,24},{8,0},{16,8},{24,16},{1,25},{9,1},{17,9},{25,17},{2,26},{10... | collective-permute-start | bytes 393224 | tf_op jit(solution)/shard_map/ppermute | solution.py:288
  44.3 0.6 pack.2
  44.9 4.9 %filter.5 = (f32[32,8,128]{2,1,0:T(8,128)S(1)}, f32[32,8,128]{2,1,0:T(8,128)S(1)}, f32[32,8,128]{2,1,0:T(8,128)S(1)}, f32[32,8,128]{2,1,0:T(8,128)S(1)}) custom-call(s32[2]{0:T(128)S(1)} %pad_add_fusion.here_ref, f32[3072,128]{1,0:T(8,128)S(1)} %bitcast.38, f32[32,128]{1,0:T(8,128)S(1)} %bitcast.46, f32[32,128]{1,0:T(8,128)S(1)} %collective-permute-done.refs_1_, ...), custom_call_target="tpu_custom_call" | custom-call | flops 9830400 | bytes 1048576 | tf_op jit(solution)/shard_map/filter/pallas_call | solution.py:101
  49.8 0.8 collective-permute-start.10
  50.6 2.8 %collective-permute-start.12 = (f32[32,8,128]{2,1,0:T(8,128)S(1)}, f32[32,8,128]{2,1,0:T(8,128)S(1)}, u32[]{:S(2)}, u32[]{:S(2)}) collective-permute-start(f32[32,8,128]{2,1,0:T(8,128)S(1)} %get-tuple-element.80), channel_id=1, source_target_pairs={{0,24},{8,0},{16,8},{24,16},{1,25},{9,1},{17,9},{25,17},{2,26},{10... | collective-permute-start | bytes 393224 | tf_op jit(solution)/shard_map/ppermute | solution.py:288
  53.5 3.7 %collective-permute-start.19 = (f32[32,512]{1,0:T(8,128)S(1)}, f32[32,512]{1,0:T(8,128)S(1)}, u32[]{:S(2)}, u32[]{:S(2)}) collective-permute-start(f32[32,512]{1,0:T(8,128)S(1)} %get-tuple-element.100), channel_id=1, source_target_pairs={{0,6},{1,7},{2,4},{3,5},{4,2},{5,3},{6,0},{7,1},{8,14},{9,15},{10,... | collective-permute-start | bytes 196616 | tf_op jit(solution)/shard_map/ppermute | solution.py:131
  57.2 0.2 collective-permute-start.14
  57.4 0.5 collective-permute-start.15
  58.0 0.7 pack.3
  58.6 1.0 collective-permute-done.19.refs_6_
  59.6 4.3 %collective-permute-start.25 = (f32[64,512]{1,0:T(8,128)S(1)}, f32[64,512]{1,0:T(8,128)S(1)}, u32[]{:S(2)}, u32[]{:S(2)}) collective-permute-start(f32[64,512]{1,0:T(8,128)S(1)} %get-tuple-element.110), channel_id=1, source_target_pairs={{0,6},{1,7},{2,4},{3,5},{4,2},{5,3},{6,0},{7,1},{8,14},{9,15},{10,... | collective-permute-start | bytes 393224 | tf_op jit(solution)/shard_map/ppermute | solution.py:131
  63.9 0.6 collective-permute-start.13
  64.5 0.6 copy-done.1
  65.1 3.5 %collective-permute-start.17 = (f32[32,512]{1,0:T(8,128)S(1)}, f32[32,512]{1,0:T(8,128)S(1)}, u32[]{:S(2)}, u32[]{:S(2)}) collective-permute-start(f32[32,512]{1,0:T(8,128)S(1)} %get-tuple-element.94), channel_id=1, source_target_pairs={{0,4},{1,5},{2,6},{3,7},{4,0},{5,1},{6,2},{7,3},{8,12},{9,13},{10,... | collective-permute-start | bytes 196616 | tf_op jit(solution)/shard_map/ppermute | solution.py:131
  68.7 0.6 copy-done.3
  69.3 2.2 %collective-permute-done.16.refs_3_ = f32[32,512]{1,0:T(8,128)S(1)} collective-permute-done((f32[32,512]{1,0:T(8,128)S(1)}, f32[32,512]{1,0:T(8,128)S(1)}, u32[]{:S(2)}, u32[]{:S(2)}) %collective-permute-start.16) | collective-permute-done | bytes 65568 | tf_op jit(solution)/shard_map/ppermute | solution.py:131
  71.5 0.6 copy-done.5
  72.2 7.1 %collective-permute-done.17.refs_4_ = f32[32,512]{1,0:T(8,128)S(1)} collective-permute-done((f32[32,512]{1,0:T(8,128)S(1)}, f32[32,512]{1,0:T(8,128)S(1)}, u32[]{:S(2)}, u32[]{:S(2)}) %collective-permute-start.17) | collective-permute-done | bytes 65568 | tf_op jit(solution)/shard_map/ppermute | solution.py:131
  79.3 0.6 copy-done.7
  79.9 0.6 copy-done.9
  80.5 2.4 %collective-permute-start.23 = (f32[64,512]{1,0:T(8,128)S(1)}, f32[64,512]{1,0:T(8,128)S(1)}, u32[]{:S(2)}, u32[]{:S(2)}) collective-permute-start(f32[64,512]{1,0:T(8,128)S(1)} %get-tuple-element.108), channel_id=1, source_target_pairs={{0,4},{1,5},{2,6},{3,7},{4,0},{5,1},{6,2},{7,3},{8,12},{9,13},{10,... | collective-permute-start | bytes 393224 | tf_op jit(solution)/shard_map/ppermute | solution.py:131
  82.9 0.5 collective-permute-start.22
  83.5 1.5 %collective-permute-start.21 = (f32[64,512]{1,0:T(8,128)S(1)}, f32[64,512]{1,0:T(8,128)S(1)}, u32[]{:S(2)}, u32[]{:S(2)}) collective-permute-start(f32[64,512]{1,0:T(8,128)S(1)} %get-tuple-element.106), channel_id=1, source_target_pairs={{0,2},{1,3},{2,0},{3,1},{4,6},{5,7},{6,4},{7,5},{8,10},{9,11},{10,... | collective-permute-start | bytes 393224 | tf_op jit(solution)/shard_map/ppermute | solution.py:131
  84.9 0.1 pad_add_fusion.1
  85.0 2.6 %unpack.1 = f32[3072,128]{1,0:T(8,128)} custom-call(s32[2]{0:T(128)S(1)} %pad_add_fusion.here_ref, f32[32,8,128]{2,1,0:T(8,128)S(1)} %get-tuple-element.59.refs_0_, f32[32,8,128]{2,1,0:T(8,128)S(1)} %get-tuple-element.72.refs_0_.refs_1_, f32[32,8,128]{2,1,0:T(8,128)S(1)} %get-tuple-element.74.refs_1_.refs_2_, ...), custom_call_target="tpu_custom_call" | custom-call | bytes 3145728 | tf_op jit(solution)/shard_map/unpack/pallas_call | solution.py:184
  87.6 4.8 %collective-permute-done.24.refs_13_ = f32[64,512]{1,0:T(8,128)S(1)} collective-permute-done((f32[64,512]{1,0:T(8,128)S(1)}, f32[64,512]{1,0:T(8,128)S(1)}, u32[]{:S(2)}, u32[]{:S(2)}) %collective-permute-start.24) | collective-permute-done | bytes 131104 | tf_op jit(solution)/shard_map/ppermute | solution.py:131
  92.4 2.8 %collective-permute-done.23.refs_12_ = f32[64,512]{1,0:T(8,128)S(1)} collective-permute-done((f32[64,512]{1,0:T(8,128)S(1)}, f32[64,512]{1,0:T(8,128)S(1)}, u32[]{:S(2)}, u32[]{:S(2)}) %collective-permute-start.23) | collective-permute-done | bytes 131104 | tf_op jit(solution)/shard_map/ppermute | solution.py:131
  95.2 1.8 %collective-permute-done.21.refs_10_ = f32[64,512]{1,0:T(8,128)S(1)} collective-permute-done((f32[64,512]{1,0:T(8,128)S(1)}, f32[64,512]{1,0:T(8,128)S(1)}, u32[]{:S(2)}, u32[]{:S(2)}) %collective-permute-start.21) | collective-permute-done | bytes 131104 | tf_op jit(solution)/shard_map/ppermute | solution.py:131
  97.1 1.8 %gram.3 = f32[384,768]{1,0:T(8,128)S(1)} custom-call(s32[2]{0:T(128)S(1)} %get-tuple-element.120.which_ref, f32[32,512]{1,0:T(8,128)S(1)} %get-tuple-element.84.refs_0_, f32[32,512]{1,0:T(8,128)S(1)} %copy-done.2, f32[32,512]{1,0:T(8,128)S(1)} %copy-done.4, f32[32,512]{1,0:T(8,128)S(1)} %copy-done.6, f32[32,512]{1,0:T(8,128)S(1)} %copy-done.8, ...), custom_call_target="tpu_custom_call" | custom-call | flops 905969664 | bytes 2752512 | tf_op jit(solution)/shard_map/gram/pallas_call | solution.py:227
  98.9 0.1 collective-permute-start.26
  99.0 1.8 %gram.2 = f32[384,768]{1,0:T(8,128)S(1)} custom-call(s32[2]{0:T(128)S(1)} %get-tuple-element.119.which_ref, f32[32,512]{1,0:T(8,128)S(1)} %get-tuple-element.84.refs_0_, f32[32,512]{1,0:T(8,128)S(1)} %copy-done.2, f32[32,512]{1,0:T(8,128)S(1)} %copy-done.4, f32[32,512]{1,0:T(8,128)S(1)} %copy-done.6, f32[32,512]{1,0:T(8,128)S(1)} %copy-done.8, ...), custom_call_target="tpu_custom_call" | custom-call | flops 905969664 | bytes 2752512 | tf_op jit(solution)/shard_map/gram/pallas_call | solution.py:227
  100.8 1.0 collective-permute-done.26
  101.8 0.7 combine.1
  102.6 1.4 collective-permute-start.28
  103.9 2.8 %collective-permute-start.29 = (f32[4,24,768]{2,1,0:T(8,128)S(1)}, f32[4,24,768]{2,1,0:T(8,128)S(1)}, u32[]{:S(2)}, u32[]{:S(2)}) collective-permute-start(f32[4,24,768]{2,1,0:T(8,128)S(1)} %get-tuple-element.115), channel_id=1, source_target_pairs={{0,24},{8,0},{16,8},{24,16},{1,25},{9,1},{17,9},{25,17},{2,26},{10... | collective-permute-start | bytes 884744 | tf_op jit(solution)/shard_map/ppermute | solution.py:288
  106.8 6.6 %collective-permute-done.27 = f32[4,24,768]{2,1,0:T(8,128)S(1)} collective-permute-done((f32[4,24,768]{2,1,0:T(8,128)S(1)}, f32[4,24,768]{2,1,0:T(8,128)S(1)}, u32[]{:S(2)}, u32[]{:S(2)}) %collective-permute-start.27) | collective-permute-done | bytes 294944 | tf_op jit(solution)/shard_map/ppermute | solution.py:288
  113.3 4.7 %collective-permute-done.28 = f32[4,24,768]{2,1,0:T(8,128)S(1)} collective-permute-done((f32[4,24,768]{2,1,0:T(8,128)S(1)}, f32[4,24,768]{2,1,0:T(8,128)S(1)}, u32[]{:S(2)}, u32[]{:S(2)}) %collective-permute-start.28) | collective-permute-done | bytes 294944 | tf_op jit(solution)/shard_map/ppermute | solution.py:288
  118.0 0.7 collective-permute-done.29
  118.7 0.1 add_add_fusion
  118.8 0.1 collective-permute-start.30
  118.9 2.7 %collective-permute-start.32 = (f32[24,768]{1,0:T(8,128)S(1)}, f32[24,768]{1,0:T(8,128)S(1)}, u32[]{:S(2)}, u32[]{:S(2)}) collective-permute-start(f32[24,768]{1,0:T(8,128)S(1)} %get-tuple-element.117), channel_id=1, source_target_pairs={{0,6},{1,7},{2,4},{3,5},{4,2},{5,3},{6,0},{7,1},{8,14},{9,15},{10,... | collective-permute-start | bytes 221192 | tf_op jit(solution)/shard_map/ppermute | solution.py:131
  121.6 0.8 collective-permute-start.31
  122.4 1.7 %collective-permute-done.30 = f32[24,768]{1,0:T(8,128)S(1)} collective-permute-done((f32[24,768]{1,0:T(8,128)S(1)}, f32[24,768]{1,0:T(8,128)S(1)}, u32[]{:S(2)}, u32[]{:S(2)}) %collective-permute-start.30) | collective-permute-done | bytes 73760 | tf_op jit(solution)/shard_map/ppermute | solution.py:131
  124.0 1.9 %collective-permute-done.32 = f32[24,768]{1,0:T(8,128)S(1)} collective-permute-done((f32[24,768]{1,0:T(8,128)S(1)}, f32[24,768]{1,0:T(8,128)S(1)}, u32[]{:S(2)}, u32[]{:S(2)}) %collective-permute-start.32) | collective-permute-done | bytes 73760 | tf_op jit(solution)/shard_map/ppermute | solution.py:131
  125.9 2.8 %collective-permute-done.31 = f32[24,768]{1,0:T(8,128)S(1)} collective-permute-done((f32[24,768]{1,0:T(8,128)S(1)}, f32[24,768]{1,0:T(8,128)S(1)}, u32[]{:S(2)}, u32[]{:S(2)}) %collective-permute-start.31) | collective-permute-done | bytes 73760 | tf_op jit(solution)/shard_map/ppermute | solution.py:131
  128.7 1.8 %collective-permute-start.35 = (f32[24,768]{1,0:T(8,128)S(1)}, f32[24,768]{1,0:T(8,128)S(1)}, u32[]{:S(2)}, u32[]{:S(2)}) collective-permute-start(f32[24,768]{1,0:T(8,128)S(1)} %fusion.2.refs_0_), channel_id=1, source_target_pairs={{0,24},{8,0},{16,8},{24,16},{1,25},{9,1},{17,9},{25,17},{2,26},{10... | collective-permute-start | bytes 221192 | tf_op jit(solution)/shard_map/ppermute | solution.py:288
  130.5 1.3 collective-permute-start.34
  131.8 1.5 %collective-permute-done.35.refs_3_ = f32[24,768]{1,0:T(8,128)S(1)} collective-permute-done((f32[24,768]{1,0:T(8,128)S(1)}, f32[24,768]{1,0:T(8,128)S(1)}, u32[]{:S(2)}, u32[]{:S(2)}) %collective-permute-start.35) | collective-permute-done | bytes 73760 | tf_op jit(solution)/shard_map/ppermute | solution.py:288
  133.3 2.0 %collective-permute-done.34.refs_2_ = f32[24,768]{1,0:T(8,128)S(1)} collective-permute-done((f32[24,768]{1,0:T(8,128)S(1)}, f32[24,768]{1,0:T(8,128)S(1)}, u32[]{:S(2)}, u32[]{:S(2)}) %collective-permute-start.34) | collective-permute-done | bytes 73760 | tf_op jit(solution)/shard_map/ppermute | solution.py:288
  135.2 1.8 %collective-permute-done.33.refs_1_ = f32[24,768]{1,0:T(8,128)S(1)} collective-permute-done((f32[24,768]{1,0:T(8,128)S(1)}, f32[24,768]{1,0:T(8,128)S(1)}, u32[]{:S(2)}, u32[]{:S(2)}) %collective-permute-start.33) | collective-permute-done | bytes 73760 | tf_op jit(solution)/shard_map/ppermute | solution.py:288
  137.0 1.3 place.1
  (47 shorter events, 0.3 us)
Async XLA Ops:
  0.6 5.2 %copy-start = (f32[2,2048]{1,0:T(2,128)S(1)}, f32[2,2048]{1,0:T(2,128)}, u32[]{:S(2)}) copy-start(f32[2,2048]{1,0:T(2,128)} %param.3) | copy-start | bytes 49156
  0.6 25.9 %all-to-all-start = ((f32[96,2,2048]{2,1,0:T(2,128)}), f32[96,2,2048]{2,1,0:T(2,128)S(1)}, u32[]{:S(2)}, u32[]{:S(2)}) async-start(f32[96,2,2048]{2,1,0:T(2,128)} %param.2), calls=%async_computation | async-start | bytes 3145728 | tf_op jit(solution)/shard_map/all_to_all | solution.py:312
  5.8 20.7 %collective-permute-start.2 = (f32[32,128]{1,0:T(8,128)S(1)}, f32[32,128]{1,0:T(8,128)S(1)}, u32[]{:S(2)}, u32[]{:S(2)}) collective-permute-start(f32[32,128]{1,0:T(8,128)S(1)} %bitcast.41), channel_id=1, source_target_pairs={{0,8},{8,16},{16,24},{24,0},{1,9},{9,17},{17,25},{25,1},{2,10},{10... | collective-permute-start | bytes 49160 | tf_op jit(solution)/shard_map/ppermute | solution.py:288
  7.8 18.7 %collective-permute-start.1 = (f32[32,128]{1,0:T(8,128)S(1)}, f32[32,128]{1,0:T(8,128)S(1)}, u32[]{:S(2)}, u32[]{:S(2)}) collective-permute-start(f32[32,128]{1,0:T(8,128)S(1)} %bitcast.42), channel_id=1, source_target_pairs={{0,16},{8,24},{16,0},{24,8},{1,17},{9,25},{17,1},{25,9},{2,18},{10... | collective-permute-start | bytes 49160 | tf_op jit(solution)/shard_map/ppermute | solution.py:288
  9.3 17.2 %collective-permute-start = (f32[32,128]{1,0:T(8,128)S(1)}, f32[32,128]{1,0:T(8,128)S(1)}, u32[]{:S(2)}, u32[]{:S(2)}) collective-permute-start(f32[32,128]{1,0:T(8,128)S(1)} %bitcast.43), channel_id=1, source_target_pairs={{0,24},{8,0},{16,8},{24,16},{1,25},{9,1},{17,9},{25,17},{2,26},{10... | collective-permute-start | bytes 49160 | tf_op jit(solution)/shard_map/ppermute | solution.py:288
  31.4 10.0 %collective-permute-start.3 = (f32[32,8,128]{2,1,0:T(8,128)S(1)}, f32[32,8,128]{2,1,0:T(8,128)S(1)}, u32[]{:S(2)}, u32[]{:S(2)}) collective-permute-start(f32[32,8,128]{2,1,0:T(8,128)S(1)} %get-tuple-element.60), channel_id=1, source_target_pairs={{0,8},{8,16},{16,24},{24,0},{1,9},{9,17},{17,25},{25,1},{2,10},{10... | collective-permute-start | bytes 393224 | tf_op jit(solution)/shard_map/ppermute | solution.py:288
  32.2 12.1 %collective-permute-start.4 = (f32[32,8,128]{2,1,0:T(8,128)S(1)}, f32[32,8,128]{2,1,0:T(8,128)S(1)}, u32[]{:S(2)}, u32[]{:S(2)}) collective-permute-start(f32[32,8,128]{2,1,0:T(8,128)S(1)} %get-tuple-element.61), channel_id=1, source_target_pairs={{0,16},{8,24},{16,0},{24,8},{1,17},{9,25},{17,1},{25,9},{2,18},{10... | collective-permute-start | bytes 393224 | tf_op jit(solution)/shard_map/ppermute | solution.py:288
  32.7 11.6 %collective-permute-start.5 = (f32[32,8,128]{2,1,0:T(8,128)S(1)}, f32[32,8,128]{2,1,0:T(8,128)S(1)}, u32[]{:S(2)}, u32[]{:S(2)}) collective-permute-start(f32[32,8,128]{2,1,0:T(8,128)S(1)} %get-tuple-element.62), channel_id=1, source_target_pairs={{0,24},{8,0},{16,8},{24,16},{1,25},{9,1},{17,9},{25,17},{2,26},{10... | collective-permute-start | bytes 393224 | tf_op jit(solution)/shard_map/ppermute | solution.py:288
  40.0 10.6 %collective-permute-start.7 = (f32[32,8,128]{2,1,0:T(8,128)S(1)}, f32[32,8,128]{2,1,0:T(8,128)S(1)}, u32[]{:S(2)}, u32[]{:S(2)}) collective-permute-start(f32[32,8,128]{2,1,0:T(8,128)S(1)} %get-tuple-element.75), channel_id=1, source_target_pairs={{0,8},{8,16},{16,24},{24,0},{1,9},{9,17},{17,25},{25,1},{2,10},{10... | collective-permute-start | bytes 393224 | tf_op jit(solution)/shard_map/ppermute | solution.py:288
  40.1 13.4 %collective-permute-start.9 = (f32[32,8,128]{2,1,0:T(8,128)S(1)}, f32[32,8,128]{2,1,0:T(8,128)S(1)}, u32[]{:S(2)}, u32[]{:S(2)}) collective-permute-start(f32[32,8,128]{2,1,0:T(8,128)S(1)} %get-tuple-element.77), channel_id=1, source_target_pairs={{0,16},{8,24},{16,0},{24,8},{1,17},{9,25},{17,1},{25,9},{2,18},{10... | collective-permute-start | bytes 393224 | tf_op jit(solution)/shard_map/ppermute | solution.py:288
  41.4 15.8 %collective-permute-start.11 = (f32[32,8,128]{2,1,0:T(8,128)S(1)}, f32[32,8,128]{2,1,0:T(8,128)S(1)}, u32[]{:S(2)}, u32[]{:S(2)}) collective-permute-start(f32[32,8,128]{2,1,0:T(8,128)S(1)} %get-tuple-element.79), channel_id=1, source_target_pairs={{0,24},{8,0},{16,8},{24,16},{1,25},{9,1},{17,9},{25,17},{2,26},{10... | collective-permute-start | bytes 393224 | tf_op jit(solution)/shard_map/ppermute | solution.py:288
  49.8 7.4 %collective-permute-start.8 = (f32[32,8,128]{2,1,0:T(8,128)S(1)}, f32[32,8,128]{2,1,0:T(8,128)S(1)}, u32[]{:S(2)}, u32[]{:S(2)}) collective-permute-start(f32[32,8,128]{2,1,0:T(8,128)S(1)} %get-tuple-element.76), channel_id=1, source_target_pairs={{0,8},{8,16},{16,24},{24,0},{1,9},{9,17},{17,25},{25,1},{2,10},{10... | collective-permute-start | bytes 393224 | tf_op jit(solution)/shard_map/ppermute | solution.py:288
  49.8 7.6 %collective-permute-start.10 = (f32[32,8,128]{2,1,0:T(8,128)S(1)}, f32[32,8,128]{2,1,0:T(8,128)S(1)}, u32[]{:S(2)}, u32[]{:S(2)}) collective-permute-start(f32[32,8,128]{2,1,0:T(8,128)S(1)} %get-tuple-element.78), channel_id=1, source_target_pairs={{0,16},{8,24},{16,0},{24,8},{1,17},{9,25},{17,1},{25,9},{2,18},{10... | collective-permute-start | bytes 393224 | tf_op jit(solution)/shard_map/ppermute | solution.py:288
  50.6 7.3 %collective-permute-start.12 = (f32[32,8,128]{2,1,0:T(8,128)S(1)}, f32[32,8,128]{2,1,0:T(8,128)S(1)}, u32[]{:S(2)}, u32[]{:S(2)}) collective-permute-start(f32[32,8,128]{2,1,0:T(8,128)S(1)} %get-tuple-element.80), channel_id=1, source_target_pairs={{0,24},{8,0},{16,8},{24,16},{1,25},{9,1},{17,9},{25,17},{2,26},{10... | collective-permute-start | bytes 393224 | tf_op jit(solution)/shard_map/ppermute | solution.py:288
  53.5 6.2 %collective-permute-start.19 = (f32[32,512]{1,0:T(8,128)S(1)}, f32[32,512]{1,0:T(8,128)S(1)}, u32[]{:S(2)}, u32[]{:S(2)}) collective-permute-start(f32[32,512]{1,0:T(8,128)S(1)} %get-tuple-element.100), channel_id=1, source_target_pairs={{0,6},{1,7},{2,4},{3,5},{4,2},{5,3},{6,0},{7,1},{8,14},{9,15},{10,... | collective-permute-start | bytes 196616 | tf_op jit(solution)/shard_map/ppermute | solution.py:131
  57.2 6.7 %collective-permute-start.6 = (f32[32,512]{1,0:T(8,128)S(1)}, f32[32,512]{1,0:T(8,128)S(1)}, u32[]{:S(2)}, u32[]{:S(2)}) collective-permute-start(f32[32,512]{1,0:T(8,128)S(1)} %get-tuple-element.71), channel_id=1, source_target_pairs={{0,7},{1,6},{2,5},{3,4},{4,3},{5,2},{6,1},{7,0},{8,15},{9,14},{10,... | collective-permute-start | bytes 196616 | tf_op jit(solution)/shard_map/ppermute | solution.py:131
  57.2 7.3 %collective-permute-start.14 = (f32[32,512]{1,0:T(8,128)S(1)}, f32[32,512]{1,0:T(8,128)S(1)}, u32[]{:S(2)}, u32[]{:S(2)}) collective-permute-start(f32[32,512]{1,0:T(8,128)S(1)} %get-tuple-element.85), channel_id=1, source_target_pairs={{0,1},{1,0},{2,3},{3,2},{4,5},{5,4},{6,7},{7,6},{8,9},{9,8},{10,11... | collective-permute-start | bytes 196616 | tf_op jit(solution)/shard_map/ppermute | solution.py:131
  57.4 11.2 %collective-permute-start.15 = (f32[32,512]{1,0:T(8,128)S(1)}, f32[32,512]{1,0:T(8,128)S(1)}, u32[]{:S(2)}, u32[]{:S(2)}) collective-permute-start(f32[32,512]{1,0:T(8,128)S(1)} %get-tuple-element.88), channel_id=1, source_target_pairs={{0,2},{1,3},{2,0},{3,1},{4,6},{5,7},{6,4},{7,5},{8,10},{9,11},{10,... | collective-permute-start | bytes 196616 | tf_op jit(solution)/shard_map/ppermute | solution.py:131
  59.6 23.8 %collective-permute-start.25 = (f32[64,512]{1,0:T(8,128)S(1)}, f32[64,512]{1,0:T(8,128)S(1)}, u32[]{:S(2)}, u32[]{:S(2)}) collective-permute-start(f32[64,512]{1,0:T(8,128)S(1)} %get-tuple-element.110), channel_id=1, source_target_pairs={{0,6},{1,7},{2,4},{3,5},{4,2},{5,3},{6,0},{7,1},{8,14},{9,15},{10,... | collective-permute-start | bytes 393224 | tf_op jit(solution)/shard_map/ppermute | solution.py:131
  63.9 21.0 %collective-permute-start.13 = (f32[64,512]{1,0:T(8,128)S(1)}, f32[64,512]{1,0:T(8,128)S(1)}, u32[]{:S(2)}, u32[]{:S(2)}) collective-permute-start(f32[64,512]{1,0:T(8,128)S(1)} %get-tuple-element.82), channel_id=1, source_target_pairs={{0,7},{1,6},{2,5},{3,4},{4,3},{5,2},{6,1},{7,0},{8,15},{9,14},{10,... | collective-permute-start | bytes 393224 | tf_op jit(solution)/shard_map/ppermute | solution.py:131
  64.5 7.0 %collective-permute-start.16 = (f32[32,512]{1,0:T(8,128)S(1)}, f32[32,512]{1,0:T(8,128)S(1)}, u32[]{:S(2)}, u32[]{:S(2)}) collective-permute-start(f32[32,512]{1,0:T(8,128)S(1)} %get-tuple-element.91), channel_id=1, source_target_pairs={{0,3},{1,2},{2,1},{3,0},{4,7},{5,6},{6,5},{7,4},{8,11},{9,10},{10,... | collective-permute-start | bytes 196616 | tf_op jit(solution)/shard_map/ppermute | solution.py:131
  64.5 0.6 copy-start.1
  65.1 14.1 %collective-permute-start.17 = (f32[32,512]{1,0:T(8,128)S(1)}, f32[32,512]{1,0:T(8,128)S(1)}, u32[]{:S(2)}, u32[]{:S(2)}) collective-permute-start(f32[32,512]{1,0:T(8,128)S(1)} %get-tuple-element.94), channel_id=1, source_target_pairs={{0,4},{1,5},{2,6},{3,7},{4,0},{5,1},{6,2},{7,3},{8,12},{9,13},{10,... | collective-permute-start | bytes 196616 | tf_op jit(solution)/shard_map/ppermute | solution.py:131
  68.7 0.6 copy-start.3
  69.3 10.6 %collective-permute-start.18 = (f32[32,512]{1,0:T(8,128)S(1)}, f32[32,512]{1,0:T(8,128)S(1)}, u32[]{:S(2)}, u32[]{:S(2)}) collective-permute-start(f32[32,512]{1,0:T(8,128)S(1)} %get-tuple-element.97), channel_id=1, source_target_pairs={{0,5},{1,4},{2,7},{3,6},{4,1},{5,0},{6,3},{7,2},{8,13},{9,12},{10,... | collective-permute-start | bytes 196616 | tf_op jit(solution)/shard_map/ppermute | solution.py:131
  71.5 0.6 copy-start.5
  79.3 0.6 copy-start.7
  79.9 0.6 copy-start.9
  80.5 11.9 %collective-permute-start.24 = (f32[64,512]{1,0:T(8,128)S(1)}, f32[64,512]{1,0:T(8,128)S(1)}, u32[]{:S(2)}, u32[]{:S(2)}) collective-permute-start(f32[64,512]{1,0:T(8,128)S(1)} %get-tuple-element.109), channel_id=1, source_target_pairs={{0,5},{1,4},{2,7},{3,6},{4,1},{5,0},{6,3},{7,2},{8,13},{9,12},{10,... | collective-permute-start | bytes 393224 | tf_op jit(solution)/shard_map/ppermute | solution.py:131
  80.5 14.7 %collective-permute-start.23 = (f32[64,512]{1,0:T(8,128)S(1)}, f32[64,512]{1,0:T(8,128)S(1)}, u32[]{:S(2)}, u32[]{:S(2)}) collective-permute-start(f32[64,512]{1,0:T(8,128)S(1)} %get-tuple-element.108), channel_id=1, source_target_pairs={{0,4},{1,5},{2,6},{3,7},{4,0},{5,1},{6,2},{7,3},{8,12},{9,13},{10,... | collective-permute-start | bytes 393224 | tf_op jit(solution)/shard_map/ppermute | solution.py:131
  82.9 12.3 %collective-permute-start.22 = (f32[64,512]{1,0:T(8,128)S(1)}, f32[64,512]{1,0:T(8,128)S(1)}, u32[]{:S(2)}, u32[]{:S(2)}) collective-permute-start(f32[64,512]{1,0:T(8,128)S(1)} %get-tuple-element.107), channel_id=1, source_target_pairs={{0,3},{1,2},{2,1},{3,0},{4,7},{5,6},{6,5},{7,4},{8,11},{9,10},{10,... | collective-permute-start | bytes 393224 | tf_op jit(solution)/shard_map/ppermute | solution.py:131
  83.5 13.6 %collective-permute-start.21 = (f32[64,512]{1,0:T(8,128)S(1)}, f32[64,512]{1,0:T(8,128)S(1)}, u32[]{:S(2)}, u32[]{:S(2)}) collective-permute-start(f32[64,512]{1,0:T(8,128)S(1)} %get-tuple-element.106), channel_id=1, source_target_pairs={{0,2},{1,3},{2,0},{3,1},{4,6},{5,7},{6,4},{7,5},{8,10},{9,11},{10,... | collective-permute-start | bytes 393224 | tf_op jit(solution)/shard_map/ppermute | solution.py:131
  84.9 12.1 %collective-permute-start.20 = (f32[64,512]{1,0:T(8,128)S(1)}, f32[64,512]{1,0:T(8,128)S(1)}, u32[]{:S(2)}, u32[]{:S(2)}) collective-permute-start(f32[64,512]{1,0:T(8,128)S(1)} %get-tuple-element.105), channel_id=1, source_target_pairs={{0,1},{1,0},{2,3},{3,2},{4,5},{5,4},{6,7},{7,6},{8,9},{9,8},{10,11... | collective-permute-start | bytes 393224 | tf_op jit(solution)/shard_map/ppermute | solution.py:131
  85.0 12.1 %copy-start.2 = (f32[32,512]{1,0:T(8,128)S(1)}, f32[32,512]{1,0:T(8,128)}, u32[]{:S(2)}) copy-start(f32[32,512]{1,0:T(8,128)} %copy-done.1) | copy-start | bytes 196612
  85.0 12.1 %copy-start.4 = (f32[32,512]{1,0:T(8,128)S(1)}, f32[32,512]{1,0:T(8,128)}, u32[]{:S(2)}) copy-start(f32[32,512]{1,0:T(8,128)} %copy-done.3) | copy-start | bytes 196612
  85.0 12.1 %copy-start.6 = (f32[32,512]{1,0:T(8,128)S(1)}, f32[32,512]{1,0:T(8,128)}, u32[]{:S(2)}) copy-start(f32[32,512]{1,0:T(8,128)} %copy-done.5) | copy-start | bytes 196612
  85.0 12.1 %copy-start.8 = (f32[32,512]{1,0:T(8,128)S(1)}, f32[32,512]{1,0:T(8,128)}, u32[]{:S(2)}) copy-start(f32[32,512]{1,0:T(8,128)} %copy-done.7) | copy-start | bytes 196612
  85.0 12.1 %copy-start.10 = (f32[32,512]{1,0:T(8,128)S(1)}, f32[32,512]{1,0:T(8,128)}, u32[]{:S(2)}) copy-start(f32[32,512]{1,0:T(8,128)} %copy-done.9) | copy-start | bytes 196612
  98.9 2.9 %collective-permute-start.26 = (f32[384,768]{1,0:T(8,128)S(1)}, f32[384,768]{1,0:T(8,128)S(1)}, u32[]{:S(2)}, u32[]{:S(2)}) collective-permute-start(f32[384,768]{1,0:T(8,128)S(1)} %gram.3), channel_id=1, source_target_pairs={{0,1},{1,0},{2,3},{3,2},{4,5},{5,4},{6,7},{7,6},{8,9},{9,8},{10,11... | collective-permute-start | bytes 3538952 | tf_op jit(solution)/shard_map/ppermute | solution.py:356
  102.5 10.8 %collective-permute-start.27 = (f32[4,24,768]{2,1,0:T(8,128)S(1)}, f32[4,24,768]{2,1,0:T(8,128)S(1)}, u32[]{:S(2)}, u32[]{:S(2)}) collective-permute-start(f32[4,24,768]{2,1,0:T(8,128)S(1)} %get-tuple-element.113), channel_id=1, source_target_pairs={{0,8},{8,16},{16,24},{24,0},{1,9},{9,17},{17,25},{25,1},{2,10},{10... | collective-permute-start | bytes 884744 | tf_op jit(solution)/shard_map/ppermute | solution.py:288
  102.6 15.4 %collective-permute-start.28 = (f32[4,24,768]{2,1,0:T(8,128)S(1)}, f32[4,24,768]{2,1,0:T(8,128)S(1)}, u32[]{:S(2)}, u32[]{:S(2)}) collective-permute-start(f32[4,24,768]{2,1,0:T(8,128)S(1)} %get-tuple-element.114), channel_id=1, source_target_pairs={{0,16},{8,24},{16,0},{24,8},{1,17},{9,25},{17,1},{25,9},{2,18},{10... | collective-permute-start | bytes 884744 | tf_op jit(solution)/shard_map/ppermute | solution.py:288
  103.9 14.8 %collective-permute-start.29 = (f32[4,24,768]{2,1,0:T(8,128)S(1)}, f32[4,24,768]{2,1,0:T(8,128)S(1)}, u32[]{:S(2)}, u32[]{:S(2)}) collective-permute-start(f32[4,24,768]{2,1,0:T(8,128)S(1)} %get-tuple-element.115), channel_id=1, source_target_pairs={{0,24},{8,0},{16,8},{24,16},{1,25},{9,1},{17,9},{25,17},{2,26},{10... | collective-permute-start | bytes 884744 | tf_op jit(solution)/shard_map/ppermute | solution.py:288
  118.8 5.2 %collective-permute-start.30 = (f32[24,768]{1,0:T(8,128)S(1)}, f32[24,768]{1,0:T(8,128)S(1)}, u32[]{:S(2)}, u32[]{:S(2)}) collective-permute-start(f32[24,768]{1,0:T(8,128)S(1)} %get-tuple-element.116), channel_id=1, source_target_pairs={{0,2},{1,3},{2,0},{3,1},{4,6},{5,7},{6,4},{7,5},{8,10},{9,11},{10,... | collective-permute-start | bytes 221192 | tf_op jit(solution)/shard_map/ppermute | solution.py:131
  118.9 7.0 %collective-permute-start.32 = (f32[24,768]{1,0:T(8,128)S(1)}, f32[24,768]{1,0:T(8,128)S(1)}, u32[]{:S(2)}, u32[]{:S(2)}) collective-permute-start(f32[24,768]{1,0:T(8,128)S(1)} %get-tuple-element.117), channel_id=1, source_target_pairs={{0,6},{1,7},{2,4},{3,5},{4,2},{5,3},{6,0},{7,1},{8,14},{9,15},{10,... | collective-permute-start | bytes 221192 | tf_op jit(solution)/shard_map/ppermute | solution.py:131
  121.6 7.0 %collective-permute-start.31 = (f32[24,768]{1,0:T(8,128)S(1)}, f32[24,768]{1,0:T(8,128)S(1)}, u32[]{:S(2)}, u32[]{:S(2)}) collective-permute-start(f32[24,768]{1,0:T(8,128)S(1)} %get-tuple-element.118), channel_id=1, source_target_pairs={{0,4},{1,5},{2,6},{3,7},{4,0},{5,1},{6,2},{7,3},{8,12},{9,13},{10,... | collective-permute-start | bytes 221192 | tf_op jit(solution)/shard_map/ppermute | solution.py:131
  128.7 4.6 %collective-permute-start.35 = (f32[24,768]{1,0:T(8,128)S(1)}, f32[24,768]{1,0:T(8,128)S(1)}, u32[]{:S(2)}, u32[]{:S(2)}) collective-permute-start(f32[24,768]{1,0:T(8,128)S(1)} %fusion.2.refs_0_), channel_id=1, source_target_pairs={{0,24},{8,0},{16,8},{24,16},{1,25},{9,1},{17,9},{25,17},{2,26},{10... | collective-permute-start | bytes 221192 | tf_op jit(solution)/shard_map/ppermute | solution.py:288
  130.5 4.7 %collective-permute-start.34 = (f32[24,768]{1,0:T(8,128)S(1)}, f32[24,768]{1,0:T(8,128)S(1)}, u32[]{:S(2)}, u32[]{:S(2)}) collective-permute-start(f32[24,768]{1,0:T(8,128)S(1)} %fusion.2.refs_0_), channel_id=1, source_target_pairs={{0,16},{8,24},{16,0},{24,8},{1,17},{9,25},{17,1},{25,9},{2,18},{10... | collective-permute-start | bytes 221192 | tf_op jit(solution)/shard_map/ppermute | solution.py:288
  131.8 5.3 %collective-permute-start.33 = (f32[24,768]{1,0:T(8,128)S(1)}, f32[24,768]{1,0:T(8,128)S(1)}, u32[]{:S(2)}, u32[]{:S(2)}) collective-permute-start(f32[24,768]{1,0:T(8,128)S(1)} %fusion.2.refs_0_), channel_id=1, source_target_pairs={{0,8},{8,16},{16,24},{24,0},{1,9},{9,17},{17,25},{25,1},{2,10},{10... | collective-permute-start | bytes 221192 | tf_op jit(solution)/shard_map/ppermute | solution.py:288

commit v5 on v4

--- a/solution.py
+++ b/solution.py
@@ -140,19 +140,23 @@
         for sub in range(subs):
             first = pl.multiple_of((group * subs + sub) * chunk, chunk)
             block = blocks[k * subs + sub]
-            for step, out in enumerate(outs):
-                target = partner(mine, band, step)
+            for step in range(band):
+                out = outs[0].at[step] if len(outs) == 1 else outs[step]
+                target = step if len(outs) == 1 else partner(mine, band, step)
                 for q in range(share):
                     out[pl.ds(first, chunk), q * LANES : (q + 1) * LANES] = block[target * share + q]
 
 
-def pack(here, blocks, space, band, share, chunk, subs):
+def pack(here, blocks, space, band, share, chunk, subs, apart):
     shape = (space * subs * chunk, share * LANES)
+    out_shape = [jax.ShapeDtypeStruct(shape, jnp.float32)] * band
+    if not apart:
+        out_shape = [jax.ShapeDtypeStruct((band,) + shape, jnp.float32)]
     return pl.pallas_call(
         functools.partial(pack_kernel, space, band, share, chunk, subs),
-        out_shape=[jax.ShapeDtypeStruct(shape, jnp.float32)] * band,
+        out_shape=out_shape,
         in_specs=[SMEM_SPEC] + [VMEM_SPEC] * len(blocks),
-        out_specs=[VMEM_SPEC] * band,
+        out_specs=[VMEM_SPEC] * len(out_shape),
         compiler_params=pltpu.CompilerParams(vmem_limit_bytes=VMEM_LIMIT),
         cost_estimate=pl.CostEstimate(
             flops=0, bytes_accessed=8 * band * space * subs * chunk * share * LANES, transcendentals=0
@@ -195,14 +199,15 @@
 def gram_kernel(band, count, space, chunk, places, which_ref, *refs):
     parts, out, wide = list(refs[:-2]), refs[-2], refs[-1]
     own = count // space
-    for offset, subs in places:
+    for offset, subs, apart in places:
         size = subs * chunk
+        taken = [parts.pop(0) for _ in range(band)] if apart else parts.pop(0)
         for step in range(band):
-            source = partner(which_ref[1], band, step, forward=False)
-            part = parts.pop(0)
+            source = partner(which_ref[1], band, step, forward=False) if apart else step
             for g in range(space):
-                first = pl.multiple_of(source * count + g * own + offset, chunk)
-                wide[pl.ds(first, size), :] = part[g * size : (g + 1) * size, :]
+                first = source * count + g * own + offset
+                first = pl.multiple_of(first, chunk) if apart else first
+                wide[pl.ds(first, size), :] = taken[step][g * size : (g + 1) * size, :]
     which = which_ref[0]
     pairs = band // 2
     picked = [wide[pl.ds(pl.multiple_of((2 * z + which) * count, SUBLANES), count), :] for z in range(pairs)]
@@ -240,47 +245,23 @@
     )(which, *parts)
 
 
-def combine_kernel(space, here_ref, a_ref, b_ref, *outs):
-    for k, out in enumerate(outs):
-        group = here_ref[0] + k
-        group = jnp.where(group >= space, group - space, group)
-        for z in range(out.shape[0]):
-            out[z] = a_ref[z, group] + b_ref[z, group]
-
-
-def combine(here, a, b):
+def combine_kernel(a_ref, b_ref, out_ref):
+    for z in range(a_ref.shape[0]):
+        for g in range(a_ref.shape[1]):
+            out_ref[g, z] = a_ref[z, g] + b_ref[z, g]
+
+
+def combine(a, b):
     pairs, space, own, columns = a.shape
     return pl.pallas_call(
-        functools.partial(combine_kernel, space),
-        out_shape=[jax.ShapeDtypeStruct((pairs, own, columns), jnp.float32)] * space,
-        in_specs=[SMEM_SPEC] + [VMEM_SPEC] * 2,
-        out_specs=[VMEM_SPEC] * space,
+        combine_kernel,
+        out_shape=jax.ShapeDtypeStruct((space, pairs, own, columns), jnp.float32),
+        in_specs=[VMEM_SPEC] * 2,
+        out_specs=VMEM_SPEC,
         compiler_params=pltpu.CompilerParams(vmem_limit_bytes=VMEM_LIMIT),
         cost_estimate=pl.CostEstimate(flops=a.size, bytes_accessed=12 * a.size, transcendentals=0),
         name="combine",
-    )(here, a, b)
-
-
-def place_kernel(space, here_ref, *refs):
-    parts, out = refs[:-1], refs[-1]
-    for k, part in enumerate(parts):
-        group = here_ref[0] - k
-        group = jnp.where(group < 0, group + space, group)
-        out[group] = part[...]
-
-
-def place(here, parts):
-    space = len(parts)
-    own, columns = parts[0].shape
-    return pl.pallas_call(
-        functools.partial(place_kernel, space),
-        out_shape=jax.ShapeDtypeStruct((space, own, columns), jnp.float32),
-        in_specs=[SMEM_SPEC] + [VMEM_SPEC] * space,
-        out_specs=VMEM_SPEC,
-        compiler_params=pltpu.CompilerParams(vmem_limit_bytes=VMEM_LIMIT),
-        cost_estimate=pl.CostEstimate(flops=0, bytes_accessed=8 * space * own * columns, transcendentals=0),
-        name="place",
-    )(here, *parts)
+    )(a, b)
 
 
 def rotate(x, axis, step):
@@ -315,31 +296,20 @@
         outs = run_filter(here, x, vs, c * chunk, space, layers, tiles, chunk)
         return [outs[0]] + [rotate(outs[k], "space", k) for k in range(1, space)]
 
-    order = sorted(range(1, band), reverse=True)
-    made = [filtered(0, arrived)]
-    if chunks > 1:
-        made.append(filtered(1, arrived))
-    parts = []
-    places = []
-    packed = pack(here, made[0], space, band, share, chunk, 1)
-    packed, arrived = lax.optimization_barrier((packed, arrived))
-    got = {0: packed[0]}
-    for k in order:
-        got[k] = exchange(packed[k], "band", k)
-    places.append((0, 1))
-    for c in range(2, chunks):
-        made.append(filtered(c, arrived))
+    made = [filtered(c, arrived) for c in range(min(chunks, 2))]
+    head = pack(here, made[0], space, band, share, chunk, 1, False)[0]
+    head, arrived = lax.optimization_barrier((head, arrived))
+    parts = [lax.all_to_all(head, "band", split_axis=0, concat_axis=0, tiled=True)]
+    places = [(0, 1, False)]
+    made += [filtered(c, arrived) for c in range(2, chunks)]
     if chunks > 1:
         late = [made[c][k] for k in range(space) for c in range(1, chunks)]
-        packed = pack(here, late, space, band, share, chunk, chunks - 1)
-        later = {0: packed[0]}
-        for k in order:
-            got[k], x = lax.optimization_barrier((got[k], packed[k]))
-            later[k] = exchange(x, "band", k)
-        places.append((chunk, chunks - 1))
-    parts += [got[k] for k in range(band)]
-    if chunks > 1:
-        parts += [later[k] for k in range(band)]
+        packed = pack(here, late, space, band, share, chunk, chunks - 1, True)
+        got = {0: packed[0]}
+        for k in reversed(range(1, band)):
+            got[k] = exchange(packed[k], "band", k)
+        parts += [got[k] for k in range(band)]
+        places.append((chunk, chunks - 1, True))
     blocks = [made[c][k] for k in range(space) for c in range(chunks)]
 
     result = unpack(here, blocks, space, rows, chunk, [chunks])
@@ -348,26 +318,21 @@
 
     pairs = band // 2
     core = b_index % 2
-    pair = b_index // 2
 
     def half(which):
         return gram(jnp.stack([which, b_index]), parts, band, count, space, chunk, places)
 
     other = lax.ppermute(half(1 - core), "band", [(i, i ^ 1) for i in range(band)])
     split = (pairs, space, own, band * count)
-    sums = combine(here, half(core).reshape(split), other.reshape(split))
-
-    mine = sums[0]
-    for k in range(1, space):
-        mine = mine + rotate(sums[k], "space", k)
-
-    final = lax.dynamic_index_in_dim(mine, pair, 0, keepdims=False)
-    for k in range(1, pairs):
-        sent = lax.dynamic_index_in_dim(mine, partner(pair, pairs, k), 0, keepdims=False)
-        final = final + exchange(sent, "band", k, 2)
-    final = final * (1.0 / (layers * space * plane))
-
-    margin = place(here, [final] + [rotate(final, "space", k) for k in range(1, space)])
+    sums = combine(half(core).reshape(split), other.reshape(split))
+
+    def swap(x, axis, groups=None):
+        return lax.all_to_all(x, axis, split_axis=0, concat_axis=0, tiled=True, axis_index_groups=groups)
+
+    over_space = jnp.sum(swap(sums, "space"), axis=0)
+    same_core = [list(range(low, band, 2)) for low in range(2)]
+    final = jnp.sum(swap(over_space, "band", same_core), axis=0) * (1.0 / (layers * space * plane))
+    margin = swap(jnp.broadcast_to(final[None], (space, own, band * count)), "space")
     return result, margin.reshape(count, band * count)
 
 

time: 139 us -> 141 us (1.014)
  blocking collectives: 0 us -> 41.4 us
  waiting for transfers between devices: 59.9 us -> 35.6 us
  starting transfers between devices: 50 us -> 37 us
  local copies, waits for them, and re-layouts: 3.19 us -> 0.74 us
    all_to_all x0 -> x3, blocking collectives: none -> 41.4 us  [swap(): lax.all_to_all(x, axis, split_axis=0, concat_axis=0, tiled=True, axis_ind...]
    ppermute x17 -> x7, waiting for transfers between devices: 26 us -> 11.1 us  [exchange(): return lax.ppermute(x, axis, pairs)]
    ppermute x17 -> x7, starting transfers between devices: 20.8 us -> 9.75 us  [exchange(): return lax.ppermute(x, axis, pairs)]
    ppermute x18 -> x12, waiting for transfers between devices: 32.9 us -> 24 us  [rotate(): return lax.ppermute(x, axis, [(i, (i + step) % size) for i in range(size)])]
    ppermute x18 -> x12, starting transfers between devices: 24 us -> 16.6 us  [rotate(): return lax.ppermute(x, axis, [(i, (i + step) % size) for i in range(size)])]
    all_to_all x0 -> x1, starting transfers between devices: none -> 5.08 us  [shards(): lax.all_to_all(head, 'band', split_axis=0, concat_axis=0, tiled=True)]
    unnamed x22 -> x3, local copies, waits for them, and re-layouts: 3.17 us -> 0.72 us
    pallas_call x2 -> x1, Pallas kernels: 1.94 us -> 0.12 us  [combine(): pl.pallas_call(combine_kernel, out_shape=jax.ShapeDtypeStruct((space, pai...]
  transfers between devices with their start and end apart: 37 -> 22, of which waited for: 17 -> 9; matrix products, arithmetic and copies ran while one was open for 0% -> 0% of each run, Pallas kernels for 11% -> 11%
where the time goes in v5:
time: 141 us; the launch traced here: 140 us
  blocking collectives  41.4 us (29%)
  starting transfers between devices  37 us (26%)
  waiting for transfers between devices  35.6 us (25%)
  Pallas kernels  24.4 us (17%)
    all_to_all x3, blocking collectives, swap(): lax.all_to_all(x, axis, split_axis=0, concat_axis=0, tiled=True, axis_ind...  41.4 us
    ppermute x12, waiting for transfers between devices, rotate(): return lax.ppermute(x, axis, [(i, (i + step) % size) for i in range(size)])  24 us
    ppermute x12, starting transfers between devices, rotate(): return lax.ppermute(x, axis, [(i, (i + step) % size) for i in range(size)])  16.6 us
    pallas_call x3, Pallas kernels, run_filter(): pl.pallas_call(functools.partial(filter_kernel, space, layers, tiles, chu...  14.6 us
    ppermute x7, waiting for transfers between devices, exchange(): return lax.ppermute(x, axis, pairs)  11.1 us
    ppermute x7, starting transfers between devices, exchange(): return lax.ppermute(x, axis, pairs)  9.75 us
    all_to_all x1, starting transfers between devices, shards(): lax.all_to_all(orbitals, 'space', split_axis=0, concat_axis=0, tiled=True)  5.18 us
    all_to_all x1, starting transfers between devices, shards(): lax.all_to_all(head, 'band', split_axis=0, concat_axis=0, tiled=True)  5.08 us
  transfers between devices with their start and end apart: 22, of which 9 were waited for; matrix products, arithmetic and copies ran while one was open for 0% of the time, Pallas kernels for 11%

profile of v5, /device:TPU:0, one launch (start us, length us, event | category | flops | bytes accessed | tf_op | source)
XLA Modules:
  0.0 140.1 jit_solution(5287427061547186643)
XLA Ops:
  0.6 0.0 copy-start
  0.6 5.2 %all-to-all-start = ((f32[96,2,2048]{2,1,0:T(2,128)}), f32[96,2,2048]{2,1,0:T(2,128)S(1)}, u32[]{:S(2)}, u32[]{:S(2)}) async-start(f32[96,2,2048]{2,1,0:T(2,128)} %param.2), calls=%async_computation | async-start | bytes 3145728 | tf_op jit(solution)/shard_map/all_to_all | solution.py:293
  5.8 0.0 copy-done
  5.8 2.0 %collective-permute-start.2 = (f32[32,128]{1,0:T(8,128)S(1)}, f32[32,128]{1,0:T(8,128)S(1)}, u32[]{:S(2)}, u32[]{:S(2)}) collective-permute-start(f32[32,128]{1,0:T(8,128)S(1)} %bitcast.27), channel_id=1, source_target_pairs={{0,8},{8,16},{16,24},{24,0},{1,9},{9,17},{17,25},{25,1},{2,10},{10... | collective-permute-start | bytes 49160 | tf_op jit(solution)/shard_map/ppermute | solution.py:269
  7.8 1.5 %collective-permute-start.1 = (f32[32,128]{1,0:T(8,128)S(1)}, f32[32,128]{1,0:T(8,128)S(1)}, u32[]{:S(2)}, u32[]{:S(2)}) collective-permute-start(f32[32,128]{1,0:T(8,128)S(1)} %bitcast.28), channel_id=1, source_target_pairs={{0,16},{8,24},{16,0},{24,8},{1,17},{9,25},{17,1},{25,9},{2,18},{10... | collective-permute-start | bytes 49160 | tf_op jit(solution)/shard_map/ppermute | solution.py:269
  9.3 1.5 %collective-permute-start = (f32[32,128]{1,0:T(8,128)S(1)}, f32[32,128]{1,0:T(8,128)S(1)}, u32[]{:S(2)}, u32[]{:S(2)}) collective-permute-start(f32[32,128]{1,0:T(8,128)S(1)} %bitcast.29), channel_id=1, source_target_pairs={{0,24},{8,0},{16,8},{24,16},{1,25},{9,1},{17,9},{25,17},{2,26},{10... | collective-permute-start | bytes 49160 | tf_op jit(solution)/shard_map/ppermute | solution.py:269
  10.8 0.1 pad_add_fusion.here_ref
  10.8 15.7 %collective-permute-done.2.refs_3_ = f32[32,128]{1,0:T(8,128)S(1)} collective-permute-done((f32[32,128]{1,0:T(8,128)S(1)}, f32[32,128]{1,0:T(8,128)S(1)}, u32[]{:S(2)}, u32[]{:S(2)}) %collective-permute-start.2) | collective-permute-done | bytes 16416 | tf_op jit(solution)/shard_map/ppermute | solution.py:269
  26.5 0.0 collective-permute-done.1.refs_2_
  26.5 0.0 collective-permute-done.refs_1_
  26.5 0.0 all-to-all-done
  26.5 4.9 %filter.4 = (f32[32,8,128]{2,1,0:T(8,128)S(1)}, f32[32,8,128]{2,1,0:T(8,128)S(1)}, f32[32,8,128]{2,1,0:T(8,128)S(1)}, f32[32,8,128]{2,1,0:T(8,128)S(1)}) custom-call(s32[2]{0:T(128)S(1)} %pad_add_fusion.here_ref, f32[3072,128]{1,0:T(8,128)S(1)} %bitcast.22, f32[32,128]{1,0:T(8,128)S(1)} %bitcast.30, f32[32,128]{1,0:T(8,128)S(1)} %collective-permute-done.refs_1_, ...), custom_call_target="tpu_custom_call" | custom-call | flops 9830400 | bytes 1048576 | tf_op jit(solution)/shard_map/filter/pallas_call | solution.py:101
  31.4 0.8 collective-permute-start.3
  32.2 0.5 collective-permute-start.4
  32.7 2.4 %collective-permute-start.5 = (f32[32,8,128]{2,1,0:T(8,128)S(1)}, f32[32,8,128]{2,1,0:T(8,128)S(1)}, u32[]{:S(2)}, u32[]{:S(2)}) collective-permute-start(f32[32,8,128]{2,1,0:T(8,128)S(1)} %get-tuple-element.30), channel_id=1, source_target_pairs={{0,24},{8,0},{16,8},{24,16},{1,25},{9,1},{17,9},{25,17},{2,26},{10... | collective-permute-start | bytes 393224 | tf_op jit(solution)/shard_map/ppermute | solution.py:269
  35.1 2.4 %collective-permute-done.3.refs_1_.refs_3_ = f32[32,8,128]{2,1,0:T(8,128)S(1)} collective-permute-done((f32[32,8,128]{2,1,0:T(8,128)S(1)}, f32[32,8,128]{2,1,0:T(8,128)S(1)}, u32[]{:S(2)}, u32[]{:S(2)}) %collective-permute-start.3) | collective-permute-done | bytes 131104 | tf_op jit(solution)/shard_map/ppermute | solution.py:269
  37.5 1.2 collective-permute-done.4.refs_2_.refs_6_
  38.8 0.0 collective-permute-done.5.refs_3_.refs_9_
  38.8 1.4 pack.2
  40.1 5.1 %all-to-all-start.1 = ((f32[8,32,512]{2,1,0:T(8,128)}), f32[8,32,512]{2,1,0:T(8,128)S(1)}, u32[]{:S(2)}, u32[]{:S(2)}) async-start(f32[8,32,512]{2,1,0:T(8,128)} %pack.2), calls=%async_computation.1 | async-start | bytes 1048576 | tf_op jit(solution)/shard_map/all_to_all | solution.py:302
  45.2 4.9 %filter.3 = (f32[32,8,128]{2,1,0:T(8,128)S(1)}, f32[32,8,128]{2,1,0:T(8,128)S(1)}, f32[32,8,128]{2,1,0:T(8,128)S(1)}, f32[32,8,128]{2,1,0:T(8,128)S(1)}) custom-call(s32[2]{0:T(128)S(1)} %pad_add_fusion.here_ref, f32[3072,128]{1,0:T(8,128)S(1)} %bitcast.23, f32[32,128]{1,0:T(8,128)S(1)} %bitcast.31, f32[32,128]{1,0:T(8,128)S(1)} %collective-permute-done.refs_1_, ...), custom_call_target="tpu_custom_call" | custom-call | flops 9830400 | bytes 1048576 | tf_op jit(solution)/shard_map/filter/pallas_call | solution.py:101
  50.1 2.1 %collective-permute-start.6 = (f32[32,8,128]{2,1,0:T(8,128)S(1)}, f32[32,8,128]{2,1,0:T(8,128)S(1)}, u32[]{:S(2)}, u32[]{:S(2)}) collective-permute-start(f32[32,8,128]{2,1,0:T(8,128)S(1)} %get-tuple-element.33), channel_id=1, source_target_pairs={{0,8},{8,16},{16,24},{24,0},{1,9},{9,17},{17,25},{25,1},{2,10},{10... | collective-permute-start | bytes 393224 | tf_op jit(solution)/shard_map/ppermute | solution.py:269
  52.2 1.3 collective-permute-start.8
  53.5 0.3 collective-permute-start.10
  53.8 4.9 %filter.5 = (f32[32,8,128]{2,1,0:T(8,128)S(1)}, f32[32,8,128]{2,1,0:T(8,128)S(1)}, f32[32,8,128]{2,1,0:T(8,128)S(1)}, f32[32,8,128]{2,1,0:T(8,128)S(1)}) custom-call(s32[2]{0:T(128)S(1)} %pad_add_fusion.here_ref, f32[3072,128]{1,0:T(8,128)S(1)} %bitcast.24, f32[32,128]{1,0:T(8,128)S(1)} %bitcast.32, f32[32,128]{1,0:T(8,128)S(1)} %collective-permute-done.refs_1_, ...), custom_call_target="tpu_custom_call" | custom-call | flops 9830400 | bytes 1048576 | tf_op jit(solution)/shard_map/filter/pallas_call | solution.py:101
  58.7 1.8 %collective-permute-start.7 = (f32[32,8,128]{2,1,0:T(8,128)S(1)}, f32[32,8,128]{2,1,0:T(8,128)S(1)}, u32[]{:S(2)}, u32[]{:S(2)}) collective-permute-start(f32[32,8,128]{2,1,0:T(8,128)S(1)} %get-tuple-element.34), channel_id=1, source_target_pairs={{0,8},{8,16},{16,24},{24,0},{1,9},{9,17},{17,25},{25,1},{2,10},{10... | collective-permute-start | bytes 393224 | tf_op jit(solution)/shard_map/ppermute | solution.py:269
  60.4 0.7 collective-permute-start.9
  61.2 0.0 collective-permute-done.6.refs_2_.refs_4_
  61.2 1.8 %collective-permute-start.11 = (f32[32,8,128]{2,1,0:T(8,128)S(1)}, f32[32,8,128]{2,1,0:T(8,128)S(1)}, u32[]{:S(2)}, u32[]{:S(2)}) collective-permute-start(f32[32,8,128]{2,1,0:T(8,128)S(1)} %get-tuple-element.38), channel_id=1, source_target_pairs={{0,24},{8,0},{16,8},{24,16},{1,25},{9,1},{17,9},{25,17},{2,26},{10... | collective-permute-start | bytes 393224 | tf_op jit(solution)/shard_map/ppermute | solution.py:269
  63.0 0.0 collective-permute-done.8.refs_4_.refs_7_
  63.0 0.0 collective-permute-done.10.refs_6_.refs_10_
  63.0 3.0 %collective-permute-done.7.refs_3_.refs_5_ = f32[32,8,128]{2,1,0:T(8,128)S(1)} collective-permute-done((f32[32,8,128]{2,1,0:T(8,128)S(1)}, f32[32,8,128]{2,1,0:T(8,128)S(1)}, u32[]{:S(2)}, u32[]{:S(2)}) %collective-permute-start.7) | collective-permute-done | bytes 131104 | tf_op jit(solution)/shard_map/ppermute | solution.py:269
  66.0 1.7 %collective-permute-done.9.refs_5_.refs_8_ = f32[32,8,128]{2,1,0:T(8,128)S(1)} collective-permute-done((f32[32,8,128]{2,1,0:T(8,128)S(1)}, f32[32,8,128]{2,1,0:T(8,128)S(1)}, u32[]{:S(2)}, u32[]{:S(2)}) %collective-permute-start.9) | collective-permute-done | bytes 131104 | tf_op jit(solution)/shard_map/ppermute | solution.py:269
  67.7 0.0 collective-permute-done.11.refs_7_.refs_11_
  67.7 1.4 pack.3
  69.1 2.7 %collective-permute-start.12 = (f32[64,512]{1,0:T(8,128)S(1)}, f32[64,512]{1,0:T(8,128)S(1)}, u32[]{:S(2)}, u32[]{:S(2)}) collective-permute-start(f32[64,512]{1,0:T(8,128)S(1)} %get-tuple-element.39), channel_id=1, source_target_pairs={{0,7},{1,6},{2,5},{3,4},{4,3},{5,2},{6,1},{7,0},{8,15},{9,14},{10,... | collective-permute-start | bytes 393224 | tf_op jit(solution)/shard_map/ppermute | solution.py:131
  71.8 0.9 collective-permute-start.13
  72.7 0.0 collective-permute-start.14
  72.7 1.4 collective-permute-start.15
  74.0 0.0 collective-permute-start.16
  74.0 2.6 %collective-permute-done.12.refs_8_ = f32[64,512]{1,0:T(8,128)S(1)} collective-permute-done((f32[64,512]{1,0:T(8,128)S(1)}, f32[64,512]{1,0:T(8,128)S(1)}, u32[]{:S(2)}, u32[]{:S(2)}) %collective-permute-start.12) | collective-permute-done | bytes 131104 | tf_op jit(solution)/shard_map/ppermute | solution.py:131
  76.7 3.0 %collective-permute-start.17 = (f32[64,512]{1,0:T(8,128)S(1)}, f32[64,512]{1,0:T(8,128)S(1)}, u32[]{:S(2)}, u32[]{:S(2)}) collective-permute-start(f32[64,512]{1,0:T(8,128)S(1)} %get-tuple-element.47), channel_id=1, source_target_pairs={{0,5},{1,4},{2,7},{3,6},{4,1},{5,0},{6,3},{7,2},{8,13},{9,12},{10,... | collective-permute-start | bytes 393224 | tf_op jit(solution)/shard_map/ppermute | solution.py:131
  79.6 0.0 collective-permute-done.13.refs_2_
  79.6 1.8 %collective-permute-start.18 = (f32[64,512]{1,0:T(8,128)S(1)}, f32[64,512]{1,0:T(8,128)}, u32[]{:S(2)}, u32[]{:S(2)}) collective-permute-start(f32[64,512]{1,0:T(8,128)S(1)} %get-tuple-element.48), channel_id=1, source_target_pairs={{0,6},{1,7},{2,4},{3,5},{4,2},{5,3},{6,0},{7,1},{8,14},{9,15},{10,... | collective-permute-start | bytes 393224 | tf_op jit(solution)/shard_map/ppermute | solution.py:131
  81.5 0.1 pad_add_fusion.1
  81.6 2.6 %unpack.1 = f32[3072,128]{1,0:T(8,128)} custom-call(s32[2]{0:T(128)S(1)} %pad_add_fusion.here_ref, f32[32,8,128]{2,1,0:T(8,128)S(1)} %get-tuple-element.27.refs_0_, f32[32,8,128]{2,1,0:T(8,128)S(1)} %get-tuple-element.26.refs_0_.refs_1_, f32[32,8,128]{2,1,0:T(8,128)S(1)} %get-tuple-element.32.refs_1_.refs_2_, ...), custom_call_target="tpu_custom_call" | custom-call | bytes 3145728 | tf_op jit(solution)/shard_map/unpack/pallas_call | solution.py:188
  84.2 0.0 collective-permute-done.14.refs_3_
  84.2 1.7 %collective-permute-done.15.refs_4_ = f32[64,512]{1,0:T(8,128)S(1)} collective-permute-done((f32[64,512]{1,0:T(8,128)}, f32[64,512]{1,0:T(8,128)S(1)}, u32[]{:S(2)}, u32[]{:S(2)}) %collective-permute-start.15) | collective-permute-done | bytes 131104 | tf_op jit(solution)/shard_map/ppermute | solution.py:131
  85.9 0.0 collective-permute-done.16.refs_5_
  85.9 6.7 %collective-permute-done.17.refs_6_ = f32[64,512]{1,0:T(8,128)S(1)} collective-permute-done((f32[64,512]{1,0:T(8,128)S(1)}, f32[64,512]{1,0:T(8,128)S(1)}, u32[]{:S(2)}, u32[]{:S(2)}) %collective-permute-start.17) | collective-permute-done | bytes 131104 | tf_op jit(solution)/shard_map/ppermute | solution.py:131
  92.7 0.0 collective-permute-done.18.refs_7_
  92.7 0.0 all-to-all-done.1.refs_0_
  92.7 2.1 %gram.3 = f32[384,768]{1,0:T(8,128)S(1)} custom-call(s32[2]{0:T(128)S(1)} %get-tuple-element.51.which_ref, f32[8,32,512]{2,1,0:T(8,128)S(1)} %all-to-all-done.1.refs_0_, f32[64,512]{1,0:T(8,128)S(1)} %get-tuple-element.42.refs_1_, f32[64,512]{1,0:T(8,128)S(1)} %collective-permute-done.13.refs_2_, f32[64,512]{1,0:T(8,128)S(1)} %collective-permute-done.14.refs_3_, ...), custom_call_target="tpu_custom_call" | custom-call | flops 905969664 | bytes 2752512 | tf_op jit(solution)/shard_map/gram/pallas_call | solution.py:232
  94.8 0.3 collective-permute-start.19
  95.2 2.1 %gram.2 = f32[384,768]{1,0:T(8,128)S(1)} custom-call(s32[2]{0:T(128)S(1)} %get-tuple-element.50.which_ref, f32[8,32,512]{2,1,0:T(8,128)S(1)} %all-to-all-done.1.refs_0_, f32[64,512]{1,0:T(8,128)S(1)} %get-tuple-element.42.refs_1_, f32[64,512]{1,0:T(8,128)S(1)} %collective-permute-done.13.refs_2_, f32[64,512]{1,0:T(8,128)S(1)} %collective-permute-done.14.refs_3_, ...), custom_call_target="tpu_custom_call" | custom-call | flops 905969664 | bytes 2752512 | tf_op jit(solution)/shard_map/gram/pallas_call | solution.py:232
  97.3 0.4 collective-permute-done.19
  97.7 0.1 combine.1
  97.9 19.1 %all_to_all.25 = f32[4,4,24,768]{3,2,1,0:T(8,128)S(1)} all-to-all(f32[4,4,24,768]{3,2,1,0:T(8,128)S(1)} %combine.1), channel_id=1, replica_groups=mesh['space'=4,'band'=8] {'space'}, dimensions={0} | all-to-all | bytes 2359296 | tf_op jit(solution)/shard_map/all_to_all | solution.py:330
  117.0 0.1 reduce_sum.18
  117.0 13.8 %all_to_all.26 = f32[4,24,768]{2,1,0:T(8,128)S(1)} all-to-all(f32[4,24,768]{2,1,0:T(8,128)S(1)} %reduce_sum.18), channel_id=1, replica_groups={{0,2,4,6},{1,3,5,7},{8,10,12,14},{9,11,13,15},{16,18,20,22},{17,19,21,2..., dimensions={0} | all-to-all | bytes 589824 | tf_op jit(solution)/shard_map/all_to_all | solution.py:330
  130.9 8.5 %all_to_all.27 = f32[4,24,768]{2,1,0:T(8,128)S(1)} all-to-all(f32[4,24,768]{2,1,0:T(8,128)S(1)} %broadcast_in_dim.2), channel_id=1, replica_groups=mesh['space'=4,'band'=8] {'space'}, dimensions={0} | all-to-all | bytes 589824 | tf_op jit(solution)/shard_map/all_to_all | solution.py:330
  139.4 0.7 copy.11
  (3 shorter events, 0.0 us)
Async XLA Ops:
  0.6 5.2 %copy-start = (f32[2,2048]{1,0:T(2,128)S(1)}, f32[2,2048]{1,0:T(2,128)}, u32[]{:S(2)}) copy-start(f32[2,2048]{1,0:T(2,128)} %param.3) | copy-start | bytes 49156
  0.6 25.9 %all-to-all-start = ((f32[96,2,2048]{2,1,0:T(2,128)}), f32[96,2,2048]{2,1,0:T(2,128)S(1)}, u32[]{:S(2)}, u32[]{:S(2)}) async-start(f32[96,2,2048]{2,1,0:T(2,128)} %param.2), calls=%async_computation | async-start | bytes 3145728 | tf_op jit(solution)/shard_map/all_to_all | solution.py:293
  5.8 20.7 %collective-permute-start.2 = (f32[32,128]{1,0:T(8,128)S(1)}, f32[32,128]{1,0:T(8,128)S(1)}, u32[]{:S(2)}, u32[]{:S(2)}) collective-permute-start(f32[32,128]{1,0:T(8,128)S(1)} %bitcast.27), channel_id=1, source_target_pairs={{0,8},{8,16},{16,24},{24,0},{1,9},{9,17},{17,25},{25,1},{2,10},{10... | collective-permute-start | bytes 49160 | tf_op jit(solution)/shard_map/ppermute | solution.py:269
  7.8 18.7 %collective-permute-start.1 = (f32[32,128]{1,0:T(8,128)S(1)}, f32[32,128]{1,0:T(8,128)S(1)}, u32[]{:S(2)}, u32[]{:S(2)}) collective-permute-start(f32[32,128]{1,0:T(8,128)S(1)} %bitcast.28), channel_id=1, source_target_pairs={{0,16},{8,24},{16,0},{24,8},{1,17},{9,25},{17,1},{25,9},{2,18},{10... | collective-permute-start | bytes 49160 | tf_op jit(solution)/shard_map/ppermute | solution.py:269
  9.3 17.2 %collective-permute-start = (f32[32,128]{1,0:T(8,128)S(1)}, f32[32,128]{1,0:T(8,128)S(1)}, u32[]{:S(2)}, u32[]{:S(2)}) collective-permute-start(f32[32,128]{1,0:T(8,128)S(1)} %bitcast.29), channel_id=1, source_target_pairs={{0,24},{8,0},{16,8},{24,16},{1,25},{9,1},{17,9},{25,17},{2,26},{10... | collective-permute-start | bytes 49160 | tf_op jit(solution)/shard_map/ppermute | solution.py:269
  31.4 6.1 %collective-permute-start.3 = (f32[32,8,128]{2,1,0:T(8,128)S(1)}, f32[32,8,128]{2,1,0:T(8,128)S(1)}, u32[]{:S(2)}, u32[]{:S(2)}) collective-permute-start(f32[32,8,128]{2,1,0:T(8,128)S(1)} %get-tuple-element.28), channel_id=1, source_target_pairs={{0,8},{8,16},{16,24},{24,0},{1,9},{9,17},{17,25},{25,1},{2,10},{10... | collective-permute-start | bytes 393224 | tf_op jit(solution)/shard_map/ppermute | solution.py:269
  32.2 6.6 %collective-permute-start.4 = (f32[32,8,128]{2,1,0:T(8,128)S(1)}, f32[32,8,128]{2,1,0:T(8,128)S(1)}, u32[]{:S(2)}, u32[]{:S(2)}) collective-permute-start(f32[32,8,128]{2,1,0:T(8,128)S(1)} %get-tuple-element.29), channel_id=1, source_target_pairs={{0,16},{8,24},{16,0},{24,8},{1,17},{9,25},{17,1},{25,9},{2,18},{10... | collective-permute-start | bytes 393224 | tf_op jit(solution)/shard_map/ppermute | solution.py:269
  32.7 6.1 %collective-permute-start.5 = (f32[32,8,128]{2,1,0:T(8,128)S(1)}, f32[32,8,128]{2,1,0:T(8,128)S(1)}, u32[]{:S(2)}, u32[]{:S(2)}) collective-permute-start(f32[32,8,128]{2,1,0:T(8,128)S(1)} %get-tuple-element.30), channel_id=1, source_target_pairs={{0,24},{8,0},{16,8},{24,16},{1,25},{9,1},{17,9},{25,17},{2,26},{10... | collective-permute-start | bytes 393224 | tf_op jit(solution)/shard_map/ppermute | solution.py:269
  40.1 52.5 %all-to-all-start.1 = ((f32[8,32,512]{2,1,0:T(8,128)}), f32[8,32,512]{2,1,0:T(8,128)S(1)}, u32[]{:S(2)}, u32[]{:S(2)}) async-start(f32[8,32,512]{2,1,0:T(8,128)} %pack.2), calls=%async_computation.1 | async-start | bytes 1048576 | tf_op jit(solution)/shard_map/all_to_all | solution.py:302
  50.1 11.1 %collective-permute-start.6 = (f32[32,8,128]{2,1,0:T(8,128)S(1)}, f32[32,8,128]{2,1,0:T(8,128)S(1)}, u32[]{:S(2)}, u32[]{:S(2)}) collective-permute-start(f32[32,8,128]{2,1,0:T(8,128)S(1)} %get-tuple-element.33), channel_id=1, source_target_pairs={{0,8},{8,16},{16,24},{24,0},{1,9},{9,17},{17,25},{25,1},{2,10},{10... | collective-permute-start | bytes 393224 | tf_op jit(solution)/shard_map/ppermute | solution.py:269
  52.2 10.8 %collective-permute-start.8 = (f32[32,8,128]{2,1,0:T(8,128)S(1)}, f32[32,8,128]{2,1,0:T(8,128)S(1)}, u32[]{:S(2)}, u32[]{:S(2)}) collective-permute-start(f32[32,8,128]{2,1,0:T(8,128)S(1)} %get-tuple-element.35), channel_id=1, source_target_pairs={{0,16},{8,24},{16,0},{24,8},{1,17},{9,25},{17,1},{25,9},{2,18},{10... | collective-permute-start | bytes 393224 | tf_op jit(solution)/shard_map/ppermute | solution.py:269
  53.5 9.5 %collective-permute-start.10 = (f32[32,8,128]{2,1,0:T(8,128)S(1)}, f32[32,8,128]{2,1,0:T(8,128)S(1)}, u32[]{:S(2)}, u32[]{:S(2)}) collective-permute-start(f32[32,8,128]{2,1,0:T(8,128)S(1)} %get-tuple-element.37), channel_id=1, source_target_pairs={{0,24},{8,0},{16,8},{24,16},{1,25},{9,1},{17,9},{25,17},{2,26},{10... | collective-permute-start | bytes 393224 | tf_op jit(solution)/shard_map/ppermute | solution.py:269
  58.7 7.3 %collective-permute-start.7 = (f32[32,8,128]{2,1,0:T(8,128)S(1)}, f32[32,8,128]{2,1,0:T(8,128)S(1)}, u32[]{:S(2)}, u32[]{:S(2)}) collective-permute-start(f32[32,8,128]{2,1,0:T(8,128)S(1)} %get-tuple-element.34), channel_id=1, source_target_pairs={{0,8},{8,16},{16,24},{24,0},{1,9},{9,17},{17,25},{25,1},{2,10},{10... | collective-permute-start | bytes 393224 | tf_op jit(solution)/shard_map/ppermute | solution.py:269
  60.4 7.3 %collective-permute-start.9 = (f32[32,8,128]{2,1,0:T(8,128)S(1)}, f32[32,8,128]{2,1,0:T(8,128)S(1)}, u32[]{:S(2)}, u32[]{:S(2)}) collective-permute-start(f32[32,8,128]{2,1,0:T(8,128)S(1)} %get-tuple-element.36), channel_id=1, source_target_pairs={{0,16},{8,24},{16,0},{24,8},{1,17},{9,25},{17,1},{25,9},{2,18},{10... | collective-permute-start | bytes 393224 | tf_op jit(solution)/shard_map/ppermute | solution.py:269
  61.2 6.5 %collective-permute-start.11 = (f32[32,8,128]{2,1,0:T(8,128)S(1)}, f32[32,8,128]{2,1,0:T(8,128)S(1)}, u32[]{:S(2)}, u32[]{:S(2)}) collective-permute-start(f32[32,8,128]{2,1,0:T(8,128)S(1)} %get-tuple-element.38), channel_id=1, source_target_pairs={{0,24},{8,0},{16,8},{24,16},{1,25},{9,1},{17,9},{25,17},{2,26},{10... | collective-permute-start | bytes 393224 | tf_op jit(solution)/shard_map/ppermute | solution.py:269
  69.1 7.6 %collective-permute-start.12 = (f32[64,512]{1,0:T(8,128)S(1)}, f32[64,512]{1,0:T(8,128)S(1)}, u32[]{:S(2)}, u32[]{:S(2)}) collective-permute-start(f32[64,512]{1,0:T(8,128)S(1)} %get-tuple-element.39), channel_id=1, source_target_pairs={{0,7},{1,6},{2,5},{3,4},{4,3},{5,2},{6,1},{7,0},{8,15},{9,14},{10,... | collective-permute-start | bytes 393224 | tf_op jit(solution)/shard_map/ppermute | solution.py:131
  71.8 7.8 %collective-permute-start.13 = (f32[64,512]{1,0:T(8,128)S(1)}, f32[64,512]{1,0:T(8,128)S(1)}, u32[]{:S(2)}, u32[]{:S(2)}) collective-permute-start(f32[64,512]{1,0:T(8,128)S(1)} %get-tuple-element.43), channel_id=1, source_target_pairs={{0,1},{1,0},{2,3},{3,2},{4,5},{5,4},{6,7},{7,6},{8,9},{9,8},{10,11... | collective-permute-start | bytes 393224 | tf_op jit(solution)/shard_map/ppermute | solution.py:131
  72.7 11.5 %collective-permute-start.14 = (f32[64,512]{1,0:T(8,128)}, f32[64,512]{1,0:T(8,128)S(1)}, u32[]{:S(2)}, u32[]{:S(2)}) collective-permute-start(f32[64,512]{1,0:T(8,128)} %get-tuple-element.44), channel_id=1, source_target_pairs={{0,2},{1,3},{2,0},{3,1},{4,6},{5,7},{6,4},{7,5},{8,10},{9,11},{10,... | collective-permute-start | bytes 393224 | tf_op jit(solution)/shard_map/ppermute | solution.py:131
  72.7 13.2 %collective-permute-start.15 = (f32[64,512]{1,0:T(8,128)}, f32[64,512]{1,0:T(8,128)S(1)}, u32[]{:S(2)}, u32[]{:S(2)}) collective-permute-start(f32[64,512]{1,0:T(8,128)} %get-tuple-element.45), channel_id=1, source_target_pairs={{0,3},{1,2},{2,1},{3,0},{4,7},{5,6},{6,5},{7,4},{8,11},{9,10},{10,... | collective-permute-start | bytes 393224 | tf_op jit(solution)/shard_map/ppermute | solution.py:131
  74.0 11.9 %collective-permute-start.16 = (f32[64,512]{1,0:T(8,128)S(1)}, f32[64,512]{1,0:T(8,128)S(1)}, u32[]{:S(2)}, u32[]{:S(2)}) collective-permute-start(f32[64,512]{1,0:T(8,128)S(1)} %get-tuple-element.46), channel_id=1, source_target_pairs={{0,4},{1,5},{2,6},{3,7},{4,0},{5,1},{6,2},{7,3},{8,12},{9,13},{10,... | collective-permute-start | bytes 393224 | tf_op jit(solution)/shard_map/ppermute | solution.py:131
  76.7 16.0 %collective-permute-start.17 = (f32[64,512]{1,0:T(8,128)S(1)}, f32[64,512]{1,0:T(8,128)S(1)}, u32[]{:S(2)}, u32[]{:S(2)}) collective-permute-start(f32[64,512]{1,0:T(8,128)S(1)} %get-tuple-element.47), channel_id=1, source_target_pairs={{0,5},{1,4},{2,7},{3,6},{4,1},{5,0},{6,3},{7,2},{8,13},{9,12},{10,... | collective-permute-start | bytes 393224 | tf_op jit(solution)/shard_map/ppermute | solution.py:131
  79.6 13.0 %collective-permute-start.18 = (f32[64,512]{1,0:T(8,128)S(1)}, f32[64,512]{1,0:T(8,128)}, u32[]{:S(2)}, u32[]{:S(2)}) collective-permute-start(f32[64,512]{1,0:T(8,128)S(1)} %get-tuple-element.48), channel_id=1, source_target_pairs={{0,6},{1,7},{2,4},{3,5},{4,2},{5,3},{6,0},{7,1},{8,14},{9,15},{10,... | collective-permute-start | bytes 393224 | tf_op jit(solution)/shard_map/ppermute | solution.py:131
  94.8 2.9 %collective-permute-start.19 = (f32[384,768]{1,0:T(8,128)S(1)}, f32[384,768]{1,0:T(8,128)S(1)}, u32[]{:S(2)}, u32[]{:S(2)}) collective-permute-start(f32[384,768]{1,0:T(8,128)S(1)} %gram.3), channel_id=1, source_target_pairs={{0,1},{1,0},{2,3},{3,2},{4,5},{5,4},{6,7},{7,6},{8,9},{9,8},{10,11... | collective-permute-start | bytes 3538952 | tf_op jit(solution)/shard_map/ppermute | solution.py:325

commit v6 on v5

--- a/solution.py
+++ b/solution.py
@@ -2,6 +2,8 @@
 
 import jax
 import jax.numpy as jnp
+import ml_dtypes
+import numpy as np
 from jax import lax
 from jax.experimental import pallas as pl
 from jax.experimental.pallas import tpu as pltpu
@@ -13,105 +15,116 @@
 VMEM_LIMIT = 40 * 1024 * 1024
 
 
-def filter_kernel(space, layers, tiles, chunk, pitch, offset, unroll, here_ref, x_ref, *refs):
+def plane_matrix():
+    wide = 2 * LANES
+    matrix = np.zeros((2 * wide, wide), np.float32)
+    for y in range(wide // NZ):
+        for z in range(NZ):
+            column = y * NZ + z
+            for step, weight in ((1, -16.0), (-1, -16.0), (2, 1.0), (-2, 1.0)):
+                matrix[y * NZ + (z + step) % NZ, column] += weight
+                row = y + step
+                if row < 0:
+                    row += 6
+                elif row >= 4:
+                    row += 2
+                matrix[row * NZ + z, column] += weight
+    return matrix.astype(ml_dtypes.bfloat16)
+
+
+def filter_kernel(space, layers, tiles, chunk, pitch, offset, here_ref, x_ref, m_ref, *refs):
     v_refs, out_refs = refs[:space], refs[space : 2 * space]
-    f0, r0, f1, r1, f2, r2, coef = refs[2 * space :]
+    f0, f1, coef, mm, hi, lo = refs[2 * space :]
     planes = space * layers
     rows = tiles * layers
-    lane = lax.broadcasted_iota(jnp.int32, (chunk, LANES), 1)
-    depth = lane % NZ
-    first_half = lane < NZ
-    starts = [depth < 1, depth < 2]
-    ends = [depth >= NZ - 1, depth >= NZ - 2]
+    quads, height, wide = f0.shape
     here = here_ref[0]
 
-    def load(tile, carry):
+    def put(f, j, v):
+        f[j] = v
+        top = v.astype(jnp.bfloat16)
+        hi[j] = top
+        lo[j] = (v - top.astype(jnp.float32)).astype(jnp.bfloat16)
+
+    for j in range(quads):
+        columns = []
+        for half in range(2):
+            column = []
+            for p in range(planes):
+                s, l = divmod(p, layers)
+                row = (2 * j + half) * layers + l
+                slab = here + s
+                slab = jnp.where(slab >= space, slab - space, slab)
+                column.append(x_ref[pl.ds((slab * pitch + offset) * rows + row, chunk, stride=rows), :])
+                w = v_refs[s][row : row + 1, :]
+                coef[j, p * chunk : (p + 1) * chunk, half * LANES : (half + 1) * LANES] = jnp.broadcast_to(
+                    0.5 * w - 1.125, (chunk, LANES)
+                )
+            columns.append(jnp.concatenate(column, axis=0))
+        put(f0, j, jnp.concatenate(columns, axis=1))
+
+    def beside(a):
+        before = jnp.concatenate([a[quads - 1 :], a[: quads - 1]], axis=0)
+        after = jnp.concatenate([a[1:], a[:1]], axis=0)
+        return jnp.concatenate([before[:, :, LANES:], after[:, :, :LANES]], axis=2)
+
+    def product():
+        top, rest = hi[...], lo[...]
+        left = jnp.concatenate([top, beside(top), rest, beside(rest)], axis=2).reshape(quads * height, 4 * wide)
+        right = jnp.concatenate([m_ref[...], m_ref[...]], axis=0)
+        got = lax.dot_general(left, right, (((1,), (0,)), ((), ())), preferred_element_type=jnp.float32)
+        mm[...] = got.reshape(quads, height, wide)
+
+    def stencil(f, j):
+        v = f[j]
+
+        def moved(k):
+            k = k % planes * chunk
+            return jnp.concatenate([v[k:], v[:k]], axis=0) if k else v
+
+        return v, (mm[j] + (moved(2) + moved(-2))) - 16.0 * (moved(1) + moved(-1))
+
+    product()
+    for j in range(quads):
+        v, s = stencil(f0, j)
+        put(f1, j, (1.0 / 96.0) * s + 0.5 * (coef[j] * v))
+    product()
+    for j in range(quads):
+        v, s = stencil(f1, j)
+        put(f0, j, ((1.0 / 48.0) * s + coef[j] * v) - f0[j])
+    product()
+    for j in range(quads):
+        v, s = stencil(f0, j)
+        y = ((1.0 / 48.0) * s + coef[j] * v) - f1[j]
         for p in range(planes):
-            s, l = divmod(p, layers)
-            row = tile * layers + l
-            slab = here + s
-            slab = jnp.where(slab >= space, slab - space, slab)
-            v = x_ref[pl.ds((slab * pitch + offset) * rows + row, chunk, stride=rows), :]
-            f0[tile, p] = v
-            r0[tile, p] = pltpu.roll(v, NZ, 1)
-            w = v_refs[s][pl.ds(row, 1), :]
-            coef[tile, p] = jnp.broadcast_to(0.25 * w - 0.5625, (chunk, LANES))
-        return carry
-
-    def stencil(f, r, tile):
-        up = jnp.where(tile == tiles - 1, 0, tile + 1)
-        down = jnp.where(tile == 0, tiles - 1, tile - 1)
-        v = [f[tile, p] for p in range(planes)]
-        pairs = {}
-
-        def pair(a, b):
-            key = (min(a, b), max(a, b))
-            if key not in pairs:
-                pairs[key] = v[a] + v[b]
-            return pairs[key]
-
-        out = []
-        for p in range(planes):
-            rolled = r[tile, p]
-            near = pair((p - 1) % planes, (p + 1) % planes)
-            far = pair((p - 2) % planes, (p + 2) % planes)
-            far = far + (f[up, p] + f[down, p])
-            near = near + (rolled + jnp.where(first_half, r[down, p], r[up, p]))
-            near = near + pltpu.roll(jnp.where(starts[0], rolled, v[p]), LANES - 1, 1)
-            near = near + pltpu.roll(jnp.where(ends[0], rolled, v[p]), 1, 1)
-            far = far + pltpu.roll(jnp.where(starts[1], rolled, v[p]), LANES - 2, 1)
-            far = far + pltpu.roll(jnp.where(ends[1], rolled, v[p]), 2, 1)
-            out.append((v[p], far - 16.0 * near))
-        return out
-
-    def first(tile, carry):
-        for p, (v, s) in enumerate(stencil(f0, r0, tile)):
-            y = (1.0 / 96.0) * s + coef[tile, p] * v
-            f1[tile, p] = y
-            r1[tile, p] = pltpu.roll(y, NZ, 1)
-        return carry
-
-    def second(tile, carry):
-        for p, (v, s) in enumerate(stencil(f1, r1, tile)):
-            y = 2.0 * ((1.0 / 96.0) * s + coef[tile, p] * v) - f0[tile, p]
-            f2[tile, p] = y
-            r2[tile, p] = pltpu.roll(y, NZ, 1)
-        return carry
-
-    def third(tile, carry):
-        for p, (v, s) in enumerate(stencil(f2, r2, tile)):
-            y = 2.0 * ((1.0 / 96.0) * s + coef[tile, p] * v) - f1[tile, p]
-            out_refs[p // layers][tile * layers + p % layers] = y
-        return carry
-
-    for step in (load, first, second, third):
-        lax.fori_loop(0, tiles, step, 0, unroll=unroll)
+            for half in range(2):
+                block = y[p * chunk : (p + 1) * chunk, half * LANES : (half + 1) * LANES]
+                out_refs[p // layers][(2 * j + half) * layers + p % layers] = block
 
 
 VMEM_SPEC = pl.BlockSpec(memory_space=pltpu.VMEM)
 SMEM_SPEC = pl.BlockSpec(memory_space=pltpu.SMEM)
 
 
-def run_filter(here, x, vs, offset, space, layers, tiles, chunk):
+def run_filter(here, x, matrix, vs, offset, space, layers, tiles, chunk):
     rows = tiles * layers
     planes = space * layers
     pitch = x.shape[0] // (space * rows)
-    field = pltpu.VMEM((tiles, planes, chunk, LANES), jnp.float32)
-    unroll = 8 if tiles % 8 == 0 and planes <= 8 else 1
-    return pl.pallas_call(
-        functools.partial(filter_kernel, space, layers, tiles, chunk, pitch, offset, unroll),
+    shape = (tiles // 2, planes * chunk, 2 * LANES)
+    return pl.pallas_call(
+        functools.partial(filter_kernel, space, layers, tiles, chunk, pitch, offset),
         out_shape=[jax.ShapeDtypeStruct((rows, chunk, LANES), jnp.float32)] * space,
-        in_specs=[SMEM_SPEC] + [VMEM_SPEC] * (1 + space),
+        in_specs=[SMEM_SPEC] + [VMEM_SPEC] * (2 + space),
         out_specs=[VMEM_SPEC] * space,
-        scratch_shapes=[field] * 7,
+        scratch_shapes=[pltpu.VMEM(shape, jnp.float32)] * 4 + [pltpu.VMEM(shape, jnp.bfloat16)] * 2,
         compiler_params=pltpu.CompilerParams(vmem_limit_bytes=VMEM_LIMIT),
         cost_estimate=pl.CostEstimate(
-            flops=75 * planes * tiles * SUBLANES * LANES,
+            flops=50 * planes * tiles * SUBLANES * LANES,
             bytes_accessed=2 * planes * tiles * chunk * LANES * 4,
             transcendentals=0,
         ),
         name="filter",
-    )(here, x, *vs)
+    )(here, x, matrix, *vs)
 
 
 def partner(index, size, k, forward=True):
@@ -245,23 +258,47 @@
     )(which, *parts)
 
 
-def combine_kernel(a_ref, b_ref, out_ref):
-    for z in range(a_ref.shape[0]):
-        for g in range(a_ref.shape[1]):
-            out_ref[g, z] = a_ref[z, g] + b_ref[z, g]
-
-
-def combine(a, b):
+def combine_kernel(space, here_ref, a_ref, b_ref, *outs):
+    for k, out in enumerate(outs):
+        group = here_ref[0] + k
+        group = jnp.where(group >= space, group - space, group)
+        for z in range(out.shape[0]):
+            out[z] = a_ref[z, group] + b_ref[z, group]
+
+
+def combine(here, a, b):
     pairs, space, own, columns = a.shape
     return pl.pallas_call(
-        combine_kernel,
-        out_shape=jax.ShapeDtypeStruct((space, pairs, own, columns), jnp.float32),
-        in_specs=[VMEM_SPEC] * 2,
-        out_specs=VMEM_SPEC,
+        functools.partial(combine_kernel, space),
+        out_shape=[jax.ShapeDtypeStruct((pairs, own, columns), jnp.float32)] * space,
+        in_specs=[SMEM_SPEC] + [VMEM_SPEC] * 2,
+        out_specs=[VMEM_SPEC] * space,
         compiler_params=pltpu.CompilerParams(vmem_limit_bytes=VMEM_LIMIT),
         cost_estimate=pl.CostEstimate(flops=a.size, bytes_accessed=12 * a.size, transcendentals=0),
         name="combine",
-    )(a, b)
+    )(here, a, b)
+
+
+def place_kernel(space, here_ref, *refs):
+    parts, out = refs[:-1], refs[-1]
+    for k, part in enumerate(parts):
+        group = here_ref[0] - k
+        group = jnp.where(group < 0, group + space, group)
+        out[group] = part[...]
+
+
+def place(here, parts):
+    space = len(parts)
+    own, columns = parts[0].shape
+    return pl.pallas_call(
+        functools.partial(place_kernel, space),
+        out_shape=jax.ShapeDtypeStruct((space, own, columns), jnp.float32),
+        in_specs=[SMEM_SPEC] + [VMEM_SPEC] * space,
+        out_specs=VMEM_SPEC,
+        compiler_params=pltpu.CompilerParams(vmem_limit_bytes=VMEM_LIMIT),
+        cost_estimate=pl.CostEstimate(flops=0, bytes_accessed=8 * space * own * columns, transcendentals=0),
+        name="place",
+    )(here, *parts)
 
 
 def rotate(x, axis, step):
@@ -288,12 +325,13 @@
         n = x.shape[0]
         return x.reshape(n, layers, tiles, LANES).transpose(0, 2, 1, 3).reshape(n * rows, LANES)
 
+    matrix = jnp.asarray(plane_matrix())
     own_v = as_rows(potential[None])
     vs = [own_v] + [rotate(own_v, "space", space - k) for k in range(1, space)]
     arrived = as_rows(lax.all_to_all(orbitals, "space", split_axis=0, concat_axis=0, tiled=True))
 
     def filtered(c, x):
-        outs = run_filter(here, x, vs, c * chunk, space, layers, tiles, chunk)
+        outs = run_filter(here, x, matrix, vs, c * chunk, space, layers, tiles, chunk)
         return [outs[0]] + [rotate(outs[k], "space", k) for k in range(1, space)]
 
     made = [filtered(c, arrived) for c in range(min(chunks, 2))]
@@ -318,21 +356,26 @@
 
     pairs = band // 2
     core = b_index % 2
+    pair = b_index // 2
 
     def half(which):
         return gram(jnp.stack([which, b_index]), parts, band, count, space, chunk, places)
 
     other = lax.ppermute(half(1 - core), "band", [(i, i ^ 1) for i in range(band)])
     split = (pairs, space, own, band * count)
-    sums = combine(half(core).reshape(split), other.reshape(split))
-
-    def swap(x, axis, groups=None):
-        return lax.all_to_all(x, axis, split_axis=0, concat_axis=0, tiled=True, axis_index_groups=groups)
-
-    over_space = jnp.sum(swap(sums, "space"), axis=0)
-    same_core = [list(range(low, band, 2)) for low in range(2)]
-    final = jnp.sum(swap(over_space, "band", same_core), axis=0) * (1.0 / (layers * space * plane))
-    margin = swap(jnp.broadcast_to(final[None], (space, own, band * count)), "space")
+    sums = combine(here, half(core).reshape(split), other.reshape(split))
+
+    mine = sums[0]
+    for k in range(1, space):
+        mine = mine + rotate(sums[k], "space", k)
+
+    final = lax.dynamic_index_in_dim(mine, pair, 0, keepdims=False)
+    for k in range(1, pairs):
+        sent = lax.dynamic_index_in_dim(mine, partner(pair, pairs, k), 0, keepdims=False)
+        final = final + exchange(sent, "band", k, 2)
+    final = final * (1.0 / (layers * space * plane))
+
+    margin = place(here, [final] + [rotate(final, "space", k) for k in range(1, space)])
     return result, margin.reshape(count, band * count)
 
 

time: 141 us -> 138 us (0.979)
  blocking collectives: 41.4 us -> 0 us
  waiting for transfers between devices: 35.6 us -> 55.4 us
  starting transfers between devices: 37 us -> 50.2 us
  local copies, waits for them, and re-layouts: 0.74 us -> 12.1 us
  Pallas kernels: 24.4 us -> 18.5 us
    all_to_all x3 -> x0, blocking collectives: 41.4 us -> none  [swap(): lax.all_to_all(x, axis, split_axis=0, concat_axis=0, tiled=True, axis_ind...]
    ppermute x12 -> x18, waiting for transfers between devices: 24 us -> 40.8 us  [rotate(): return lax.ppermute(x, axis, [(i, (i + step) % size) for i in range(size)])]
    unnamed x3 -> x48, local copies, waits for them, and re-layouts: 0.72 us -> 12.1 us
    pallas_call x3, Pallas kernels: 14.6 us -> 6.89 us  [run_filter(): pl.pallas_call(functools.partial(filter_kernel, space, layers, tiles, chu...]
    ppermute x12 -> x18, starting transfers between devices: 16.6 us -> 23.6 us  [rotate(): return lax.ppermute(x, axis, [(i, (i + step) % size) for i in range(size)])]
    ppermute x7 -> x10, starting transfers between devices: 9.75 us -> 14.9 us  [exchange(): return lax.ppermute(x, axis, pairs)]
    ppermute x7 -> x10, waiting for transfers between devices: 11.1 us -> 14.2 us  [exchange(): return lax.ppermute(x, axis, pairs)]
    pallas_call x1 -> x2, Pallas kernels: 0.12 us -> 1.94 us  [the longest x1 1.28 us: place(): pl.pallas_call(functools.partial(place_kernel, space), out_shape=jax.Shap...]
  transfers between devices with their start and end apart: 22 -> 31, of which waited for: 9 -> 15; matrix products, arithmetic and copies ran while one was open for 0% -> 0% of each run, Pallas kernels for 11% -> 8%
where the time goes in v6:
time: 138 us; the launch traced here: 137 us
  waiting for transfers between devices  55.4 us (40%)
  starting transfers between devices  50.2 us (36%)
  Pallas kernels  18.5 us (13%)
  local copies, waits for them, and re-layouts  12.1 us (9%)
    ppermute x18, waiting for transfers between devices, rotate(): return lax.ppermute(x, axis, [(i, (i + step) % size) for i in range(size)])  40.8 us
    ppermute x18, starting transfers between devices, rotate(): return lax.ppermute(x, axis, [(i, (i + step) % size) for i in range(size)])  23.6 us
    ppermute x10, starting transfers between devices, exchange(): return lax.ppermute(x, axis, pairs)  14.9 us
    ppermute x10, waiting for transfers between devices, exchange(): return lax.ppermute(x, axis, pairs)  14.2 us
    unnamed x48, local copies, waits for them, and re-layouts  12.1 us
    pallas_call x3, Pallas kernels, run_filter(): pl.pallas_call(functools.partial(filter_kernel, space, layers, tiles, chu...  6.89 us
    all_to_all x1, starting transfers between devices, shards(): lax.all_to_all(orbitals, 'space', split_axis=0, concat_axis=0, tiled=True)  5.31 us
    all_to_all x1, starting transfers between devices, shards(): lax.all_to_all(head, 'band', split_axis=0, concat_axis=0, tiled=True)  5.08 us
  transfers between devices with their start and end apart: 31, of which 15 were waited for; matrix products, arithmetic and copies ran while one was open for 0% of the time, Pallas kernels for 8%

profile of v6, /device:TPU:0, one launch (start us, length us, event | category | flops | bytes accessed | tf_op | source)
XLA Modules:
  0.0 137.3 jit_solution(14829777007227933325)
XLA Ops:
  0.7 5.3 %all-to-all-start = ((f32[96,2,2048]{2,1,0:T(2,128)}), f32[96,2,2048]{2,1,0:T(2,128)S(1)}, u32[]{:S(2)}, u32[]{:S(2)}) async-start(f32[96,2,2048]{2,1,0:T(2,128)} %param.3), calls=%async_computation | async-start | bytes 3145728 | tf_op jit(solution)/shard_map/all_to_all | solution.py:331
  6.0 2.0 %collective-permute-start.2 = (f32[32,128]{1,0:T(8,128)S(1)}, f32[32,128]{1,0:T(8,128)S(1)}, u32[]{:S(2)}, u32[]{:S(2)}) collective-permute-start(f32[32,128]{1,0:T(8,128)S(1)} %bitcast.41), channel_id=1, source_target_pairs={{0,8},{8,16},{16,24},{24,0},{1,9},{9,17},{17,25},{25,1},{2,10},{10... | collective-permute-start | bytes 49160 | tf_op jit(solution)/shard_map/ppermute | solution.py:306
  8.0 1.5 %collective-permute-start.1 = (f32[32,128]{1,0:T(8,128)S(1)}, f32[32,128]{1,0:T(8,128)S(1)}, u32[]{:S(2)}, u32[]{:S(2)}) collective-permute-start(f32[32,128]{1,0:T(8,128)S(1)} %bitcast.42), channel_id=1, source_target_pairs={{0,16},{8,24},{16,0},{24,8},{1,17},{9,25},{17,1},{25,9},{2,18},{10... | collective-permute-start | bytes 49160 | tf_op jit(solution)/shard_map/ppermute | solution.py:306
  9.4 1.5 %collective-permute-start = (f32[32,128]{1,0:T(8,128)S(1)}, f32[32,128]{1,0:T(8,128)S(1)}, u32[]{:S(2)}, u32[]{:S(2)}) collective-permute-start(f32[32,128]{1,0:T(8,128)S(1)} %bitcast.43), channel_id=1, source_target_pairs={{0,24},{8,0},{16,8},{24,16},{1,25},{9,1},{17,9},{25,17},{2,26},{10... | collective-permute-start | bytes 49160 | tf_op jit(solution)/shard_map/ppermute | solution.py:306
  11.0 15.6 %collective-permute-done.2.refs_3_ = f32[32,128]{1,0:T(8,128)S(1)} collective-permute-done((f32[32,128]{1,0:T(8,128)S(1)}, f32[32,128]{1,0:T(8,128)S(1)}, u32[]{:S(2)}, u32[]{:S(2)}) %collective-permute-start.2) | collective-permute-done | bytes 16416 | tf_op jit(solution)/shard_map/ppermute | solution.py:306
  26.7 2.3 %filter.4 = (f32[32,8,128]{2,1,0:T(8,128)S(1)}, f32[32,8,128]{2,1,0:T(8,128)S(1)}, f32[32,8,128]{2,1,0:T(8,128)S(1)}, f32[32,8,128]{2,1,0:T(8,128)S(1)}) custom-call(s32[2]{0:T(128)S(1)} %pad_add_fusion.here_ref, f32[3072,128]{1,0:T(8,128)S(1)} %bitcast.36, bf16[512,256]{1,0:T(8,128)(2,1)S(1)} %copy-done, f32[32,128]{1,0:T(8,128)S(1)} %bitcast.44, ...), custom_call_target="tpu_custom_call" | custom-call | flops 6553600 | bytes 1048576 | tf_op jit(solution)/shard_map/filter/pallas_call | solution.py:114
  29.0 0.8 collective-permute-start.3
  30.3 2.4 %collective-permute-start.5 = (f32[32,8,128]{2,1,0:T(8,128)S(1)}, f32[32,8,128]{2,1,0:T(8,128)S(1)}, u32[]{:S(2)}, u32[]{:S(2)}) collective-permute-start(f32[32,8,128]{2,1,0:T(8,128)S(1)} %get-tuple-element.34), channel_id=1, source_target_pairs={{0,24},{8,0},{16,8},{24,16},{1,25},{9,1},{17,9},{25,17},{2,26},{10... | collective-permute-start | bytes 393224 | tf_op jit(solution)/shard_map/ppermute | solution.py:306
  32.7 2.4 %collective-permute-done.3.refs_1_.refs_3_ = f32[32,8,128]{2,1,0:T(8,128)S(1)} collective-permute-done((f32[32,8,128]{2,1,0:T(8,128)S(1)}, f32[32,8,128]{2,1,0:T(8,128)S(1)}, u32[]{:S(2)}, u32[]{:S(2)}) %collective-permute-start.3) | collective-permute-done | bytes 131104 | tf_op jit(solution)/shard_map/ppermute | solution.py:306
  35.1 1.2 collective-permute-done.4.refs_2_.refs_6_
  36.3 1.4 %pack.2 = f32[8,32,512]{2,1,0:T(8,128)} custom-call(s32[2]{0:T(128)S(1)} %pad_add_fusion.here_ref, f32[32,8,128]{2,1,0:T(8,128)S(1)} %get-tuple-element.31.refs_0_, f32[32,8,128]{2,1,0:T(8,128)S(1)} %collective-permute-done.3.refs_1_.refs_3_, f32[32,8,128]{2,1,0:T(8,128)S(1)} %collective-permute-done.4.refs_2_.refs_6_, ...), custom_call_target="tpu_custom_call" | custom-call | bytes 1048576 | tf_op jit(solution)/shard_map/pack/pallas_call | solution.py:168
  37.7 5.1 %all-to-all-start.1 = ((f32[8,32,512]{2,1,0:T(8,128)}), f32[8,32,512]{2,1,0:T(8,128)S(1)}, u32[]{:S(2)}, u32[]{:S(2)}) async-start(f32[8,32,512]{2,1,0:T(8,128)} %pack.2), calls=%async_computation.1 | async-start | bytes 1048576 | tf_op jit(solution)/shard_map/all_to_all | solution.py:340
  42.8 2.3 %filter.3 = (f32[32,8,128]{2,1,0:T(8,128)S(1)}, f32[32,8,128]{2,1,0:T(8,128)S(1)}, f32[32,8,128]{2,1,0:T(8,128)S(1)}, f32[32,8,128]{2,1,0:T(8,128)S(1)}) custom-call(s32[2]{0:T(128)S(1)} %pad_add_fusion.here_ref, f32[3072,128]{1,0:T(8,128)S(1)} %bitcast.37, bf16[512,256]{1,0:T(8,128)(2,1)S(1)} %copy-done, f32[32,128]{1,0:T(8,128)S(1)} %bitcast.45, ...), custom_call_target="tpu_custom_call" | custom-call | flops 6553600 | bytes 1048576 | tf_op jit(solution)/shard_map/filter/pallas_call | solution.py:114
  45.2 2.1 %collective-permute-start.6 = (f32[32,8,128]{2,1,0:T(8,128)S(1)}, f32[32,8,128]{2,1,0:T(8,128)S(1)}, u32[]{:S(2)}, u32[]{:S(2)}) collective-permute-start(f32[32,8,128]{2,1,0:T(8,128)S(1)} %get-tuple-element.37), channel_id=1, source_target_pairs={{0,8},{8,16},{16,24},{24,0},{1,9},{9,17},{17,25},{25,1},{2,10},{10... | collective-permute-start | bytes 393224 | tf_op jit(solution)/shard_map/ppermute | solution.py:306
  47.2 1.3 collective-permute-start.8
  48.8 0.7 copy-done.3
  49.6 0.7 copy-done.5
  50.3 0.7 copy-done.7
  51.6 2.3 %filter.5 = (f32[32,8,128]{2,1,0:T(8,128)S(1)}, f32[32,8,128]{2,1,0:T(8,128)S(1)}, f32[32,8,128]{2,1,0:T(8,128)S(1)}, f32[32,8,128]{2,1,0:T(8,128)S(1)}) custom-call(s32[2]{0:T(128)S(1)} %copy-done.9, f32[3072,128]{1,0:T(8,128)S(1)} %bitcast.38, bf16[512,256]{1,0:T(8,128)(2,1)S(1)} %copy-done, f32[32,128]{1,0:T(8,128)S(1)} %bitcast.46, ...), custom_call_target="tpu_custom_call" | custom-call | flops 6553600 | bytes 1048576 | tf_op jit(solution)/shard_map/filter/pallas_call | solution.py:114
  53.9 1.8 %collective-permute-start.7 = (f32[32,8,128]{2,1,0:T(8,128)S(1)}, f32[32,8,128]{2,1,0:T(8,128)S(1)}, u32[]{:S(2)}, u32[]{:S(2)}) collective-permute-start(f32[32,8,128]{2,1,0:T(8,128)S(1)} %get-tuple-element.38), channel_id=1, source_target_pairs={{0,8},{8,16},{16,24},{24,0},{1,9},{9,17},{17,25},{25,1},{2,10},{10... | collective-permute-start | bytes 393224 | tf_op jit(solution)/shard_map/ppermute | solution.py:306
  55.7 0.7 collective-permute-start.9
  56.4 1.8 %collective-permute-start.11 = (f32[32,8,128]{2,1,0:T(8,128)S(1)}, f32[32,8,128]{2,1,0:T(8,128)S(1)}, u32[]{:S(2)}, u32[]{:S(2)}) collective-permute-start(f32[32,8,128]{2,1,0:T(8,128)S(1)} %get-tuple-element.42), channel_id=1, source_target_pairs={{0,24},{8,0},{16,8},{24,16},{1,25},{9,1},{17,9},{25,17},{2,26},{10... | collective-permute-start | bytes 393224 | tf_op jit(solution)/shard_map/ppermute | solution.py:306
  58.2 3.0 %collective-permute-done.7.refs_3_.refs_5_ = f32[32,8,128]{2,1,0:T(8,128)S(1)} collective-permute-done((f32[32,8,128]{2,1,0:T(8,128)S(1)}, f32[32,8,128]{2,1,0:T(8,128)S(1)}, u32[]{:S(2)}, u32[]{:S(2)}) %collective-permute-start.7) | collective-permute-done | bytes 131104 | tf_op jit(solution)/shard_map/ppermute | solution.py:306
  61.2 1.7 %collective-permute-done.9.refs_5_.refs_8_ = f32[32,8,128]{2,1,0:T(8,128)S(1)} collective-permute-done((f32[32,8,128]{2,1,0:T(8,128)S(1)}, f32[32,8,128]{2,1,0:T(8,128)S(1)}, u32[]{:S(2)}, u32[]{:S(2)}) %collective-permute-start.9) | collective-permute-done | bytes 131104 | tf_op jit(solution)/shard_map/ppermute | solution.py:306
  63.0 1.4 %pack.3 = (f32[64,512]{1,0:T(8,128)S(1)}, f32[64,512]{1,0:T(8,128)S(1)}, f32[64,512]{1,0:T(8,128)}, f32[64,512]{1,0:T(8,128)}, f32[64,512]{1,0:T(8,128)S(1)}, /*...) custom-call(s32[2]{0:T(128)S(1)} %copy-done.10, ...), custom_call_target="tpu_custom_call" | custom-call | bytes 2097152 | tf_op jit(solution)/shard_map/pack/pallas_call | solution.py:168
  64.3 2.7 %collective-permute-start.12 = (f32[64,512]{1,0:T(8,128)S(1)}, f32[64,512]{1,0:T(8,128)S(1)}, u32[]{:S(2)}, u32[]{:S(2)}) collective-permute-start(f32[64,512]{1,0:T(8,128)S(1)} %get-tuple-element.43), channel_id=1, source_target_pairs={{0,7},{1,6},{2,5},{3,4},{4,3},{5,2},{6,1},{7,0},{8,15},{9,14},{10,... | collective-permute-start | bytes 393224 | tf_op jit(solution)/shard_map/ppermute | solution.py:144
  67.0 0.9 collective-permute-start.13
  67.9 1.4 collective-permute-start.15
  69.3 2.6 %collective-permute-done.12.refs_8_ = f32[64,512]{1,0:T(8,128)S(1)} collective-permute-done((f32[64,512]{1,0:T(8,128)S(1)}, f32[64,512]{1,0:T(8,128)S(1)}, u32[]{:S(2)}, u32[]{:S(2)}) %collective-permute-start.12) | collective-permute-done | bytes 131104 | tf_op jit(solution)/shard_map/ppermute | solution.py:144
  71.9 0.6 copy-done.12
  72.5 2.9 %collective-permute-start.17 = (f32[64,512]{1,0:T(8,128)S(1)}, f32[64,512]{1,0:T(8,128)S(1)}, u32[]{:S(2)}, u32[]{:S(2)}) collective-permute-start(f32[64,512]{1,0:T(8,128)S(1)} %get-tuple-element.51), channel_id=1, source_target_pairs={{0,5},{1,4},{2,7},{3,6},{4,1},{5,0},{6,3},{7,2},{8,13},{9,12},{10,... | collective-permute-start | bytes 393224 | tf_op jit(solution)/shard_map/ppermute | solution.py:144
  75.5 1.9 %collective-permute-start.18 = (f32[64,512]{1,0:T(8,128)S(1)}, f32[64,512]{1,0:T(8,128)}, u32[]{:S(2)}, u32[]{:S(2)}) collective-permute-start(f32[64,512]{1,0:T(8,128)S(1)} %get-tuple-element.52), channel_id=1, source_target_pairs={{0,6},{1,7},{2,4},{3,5},{4,2},{5,3},{6,0},{7,1},{8,14},{9,15},{10,... | collective-permute-start | bytes 393224 | tf_op jit(solution)/shard_map/ppermute | solution.py:144
  78.0 2.6 %unpack.1 = f32[3072,128]{1,0:T(8,128)} custom-call(s32[2]{0:T(128)S(1)} %copy-done.11, f32[32,8,128]{2,1,0:T(8,128)S(1)} %get-tuple-element.31.refs_0_, f32[32,8,128]{2,1,0:T(8,128)S(1)} %get-tuple-element.30.refs_0_.refs_1_, f32[32,8,128]{2,1,0:T(8,128)S(1)} %get-tuple-element.36.refs_1_.refs_2_, f32[32,8,128]{2,1,0:T(8,128)S(1)} %collective-permute-done.3.refs_1_.refs_3_, ...), custom_call_target="tpu_custom_call" | custom-call | bytes 3145728 | tf_op jit(solution)/shard_map/unpack/pallas_call | solution.py:201
  80.7 0.7 copy-done.16
  81.3 0.7 copy-done.18
  82.0 0.7 copy-done.20
  82.6 4.8 %collective-permute-done.17.refs_6_ = f32[64,512]{1,0:T(8,128)S(1)} collective-permute-done((f32[64,512]{1,0:T(8,128)S(1)}, f32[64,512]{1,0:T(8,128)S(1)}, u32[]{:S(2)}, u32[]{:S(2)}) %collective-permute-start.17) | collective-permute-done | bytes 131104 | tf_op jit(solution)/shard_map/ppermute | solution.py:144
  87.4 0.6 copy-done.22
  88.1 0.9 copy-done.13
  89.0 0.9 copy-done.15
  89.9 0.9 copy-done.17
  90.8 0.9 copy-done.19
  91.7 0.9 copy-done.21
  92.6 0.9 copy-done.23
  93.5 2.1 %gram.3 = f32[384,768]{1,0:T(8,128)S(1)} custom-call(s32[2]{0:T(128)S(1)} %get-tuple-element.62.which_ref, f32[8,32,512]{2,1,0:T(8,128)S(1)} %all-to-all-done.1.refs_0_, f32[64,512]{1,0:T(8,128)S(1)} %get-tuple-element.46.refs_1_, f32[64,512]{1,0:T(8,128)S(1)} %copy-done.15, f32[64,512]{1,0:T(8,128)S(1)} %copy-done.17, f32[64,512]{1,0:T(8,128)S(1)} %copy-done.19, ...), custom_call_target="tpu_custom_call" | custom-call | flops 905969664 | bytes 2752512 | tf_op jit(solution)/shard_map/gram/pallas_call | solution.py:245
  95.6 1.3 collective-permute-start.19
  96.9 2.1 %gram.2 = f32[384,768]{1,0:T(8,128)S(1)} custom-call(s32[2]{0:T(128)S(1)} %get-tuple-element.61.which_ref, f32[8,32,512]{2,1,0:T(8,128)S(1)} %all-to-all-done.1.refs_0_, f32[64,512]{1,0:T(8,128)S(1)} %get-tuple-element.46.refs_1_, f32[64,512]{1,0:T(8,128)S(1)} %copy-done.15, f32[64,512]{1,0:T(8,128)S(1)} %copy-done.17, f32[64,512]{1,0:T(8,128)S(1)} %copy-done.19, ...), custom_call_target="tpu_custom_call" | custom-call | flops 905969664 | bytes 2752512 | tf_op jit(solution)/shard_map/gram/pallas_call | solution.py:245
  99.4 0.7 combine.1
  100.1 1.6 %collective-permute-start.20 = (f32[4,24,768]{2,1,0:T(8,128)S(1)}, f32[4,24,768]{2,1,0:T(8,128)S(1)}, u32[]{:S(2)}, u32[]{:S(2)}) collective-permute-start(f32[4,24,768]{2,1,0:T(8,128)S(1)} %get-tuple-element.55), channel_id=1, source_target_pairs={{0,8},{8,16},{16,24},{24,0},{1,9},{9,17},{17,25},{25,1},{2,10},{10... | collective-permute-start | bytes 884744 | tf_op jit(solution)/shard_map/ppermute | solution.py:306
  101.7 0.8 collective-permute-start.21
  102.5 1.6 %collective-permute-start.22 = (f32[4,24,768]{2,1,0:T(8,128)S(1)}, f32[4,24,768]{2,1,0:T(8,128)S(1)}, u32[]{:S(2)}, u32[]{:S(2)}) collective-permute-start(f32[4,24,768]{2,1,0:T(8,128)S(1)} %get-tuple-element.57), channel_id=1, source_target_pairs={{0,24},{8,0},{16,8},{24,16},{1,25},{9,1},{17,9},{25,17},{2,26},{10... | collective-permute-start | bytes 884744 | tf_op jit(solution)/shard_map/ppermute | solution.py:306
  104.1 6.8 %collective-permute-done.20 = f32[4,24,768]{2,1,0:T(8,128)S(1)} collective-permute-done((f32[4,24,768]{2,1,0:T(8,128)S(1)}, f32[4,24,768]{2,1,0:T(8,128)S(1)}, u32[]{:S(2)}, u32[]{:S(2)}) %collective-permute-start.20) | collective-permute-done | bytes 294944 | tf_op jit(solution)/shard_map/ppermute | solution.py:306
  110.9 5.7 %collective-permute-done.21 = f32[4,24,768]{2,1,0:T(8,128)S(1)} collective-permute-done((f32[4,24,768]{2,1,0:T(8,128)S(1)}, f32[4,24,768]{2,1,0:T(8,128)S(1)}, u32[]{:S(2)}, u32[]{:S(2)}) %collective-permute-start.21) | collective-permute-done | bytes 294944 | tf_op jit(solution)/shard_map/ppermute | solution.py:306
  116.8 2.5 %collective-permute-start.23 = (f32[24,768]{1,0:T(8,128)S(1)}, f32[24,768]{1,0:T(8,128)S(1)}, u32[]{:S(2)}, u32[]{:S(2)}) collective-permute-start(f32[24,768]{1,0:T(8,128)S(1)} %get-tuple-element.58), channel_id=1, source_target_pairs={{0,2},{1,3},{2,0},{3,1},{4,6},{5,7},{6,4},{7,5},{8,10},{9,11},{10,... | collective-permute-start | bytes 221192 | tf_op jit(solution)/shard_map/ppermute | solution.py:144
  119.3 2.7 %collective-permute-start.25 = (f32[24,768]{1,0:T(8,128)S(1)}, f32[24,768]{1,0:T(8,128)S(1)}, u32[]{:S(2)}, u32[]{:S(2)}) collective-permute-start(f32[24,768]{1,0:T(8,128)S(1)} %get-tuple-element.59), channel_id=1, source_target_pairs={{0,6},{1,7},{2,4},{3,5},{4,2},{5,3},{6,0},{7,1},{8,14},{9,15},{10,... | collective-permute-start | bytes 221192 | tf_op jit(solution)/shard_map/ppermute | solution.py:144
  121.9 4.7 %collective-permute-done.25 = f32[24,768]{1,0:T(8,128)S(1)} collective-permute-done((f32[24,768]{1,0:T(8,128)S(1)}, f32[24,768]{1,0:T(8,128)S(1)}, u32[]{:S(2)}, u32[]{:S(2)}) %collective-permute-start.25) | collective-permute-done | bytes 73760 | tf_op jit(solution)/shard_map/ppermute | solution.py:144
  126.7 2.1 %collective-permute-done.24 = f32[24,768]{1,0:T(8,128)S(1)} collective-permute-done((f32[24,768]{1,0:T(8,128)S(1)}, f32[24,768]{1,0:T(8,128)S(1)}, u32[]{:S(2)}, u32[]{:S(2)}) %collective-permute-start.24) | collective-permute-done | bytes 73760 | tf_op jit(solution)/shard_map/ppermute | solution.py:144
  128.7 1.0 collective-permute-start.28
  129.7 1.1 collective-permute-start.27
  130.7 1.0 collective-permute-start.26
  131.7 1.7 %collective-permute-done.28.refs_3_ = f32[24,768]{1,0:T(8,128)S(1)} collective-permute-done((f32[24,768]{1,0:T(8,128)S(1)}, f32[24,768]{1,0:T(8,128)S(1)}, u32[]{:S(2)}, u32[]{:S(2)}) %collective-permute-start.28) | collective-permute-done | bytes 73760 | tf_op jit(solution)/shard_map/ppermute | solution.py:306
  133.4 1.4 %collective-permute-done.27.refs_2_ = f32[24,768]{1,0:T(8,128)S(1)} collective-permute-done((f32[24,768]{1,0:T(8,128)S(1)}, f32[24,768]{1,0:T(8,128)S(1)}, u32[]{:S(2)}, u32[]{:S(2)}) %collective-permute-start.27) | collective-permute-done | bytes 73760 | tf_op jit(solution)/shard_map/ppermute | solution.py:306
  134.8 1.2 collective-permute-done.26.refs_1_
  136.0 1.3 place.1
  (61 shorter events, 2.8 us)
Async XLA Ops:
  0.6 26.0 %copy-start = (bf16[512,256]{1,0:T(8,128)(2,1)S(1)}, bf16[512,256]{1,0:T(8,128)(2,1)}, u32[]{:S(2)}) copy-start(bf16[512,256]{1,0:T(8,128)(2,1)} %constant.50.clone.m_ref) | copy-start | bytes 786436
  0.6 5.3 %copy-start.1 = (f32[2,2048]{1,0:T(2,128)S(1)}, f32[2,2048]{1,0:T(2,128)}, u32[]{:S(2)}) copy-start(f32[2,2048]{1,0:T(2,128)} %param.4) | copy-start | bytes 49156
  0.7 26.0 %all-to-all-start = ((f32[96,2,2048]{2,1,0:T(2,128)}), f32[96,2,2048]{2,1,0:T(2,128)S(1)}, u32[]{:S(2)}, u32[]{:S(2)}) async-start(f32[96,2,2048]{2,1,0:T(2,128)} %param.3), calls=%async_computation | async-start | bytes 3145728 | tf_op jit(solution)/shard_map/all_to_all | solution.py:331
  6.0 20.7 %collective-permute-start.2 = (f32[32,128]{1,0:T(8,128)S(1)}, f32[32,128]{1,0:T(8,128)S(1)}, u32[]{:S(2)}, u32[]{:S(2)}) collective-permute-start(f32[32,128]{1,0:T(8,128)S(1)} %bitcast.41), channel_id=1, source_target_pairs={{0,8},{8,16},{16,24},{24,0},{1,9},{9,17},{17,25},{25,1},{2,10},{10... | collective-permute-start | bytes 49160 | tf_op jit(solution)/shard_map/ppermute | solution.py:306
  8.0 18.7 %collective-permute-start.1 = (f32[32,128]{1,0:T(8,128)S(1)}, f32[32,128]{1,0:T(8,128)S(1)}, u32[]{:S(2)}, u32[]{:S(2)}) collective-permute-start(f32[32,128]{1,0:T(8,128)S(1)} %bitcast.42), channel_id=1, source_target_pairs={{0,16},{8,24},{16,0},{24,8},{1,17},{9,25},{17,1},{25,9},{2,18},{10... | collective-permute-start | bytes 49160 | tf_op jit(solution)/shard_map/ppermute | solution.py:306
  9.4 17.2 %collective-permute-start = (f32[32,128]{1,0:T(8,128)S(1)}, f32[32,128]{1,0:T(8,128)S(1)}, u32[]{:S(2)}, u32[]{:S(2)}) collective-permute-start(f32[32,128]{1,0:T(8,128)S(1)} %bitcast.43), channel_id=1, source_target_pairs={{0,24},{8,0},{16,8},{24,16},{1,25},{9,1},{17,9},{25,17},{2,26},{10... | collective-permute-start | bytes 49160 | tf_op jit(solution)/shard_map/ppermute | solution.py:306
  11.0 31.8 %copy-start.8 = (s32[2]{0:T(128)}, s32[2]{0:T(128)S(1)}, u32[]{:S(2)}) copy-start(s32[2]{0:T(128)S(1)} %pad_add_fusion.here_ref) | copy-start | bytes 28
  26.6 16.2 %copy-start.2 = (f32[32,128]{1,0:T(8,128)}, f32[32,128]{1,0:T(8,128)S(1)}, u32[]{:S(2)}) copy-start(f32[32,128]{1,0:T(8,128)S(1)} %collective-permute-done.2.refs_3_) | copy-start | bytes 49156
  26.6 16.2 %copy-start.4 = (f32[32,128]{1,0:T(8,128)}, f32[32,128]{1,0:T(8,128)S(1)}, u32[]{:S(2)}) copy-start(f32[32,128]{1,0:T(8,128)S(1)} %collective-permute-done.1.refs_2_) | copy-start | bytes 49156
  26.7 16.2 %copy-start.6 = (f32[32,128]{1,0:T(8,128)}, f32[32,128]{1,0:T(8,128)S(1)}, u32[]{:S(2)}) copy-start(f32[32,128]{1,0:T(8,128)S(1)} %collective-permute-done.refs_1_) | copy-start | bytes 49156
  29.0 6.1 %collective-permute-start.3 = (f32[32,8,128]{2,1,0:T(8,128)S(1)}, f32[32,8,128]{2,1,0:T(8,128)S(1)}, u32[]{:S(2)}, u32[]{:S(2)}) collective-permute-start(f32[32,8,128]{2,1,0:T(8,128)S(1)} %get-tuple-element.32), channel_id=1, source_target_pairs={{0,8},{8,16},{16,24},{24,0},{1,9},{9,17},{17,25},{25,1},{2,10},{10... | collective-permute-start | bytes 393224 | tf_op jit(solution)/shard_map/ppermute | solution.py:306
  29.7 6.6 %collective-permute-start.4 = (f32[32,8,128]{2,1,0:T(8,128)S(1)}, f32[32,8,128]{2,1,0:T(8,128)S(1)}, u32[]{:S(2)}, u32[]{:S(2)}) collective-permute-start(f32[32,8,128]{2,1,0:T(8,128)S(1)} %get-tuple-element.33), channel_id=1, source_target_pairs={{0,16},{8,24},{16,0},{24,8},{1,17},{9,25},{17,1},{25,9},{2,18},{10... | collective-permute-start | bytes 393224 | tf_op jit(solution)/shard_map/ppermute | solution.py:306
  30.3 6.0 %collective-permute-start.5 = (f32[32,8,128]{2,1,0:T(8,128)S(1)}, f32[32,8,128]{2,1,0:T(8,128)S(1)}, u32[]{:S(2)}, u32[]{:S(2)}) collective-permute-start(f32[32,8,128]{2,1,0:T(8,128)S(1)} %get-tuple-element.34), channel_id=1, source_target_pairs={{0,24},{8,0},{16,8},{24,16},{1,25},{9,1},{17,9},{25,17},{2,26},{10... | collective-permute-start | bytes 393224 | tf_op jit(solution)/shard_map/ppermute | solution.py:306
  37.7 50.4 %all-to-all-start.1 = ((f32[8,32,512]{2,1,0:T(8,128)}), f32[8,32,512]{2,1,0:T(8,128)S(1)}, u32[]{:S(2)}, u32[]{:S(2)}) async-start(f32[8,32,512]{2,1,0:T(8,128)} %pack.2), calls=%async_computation.1 | async-start | bytes 1048576 | tf_op jit(solution)/shard_map/all_to_all | solution.py:340
  45.1 17.8 %copy-start.10 = (s32[2]{0:T(128)S(1)}, s32[2]{0:T(128)}, u32[]{:S(2)}) copy-start(s32[2]{0:T(128)} %copy-done.8) | copy-start | bytes 28
  45.2 11.3 %collective-permute-start.6 = (f32[32,8,128]{2,1,0:T(8,128)S(1)}, f32[32,8,128]{2,1,0:T(8,128)S(1)}, u32[]{:S(2)}, u32[]{:S(2)}) collective-permute-start(f32[32,8,128]{2,1,0:T(8,128)S(1)} %get-tuple-element.37), channel_id=1, source_target_pairs={{0,8},{8,16},{16,24},{24,0},{1,9},{9,17},{17,25},{25,1},{2,10},{10... | collective-permute-start | bytes 393224 | tf_op jit(solution)/shard_map/ppermute | solution.py:306
  47.2 11.0 %collective-permute-start.8 = (f32[32,8,128]{2,1,0:T(8,128)S(1)}, f32[32,8,128]{2,1,0:T(8,128)S(1)}, u32[]{:S(2)}, u32[]{:S(2)}) collective-permute-start(f32[32,8,128]{2,1,0:T(8,128)S(1)} %get-tuple-element.39), channel_id=1, source_target_pairs={{0,16},{8,24},{16,0},{24,8},{1,17},{9,25},{17,1},{25,9},{2,18},{10... | collective-permute-start | bytes 393224 | tf_op jit(solution)/shard_map/ppermute | solution.py:306
  48.5 9.7 %collective-permute-start.10 = (f32[32,8,128]{2,1,0:T(8,128)S(1)}, f32[32,8,128]{2,1,0:T(8,128)S(1)}, u32[]{:S(2)}, u32[]{:S(2)}) collective-permute-start(f32[32,8,128]{2,1,0:T(8,128)S(1)} %get-tuple-element.41), channel_id=1, source_target_pairs={{0,24},{8,0},{16,8},{24,16},{1,25},{9,1},{17,9},{25,17},{2,26},{10... | collective-permute-start | bytes 393224 | tf_op jit(solution)/shard_map/ppermute | solution.py:306
  48.8 0.7 copy-start.3
  49.6 0.7 copy-start.5
  50.3 0.7 copy-start.7
  51.0 0.6 copy-start.9
  53.9 7.3 %collective-permute-start.7 = (f32[32,8,128]{2,1,0:T(8,128)S(1)}, f32[32,8,128]{2,1,0:T(8,128)S(1)}, u32[]{:S(2)}, u32[]{:S(2)}) collective-permute-start(f32[32,8,128]{2,1,0:T(8,128)S(1)} %get-tuple-element.38), channel_id=1, source_target_pairs={{0,8},{8,16},{16,24},{24,0},{1,9},{9,17},{17,25},{25,1},{2,10},{10... | collective-permute-start | bytes 393224 | tf_op jit(solution)/shard_map/ppermute | solution.py:306
  55.7 7.3 %collective-permute-start.9 = (f32[32,8,128]{2,1,0:T(8,128)S(1)}, f32[32,8,128]{2,1,0:T(8,128)S(1)}, u32[]{:S(2)}, u32[]{:S(2)}) collective-permute-start(f32[32,8,128]{2,1,0:T(8,128)S(1)} %get-tuple-element.40), channel_id=1, source_target_pairs={{0,16},{8,24},{16,0},{24,8},{1,17},{9,25},{17,1},{25,9},{2,18},{10... | collective-permute-start | bytes 393224 | tf_op jit(solution)/shard_map/ppermute | solution.py:306
  56.4 6.5 %collective-permute-start.11 = (f32[32,8,128]{2,1,0:T(8,128)S(1)}, f32[32,8,128]{2,1,0:T(8,128)S(1)}, u32[]{:S(2)}, u32[]{:S(2)}) collective-permute-start(f32[32,8,128]{2,1,0:T(8,128)S(1)} %get-tuple-element.42), channel_id=1, source_target_pairs={{0,24},{8,0},{16,8},{24,16},{1,25},{9,1},{17,9},{25,17},{2,26},{10... | collective-permute-start | bytes 393224 | tf_op jit(solution)/shard_map/ppermute | solution.py:306
  64.3 7.6 %collective-permute-start.12 = (f32[64,512]{1,0:T(8,128)S(1)}, f32[64,512]{1,0:T(8,128)S(1)}, u32[]{:S(2)}, u32[]{:S(2)}) collective-permute-start(f32[64,512]{1,0:T(8,128)S(1)} %get-tuple-element.43), channel_id=1, source_target_pairs={{0,7},{1,6},{2,5},{3,4},{4,3},{5,2},{6,1},{7,0},{8,15},{9,14},{10,... | collective-permute-start | bytes 393224 | tf_op jit(solution)/shard_map/ppermute | solution.py:144
  67.0 8.5 %collective-permute-start.13 = (f32[64,512]{1,0:T(8,128)S(1)}, f32[64,512]{1,0:T(8,128)S(1)}, u32[]{:S(2)}, u32[]{:S(2)}) collective-permute-start(f32[64,512]{1,0:T(8,128)S(1)} %get-tuple-element.47), channel_id=1, source_target_pairs={{0,1},{1,0},{2,3},{3,2},{4,5},{5,4},{6,7},{7,6},{8,9},{9,8},{10,11... | collective-permute-start | bytes 393224 | tf_op jit(solution)/shard_map/ppermute | solution.py:144
  67.9 12.7 %collective-permute-start.14 = (f32[64,512]{1,0:T(8,128)}, f32[64,512]{1,0:T(8,128)S(1)}, u32[]{:S(2)}, u32[]{:S(2)}) collective-permute-start(f32[64,512]{1,0:T(8,128)} %get-tuple-element.48), channel_id=1, source_target_pairs={{0,2},{1,3},{2,0},{3,1},{4,6},{5,7},{6,4},{7,5},{8,10},{9,11},{10,... | collective-permute-start | bytes 393224 | tf_op jit(solution)/shard_map/ppermute | solution.py:144
  67.9 13.4 %collective-permute-start.15 = (f32[64,512]{1,0:T(8,128)}, f32[64,512]{1,0:T(8,128)S(1)}, u32[]{:S(2)}, u32[]{:S(2)}) collective-permute-start(f32[64,512]{1,0:T(8,128)} %get-tuple-element.49), channel_id=1, source_target_pairs={{0,3},{1,2},{2,1},{3,0},{4,7},{5,6},{6,5},{7,4},{8,11},{9,10},{10,... | collective-permute-start | bytes 393224 | tf_op jit(solution)/shard_map/ppermute | solution.py:144
  69.3 12.7 %collective-permute-start.16 = (f32[64,512]{1,0:T(8,128)S(1)}, f32[64,512]{1,0:T(8,128)S(1)}, u32[]{:S(2)}, u32[]{:S(2)}) collective-permute-start(f32[64,512]{1,0:T(8,128)S(1)} %get-tuple-element.50), channel_id=1, source_target_pairs={{0,4},{1,5},{2,6},{3,7},{4,0},{5,1},{6,2},{7,3},{8,12},{9,13},{10,... | collective-permute-start | bytes 393224 | tf_op jit(solution)/shard_map/ppermute | solution.py:144
  71.9 0.6 copy-start.12
  72.5 14.9 %collective-permute-start.17 = (f32[64,512]{1,0:T(8,128)S(1)}, f32[64,512]{1,0:T(8,128)S(1)}, u32[]{:S(2)}, u32[]{:S(2)}) collective-permute-start(f32[64,512]{1,0:T(8,128)S(1)} %get-tuple-element.51), channel_id=1, source_target_pairs={{0,5},{1,4},{2,7},{3,6},{4,1},{5,0},{6,3},{7,2},{8,13},{9,12},{10,... | collective-permute-start | bytes 393224 | tf_op jit(solution)/shard_map/ppermute | solution.py:144
  75.5 5.2 %copy-start.14 = (f32[64,512]{1,0:T(8,128)}, f32[64,512]{1,0:T(8,128)S(1)}, u32[]{:S(2)}) copy-start(f32[64,512]{1,0:T(8,128)S(1)} %collective-permute-done.13.refs_2_) | copy-start | bytes 393220
  75.5 12.6 %collective-permute-start.18 = (f32[64,512]{1,0:T(8,128)S(1)}, f32[64,512]{1,0:T(8,128)}, u32[]{:S(2)}, u32[]{:S(2)}) collective-permute-start(f32[64,512]{1,0:T(8,128)S(1)} %get-tuple-element.52), channel_id=1, source_target_pairs={{0,6},{1,7},{2,4},{3,5},{4,2},{5,3},{6,0},{7,1},{8,14},{9,15},{10,... | collective-permute-start | bytes 393224 | tf_op jit(solution)/shard_map/ppermute | solution.py:144
  77.4 0.6 copy-start.11
  80.7 0.7 copy-start.16
  81.3 0.7 copy-start.18
  82.0 0.7 copy-start.20
  87.4 0.6 copy-start.22
  88.1 0.9 copy-start.13
  89.0 0.9 copy-start.15
  89.9 0.9 copy-start.17
  90.8 0.9 copy-start.19
  91.7 0.9 copy-start.21
  92.6 0.9 copy-start.23
  95.6 3.8 %collective-permute-start.19 = (f32[384,768]{1,0:T(8,128)S(1)}, f32[384,768]{1,0:T(8,128)S(1)}, u32[]{:S(2)}, u32[]{:S(2)}) collective-permute-start(f32[384,768]{1,0:T(8,128)S(1)} %gram.3), channel_id=1, source_target_pairs={{0,1},{1,0},{2,3},{3,2},{4,5},{5,4},{6,7},{7,6},{8,9},{9,8},{10,11... | collective-permute-start | bytes 3538952 | tf_op jit(solution)/shard_map/ppermute | solution.py:364
  100.1 10.8 %collective-permute-start.20 = (f32[4,24,768]{2,1,0:T(8,128)S(1)}, f32[4,24,768]{2,1,0:T(8,128)S(1)}, u32[]{:S(2)}, u32[]{:S(2)}) collective-permute-start(f32[4,24,768]{2,1,0:T(8,128)S(1)} %get-tuple-element.55), channel_id=1, source_target_pairs={{0,8},{8,16},{16,24},{24,0},{1,9},{9,17},{17,25},{25,1},{2,10},{10... | collective-permute-start | bytes 884744 | tf_op jit(solution)/shard_map/ppermute | solution.py:306
  101.7 14.9 %collective-permute-start.21 = (f32[4,24,768]{2,1,0:T(8,128)S(1)}, f32[4,24,768]{2,1,0:T(8,128)S(1)}, u32[]{:S(2)}, u32[]{:S(2)}) collective-permute-start(f32[4,24,768]{2,1,0:T(8,128)S(1)} %get-tuple-element.56), channel_id=1, source_target_pairs={{0,16},{8,24},{16,0},{24,8},{1,17},{9,25},{17,1},{25,9},{2,18},{10... | collective-permute-start | bytes 884744 | tf_op jit(solution)/shard_map/ppermute | solution.py:306
  102.5 14.2 %collective-permute-start.22 = (f32[4,24,768]{2,1,0:T(8,128)S(1)}, f32[4,24,768]{2,1,0:T(8,128)S(1)}, u32[]{:S(2)}, u32[]{:S(2)}) collective-permute-start(f32[4,24,768]{2,1,0:T(8,128)S(1)} %get-tuple-element.57), channel_id=1, source_target_pairs={{0,24},{8,0},{16,8},{24,16},{1,25},{9,1},{17,9},{25,17},{2,26},{10... | collective-permute-start | bytes 884744 | tf_op jit(solution)/shard_map/ppermute | solution.py:306
  116.8 5.2 %collective-permute-start.23 = (f32[24,768]{1,0:T(8,128)S(1)}, f32[24,768]{1,0:T(8,128)S(1)}, u32[]{:S(2)}, u32[]{:S(2)}) collective-permute-start(f32[24,768]{1,0:T(8,128)S(1)} %get-tuple-element.58), channel_id=1, source_target_pairs={{0,2},{1,3},{2,0},{3,1},{4,6},{5,7},{6,4},{7,5},{8,10},{9,11},{10,... | collective-permute-start | bytes 221192 | tf_op jit(solution)/shard_map/ppermute | solution.py:144
  119.3 7.4 %collective-permute-start.25 = (f32[24,768]{1,0:T(8,128)S(1)}, f32[24,768]{1,0:T(8,128)S(1)}, u32[]{:S(2)}, u32[]{:S(2)}) collective-permute-start(f32[24,768]{1,0:T(8,128)S(1)} %get-tuple-element.59), channel_id=1, source_target_pairs={{0,6},{1,7},{2,4},{3,5},{4,2},{5,3},{6,0},{7,1},{8,14},{9,15},{10,... | collective-permute-start | bytes 221192 | tf_op jit(solution)/shard_map/ppermute | solution.py:144
  121.9 6.8 %collective-permute-start.24 = (f32[24,768]{1,0:T(8,128)S(1)}, f32[24,768]{1,0:T(8,128)S(1)}, u32[]{:S(2)}, u32[]{:S(2)}) collective-permute-start(f32[24,768]{1,0:T(8,128)S(1)} %get-tuple-element.60), channel_id=1, source_target_pairs={{0,4},{1,5},{2,6},{3,7},{4,0},{5,1},{6,2},{7,3},{8,12},{9,13},{10,... | collective-permute-start | bytes 221192 | tf_op jit(solution)/shard_map/ppermute | solution.py:144
  128.7 4.7 %collective-permute-start.28 = (f32[24,768]{1,0:T(8,128)S(1)}, f32[24,768]{1,0:T(8,128)S(1)}, u32[]{:S(2)}, u32[]{:S(2)}) collective-permute-start(f32[24,768]{1,0:T(8,128)S(1)} %fusion.2.refs_0_), channel_id=1, source_target_pairs={{0,24},{8,0},{16,8},{24,16},{1,25},{9,1},{17,9},{25,17},{2,26},{10... | collective-permute-start | bytes 221192 | tf_op jit(solution)/shard_map/ppermute | solution.py:306
  129.7 5.1 %collective-permute-start.27 = (f32[24,768]{1,0:T(8,128)S(1)}, f32[24,768]{1,0:T(8,128)S(1)}, u32[]{:S(2)}, u32[]{:S(2)}) collective-permute-start(f32[24,768]{1,0:T(8,128)S(1)} %fusion.2.refs_0_), channel_id=1, source_target_pairs={{0,16},{8,24},{16,0},{24,8},{1,17},{9,25},{17,1},{25,9},{2,18},{10... | collective-permute-start | bytes 221192 | tf_op jit(solution)/shard_map/ppermute | solution.py:306
  130.7 5.3 %collective-permute-start.26 = (f32[24,768]{1,0:T(8,128)S(1)}, f32[24,768]{1,0:T(8,128)S(1)}, u32[]{:S(2)}, u32[]{:S(2)}) collective-permute-start(f32[24,768]{1,0:T(8,128)S(1)} %fusion.2.refs_0_), channel_id=1, source_target_pairs={{0,8},{8,16},{16,24},{24,0},{1,9},{9,17},{17,25},{25,1},{2,10},{10... | collective-permute-start | bytes 221192 | tf_op jit(solution)/shard_map/ppermute | solution.py:306

commit v7 on v6

--- a/solution.py
+++ b/solution.py
@@ -12,7 +12,7 @@
 NZ = 64
 LANES = 128
 SUBLANES = 8
-VMEM_LIMIT = 40 * 1024 * 1024
+VMEM_LIMIT = 12 * 1024 * 1024
 
 
 def plane_matrix():
@@ -209,8 +209,24 @@
     )(here, *blocks)
 
 
+def half_product(band, count, which, hi, lo, out):
+    def picked(x):
+        return jnp.concatenate([x[2 * z + which] for z in range(band // 2)], axis=0)
+
+    def dot(a, b):
+        return lax.dot_general(a, b, (((1,), (1,)), ((), ())), preferred_element_type=jnp.float32)
+
+    left_hi, left_lo = picked(hi), picked(lo)
+    per_step = max(n for n in range(1, band + 1) if band % n == 0 and n * count <= 384)
+    for b in range(0, band, per_step):
+        right_hi = jnp.concatenate([hi[b + n] for n in range(per_step)], axis=0)
+        right_lo = jnp.concatenate([lo[b + n] for n in range(per_step)], axis=0)
+        columns = slice(b * count, (b + per_step) * count)
+        out[:, columns] = dot(left_hi, right_hi) + (dot(left_hi, right_lo) + dot(left_lo, right_hi))
+
+
 def gram_kernel(band, count, space, chunk, places, which_ref, *refs):
-    parts, out, wide = list(refs[:-2]), refs[-2], refs[-1]
+    parts, (out, hi, lo, wide) = list(refs[:-4]), refs[-4:]
     own = count // space
     for offset, subs, apart in places:
         size = subs * chunk
@@ -218,44 +234,48 @@
         for step in range(band):
             source = partner(which_ref[1], band, step, forward=False) if apart else step
             for g in range(space):
-                first = source * count + g * own + offset
-                first = pl.multiple_of(first, chunk) if apart else first
-                wide[pl.ds(first, size), :] = taken[step][g * size : (g + 1) * size, :]
-    which = which_ref[0]
-    pairs = band // 2
-    picked = [wide[pl.ds(pl.multiple_of((2 * z + which) * count, SUBLANES), count), :] for z in range(pairs)]
-    left = jnp.concatenate(picked, axis=0)
-    left_hi = left.astype(jnp.bfloat16)
-    left_lo = (left - left_hi.astype(jnp.float32)).astype(jnp.bfloat16)
-    total = band * count
-    step = 256 if total % 256 == 0 else total
-
-    def dot(a, b):
-        return lax.dot_general(a, b, (((1,), (1,)), ((), ())), preferred_element_type=jnp.float32)
-
-    for c in range(0, total, step):
-        right = wide[c : c + step, :]
-        hi = right.astype(jnp.bfloat16)
-        lo = (right - hi.astype(jnp.float32)).astype(jnp.bfloat16)
-        out[:, c : c + step] = dot(left_hi, hi) + (dot(left_hi, lo) + dot(left_lo, hi))
+                wide[source, g * own + offset : g * own + offset + size, :] = taken[step][g * size : (g + 1) * size, :]
+    for b in range(band):
+        top = wide[b].astype(jnp.bfloat16)
+        hi[b] = top
+        lo[b] = (wide[b] - top.astype(jnp.float32)).astype(jnp.bfloat16)
+    half_product(band, count, 1 - which_ref[0], hi, lo, out)
+
+
+def own_gram_kernel(band, count, which_ref, hi, lo, out):
+    half_product(band, count, which_ref[0], hi, lo, out)
 
 
 def gram(which, parts, band, count, space, chunk, places):
     cells = parts[0].shape[-1]
-    return pl.pallas_call(
+    half = jax.ShapeDtypeStruct((band // 2 * count, band * count), jnp.float32)
+    narrow = jax.ShapeDtypeStruct((band, count, cells), jnp.bfloat16)
+    params = pltpu.CompilerParams(vmem_limit_bytes=VMEM_LIMIT)
+    cost = pl.CostEstimate(
+        flops=3 * band * band * count * count * cells,
+        bytes_accessed=4 * band * count * (cells + band * count // 2),
+        transcendentals=0,
+    )
+    other, hi, lo = pl.pallas_call(
         functools.partial(gram_kernel, band, count, space, chunk, places),
-        out_shape=jax.ShapeDtypeStruct((band // 2 * count, band * count), jnp.float32),
+        out_shape=[half, narrow, narrow],
         in_specs=[SMEM_SPEC] + [VMEM_SPEC] * len(parts),
-        out_specs=VMEM_SPEC,
-        scratch_shapes=[pltpu.VMEM((band * count, cells), jnp.float32)],
-        compiler_params=pltpu.CompilerParams(vmem_limit_bytes=VMEM_LIMIT),
-        cost_estimate=pl.CostEstimate(
-            flops=3 * band * band * count * count * cells,
-            bytes_accessed=4 * band * count * (cells + band * count // 2),
-            transcendentals=0,
-        ),
+        out_specs=[VMEM_SPEC] * 3,
+        scratch_shapes=[pltpu.VMEM((band, count, cells), jnp.float32)],
+        compiler_params=params,
+        cost_estimate=cost,
         name="gram",
     )(which, *parts)
+    own = pl.pallas_call(
+        functools.partial(own_gram_kernel, band, count),
+        out_shape=half,
+        in_specs=[SMEM_SPEC] + [VMEM_SPEC] * 2,
+        out_specs=VMEM_SPEC,
+        compiler_params=params,
+        cost_estimate=cost,
+        name="own_gram",
+    )(which, hi, lo)
+    return own, other
 
 
 def combine_kernel(space, here_ref, a_ref, b_ref, *outs):
@@ -335,6 +355,7 @@
         return [outs[0]] + [rotate(outs[k], "space", k) for k in range(1, space)]
 
     made = [filtered(c, arrived) for c in range(min(chunks, 2))]
+    made[0], made[-1][0] = lax.optimization_barrier((made[0], made[-1][0]))
     head = pack(here, made[0], space, band, share, chunk, 1, False)[0]
     head, arrived = lax.optimization_barrier((head, arrived))
     parts = [lax.all_to_all(head, "band", split_axis=0, concat_axis=0, tiled=True)]
@@ -358,12 +379,10 @@
     core = b_index % 2
     pair = b_index // 2
 
-    def half(which):
-        return gram(jnp.stack([which, b_index]), parts, band, count, space, chunk, places)
-
-    other = lax.ppermute(half(1 - core), "band", [(i, i ^ 1) for i in range(band)])
+    own_half, other = gram(jnp.stack([core, b_index]), parts, band, count, space, chunk, places)
+    other = lax.ppermute(other, "band", [(i, i ^ 1) for i in range(band)])
     split = (pairs, space, own, band * count)
-    sums = combine(here, half(core).reshape(split), other.reshape(split))
+    sums = combine(here, own_half.reshape(split), other.reshape(split))
 
     mine = sums[0]
     for k in range(1, space):

time: 138 us -> 131 us (0.949)
  local copies, waits for them, and re-layouts: 12.1 us -> 3.57 us
    unnamed x48 -> x24, local copies, waits for them, and re-layouts: 12.1 us -> 3.54 us
    ppermute x10, waiting for transfers between devices: 14.2 us -> 17.6 us  [exchange(): return lax.ppermute(x, axis, pairs)]
    ppermute x18, waiting for transfers between devices: 40.8 us -> 38.1 us  [rotate(): return lax.ppermute(x, axis, [(i, (i + step) % size) for i in range(size)])]
    pallas_call x0 -> x1, Pallas kernels: none -> 1.92 us  [gram(): pl.pallas_call(functools.partial(own_gram_kernel, band, count), out_shape...]
    pallas_call x2 -> x1, Pallas kernels: 4.27 us -> 2.7 us  [gram(): pl.pallas_call(functools.partial(gram_kernel, band, count, space, chunk,...]
  transfers between devices with their start and end apart: 31 -> 31, of which waited for: 15 -> 16; matrix products, arithmetic and copies ran while one was open for 0% -> 0% of each run, Pallas kernels for 8% -> 9%
where the time goes in v7:
time: 131 us; the launch traced here: 130 us
  waiting for transfers between devices  56.3 us (43%)
  starting transfers between devices  49.6 us (38%)
  Pallas kernels  19.5 us (15%)
  local copies, waits for them, and re-layouts  3.57 us (3%)
    ppermute x18, waiting for transfers between devices, rotate(): return lax.ppermute(x, axis, [(i, (i + step) % size) for i in range(size)])  38.1 us
    ppermute x18, starting transfers between devices, rotate(): return lax.ppermute(x, axis, [(i, (i + step) % size) for i in range(size)])  23.6 us
    ppermute x10, waiting for transfers between devices, exchange(): return lax.ppermute(x, axis, pairs)  17.6 us
    ppermute x10, starting transfers between devices, exchange(): return lax.ppermute(x, axis, pairs)  15.3 us
    pallas_call x3, Pallas kernels, run_filter(): pl.pallas_call(functools.partial(filter_kernel, space, layers, tiles, chu...  7.62 us
    all_to_all x1, starting transfers between devices, shards(): lax.all_to_all(orbitals, 'space', split_axis=0, concat_axis=0, tiled=True)  5.31 us
    all_to_all x1, starting transfers between devices, shards(): lax.all_to_all(head, 'band', split_axis=0, concat_axis=0, tiled=True)  5.08 us
    unnamed x24, local copies, waits for them, and re-layouts  3.54 us
  transfers between devices with their start and end apart: 31, of which 16 were waited for; matrix products, arithmetic and copies ran while one was open for 0% of the time, Pallas kernels for 9%

profile of v7, /device:TPU:0, one launch (start us, length us, event | category | flops | bytes accessed | tf_op | source)
XLA Modules:
  0.0 130.0 jit_solution(11427020264749427972)
XLA Ops:
  0.6 0.0 copy-start
  0.7 5.3 %all-to-all-start = ((f32[96,2,2048]{2,1,0:T(2,128)}), f32[96,2,2048]{2,1,0:T(2,128)S(1)}, u32[]{:S(2)}, u32[]{:S(2)}) async-start(f32[96,2,2048]{2,1,0:T(2,128)} %param.3), calls=%async_computation | async-start | bytes 3145728 | tf_op jit(solution)/shard_map/all_to_all | solution.py:351
  6.0 2.0 %collective-permute-start.2 = (f32[32,128]{1,0:T(8,128)S(1)}, f32[32,128]{1,0:T(8,128)S(1)}, u32[]{:S(2)}, u32[]{:S(2)}) collective-permute-start(f32[32,128]{1,0:T(8,128)S(1)} %bitcast.40), channel_id=1, source_target_pairs={{0,8},{8,16},{16,24},{24,0},{1,9},{9,17},{17,25},{25,1},{2,10},{10... | collective-permute-start | bytes 49160 | tf_op jit(solution)/shard_map/ppermute | solution.py:326
  8.0 1.5 %collective-permute-start.1 = (f32[32,128]{1,0:T(8,128)S(1)}, f32[32,128]{1,0:T(8,128)S(1)}, u32[]{:S(2)}, u32[]{:S(2)}) collective-permute-start(f32[32,128]{1,0:T(8,128)S(1)} %bitcast.41), channel_id=1, source_target_pairs={{0,16},{8,24},{16,0},{24,8},{1,17},{9,25},{17,1},{25,9},{2,18},{10... | collective-permute-start | bytes 49160 | tf_op jit(solution)/shard_map/ppermute | solution.py:326
  9.4 1.5 %collective-permute-start = (f32[32,128]{1,0:T(8,128)S(1)}, f32[32,128]{1,0:T(8,128)S(1)}, u32[]{:S(2)}, u32[]{:S(2)}) collective-permute-start(f32[32,128]{1,0:T(8,128)S(1)} %bitcast.42), channel_id=1, source_target_pairs={{0,24},{8,0},{16,8},{24,16},{1,25},{9,1},{17,9},{25,17},{2,26},{10... | collective-permute-start | bytes 49160 | tf_op jit(solution)/shard_map/ppermute | solution.py:326
  10.9 0.1 pad_add_fusion.here_ref
  11.0 15.6 %collective-permute-done.2.refs_3_ = f32[32,128]{1,0:T(8,128)S(1)} collective-permute-done((f32[32,128]{1,0:T(8,128)S(1)}, f32[32,128]{1,0:T(8,128)S(1)}, u32[]{:S(2)}, u32[]{:S(2)}) %collective-permute-start.2) | collective-permute-done | bytes 16416 | tf_op jit(solution)/shard_map/ppermute | solution.py:326
  26.6 0.0 collective-permute-done.1.refs_2_
  26.7 2.3 %filter.3 = (f32[32,8,128]{2,1,0:T(8,128)S(1)}, f32[32,8,128]{2,1,0:T(8,128)S(1)}, f32[32,8,128]{2,1,0:T(8,128)S(1)}, f32[32,8,128]{2,1,0:T(8,128)S(1)}) custom-call(s32[2]{0:T(128)S(1)} %pad_add_fusion.here_ref, f32[3072,128]{1,0:T(8,128)S(1)} %bitcast.35, bf16[512,256]{1,0:T(8,128)(2,1)S(1)} %copy-done, f32[32,128]{1,0:T(8,128)S(1)} %bitcast.43, ...), custom_call_target="tpu_custom_call" | custom-call | flops 6553600 | bytes 1048576 | tf_op jit(solution)/shard_map/filter/pallas_call | solution.py:114
  29.0 0.8 collective-permute-start.3
  29.7 0.5 collective-permute-start.4
  30.3 2.4 %collective-permute-start.5 = (f32[32,8,128]{2,1,0:T(8,128)S(1)}, f32[32,8,128]{2,1,0:T(8,128)S(1)}, u32[]{:S(2)}, u32[]{:S(2)}) collective-permute-start(f32[32,8,128]{2,1,0:T(8,128)S(1)} %get-tuple-element.41), channel_id=1, source_target_pairs={{0,24},{8,0},{16,8},{24,16},{1,25},{9,1},{17,9},{25,17},{2,26},{10... | collective-permute-start | bytes 393224 | tf_op jit(solution)/shard_map/ppermute | solution.py:326
  32.7 3.0 %filter.4 = (f32[32,8,128]{2,1,0:T(8,128)S(1)}, f32[32,8,128]{2,1,0:T(8,128)}, f32[32,8,128]{2,1,0:T(8,128)}, f32[32,8,128]{2,1,0:T(8,128)}) custom-call(s32[2]{0:T(128)S(1)} %pad_add_fusion.here_ref, f32[3072,128]{1,0:T(8,128)S(1)} %bitcast.36, bf16[512,256]{1,0:T(8,128)(2,1)S(1)} %copy-done, f32[32,128]{1,0:T(8,128)S(1)} %bitcast.44, ...), custom_call_target="tpu_custom_call" | custom-call | flops 6553600 | bytes 1048576 | tf_op jit(solution)/shard_map/filter/pallas_call | solution.py:114
  35.7 0.6 collective-permute-done.4.refs_2_.refs_6_
  36.3 1.4 %pack.2 = f32[8,32,512]{2,1,0:T(8,128)} custom-call(s32[2]{0:T(128)S(1)} %pad_add_fusion.here_ref, f32[32,8,128]{2,1,0:T(8,128)S(1)} %get-tuple-element.44.refs_0_, f32[32,8,128]{2,1,0:T(8,128)S(1)} %collective-permute-done.3.refs_1_.refs_3_, f32[32,8,128]{2,1,0:T(8,128)S(1)} %collective-permute-done.4.refs_2_.refs_6_, ...), custom_call_target="tpu_custom_call" | custom-call | bytes 1048576 | tf_op jit(solution)/shard_map/pack/pallas_call | solution.py:168
  37.7 5.1 %all-to-all-start.1 = ((f32[8,32,512]{2,1,0:T(8,128)}), f32[8,32,512]{2,1,0:T(8,128)S(1)}, u32[]{:S(2)}, u32[]{:S(2)}) async-start(f32[8,32,512]{2,1,0:T(8,128)} %pack.2), calls=%async_computation.1 | async-start | bytes 1048576 | tf_op jit(solution)/shard_map/all_to_all | solution.py:361
  42.8 2.1 %collective-permute-start.6 = (f32[32,8,128]{2,1,0:T(8,128)}, f32[32,8,128]{2,1,0:T(8,128)S(1)}, u32[]{:S(2)}, u32[]{:S(2)}) collective-permute-start(f32[32,8,128]{2,1,0:T(8,128)} %get-tuple-element.50), channel_id=1, source_target_pairs={{0,8},{8,16},{16,24},{24,0},{1,9},{9,17},{17,25},{25,1},{2,10},{10... | collective-permute-start | bytes 393224 | tf_op jit(solution)/shard_map/ppermute | solution.py:326
  44.9 1.3 collective-permute-start.8
  46.2 0.3 collective-permute-start.10
  46.5 0.7 copy-done.3
  47.2 0.7 copy-done.5
  47.9 0.7 copy-done.7
  48.7 0.7 copy-done.9
  49.3 2.3 %filter.5 = (f32[32,8,128]{2,1,0:T(8,128)S(1)}, f32[32,8,128]{2,1,0:T(8,128)S(1)}, f32[32,8,128]{2,1,0:T(8,128)S(1)}, f32[32,8,128]{2,1,0:T(8,128)S(1)}) custom-call(s32[2]{0:T(128)S(1)} %copy-done.9, f32[3072,128]{1,0:T(8,128)S(1)} %bitcast.37, bf16[512,256]{1,0:T(8,128)(2,1)S(1)} %copy-done, f32[32,128]{1,0:T(8,128)S(1)} %bitcast.45, ...), custom_call_target="tpu_custom_call" | custom-call | flops 6553600 | bytes 1048576 | tf_op jit(solution)/shard_map/filter/pallas_call | solution.py:114
  51.6 1.7 %collective-permute-start.7 = (f32[32,8,128]{2,1,0:T(8,128)S(1)}, f32[32,8,128]{2,1,0:T(8,128)S(1)}, u32[]{:S(2)}, u32[]{:S(2)}) collective-permute-start(f32[32,8,128]{2,1,0:T(8,128)S(1)} %get-tuple-element.51), channel_id=1, source_target_pairs={{0,8},{8,16},{16,24},{24,0},{1,9},{9,17},{17,25},{25,1},{2,10},{10... | collective-permute-start | bytes 393224 | tf_op jit(solution)/shard_map/ppermute | solution.py:326
  53.4 0.7 collective-permute-start.9
  54.1 1.8 %collective-permute-start.11 = (f32[32,8,128]{2,1,0:T(8,128)S(1)}, f32[32,8,128]{2,1,0:T(8,128)S(1)}, u32[]{:S(2)}, u32[]{:S(2)}) collective-permute-start(f32[32,8,128]{2,1,0:T(8,128)S(1)} %get-tuple-element.55), channel_id=1, source_target_pairs={{0,24},{8,0},{16,8},{24,16},{1,25},{9,1},{17,9},{25,17},{2,26},{10... | collective-permute-start | bytes 393224 | tf_op jit(solution)/shard_map/ppermute | solution.py:326
  55.9 3.1 %collective-permute-done.7.refs_3_.refs_5_ = f32[32,8,128]{2,1,0:T(8,128)S(1)} collective-permute-done((f32[32,8,128]{2,1,0:T(8,128)S(1)}, f32[32,8,128]{2,1,0:T(8,128)S(1)}, u32[]{:S(2)}, u32[]{:S(2)}) %collective-permute-start.7) | collective-permute-done | bytes 131104 | tf_op jit(solution)/shard_map/ppermute | solution.py:326
  59.0 1.6 %collective-permute-done.9.refs_5_.refs_8_ = f32[32,8,128]{2,1,0:T(8,128)S(1)} collective-permute-done((f32[32,8,128]{2,1,0:T(8,128)S(1)}, f32[32,8,128]{2,1,0:T(8,128)S(1)}, u32[]{:S(2)}, u32[]{:S(2)}) %collective-permute-start.9) | collective-permute-done | bytes 131104 | tf_op jit(solution)/shard_map/ppermute | solution.py:326
  60.6 1.3 %pack.3 = (f32[64,512]{1,0:T(8,128)S(1)}, f32[64,512]{1,0:T(8,128)S(1)}, f32[64,512]{1,0:T(8,128)}, f32[64,512]{1,0:T(8,128)S(1)}, f32[64,512]{1,0:T(8,128)S(1)}...) custom-call(s32[2]{0:T(128)S(1)} %copy-done.10, ...), custom_call_target="tpu_custom_call" | custom-call | bytes 2097152 | tf_op jit(solution)/shard_map/pack/pallas_call | solution.py:168
  61.9 2.7 %collective-permute-start.12 = (f32[64,512]{1,0:T(8,128)S(1)}, f32[64,512]{1,0:T(8,128)S(1)}, u32[]{:S(2)}, u32[]{:S(2)}) collective-permute-start(f32[64,512]{1,0:T(8,128)S(1)} %get-tuple-element.56), channel_id=1, source_target_pairs={{0,7},{1,6},{2,5},{3,4},{4,3},{5,2},{6,1},{7,0},{8,15},{9,14},{10,... | collective-permute-start | bytes 393224 | tf_op jit(solution)/shard_map/ppermute | solution.py:144
  64.6 0.9 collective-permute-start.13
  65.5 1.4 %collective-permute-start.15 = (f32[64,512]{1,0:T(8,128)S(1)}, f32[64,512]{1,0:T(8,128)S(1)}, u32[]{:S(2)}, u32[]{:S(2)}) collective-permute-start(f32[64,512]{1,0:T(8,128)S(1)} %get-tuple-element.62), channel_id=1, source_target_pairs={{0,3},{1,2},{2,1},{3,0},{4,7},{5,6},{6,5},{7,4},{8,11},{9,10},{10,... | collective-permute-start | bytes 393224 | tf_op jit(solution)/shard_map/ppermute | solution.py:144
  66.9 2.6 %collective-permute-done.12.refs_8_ = f32[64,512]{1,0:T(8,128)S(1)} collective-permute-done((f32[64,512]{1,0:T(8,128)S(1)}, f32[64,512]{1,0:T(8,128)S(1)}, u32[]{:S(2)}, u32[]{:S(2)}) %collective-permute-start.12) | collective-permute-done | bytes 131104 | tf_op jit(solution)/shard_map/ppermute | solution.py:144
  69.5 2.9 %collective-permute-start.17 = (f32[64,512]{1,0:T(8,128)S(1)}, f32[64,512]{1,0:T(8,128)}, u32[]{:S(2)}, u32[]{:S(2)}) collective-permute-start(f32[64,512]{1,0:T(8,128)S(1)} %get-tuple-element.64), channel_id=1, source_target_pairs={{0,5},{1,4},{2,7},{3,6},{4,1},{5,0},{6,3},{7,2},{8,13},{9,12},{10,... | collective-permute-start | bytes 393224 | tf_op jit(solution)/shard_map/ppermute | solution.py:144
  72.5 1.9 %collective-permute-start.18 = (f32[64,512]{1,0:T(8,128)S(1)}, f32[64,512]{1,0:T(8,128)}, u32[]{:S(2)}, u32[]{:S(2)}) collective-permute-start(f32[64,512]{1,0:T(8,128)S(1)} %get-tuple-element.65), channel_id=1, source_target_pairs={{0,6},{1,7},{2,4},{3,5},{4,2},{5,3},{6,0},{7,1},{8,14},{9,15},{10,... | collective-permute-start | bytes 393224 | tf_op jit(solution)/shard_map/ppermute | solution.py:144
  74.3 0.1 pad_add_fusion.1.which_ref
  74.4 0.7 copy-done.11
  75.1 2.6 %unpack.1 = f32[3072,128]{1,0:T(8,128)} custom-call(s32[2]{0:T(128)S(1)} %copy-done.11, f32[32,8,128]{2,1,0:T(8,128)S(1)} %get-tuple-element.44.refs_0_, f32[32,8,128]{2,1,0:T(8,128)S(1)} %get-tuple-element.43.refs_0_.refs_1_, f32[32,8,128]{2,1,0:T(8,128)S(1)} %get-tuple-element.49.refs_1_.refs_2_, f32[32,8,128]{2,1,0:T(8,128)S(1)} %collective-permute-done.3.refs_1_.refs_3_, ...), custom_call_target="tpu_custom_call" | custom-call | bytes 3145728 | tf_op jit(solution)/shard_map/unpack/pallas_call | solution.py:201
  77.7 1.1 collective-permute-done.15.refs_4_
  78.8 6.9 %collective-permute-done.17.refs_6_ = f32[64,512]{1,0:T(8,128)} collective-permute-done((f32[64,512]{1,0:T(8,128)S(1)}, f32[64,512]{1,0:T(8,128)}, u32[]{:S(2)}, u32[]{:S(2)}) %collective-permute-start.17) | collective-permute-done | bytes 131104 | tf_op jit(solution)/shard_map/ppermute | solution.py:144
  85.6 2.7 %gram.1 = (f32[384,768]{1,0:T(8,128)S(1)}, bf16[8,96,512]{2,1,0:T(8,128)(2,1)S(1)}, bf16[8,96,512]{2,1,0:T(8,128)(2,1)S(1)}) custom-call(s32[2]{0:T(128)S(1)} %pad_add_fusion.1.which_ref, f32[8,32,512]{2,1,0:T(8,128)S(1)} %all-to-all-done.1.refs_0_, f32[64,512]{1,0:T(8,128)S(1)} %get-tuple-element.59.refs_1_, f32[64,512]{1,0:T(8,128)S(1)} %collective-permute-done.13.refs_2_, ...), custom_call_target="tpu_custom_call" | custom-call | flops 905969664 | bytes 2752512 | tf_op jit(solution)/shard_map/gram/pallas_call | solution.py:259
  88.3 0.3 collective-permute-start.19
  88.7 1.9 %own_gram.1 = f32[384,768]{1,0:T(8,128)S(1)} custom-call(s32[2]{0:T(128)S(1)} %pad_add_fusion.1.which_ref, bf16[8,96,512]{2,1,0:T(8,128)(2,1)S(1)} %get-tuple-element.67.hi, bf16[8,96,512]{2,1,0:T(8,128)(2,1)S(1)} %get-tuple-element.68.lo), custom_call_target="tpu_custom_call" | custom-call | flops 905969664 | bytes 2752512 | tf_op jit(solution)/shard_map/own_gram/pallas_call | solution.py:269
  90.6 0.7 collective-permute-done.19
  91.3 0.7 combine.1
  91.9 1.8 %collective-permute-start.20 = (f32[4,24,768]{2,1,0:T(8,128)S(1)}, f32[4,24,768]{2,1,0:T(8,128)S(1)}, u32[]{:S(2)}, u32[]{:S(2)}) collective-permute-start(f32[4,24,768]{2,1,0:T(8,128)S(1)} %get-tuple-element.71), channel_id=1, source_target_pairs={{0,8},{8,16},{16,24},{24,0},{1,9},{9,17},{17,25},{25,1},{2,10},{10... | collective-permute-start | bytes 884744 | tf_op jit(solution)/shard_map/ppermute | solution.py:326
  93.7 1.0 collective-permute-start.21
  94.7 1.3 collective-permute-start.22
  96.0 6.8 %collective-permute-done.20 = f32[4,24,768]{2,1,0:T(8,128)S(1)} collective-permute-done((f32[4,24,768]{2,1,0:T(8,128)S(1)}, f32[4,24,768]{2,1,0:T(8,128)S(1)}, u32[]{:S(2)}, u32[]{:S(2)}) %collective-permute-start.20) | collective-permute-done | bytes 294944 | tf_op jit(solution)/shard_map/ppermute | solution.py:326
  102.8 5.6 %collective-permute-done.21 = f32[4,24,768]{2,1,0:T(8,128)S(1)} collective-permute-done((f32[4,24,768]{2,1,0:T(8,128)S(1)}, f32[4,24,768]{2,1,0:T(8,128)S(1)}, u32[]{:S(2)}, u32[]{:S(2)}) %collective-permute-start.21) | collective-permute-done | bytes 294944 | tf_op jit(solution)/shard_map/ppermute | solution.py:326
  108.4 0.1 add_add_fusion
  108.5 3.5 %collective-permute-start.23 = (f32[24,768]{1,0:T(8,128)S(1)}, f32[24,768]{1,0:T(8,128)S(1)}, u32[]{:S(2)}, u32[]{:S(2)}) collective-permute-start(f32[24,768]{1,0:T(8,128)S(1)} %get-tuple-element.74), channel_id=1, source_target_pairs={{0,2},{1,3},{2,0},{3,1},{4,6},{5,7},{6,4},{7,5},{8,10},{9,11},{10,... | collective-permute-start | bytes 221192 | tf_op jit(solution)/shard_map/ppermute | solution.py:144
  112.0 2.0 %collective-permute-start.25 = (f32[24,768]{1,0:T(8,128)S(1)}, f32[24,768]{1,0:T(8,128)S(1)}, u32[]{:S(2)}, u32[]{:S(2)}) collective-permute-start(f32[24,768]{1,0:T(8,128)S(1)} %get-tuple-element.75), channel_id=1, source_target_pairs={{0,6},{1,7},{2,4},{3,5},{4,2},{5,3},{6,0},{7,1},{8,14},{9,15},{10,... | collective-permute-start | bytes 221192 | tf_op jit(solution)/shard_map/ppermute | solution.py:144
  114.0 0.4 collective-permute-done.23
  114.5 4.4 %collective-permute-done.25 = f32[24,768]{1,0:T(8,128)S(1)} collective-permute-done((f32[24,768]{1,0:T(8,128)S(1)}, f32[24,768]{1,0:T(8,128)S(1)}, u32[]{:S(2)}, u32[]{:S(2)}) %collective-permute-start.25) | collective-permute-done | bytes 73760 | tf_op jit(solution)/shard_map/ppermute | solution.py:144
  118.8 2.3 %collective-permute-done.24 = f32[24,768]{1,0:T(8,128)S(1)} collective-permute-done((f32[24,768]{1,0:T(8,128)S(1)}, f32[24,768]{1,0:T(8,128)S(1)}, u32[]{:S(2)}, u32[]{:S(2)}) %collective-permute-start.24) | collective-permute-done | bytes 73760 | tf_op jit(solution)/shard_map/ppermute | solution.py:144
  121.1 1.3 %collective-permute-start.28 = (f32[24,768]{1,0:T(8,128)S(1)}, f32[24,768]{1,0:T(8,128)S(1)}, u32[]{:S(2)}, u32[]{:S(2)}) collective-permute-start(f32[24,768]{1,0:T(8,128)S(1)} %fusion.2.refs_0_), channel_id=1, source_target_pairs={{0,24},{8,0},{16,8},{24,16},{1,25},{9,1},{17,9},{25,17},{2,26},{10... | collective-permute-start | bytes 221192 | tf_op jit(solution)/shard_map/ppermute | solution.py:326
  122.4 1.1 collective-permute-start.27
  123.5 0.5 collective-permute-start.26
  124.1 1.5 %collective-permute-done.28.refs_3_ = f32[24,768]{1,0:T(8,128)S(1)} collective-permute-done((f32[24,768]{1,0:T(8,128)S(1)}, f32[24,768]{1,0:T(8,128)S(1)}, u32[]{:S(2)}, u32[]{:S(2)}) %collective-permute-start.28) | collective-permute-done | bytes 73760 | tf_op jit(solution)/shard_map/ppermute | solution.py:326
  125.5 2.1 %collective-permute-done.27.refs_2_ = f32[24,768]{1,0:T(8,128)S(1)} collective-permute-done((f32[24,768]{1,0:T(8,128)S(1)}, f32[24,768]{1,0:T(8,128)S(1)}, u32[]{:S(2)}, u32[]{:S(2)}) %collective-permute-start.27) | collective-permute-done | bytes 73760 | tf_op jit(solution)/shard_map/ppermute | solution.py:326
  127.6 1.2 collective-permute-done.26.refs_1_
  128.8 1.3 place.1
  (37 shorter events, 0.1 us)
Async XLA Ops:
  0.6 26.0 %copy-start = (bf16[512,256]{1,0:T(8,128)(2,1)S(1)}, bf16[512,256]{1,0:T(8,128)(2,1)}, u32[]{:S(2)}) copy-start(bf16[512,256]{1,0:T(8,128)(2,1)} %constant.50.clone.m_ref) | copy-start | bytes 786436
  0.6 5.3 %copy-start.1 = (f32[2,2048]{1,0:T(2,128)S(1)}, f32[2,2048]{1,0:T(2,128)}, u32[]{:S(2)}) copy-start(f32[2,2048]{1,0:T(2,128)} %param.4) | copy-start | bytes 49156
  0.7 26.0 %all-to-all-start = ((f32[96,2,2048]{2,1,0:T(2,128)}), f32[96,2,2048]{2,1,0:T(2,128)S(1)}, u32[]{:S(2)}, u32[]{:S(2)}) async-start(f32[96,2,2048]{2,1,0:T(2,128)} %param.3), calls=%async_computation | async-start | bytes 3145728 | tf_op jit(solution)/shard_map/all_to_all | solution.py:351
  6.0 20.7 %collective-permute-start.2 = (f32[32,128]{1,0:T(8,128)S(1)}, f32[32,128]{1,0:T(8,128)S(1)}, u32[]{:S(2)}, u32[]{:S(2)}) collective-permute-start(f32[32,128]{1,0:T(8,128)S(1)} %bitcast.40), channel_id=1, source_target_pairs={{0,8},{8,16},{16,24},{24,0},{1,9},{9,17},{17,25},{25,1},{2,10},{10... | collective-permute-start | bytes 49160 | tf_op jit(solution)/shard_map/ppermute | solution.py:326
  8.0 18.7 %collective-permute-start.1 = (f32[32,128]{1,0:T(8,128)S(1)}, f32[32,128]{1,0:T(8,128)S(1)}, u32[]{:S(2)}, u32[]{:S(2)}) collective-permute-start(f32[32,128]{1,0:T(8,128)S(1)} %bitcast.41), channel_id=1, source_target_pairs={{0,16},{8,24},{16,0},{24,8},{1,17},{9,25},{17,1},{25,9},{2,18},{10... | collective-permute-start | bytes 49160 | tf_op jit(solution)/shard_map/ppermute | solution.py:326
  9.4 17.2 %collective-permute-start = (f32[32,128]{1,0:T(8,128)S(1)}, f32[32,128]{1,0:T(8,128)S(1)}, u32[]{:S(2)}, u32[]{:S(2)}) collective-permute-start(f32[32,128]{1,0:T(8,128)S(1)} %bitcast.42), channel_id=1, source_target_pairs={{0,24},{8,0},{16,8},{24,16},{1,25},{9,1},{17,9},{25,17},{2,26},{10... | collective-permute-start | bytes 49160 | tf_op jit(solution)/shard_map/ppermute | solution.py:326
  11.0 25.3 %copy-start.8 = (s32[2]{0:T(128)}, s32[2]{0:T(128)S(1)}, u32[]{:S(2)}) copy-start(s32[2]{0:T(128)S(1)} %pad_add_fusion.here_ref) | copy-start | bytes 28
  26.6 9.1 %copy-start.2 = (f32[32,128]{1,0:T(8,128)}, f32[32,128]{1,0:T(8,128)S(1)}, u32[]{:S(2)}) copy-start(f32[32,128]{1,0:T(8,128)S(1)} %collective-permute-done.2.refs_3_) | copy-start | bytes 49156
  26.6 9.1 %copy-start.4 = (f32[32,128]{1,0:T(8,128)}, f32[32,128]{1,0:T(8,128)S(1)}, u32[]{:S(2)}) copy-start(f32[32,128]{1,0:T(8,128)S(1)} %collective-permute-done.1.refs_2_) | copy-start | bytes 49156
  26.7 9.1 %copy-start.6 = (f32[32,128]{1,0:T(8,128)}, f32[32,128]{1,0:T(8,128)S(1)}, u32[]{:S(2)}) copy-start(f32[32,128]{1,0:T(8,128)S(1)} %collective-permute-done.refs_1_) | copy-start | bytes 49156
  29.0 6.7 %collective-permute-start.3 = (f32[32,8,128]{2,1,0:T(8,128)S(1)}, f32[32,8,128]{2,1,0:T(8,128)S(1)}, u32[]{:S(2)}, u32[]{:S(2)}) collective-permute-start(f32[32,8,128]{2,1,0:T(8,128)S(1)} %get-tuple-element.39), channel_id=1, source_target_pairs={{0,8},{8,16},{16,24},{24,0},{1,9},{9,17},{17,25},{25,1},{2,10},{10... | collective-permute-start | bytes 393224 | tf_op jit(solution)/shard_map/ppermute | solution.py:326
  29.7 6.6 %collective-permute-start.4 = (f32[32,8,128]{2,1,0:T(8,128)S(1)}, f32[32,8,128]{2,1,0:T(8,128)S(1)}, u32[]{:S(2)}, u32[]{:S(2)}) collective-permute-start(f32[32,8,128]{2,1,0:T(8,128)S(1)} %get-tuple-element.40), channel_id=1, source_target_pairs={{0,16},{8,24},{16,0},{24,8},{1,17},{9,25},{17,1},{25,9},{2,18},{10... | collective-permute-start | bytes 393224 | tf_op jit(solution)/shard_map/ppermute | solution.py:326
  30.3 6.0 %collective-permute-start.5 = (f32[32,8,128]{2,1,0:T(8,128)S(1)}, f32[32,8,128]{2,1,0:T(8,128)S(1)}, u32[]{:S(2)}, u32[]{:S(2)}) collective-permute-start(f32[32,8,128]{2,1,0:T(8,128)S(1)} %get-tuple-element.41), channel_id=1, source_target_pairs={{0,24},{8,0},{16,8},{24,16},{1,25},{9,1},{17,9},{25,17},{2,26},{10... | collective-permute-start | bytes 393224 | tf_op jit(solution)/shard_map/ppermute | solution.py:326
  37.7 47.9 %all-to-all-start.1 = ((f32[8,32,512]{2,1,0:T(8,128)}), f32[8,32,512]{2,1,0:T(8,128)S(1)}, u32[]{:S(2)}, u32[]{:S(2)}) async-start(f32[8,32,512]{2,1,0:T(8,128)} %pack.2), calls=%async_computation.1 | async-start | bytes 1048576 | tf_op jit(solution)/shard_map/all_to_all | solution.py:361
  42.8 17.8 %copy-start.10 = (s32[2]{0:T(128)S(1)}, s32[2]{0:T(128)}, u32[]{:S(2)}) copy-start(s32[2]{0:T(128)} %copy-done.8) | copy-start | bytes 28
  42.8 11.3 %collective-permute-start.6 = (f32[32,8,128]{2,1,0:T(8,128)}, f32[32,8,128]{2,1,0:T(8,128)S(1)}, u32[]{:S(2)}, u32[]{:S(2)}) collective-permute-start(f32[32,8,128]{2,1,0:T(8,128)} %get-tuple-element.50), channel_id=1, source_target_pairs={{0,8},{8,16},{16,24},{24,0},{1,9},{9,17},{17,25},{25,1},{2,10},{10... | collective-permute-start | bytes 393224 | tf_op jit(solution)/shard_map/ppermute | solution.py:326
  44.9 11.0 %collective-permute-start.8 = (f32[32,8,128]{2,1,0:T(8,128)}, f32[32,8,128]{2,1,0:T(8,128)S(1)}, u32[]{:S(2)}, u32[]{:S(2)}) collective-permute-start(f32[32,8,128]{2,1,0:T(8,128)} %get-tuple-element.52), channel_id=1, source_target_pairs={{0,16},{8,24},{16,0},{24,8},{1,17},{9,25},{17,1},{25,9},{2,18},{10... | collective-permute-start | bytes 393224 | tf_op jit(solution)/shard_map/ppermute | solution.py:326
  46.2 9.8 %collective-permute-start.10 = (f32[32,8,128]{2,1,0:T(8,128)}, f32[32,8,128]{2,1,0:T(8,128)S(1)}, u32[]{:S(2)}, u32[]{:S(2)}) collective-permute-start(f32[32,8,128]{2,1,0:T(8,128)} %get-tuple-element.54), channel_id=1, source_target_pairs={{0,24},{8,0},{16,8},{24,16},{1,25},{9,1},{17,9},{25,17},{2,26},{10... | collective-permute-start | bytes 393224 | tf_op jit(solution)/shard_map/ppermute | solution.py:326
  46.5 0.7 copy-start.3
  47.2 0.7 copy-start.5
  47.9 0.7 copy-start.7
  48.7 0.7 copy-start.9
  51.6 7.3 %collective-permute-start.7 = (f32[32,8,128]{2,1,0:T(8,128)S(1)}, f32[32,8,128]{2,1,0:T(8,128)S(1)}, u32[]{:S(2)}, u32[]{:S(2)}) collective-permute-start(f32[32,8,128]{2,1,0:T(8,128)S(1)} %get-tuple-element.51), channel_id=1, source_target_pairs={{0,8},{8,16},{16,24},{24,0},{1,9},{9,17},{17,25},{25,1},{2,10},{10... | collective-permute-start | bytes 393224 | tf_op jit(solution)/shard_map/ppermute | solution.py:326
  53.4 7.2 %collective-permute-start.9 = (f32[32,8,128]{2,1,0:T(8,128)S(1)}, f32[32,8,128]{2,1,0:T(8,128)S(1)}, u32[]{:S(2)}, u32[]{:S(2)}) collective-permute-start(f32[32,8,128]{2,1,0:T(8,128)S(1)} %get-tuple-element.53), channel_id=1, source_target_pairs={{0,16},{8,24},{16,0},{24,8},{1,17},{9,25},{17,1},{25,9},{2,18},{10... | collective-permute-start | bytes 393224 | tf_op jit(solution)/shard_map/ppermute | solution.py:326
  54.1 6.5 %collective-permute-start.11 = (f32[32,8,128]{2,1,0:T(8,128)S(1)}, f32[32,8,128]{2,1,0:T(8,128)S(1)}, u32[]{:S(2)}, u32[]{:S(2)}) collective-permute-start(f32[32,8,128]{2,1,0:T(8,128)S(1)} %get-tuple-element.55), channel_id=1, source_target_pairs={{0,24},{8,0},{16,8},{24,16},{1,25},{9,1},{17,9},{25,17},{2,26},{10... | collective-permute-start | bytes 393224 | tf_op jit(solution)/shard_map/ppermute | solution.py:326
  61.9 7.6 %collective-permute-start.12 = (f32[64,512]{1,0:T(8,128)S(1)}, f32[64,512]{1,0:T(8,128)S(1)}, u32[]{:S(2)}, u32[]{:S(2)}) collective-permute-start(f32[64,512]{1,0:T(8,128)S(1)} %get-tuple-element.56), channel_id=1, source_target_pairs={{0,7},{1,6},{2,5},{3,4},{4,3},{5,2},{6,1},{7,0},{8,15},{9,14},{10,... | collective-permute-start | bytes 393224 | tf_op jit(solution)/shard_map/ppermute | solution.py:144
  64.6 7.8 %collective-permute-start.13 = (f32[64,512]{1,0:T(8,128)S(1)}, f32[64,512]{1,0:T(8,128)S(1)}, u32[]{:S(2)}, u32[]{:S(2)}) collective-permute-start(f32[64,512]{1,0:T(8,128)S(1)} %get-tuple-element.60), channel_id=1, source_target_pairs={{0,1},{1,0},{2,3},{3,2},{4,5},{5,4},{6,7},{7,6},{8,9},{9,8},{10,11... | collective-permute-start | bytes 393224 | tf_op jit(solution)/shard_map/ppermute | solution.py:144
  65.5 12.2 %collective-permute-start.14 = (f32[64,512]{1,0:T(8,128)}, f32[64,512]{1,0:T(8,128)S(1)}, u32[]{:S(2)}, u32[]{:S(2)}) collective-permute-start(f32[64,512]{1,0:T(8,128)} %get-tuple-element.61), channel_id=1, source_target_pairs={{0,2},{1,3},{2,0},{3,1},{4,6},{5,7},{6,4},{7,5},{8,10},{9,11},{10,... | collective-permute-start | bytes 393224 | tf_op jit(solution)/shard_map/ppermute | solution.py:144
  65.5 13.2 %collective-permute-start.15 = (f32[64,512]{1,0:T(8,128)S(1)}, f32[64,512]{1,0:T(8,128)S(1)}, u32[]{:S(2)}, u32[]{:S(2)}) collective-permute-start(f32[64,512]{1,0:T(8,128)S(1)} %get-tuple-element.62), channel_id=1, source_target_pairs={{0,3},{1,2},{2,1},{3,0},{4,7},{5,6},{6,5},{7,4},{8,11},{9,10},{10,... | collective-permute-start | bytes 393224 | tf_op jit(solution)/shard_map/ppermute | solution.py:144
  66.9 11.9 %collective-permute-start.16 = (f32[64,512]{1,0:T(8,128)S(1)}, f32[64,512]{1,0:T(8,128)S(1)}, u32[]{:S(2)}, u32[]{:S(2)}) collective-permute-start(f32[64,512]{1,0:T(8,128)S(1)} %get-tuple-element.63), channel_id=1, source_target_pairs={{0,4},{1,5},{2,6},{3,7},{4,0},{5,1},{6,2},{7,3},{8,12},{9,13},{10,... | collective-permute-start | bytes 393224 | tf_op jit(solution)/shard_map/ppermute | solution.py:144
  69.5 16.1 %collective-permute-start.17 = (f32[64,512]{1,0:T(8,128)S(1)}, f32[64,512]{1,0:T(8,128)}, u32[]{:S(2)}, u32[]{:S(2)}) collective-permute-start(f32[64,512]{1,0:T(8,128)S(1)} %get-tuple-element.64), channel_id=1, source_target_pairs={{0,5},{1,4},{2,7},{3,6},{4,1},{5,0},{6,3},{7,2},{8,13},{9,12},{10,... | collective-permute-start | bytes 393224 | tf_op jit(solution)/shard_map/ppermute | solution.py:144
  72.5 13.2 %collective-permute-start.18 = (f32[64,512]{1,0:T(8,128)S(1)}, f32[64,512]{1,0:T(8,128)}, u32[]{:S(2)}, u32[]{:S(2)}) collective-permute-start(f32[64,512]{1,0:T(8,128)S(1)} %get-tuple-element.65), channel_id=1, source_target_pairs={{0,6},{1,7},{2,4},{3,5},{4,2},{5,3},{6,0},{7,1},{8,14},{9,15},{10,... | collective-permute-start | bytes 393224 | tf_op jit(solution)/shard_map/ppermute | solution.py:144
  74.4 0.7 copy-start.11
  88.3 2.9 %collective-permute-start.19 = (f32[384,768]{1,0:T(8,128)S(1)}, f32[384,768]{1,0:T(8,128)S(1)}, u32[]{:S(2)}, u32[]{:S(2)}) collective-permute-start(f32[384,768]{1,0:T(8,128)S(1)} %get-tuple-element.69), channel_id=1, source_target_pairs={{0,1},{1,0},{2,3},{3,2},{4,5},{5,4},{6,7},{7,6},{8,9},{9,8},{10,11... | collective-permute-start | bytes 3538952 | tf_op jit(solution)/shard_map/ppermute | solution.py:383
  91.9 10.8 %collective-permute-start.20 = (f32[4,24,768]{2,1,0:T(8,128)S(1)}, f32[4,24,768]{2,1,0:T(8,128)S(1)}, u32[]{:S(2)}, u32[]{:S(2)}) collective-permute-start(f32[4,24,768]{2,1,0:T(8,128)S(1)} %get-tuple-element.71), channel_id=1, source_target_pairs={{0,8},{8,16},{16,24},{24,0},{1,9},{9,17},{17,25},{25,1},{2,10},{10... | collective-permute-start | bytes 884744 | tf_op jit(solution)/shard_map/ppermute | solution.py:326
  93.7 14.7 %collective-permute-start.21 = (f32[4,24,768]{2,1,0:T(8,128)S(1)}, f32[4,24,768]{2,1,0:T(8,128)S(1)}, u32[]{:S(2)}, u32[]{:S(2)}) collective-permute-start(f32[4,24,768]{2,1,0:T(8,128)S(1)} %get-tuple-element.72), channel_id=1, source_target_pairs={{0,16},{8,24},{16,0},{24,8},{1,17},{9,25},{17,1},{25,9},{2,18},{10... | collective-permute-start | bytes 884744 | tf_op jit(solution)/shard_map/ppermute | solution.py:326
  94.7 13.7 %collective-permute-start.22 = (f32[4,24,768]{2,1,0:T(8,128)S(1)}, f32[4,24,768]{2,1,0:T(8,128)S(1)}, u32[]{:S(2)}, u32[]{:S(2)}) collective-permute-start(f32[4,24,768]{2,1,0:T(8,128)S(1)} %get-tuple-element.73), channel_id=1, source_target_pairs={{0,24},{8,0},{16,8},{24,16},{1,25},{9,1},{17,9},{25,17},{2,26},{10... | collective-permute-start | bytes 884744 | tf_op jit(solution)/shard_map/ppermute | solution.py:326
  108.5 6.0 %collective-permute-start.23 = (f32[24,768]{1,0:T(8,128)S(1)}, f32[24,768]{1,0:T(8,128)S(1)}, u32[]{:S(2)}, u32[]{:S(2)}) collective-permute-start(f32[24,768]{1,0:T(8,128)S(1)} %get-tuple-element.74), channel_id=1, source_target_pairs={{0,2},{1,3},{2,0},{3,1},{4,6},{5,7},{6,4},{7,5},{8,10},{9,11},{10,... | collective-permute-start | bytes 221192 | tf_op jit(solution)/shard_map/ppermute | solution.py:144
  112.0 6.8 %collective-permute-start.25 = (f32[24,768]{1,0:T(8,128)S(1)}, f32[24,768]{1,0:T(8,128)S(1)}, u32[]{:S(2)}, u32[]{:S(2)}) collective-permute-start(f32[24,768]{1,0:T(8,128)S(1)} %get-tuple-element.75), channel_id=1, source_target_pairs={{0,6},{1,7},{2,4},{3,5},{4,2},{5,3},{6,0},{7,1},{8,14},{9,15},{10,... | collective-permute-start | bytes 221192 | tf_op jit(solution)/shard_map/ppermute | solution.py:144
  114.0 7.1 %collective-permute-start.24 = (f32[24,768]{1,0:T(8,128)S(1)}, f32[24,768]{1,0:T(8,128)S(1)}, u32[]{:S(2)}, u32[]{:S(2)}) collective-permute-start(f32[24,768]{1,0:T(8,128)S(1)} %get-tuple-element.76), channel_id=1, source_target_pairs={{0,4},{1,5},{2,6},{3,7},{4,0},{5,1},{6,2},{7,3},{8,12},{9,13},{10,... | collective-permute-start | bytes 221192 | tf_op jit(solution)/shard_map/ppermute | solution.py:144
  121.1 4.4 %collective-permute-start.28 = (f32[24,768]{1,0:T(8,128)S(1)}, f32[24,768]{1,0:T(8,128)S(1)}, u32[]{:S(2)}, u32[]{:S(2)}) collective-permute-start(f32[24,768]{1,0:T(8,128)S(1)} %fusion.2.refs_0_), channel_id=1, source_target_pairs={{0,24},{8,0},{16,8},{24,16},{1,25},{9,1},{17,9},{25,17},{2,26},{10... | collective-permute-start | bytes 221192 | tf_op jit(solution)/shard_map/ppermute | solution.py:326
  122.4 5.1 %collective-permute-start.27 = (f32[24,768]{1,0:T(8,128)S(1)}, f32[24,768]{1,0:T(8,128)S(1)}, u32[]{:S(2)}, u32[]{:S(2)}) collective-permute-start(f32[24,768]{1,0:T(8,128)S(1)} %fusion.2.refs_0_), channel_id=1, source_target_pairs={{0,16},{8,24},{16,0},{24,8},{1,17},{9,25},{17,1},{25,9},{2,18},{10... | collective-permute-start | bytes 221192 | tf_op jit(solution)/shard_map/ppermute | solution.py:326
  123.5 5.3 %collective-permute-start.26 = (f32[24,768]{1,0:T(8,128)S(1)}, f32[24,768]{1,0:T(8,128)S(1)}, u32[]{:S(2)}, u32[]{:S(2)}) collective-permute-start(f32[24,768]{1,0:T(8,128)S(1)} %fusion.2.refs_0_), channel_id=1, source_target_pairs={{0,8},{8,16},{16,24},{24,0},{1,9},{9,17},{17,25},{25,1},{2,10},{10... | collective-permute-start | bytes 221192 | tf_op jit(solution)/shard_map/ppermute | solution.py:326

commit v8 on v6

v8 whole, which is shorter than its diff:
```python
import functools

import jax
import jax.numpy as jnp
import ml_dtypes
import numpy as np
from jax import lax
from jax.experimental import pallas as pl
from jax.experimental.pallas import tpu as pltpu
from jax.sharding import PartitionSpec as P

NZ = 64
LANES = 128
SUBLANES = 8
VMEM_LIMIT = 12 * 1024 * 1024
PARTS = 2


def plane_matrix():
    wide = 2 * LANES
    matrix = np.zeros((2 * wide, wide), np.float32)
    for y in range(wide // NZ):
        for z in range(NZ):
            column = y * NZ + z
            for step, weight in ((1, -16.0), (-1, -16.0), (2, 1.0), (-2, 1.0)):
                matrix[y * NZ + (z + step) % NZ, column] += weight
                row = y + step
                if row < 0:
                    row += 6
                elif row >= 4:
                    row += 2
                matrix[row * NZ + z, column] += weight
    return matrix.astype(ml_dtypes.bfloat16)


def filter_kernel(space, layers, tiles, chunk, pitch, offset, x_ref, m_ref, *refs):
    f0, f1, coef, mm, hi, lo = refs[-6:]
    rows = tiles * layers
    if len(refs) == 2 * space + 7:
        joined = refs[2 * space]
        for s in range(space):
            joined[s * rows : (s + 1) * rows, :] = refs[s][...]
        out_refs = refs[space : 2 * space]
    else:
        joined, out_refs = refs[0], refs[1 : 1 + space]
    planes = space * layers
    quads, height, wide = f0.shape
    here = lax.axis_index("space")

    def put(f, j, v):
        f[j] = v
        top = v.astype(jnp.bfloat16)
        hi[j] = top
        lo[j] = (v - top.astype(jnp.float32)).astype(jnp.bfloat16)

    for j in range(quads):
        columns = []
        for half in range(2):
            column = []
            for p in range(planes):
                s, l = divmod(p, layers)
                row = (2 * j + half) * layers + l
                slab = here + s
                slab = jnp.where(slab >= space, slab - space, slab)
                column.append(x_ref[pl.ds((slab * pitch + offset) * rows + row, chunk, stride=rows), :])
                w = joined[s * rows + row : s * rows + row + 1, :]
                coef[j, p * chunk : (p + 1) * chunk, half * LANES : (half + 1) * LANES] = jnp.broadcast_to(
                    0.5 * w - 1.125, (chunk, LANES)
                )
            columns.append(jnp.concatenate(column, axis=0))
        put(f0, j, jnp.concatenate(columns, axis=1))

    def beside(a):
        before = jnp.concatenate([a[quads - 1 :], a[: quads - 1]], axis=0)
        after = jnp.concatenate([a[1:], a[:1]], axis=0)
        return jnp.concatenate([before[:, :, LANES:], after[:, :, :LANES]], axis=2)

    def product():
        top, rest = hi[...], lo[...]
        left = jnp.concatenate([top, beside(top), rest, beside(rest)], axis=2).reshape(quads * height, 4 * wide)
        right = jnp.concatenate([m_ref[...], m_ref[...]], axis=0)
        got = lax.dot_general(left, right, (((1,), (0,)), ((), ())), preferred_element_type=jnp.float32)
        mm[...] = got.reshape(quads, height, wide)

    def stencil(f, j):
        v = f[j]

        def moved(k):
            k = k % planes * chunk
            return jnp.concatenate([v[k:], v[:k]], axis=0) if k else v

        return v, (mm[j] + (moved(2) + moved(-2))) - 16.0 * (moved(1) + moved(-1))

    product()
    for j in range(quads):
        v, s = stencil(f0, j)
        put(f1, j, (1.0 / 96.0) * s + 0.5 * (coef[j] * v))
    product()
    for j in range(quads):
        v, s = stencil(f1, j)
        put(f0, j, ((1.0 / 48.0) * s + coef[j] * v) - f0[j])
    product()
    for j in range(quads):
        v, s = stencil(f0, j)
        y = ((1.0 / 48.0) * s + coef[j] * v) - f1[j]
        for p in range(planes):
            for half in range(2):
                block = y[p * chunk : (p + 1) * chunk, half * LANES : (half + 1) * LANES]
                out_refs[p // layers][(2 * j + half) * layers + p % layers] = block


VMEM_SPEC = pl.BlockSpec(memory_space=pltpu.VMEM)


def run_filter(x, matrix, vs, offset, space, layers, tiles, chunk):
    rows = tiles * layers
    planes = space * layers
    pitch = x.shape[0] // (space * rows)
    shape = (tiles // 2, planes * chunk, 2 * LANES)
    out_shape = [jax.ShapeDtypeStruct((rows, chunk, LANES), jnp.float32)] * space
    if len(vs) > 1:
        out_shape.append(jax.ShapeDtypeStruct((space * rows, LANES), jnp.float32))
    return pl.pallas_call(
        functools.partial(filter_kernel, space, layers, tiles, chunk, pitch, offset),
        out_shape=out_shape,
        in_specs=[VMEM_SPEC] * (2 + len(vs)),
        out_specs=[VMEM_SPEC] * len(out_shape),
        scratch_shapes=[pltpu.VMEM(shape, jnp.float32)] * 4 + [pltpu.VMEM(shape, jnp.bfloat16)] * 2,
        compiler_params=pltpu.CompilerParams(vmem_limit_bytes=VMEM_LIMIT),
        cost_estimate=pl.CostEstimate(
            flops=50 * planes * tiles * SUBLANES * LANES,
            bytes_accessed=2 * planes * tiles * chunk * LANES * 4,
            transcendentals=0,
        ),
        name="filter",
    )(x, matrix, *vs)


def partner(index, size, k, forward=True):
    if size & (size - 1) == 0:
        return index ^ k
    moved = index + k if forward else index - k + size
    return jnp.where(moved >= size, moved - size, moved)


def exchange(x, axis, k, pitch=1):
    size = lax.axis_size(axis) // pitch
    power = size & (size - 1) == 0
    pairs = []
    for i in range(size):
        target = i ^ k if power else (i + k) % size
        pairs += [(i * pitch + low, target * pitch + low) for low in range(pitch)]
    return lax.ppermute(x, axis, pairs)


def pack_kernel(space, band, share, chunk, subs, *refs):
    blocks, outs = refs[: space * subs], refs[space * subs :]
    here, mine = lax.axis_index("space"), lax.axis_index("band")
    for k in range(space):
        group = here - k
        group = jnp.where(group < 0, group + space, group)
        for sub in range(subs):
            first = pl.multiple_of((group * subs + sub) * chunk, chunk)
            block = blocks[k * subs + sub]
            for step in range(band):
                out = outs[0].at[step] if len(outs) == 1 else outs[step]
                target = step if len(outs) == 1 else partner(mine, band, step)
                for q in range(share):
                    out[pl.ds(first, chunk), q * LANES : (q + 1) * LANES] = block[target * share + q]


def pack(blocks, space, band, share, chunk, subs, apart):
    shape = (space * subs * chunk, share * LANES)
    out_shape = [jax.ShapeDtypeStruct(shape, jnp.float32)] * band
    if not apart:
        out_shape = [jax.ShapeDtypeStruct((band,) + shape, jnp.float32)]
    return pl.pallas_call(
        functools.partial(pack_kernel, space, band, share, chunk, subs),
        out_shape=out_shape,
        in_specs=[VMEM_SPEC] * len(blocks),
        out_specs=[VMEM_SPEC] * len(out_shape),
        compiler_params=pltpu.CompilerParams(vmem_limit_bytes=VMEM_LIMIT),
        cost_estimate=pl.CostEstimate(
            flops=0, bytes_accessed=8 * band * space * subs * chunk * share * LANES, transcendentals=0
        ),
        name="pack",
    )(*blocks)


def unpack_kernel(space, rows, chunk, subs_of, *refs):
    blocks, out = refs[:-1], refs[-1]
    here = lax.axis_index("space")
    start = 0
    taken = 0
    for subs in subs_of:
        for k in range(space):
            group = here - k
            group = jnp.where(group < 0, group + space, group)
            for sub in range(subs):
                block = blocks[taken + k * subs + sub]
                first = (start + (group * subs + sub) * chunk) * rows
                for row in range(rows):
                    out[pl.ds(first + row, chunk, stride=rows), :] = block[row]
        taken += space * subs
        start += space * subs * chunk


def unpack(blocks, space, rows, chunk, subs_of):
    count = sum(subs_of) * space * chunk
    return pl.pallas_call(
        functools.partial(unpack_kernel, space, rows, chunk, subs_of),
        out_shape=jax.ShapeDtypeStruct((count * rows, LANES), jnp.float32),
        in_specs=[VMEM_SPEC] * len(blocks),
        out_specs=VMEM_SPEC,
        compiler_params=pltpu.CompilerParams(vmem_limit_bytes=VMEM_LIMIT),
        cost_estimate=pl.CostEstimate(flops=0, bytes_accessed=8 * count * rows * LANES, transcendentals=0),
        name="unpack",
    )(*blocks)


def half_product(band, count, which, hi, lo, first, out):
    def picked(x):
        return jnp.concatenate([x[2 * z + which] for z in range(band // 2)], axis=0)

    def dot(a, b):
        return lax.dot_general(a, b, (((1,), (1,)), ((), ())), preferred_element_type=jnp.float32)

    cells = hi.shape[-1]
    left_hi, left_lo = picked(hi), picked(lo)
    width = out.shape[1]
    bands = slice(first // count, (first + width) // count)
    right_hi = hi[bands].reshape(width, cells)
    right_lo = lo[bands].reshape(width, cells)
    for c in range(0, width, 256):
        columns = slice(c, min(c + 256, width))
        top, rest = right_hi[columns], right_lo[columns]
        out[:, columns] = dot(left_hi, top) + (dot(left_hi, rest) + dot(left_lo, top))


def gram_kernel(band, count, space, chunk, places, *refs):
    parts, (*outs, hi, lo, wide) = list(refs[: -3 - PARTS]), refs[-3 - PARTS :]
    own = count // space
    mine = lax.axis_index("band")
    for offset, subs, apart in places:
        size = subs * chunk
        taken = [parts.pop(0) for _ in range(band)] if apart else parts.pop(0)
        for step in range(band):
            source = partner(mine, band, step, forward=False) if apart else step
            for g in range(space):
                wide[source, g * own + offset : g * own + offset + size, :] = taken[step][g * size : (g + 1) * size, :]
    for b in range(band):
        top = wide[b].astype(jnp.bfloat16)
        hi[b] = top
        lo[b] = (wide[b] - top.astype(jnp.float32)).astype(jnp.bfloat16)
    for n, out in enumerate(outs):
        half_product(band, count, 1 - mine % 2, hi, lo, n * out.shape[1], out)


def own_gram_kernel(band, count, first, hi, lo, out):
    half_product(band, count, lax.axis_index("band") % 2, hi, lo, first, out)


def gram(parts, band, count, space, chunk, places):
    cells = parts[0].shape[-1]
    half = jax.ShapeDtypeStruct((band // 2 * count, band * count // PARTS), jnp.float32)
    narrow = jax.ShapeDtypeStruct((band, count, cells), jnp.bfloat16)
    return pl.pallas_call(
        functools.partial(gram_kernel, band, count, space, chunk, places),
        out_shape=[half] * PARTS + [narrow, narrow],
        in_specs=[VMEM_SPEC] * len(parts),
        out_specs=[VMEM_SPEC] * (PARTS + 2),
        scratch_shapes=[pltpu.VMEM((band, count, cells), jnp.float32)],
        compiler_params=pltpu.CompilerParams(vmem_limit_bytes=VMEM_LIMIT),
        cost_estimate=pl.CostEstimate(
            flops=3 * band * band * count * count * cells,
            bytes_accessed=4 * band * count * (cells + band * count // 2),
            transcendentals=0,
        ),
        name="gram",
    )(*parts)


def own_gram(hi, lo, first, width):
    band, count, cells = hi.shape
    return pl.pallas_call(
        functools.partial(own_gram_kernel, band, count, first),
        out_shape=jax.ShapeDtypeStruct((band // 2 * count, width), jnp.float32),
        in_specs=[VMEM_SPEC] * 2,
        out_specs=VMEM_SPEC,
        compiler_params=pltpu.CompilerParams(vmem_limit_bytes=VMEM_LIMIT),
        cost_estimate=pl.CostEstimate(
            flops=3 * band * count * width * cells, bytes_accessed=4 * band * count * cells, transcendentals=0
        ),
        name="own_gram",
    )(hi, lo)


def combine_kernel(space, a_ref, b_ref, *outs):
    for k, out in enumerate(outs):
        group = lax.axis_index("space") + k
        group = jnp.where(group >= space, group - space, group)
        for z in range(out.shape[0]):
            out[z] = a_ref[z, group] + b_ref[z, group]


def combine(a, b):
    pairs, space, own, columns = a.shape
    return pl.pallas_call(
        functools.partial(combine_kernel, space),
        out_shape=[jax.ShapeDtypeStruct((pairs, own, columns), jnp.float32)] * space,
        in_specs=[VMEM_SPEC] * 2,
        out_specs=[VMEM_SPEC] * space,
        compiler_params=pltpu.CompilerParams(vmem_limit_bytes=VMEM_LIMIT),
        cost_estimate=pl.CostEstimate(flops=a.size, bytes_accessed=12 * a.size, transcendentals=0),
        name="combine",
    )(a, b)


def place_kernel(space, *refs):
    parts, out = refs[:-1], refs[-1]
    width = parts[0].shape[1]
    for n, part in enumerate(parts):
        h, k = divmod(n, space)
        group = lax.axis_index("space") - k
        group = jnp.where(group < 0, group + space, group)
        out[group, :, h * width : (h + 1) * width] = part[...]


def place(parts, space):
    own, width = parts[0].shape
    columns = width * len(parts) // space
    return pl.pallas_call(
        functools.partial(place_kernel, space),
        out_shape=jax.ShapeDtypeStruct((space, own, columns), jnp.float32),
        in_specs=[VMEM_SPEC] * len(parts),
        out_specs=VMEM_SPEC,
        compiler_params=pltpu.CompilerParams(vmem_limit_bytes=VMEM_LIMIT),
        cost_estimate=pl.CostEstimate(flops=0, bytes_accessed=8 * space * own * columns, transcendentals=0),
        name="place",
    )(*parts)


def rotate(x, axis, step):
    size = lax.axis_size(axis)
    return lax.ppermute(x, axis, [(i, (i + step) % size) for i in range(size)])


def shards(orbitals, potential):
    space = lax.axis_size("space")
    band = lax.axis_size("band")
    count, layers, plane = orbitals.shape
    tiles = plane // LANES
    rows = tiles * layers
    share = rows // band
    own = count // space
    chunk = max(c for c in range(1, SUBLANES + 1) if own % c == 0)
    chunks = own // chunk


    def as_rows(x):
        n = x.shape[0]
        return x.reshape(n, layers, tiles, LANES).transpose(0, 2, 1, 3).reshape(n * rows, LANES)

    matrix = jnp.asarray(plane_matrix())
    own_v = as_rows(potential[None])
    vs = [own_v] + [rotate(own_v, "space", space - k) for k in range(1, space)]
    arrived = as_rows(lax.all_to_all(orbitals, "space", split_axis=0, concat_axis=0, tiled=True))

    def filtered(c, x):
        outs = run_filter(x, matrix, vs, c * chunk, space, layers, tiles, chunk)
        vs[:] = [outs[-1]] if len(vs) > 1 else vs
        return [outs[0]] + [rotate(outs[k], "space", k) for k in range(1, space)]

    made = [filtered(c, arrived) for c in range(min(chunks, 2))]
    made[0], made[-1][0] = lax.optimization_barrier((made[0], made[-1][0]))
    head = pack(made[0], space, band, share, chunk, 1, False)[0]
    head, arrived = lax.optimization_barrier((head, arrived))
    parts = [lax.all_to_all(head, "band", split_axis=0, concat_axis=0, tiled=True)]
    places = [(0, 1, False)]
    made += [filtered(c, arrived) for c in range(2, chunks)]
    if chunks > 1:
        late = [made[c][k] for k in range(space) for c in range(1, chunks)]
        packed = pack(late, space, band, share, chunk, chunks - 1, True)
        got = {0: packed[0]}
        for k in reversed(range(1, band)):
            got[k] = exchange(packed[k], "band", k)
        parts += [got[k] for k in range(band)]
        places.append((chunk, chunks - 1, True))
    blocks = [made[c][k] for k in range(space) for c in range(chunks)]

    result = unpack(blocks, space, rows, chunk, [chunks])
    parts[-1], result = lax.optimization_barrier((parts[-1], result))
    result = result.reshape(count, tiles, layers, LANES).transpose(0, 2, 1, 3).reshape(count, layers, plane)

    pairs = band // 2
    pair = lax.axis_index("band") // 2
    scale = 1.0 / (layers * space * plane)

    *others, hi, lo = gram(parts, band, count, space, chunk, places)
    others = [lax.ppermute(x, "band", [(i, i ^ 1) for i in range(band)]) for x in others]
    width = band * count // PARTS
    split = (pairs, space, own, width)
    placed = []
    for h in range(PARTS):
        sums = combine(own_gram(hi, lo, h * width, width).reshape(split), others[h].reshape(split))
        sums, hi = lax.optimization_barrier((sums, hi))
        mine = sums[0]
        for k in range(1, space):
            mine = mine + rotate(sums[k], "space", k)
        final = lax.dynamic_index_in_dim(mine, pair, 0, keepdims=False)
        for k in range(1, pairs):
            sent = lax.dynamic_index_in_dim(mine, partner(pair, pairs, k), 0, keepdims=False)
            final = final + exchange(sent, "band", k, 2)
        final = final * scale
        placed += [final] + [rotate(final, "space", k) for k in range(1, space)]
    return result, place(placed, space).reshape(count, band * count)


def solution(mesh):
    return jax.shard_map(
        shards,
        mesh=mesh,
        in_specs=(P("band", "space", None), P("space", None)),
        out_specs=(P("band", "space", None), P("band", None)),
        check_vma=False,
    )
```

time: 138 us -> 121 us (0.88)
  waiting for transfers between devices: 55.4 us -> 42.1 us
  starting transfers between devices: 50.2 us -> 61.6 us
  local copies, waits for them, and re-layouts: 12.1 us -> 3.16 us
  Pallas kernels: 18.5 us -> 12.4 us
    ppermute x18 -> x24, waiting for transfers between devices: 40.8 us -> 29.3 us  [rotate(): return lax.ppermute(x, axis, [(i, (i + step) % size) for i in range(size)])]
    unnamed x48 -> x12, local copies, waits for them, and re-layouts: 12.1 us -> 3.12 us
    ppermute x18 -> x24, starting transfers between devices: 23.6 us -> 31.9 us  [rotate(): return lax.ppermute(x, axis, [(i, (i + step) % size) for i in range(size)])]
    ppermute x10 -> x13, starting transfers between devices: 14.9 us -> 18.8 us  [exchange(): return lax.ppermute(x, axis, pairs)]
    pallas_call x2 -> x1, Pallas kernels: 4.27 us -> 1.64 us  [gram(): pl.pallas_call(functools.partial(gram_kernel, band, count, space, chunk,...]
    ppermute x10 -> x13, waiting for transfers between devices: 14.2 us -> 12 us  [exchange(): return lax.ppermute(x, axis, pairs)]
    pallas_call x2, Pallas kernels: 2.78 us -> 0.98 us  [pack(): pl.pallas_call(functools.partial(pack_kernel, space, band, share, chunk,...]
    pallas_call x3, Pallas kernels: 6.89 us -> 5.26 us  [run_filter(): pl.pallas_call(functools.partial(filter_kernel, space, layers, tiles, chu...]
  transfers between devices with their start and end apart: 31 -> 41, of which waited for: 15 -> 16; matrix products, arithmetic and copies ran while one was open for 0% -> 1% of each run, Pallas kernels for 8% -> 6%
where the time goes in v8:
time: 121 us
  starting transfers between devices  61.6 us (51%)
  waiting for transfers between devices  42.1 us (35%)
  Pallas kernels  12.4 us (10%)
  local copies, waits for them, and re-layouts  3.16 us (3%)
    ppermute x24, starting transfers between devices, rotate(): return lax.ppermute(x, axis, [(i, (i + step) % size) for i in range(size)])  31.9 us
    ppermute x24, waiting for transfers between devices, rotate(): return lax.ppermute(x, axis, [(i, (i + step) % size) for i in range(size)])  29.3 us
    ppermute x13, starting transfers between devices, exchange(): return lax.ppermute(x, axis, pairs)  18.8 us
    ppermute x13, waiting for transfers between devices, exchange(): return lax.ppermute(x, axis, pairs)  12 us
    all_to_all x1, starting transfers between devices, shards(): lax.all_to_all(orbitals, 'space', split_axis=0, concat_axis=0, tiled=True)  5.31 us
    pallas_call x3, Pallas kernels, run_filter(): pl.pallas_call(functools.partial(filter_kernel, space, layers, tiles, chu...  5.26 us
    all_to_all x1, starting transfers between devices, shards(): lax.all_to_all(head, 'band', split_axis=0, concat_axis=0, tiled=True)  4.99 us
    unnamed x12, local copies, waits for them, and re-layouts  3.12 us
  transfers between devices with their start and end apart: 41, of which 16 were waited for; matrix products, arithmetic and copies ran while one was open for 1% of the time, Pallas kernels for 6%

profile of v8, /device:TPU:0, one launch (start us, length us, event | category | flops | bytes accessed | tf_op | source)
XLA Modules:
  0.0 121.1 jit_solution(7766378283208866294)
XLA Ops:
  0.7 5.3 %all-to-all-start = ((f32[96,2,2048]{2,1,0:T(2,128)}), f32[96,2,2048]{2,1,0:T(2,128)S(1)}, u32[]{:S(2)}, u32[]{:S(2)}) async-start(f32[96,2,2048]{2,1,0:T(2,128)} %param.3), calls=%async_computation | async-start | bytes 3145728 | tf_op jit(solution)/shard_map/all_to_all | solution.py:367
  6.0 2.9 %collective-permute-start = (f32[32,128]{1,0:T(8,128)S(1)}, f32[32,128]{1,0:T(8,128)S(1)}, u32[]{:S(2)}, u32[]{:S(2)}) collective-permute-start(f32[32,128]{1,0:T(8,128)S(1)} %bitcast.55), channel_id=1, source_target_pairs={{0,24},{8,0},{16,8},{24,16},{1,25},{9,1},{17,9},{25,17},{2,26},{10... | collective-permute-start | bytes 49160 | tf_op jit(solution)/shard_map/ppermute | solution.py:345
  8.9 0.6 collective-permute-start.1
  9.4 0.6 collective-permute-start.2
  10.0 15.7 %collective-permute-done.refs_1_ = f32[32,128]{1,0:T(8,128)S(1)} collective-permute-done((f32[32,128]{1,0:T(8,128)S(1)}, f32[32,128]{1,0:T(8,128)S(1)}, u32[]{:S(2)}, u32[]{:S(2)}) %collective-permute-start) | collective-permute-done | bytes 16416 | tf_op jit(solution)/shard_map/ppermute | solution.py:345
  25.7 1.1 collective-permute-done.2.refs_3_
  26.8 1.8 %filter.3 = (f32[32,8,128]{2,1,0:T(8,128)S(1)}, f32[32,8,128]{2,1,0:T(8,128)S(1)}, f32[32,8,128]{2,1,0:T(8,128)S(1)}, f32[32,8,128]{2,1,0:T(8,128)S(1)}, f32[128,128]{1,0:T(8,128)S(1)}) custom-call(f32[3072,128]{1,0:T(8,128)S(1)} %bitcast.48, bf16[512,256]{1,0:T(8,128)(2,1)S(1)} %copy-done, f32[32,128]{1,0:T(8,128)S(1)} %bitcast.58, ...), custom_call_target="tpu_custom_call" | custom-call | flops 6553600 | bytes 1048576 | tf_op jit(solution)/shard_map/filter/pallas_call | solution.py:123
  28.6 0.6 collective-permute-start.3
  29.2 0.6 collective-permute-start.4
  29.8 2.4 %collective-permute-start.5 = (f32[32,8,128]{2,1,0:T(8,128)S(1)}, f32[32,8,128]{2,1,0:T(8,128)S(1)}, u32[]{:S(2)}, u32[]{:S(2)}) collective-permute-start(f32[32,8,128]{2,1,0:T(8,128)S(1)} %get-tuple-element.56), channel_id=1, source_target_pairs={{0,24},{8,0},{16,8},{24,16},{1,25},{9,1},{17,9},{25,17},{2,26},{10... | collective-permute-start | bytes 393224 | tf_op jit(solution)/shard_map/ppermute | solution.py:345
  32.1 1.8 %filter.4 = (f32[32,8,128]{2,1,0:T(8,128)S(1)}, f32[32,8,128]{2,1,0:T(8,128)S(1)}, f32[32,8,128]{2,1,0:T(8,128)S(1)}, f32[32,8,128]{2,1,0:T(8,128)S(1)}) custom-call(f32[3072,128]{1,0:T(8,128)S(1)} %bitcast.49, bf16[512,256]{1,0:T(8,128)(2,1)S(1)} %copy-done, f32[128,128]{1,0:T(8,128)S(1)} %get-tuple-element.57.refs_0_), custom_call_target="tpu_custom_call" | custom-call | flops 6553600 | bytes 1048576 | tf_op jit(solution)/shard_map/filter/pallas_call | solution.py:123
  33.9 1.0 collective-permute-done.3.refs_1_.refs_3_
  34.9 0.7 collective-permute-done.4.refs_2_.refs_6_
  35.5 0.9 pack.2
  36.4 5.0 %all-to-all-start.1 = ((f32[8,32,512]{2,1,0:T(8,128)}), f32[8,32,512]{2,1,0:T(8,128)S(1)}, u32[]{:S(2)}, u32[]{:S(2)}) async-start(f32[8,32,512]{2,1,0:T(8,128)} %pack.2), calls=%async_computation.1 | async-start | bytes 1048576 | tf_op jit(solution)/shard_map/all_to_all | solution.py:378
  41.4 2.5 %collective-permute-start.6 = (f32[32,8,128]{2,1,0:T(8,128)S(1)}, f32[32,8,128]{2,1,0:T(8,128)S(1)}, u32[]{:S(2)}, u32[]{:S(2)}) collective-permute-start(f32[32,8,128]{2,1,0:T(8,128)S(1)} %get-tuple-element.66), channel_id=1, source_target_pairs={{0,8},{8,16},{16,24},{24,0},{1,9},{9,17},{17,25},{25,1},{2,10},{10... | collective-permute-start | bytes 393224 | tf_op jit(solution)/shard_map/ppermute | solution.py:345
  43.9 1.0 collective-permute-start.8
  44.9 0.7 collective-permute-start.10
  45.7 1.8 %filter.5 = (f32[32,8,128]{2,1,0:T(8,128)S(1)}, f32[32,8,128]{2,1,0:T(8,128)S(1)}, f32[32,8,128]{2,1,0:T(8,128)S(1)}, f32[32,8,128]{2,1,0:T(8,128)S(1)}) custom-call(f32[3072,128]{1,0:T(8,128)S(1)} %bitcast.50, bf16[512,256]{1,0:T(8,128)(2,1)S(1)} %copy-done, f32[128,128]{1,0:T(8,128)S(1)} %get-tuple-element.57.refs_0_), custom_call_target="tpu_custom_call" | custom-call | flops 6553600 | bytes 1048576 | tf_op jit(solution)/shard_map/filter/pallas_call | solution.py:123
  47.4 1.3 %collective-permute-start.7 = (f32[32,8,128]{2,1,0:T(8,128)S(1)}, f32[32,8,128]{2,1,0:T(8,128)S(1)}, u32[]{:S(2)}, u32[]{:S(2)}) collective-permute-start(f32[32,8,128]{2,1,0:T(8,128)S(1)} %get-tuple-element.67), channel_id=1, source_target_pairs={{0,8},{8,16},{16,24},{24,0},{1,9},{9,17},{17,25},{25,1},{2,10},{10... | collective-permute-start | bytes 393224 | tf_op jit(solution)/shard_map/ppermute | solution.py:345
  48.8 1.0 collective-permute-start.9
  49.8 1.4 %collective-permute-start.11 = (f32[32,8,128]{2,1,0:T(8,128)S(1)}, f32[32,8,128]{2,1,0:T(8,128)S(1)}, u32[]{:S(2)}, u32[]{:S(2)}) collective-permute-start(f32[32,8,128]{2,1,0:T(8,128)S(1)} %get-tuple-element.71), channel_id=1, source_target_pairs={{0,24},{8,0},{16,8},{24,16},{1,25},{9,1},{17,9},{25,17},{2,26},{10... | collective-permute-start | bytes 393224 | tf_op jit(solution)/shard_map/ppermute | solution.py:345
  51.2 0.7 collective-permute-done.8.refs_4_.refs_7_
  51.9 3.0 %collective-permute-done.7.refs_3_.refs_5_ = f32[32,8,128]{2,1,0:T(8,128)S(1)} collective-permute-done((f32[32,8,128]{2,1,0:T(8,128)S(1)}, f32[32,8,128]{2,1,0:T(8,128)S(1)}, u32[]{:S(2)}, u32[]{:S(2)}) %collective-permute-start.7) | collective-permute-done | bytes 131104 | tf_op jit(solution)/shard_map/ppermute | solution.py:345
  54.9 2.1 %collective-permute-done.9.refs_5_.refs_8_ = f32[32,8,128]{2,1,0:T(8,128)S(1)} collective-permute-done((f32[32,8,128]{2,1,0:T(8,128)S(1)}, f32[32,8,128]{2,1,0:T(8,128)S(1)}, u32[]{:S(2)}, u32[]{:S(2)}) %collective-permute-start.9) | collective-permute-done | bytes 131104 | tf_op jit(solution)/shard_map/ppermute | solution.py:345
  57.1 3.1 %collective-permute-start.12 = (f32[64,512]{1,0:T(8,128)S(1)}, f32[64,512]{1,0:T(8,128)S(1)}, u32[]{:S(2)}, u32[]{:S(2)}) collective-permute-start(f32[64,512]{1,0:T(8,128)S(1)} %get-tuple-element.72), channel_id=1, source_target_pairs={{0,7},{1,6},{2,5},{3,4},{4,3},{5,2},{6,1},{7,0},{8,15},{9,14},{10,... | collective-permute-start | bytes 393224 | tf_op jit(solution)/shard_map/ppermute | solution.py:153
  60.2 0.6 collective-permute-start.13
  60.7 1.4 %collective-permute-start.15 = (f32[64,512]{1,0:T(8,128)S(1)}, f32[64,512]{1,0:T(8,128)S(1)}, u32[]{:S(2)}, u32[]{:S(2)}) collective-permute-start(f32[64,512]{1,0:T(8,128)S(1)} %get-tuple-element.78), channel_id=1, source_target_pairs={{0,3},{1,2},{2,1},{3,0},{4,7},{5,6},{6,5},{7,4},{8,11},{9,10},{10,... | collective-permute-start | bytes 393224 | tf_op jit(solution)/shard_map/ppermute | solution.py:153
  62.1 2.6 %collective-permute-done.12.refs_8_ = f32[64,512]{1,0:T(8,128)S(1)} collective-permute-done((f32[64,512]{1,0:T(8,128)S(1)}, f32[64,512]{1,0:T(8,128)S(1)}, u32[]{:S(2)}, u32[]{:S(2)}) %collective-permute-start.12) | collective-permute-done | bytes 131104 | tf_op jit(solution)/shard_map/ppermute | solution.py:153
  64.7 3.4 %collective-permute-start.17 = (f32[64,512]{1,0:T(8,128)S(1)}, f32[64,512]{1,0:T(8,128)S(1)}, u32[]{:S(2)}, u32[]{:S(2)}) collective-permute-start(f32[64,512]{1,0:T(8,128)S(1)} %get-tuple-element.80), channel_id=1, source_target_pairs={{0,5},{1,4},{2,7},{3,6},{4,1},{5,0},{6,3},{7,2},{8,13},{9,12},{10,... | collective-permute-start | bytes 393224 | tf_op jit(solution)/shard_map/ppermute | solution.py:153
  68.2 1.5 %collective-permute-start.18 = (f32[64,512]{1,0:T(8,128)S(1)}, f32[64,512]{1,0:T(8,128)S(1)}, u32[]{:S(2)}, u32[]{:S(2)}) collective-permute-start(f32[64,512]{1,0:T(8,128)S(1)} %get-tuple-element.81), channel_id=1, source_target_pairs={{0,6},{1,7},{2,4},{3,5},{4,2},{5,3},{6,0},{7,1},{8,14},{9,15},{10,... | collective-permute-start | bytes 393224 | tf_op jit(solution)/shard_map/ppermute | solution.py:153
  69.6 2.1 %unpack.1 = f32[3072,128]{1,0:T(8,128)} custom-call(f32[32,8,128]{2,1,0:T(8,128)S(1)} %get-tuple-element.60.refs_0_, f32[32,8,128]{2,1,0:T(8,128)S(1)} %get-tuple-element.59.refs_0_.refs_1_, f32[32,8,128]{2,1,0:T(8,128)S(1)} %get-tuple-element.65.refs_1_.refs_2_, f32[32,8,128]{2,1,0:T(8,128)S(1)} %collective-permute-done.3.refs_1_.refs_3_, ...), custom_call_target="tpu_custom_call" | custom-call | bytes 3145728 | tf_op jit(solution)/shard_map/unpack/pallas_call | solution.py:210
  71.7 2.3 %collective-permute-done.15.refs_4_ = f32[64,512]{1,0:T(8,128)S(1)} collective-permute-done((f32[64,512]{1,0:T(8,128)S(1)}, f32[64,512]{1,0:T(8,128)S(1)}, u32[]{:S(2)}, u32[]{:S(2)}) %collective-permute-start.15) | collective-permute-done | bytes 131104 | tf_op jit(solution)/shard_map/ppermute | solution.py:153
  74.0 6.8 %collective-permute-done.17.refs_6_ = f32[64,512]{1,0:T(8,128)S(1)} collective-permute-done((f32[64,512]{1,0:T(8,128)S(1)}, f32[64,512]{1,0:T(8,128)S(1)}, u32[]{:S(2)}, u32[]{:S(2)}) %collective-permute-start.17) | collective-permute-done | bytes 131104 | tf_op jit(solution)/shard_map/ppermute | solution.py:153
  80.8 0.7 copy-done.2
  81.5 0.6 copy-done.4
  82.1 0.9 copy-done.3
  83.0 0.9 copy-done.5
  83.9 1.6 %gram.1 = (f32[384,384]{1,0:T(8,128)S(1)}, f32[384,384]{1,0:T(8,128)S(1)}, bf16[8,96,512]{2,1,0:T(8,128)(2,1)S(1)}, bf16[8,96,512]{2,1,0:T(8,128)(2,1)S(1)}) custom-call(f32[8,32,512]{2,1,0:T(8,128)S(1)} %all-to-all-done.1.refs_0_, f32[64,512]{1,0:T(8,128)S(1)} %get-tuple-element.75.refs_1_, f32[64,512]{1,0:T(8,128)S(1)} %collective-permute-done.13.refs_2_, ...), custom_call_target="tpu_custom_call" | custom-call | flops 905969664 | bytes 2752512 | tf_op jit(solution)/shard_map/gram/pallas_call | solution.py:267
  85.8 0.4 collective-permute-start.29
  86.2 0.8 own_gram.2
  87.0 0.7 collective-permute-done.19
  87.7 2.2 %collective-permute-start.22 = (f32[4,24,384]{2,1,0:T(8,128)S(1)}, f32[4,24,384]{2,1,0:T(8,128)S(1)}, u32[]{:S(2)}, u32[]{:S(2)}) collective-permute-start(f32[4,24,384]{2,1,0:T(8,128)S(1)} %get-tuple-element.93), channel_id=1, source_target_pairs={{0,24},{8,0},{16,8},{24,16},{1,25},{9,1},{17,9},{25,17},{2,26},{10... | collective-permute-start | bytes 442376 | tf_op jit(solution)/shard_map/ppermute | solution.py:345
  90.0 1.0 collective-permute-start.21
  91.0 0.8 own_gram.3
  91.9 3.0 %collective-permute-start.32 = (f32[4,24,384]{2,1,0:T(8,128)S(1)}, f32[4,24,384]{2,1,0:T(8,128)S(1)}, u32[]{:S(2)}, u32[]{:S(2)}) collective-permute-start(f32[4,24,384]{2,1,0:T(8,128)S(1)} %get-tuple-element.103), channel_id=1, source_target_pairs={{0,24},{8,0},{16,8},{24,16},{1,25},{9,1},{17,9},{25,17},{2,26},{10... | collective-permute-start | bytes 442376 | tf_op jit(solution)/shard_map/ppermute | solution.py:345
  94.8 1.0 collective-permute-start.31
  95.9 1.3 %collective-permute-start.30 = (f32[4,24,384]{2,1,0:T(8,128)S(1)}, f32[4,24,384]{2,1,0:T(8,128)S(1)}, u32[]{:S(2)}, u32[]{:S(2)}) collective-permute-start(f32[4,24,384]{2,1,0:T(8,128)S(1)} %get-tuple-element.101), channel_id=1, source_target_pairs={{0,8},{8,16},{16,24},{24,0},{1,9},{9,17},{17,25},{25,1},{2,10},{10... | collective-permute-start | bytes 442376 | tf_op jit(solution)/shard_map/ppermute | solution.py:345
  97.1 3.5 %collective-permute-done.21 = f32[4,24,384]{2,1,0:T(8,128)} collective-permute-done((f32[4,24,384]{2,1,0:T(8,128)S(1)}, f32[4,24,384]{2,1,0:T(8,128)}, u32[]{:S(2)}, u32[]{:S(2)}) %collective-permute-start.21) | collective-permute-done | bytes 147488 | tf_op jit(solution)/shard_map/ppermute | solution.py:345
  100.6 1.0 add_add_fusion.1
  101.7 2.6 %collective-permute-start.25 = (f32[24,384]{1,0:T(8,128)S(1)}, f32[24,384]{1,0:T(8,128)S(1)}, u32[]{:S(2)}, u32[]{:S(2)}) collective-permute-start(f32[24,384]{1,0:T(8,128)S(1)} %get-tuple-element.108), channel_id=1, source_target_pairs={{0,6},{1,7},{2,4},{3,5},{4,2},{5,3},{6,0},{7,1},{8,14},{9,15},{10,... | collective-permute-start | bytes 110600 | tf_op jit(solution)/shard_map/ppermute | solution.py:153
  104.2 1.9 %collective-permute-start.24 = (f32[24,384]{1,0:T(8,128)S(1)}, f32[24,384]{1,0:T(8,128)S(1)}, u32[]{:S(2)}, u32[]{:S(2)}) collective-permute-start(f32[24,384]{1,0:T(8,128)S(1)} %get-tuple-element.109), channel_id=1, source_target_pairs={{0,4},{1,5},{2,6},{3,7},{4,0},{5,1},{6,2},{7,3},{8,12},{9,13},{10,... | collective-permute-start | bytes 110600 | tf_op jit(solution)/shard_map/ppermute | solution.py:153
  106.2 2.6 %collective-permute-start.35 = (f32[24,384]{1,0:T(8,128)S(1)}, f32[24,384]{1,0:T(8,128)S(1)}, u32[]{:S(2)}, u32[]{:S(2)}) collective-permute-start(f32[24,384]{1,0:T(8,128)S(1)} %get-tuple-element.105), channel_id=1, source_target_pairs={{0,6},{1,7},{2,4},{3,5},{4,2},{5,3},{6,0},{7,1},{8,14},{9,15},{10,... | collective-permute-start | bytes 110600 | tf_op jit(solution)/shard_map/ppermute | solution.py:153
  108.8 1.0 collective-permute-start.34
  109.7 0.9 collective-permute-start.33
  110.7 0.2 collective-permute-start.26
  111.0 1.0 collective-permute-start.27
  112.0 0.2 collective-permute-done.35
  112.2 2.5 %collective-permute-start.28 = (f32[24,384]{1,0:T(8,128)S(1)}, f32[24,384]{1,0:T(8,128)S(1)}, u32[]{:S(2)}, u32[]{:S(2)}) collective-permute-start(f32[24,384]{1,0:T(8,128)S(1)} %fusion.5.refs_0_), channel_id=1, source_target_pairs={{0,24},{8,0},{16,8},{24,16},{1,25},{9,1},{17,9},{25,17},{2,26},{10... | collective-permute-start | bytes 110600 | tf_op jit(solution)/shard_map/ppermute | solution.py:345
  114.8 1.1 collective-permute-start.37
  115.9 2.8 %collective-permute-start.38 = (f32[24,384]{1,0:T(8,128)S(1)}, f32[24,384]{1,0:T(8,128)S(1)}, u32[]{:S(2)}, u32[]{:S(2)}) collective-permute-start(f32[24,384]{1,0:T(8,128)S(1)} %fusion.2.refs_4_), channel_id=1, source_target_pairs={{0,24},{8,0},{16,8},{24,16},{1,25},{9,1},{17,9},{25,17},{2,26},{10... | collective-permute-start | bytes 110600 | tf_op jit(solution)/shard_map/ppermute | solution.py:345
  118.8 0.9 collective-permute-done.36.refs_5_
  119.7 0.7 collective-permute-done.38.refs_7_
  120.4 0.7 place.1
  (48 shorter events, 0.8 us)
Async XLA Ops:
  0.6 26.2 %copy-start = (bf16[512,256]{1,0:T(8,128)(2,1)S(1)}, bf16[512,256]{1,0:T(8,128)(2,1)}, u32[]{:S(2)}) copy-start(bf16[512,256]{1,0:T(8,128)(2,1)} %constant.45.clone.m_ref) | copy-start | bytes 786436
  0.6 5.3 %copy-start.1 = (f32[2,2048]{1,0:T(2,128)S(1)}, f32[2,2048]{1,0:T(2,128)}, u32[]{:S(2)}) copy-start(f32[2,2048]{1,0:T(2,128)} %param.4) | copy-start | bytes 49156
  0.7 26.2 %all-to-all-start = ((f32[96,2,2048]{2,1,0:T(2,128)}), f32[96,2,2048]{2,1,0:T(2,128)S(1)}, u32[]{:S(2)}, u32[]{:S(2)}) async-start(f32[96,2,2048]{2,1,0:T(2,128)} %param.3), calls=%async_computation | async-start | bytes 3145728 | tf_op jit(solution)/shard_map/all_to_all | solution.py:367
  6.0 19.8 %collective-permute-start = (f32[32,128]{1,0:T(8,128)S(1)}, f32[32,128]{1,0:T(8,128)S(1)}, u32[]{:S(2)}, u32[]{:S(2)}) collective-permute-start(f32[32,128]{1,0:T(8,128)S(1)} %bitcast.55), channel_id=1, source_target_pairs={{0,24},{8,0},{16,8},{24,16},{1,25},{9,1},{17,9},{25,17},{2,26},{10... | collective-permute-start | bytes 49160 | tf_op jit(solution)/shard_map/ppermute | solution.py:345
  8.9 16.9 %collective-permute-start.1 = (f32[32,128]{1,0:T(8,128)S(1)}, f32[32,128]{1,0:T(8,128)S(1)}, u32[]{:S(2)}, u32[]{:S(2)}) collective-permute-start(f32[32,128]{1,0:T(8,128)S(1)} %bitcast.56), channel_id=1, source_target_pairs={{0,16},{8,24},{16,0},{24,8},{1,17},{9,25},{17,1},{25,9},{2,18},{10... | collective-permute-start | bytes 49160 | tf_op jit(solution)/shard_map/ppermute | solution.py:345
  9.4 17.4 %collective-permute-start.2 = (f32[32,128]{1,0:T(8,128)S(1)}, f32[32,128]{1,0:T(8,128)S(1)}, u32[]{:S(2)}, u32[]{:S(2)}) collective-permute-start(f32[32,128]{1,0:T(8,128)S(1)} %bitcast.57), channel_id=1, source_target_pairs={{0,8},{8,16},{16,24},{24,0},{1,9},{9,17},{17,25},{25,1},{2,10},{10... | collective-permute-start | bytes 49160 | tf_op jit(solution)/shard_map/ppermute | solution.py:345
  28.6 6.3 %collective-permute-start.3 = (f32[32,8,128]{2,1,0:T(8,128)S(1)}, f32[32,8,128]{2,1,0:T(8,128)S(1)}, u32[]{:S(2)}, u32[]{:S(2)}) collective-permute-start(f32[32,8,128]{2,1,0:T(8,128)S(1)} %get-tuple-element.54), channel_id=1, source_target_pairs={{0,8},{8,16},{16,24},{24,0},{1,9},{9,17},{17,25},{25,1},{2,10},{10... | collective-permute-start | bytes 393224 | tf_op jit(solution)/shard_map/ppermute | solution.py:345
  29.2 6.4 %collective-permute-start.4 = (f32[32,8,128]{2,1,0:T(8,128)S(1)}, f32[32,8,128]{2,1,0:T(8,128)S(1)}, u32[]{:S(2)}, u32[]{:S(2)}) collective-permute-start(f32[32,8,128]{2,1,0:T(8,128)S(1)} %get-tuple-element.55), channel_id=1, source_target_pairs={{0,16},{8,24},{16,0},{24,8},{1,17},{9,25},{17,1},{25,9},{2,18},{10... | collective-permute-start | bytes 393224 | tf_op jit(solution)/shard_map/ppermute | solution.py:345
  29.8 5.8 %collective-permute-start.5 = (f32[32,8,128]{2,1,0:T(8,128)S(1)}, f32[32,8,128]{2,1,0:T(8,128)S(1)}, u32[]{:S(2)}, u32[]{:S(2)}) collective-permute-start(f32[32,8,128]{2,1,0:T(8,128)S(1)} %get-tuple-element.56), channel_id=1, source_target_pairs={{0,24},{8,0},{16,8},{24,16},{1,25},{9,1},{17,9},{25,17},{2,26},{10... | collective-permute-start | bytes 393224 | tf_op jit(solution)/shard_map/ppermute | solution.py:345
  36.4 45.7 %all-to-all-start.1 = ((f32[8,32,512]{2,1,0:T(8,128)}), f32[8,32,512]{2,1,0:T(8,128)S(1)}, u32[]{:S(2)}, u32[]{:S(2)}) async-start(f32[8,32,512]{2,1,0:T(8,128)} %pack.2), calls=%async_computation.1 | async-start | bytes 1048576 | tf_op jit(solution)/shard_map/all_to_all | solution.py:378
  41.4 8.4 %collective-permute-start.6 = (f32[32,8,128]{2,1,0:T(8,128)S(1)}, f32[32,8,128]{2,1,0:T(8,128)S(1)}, u32[]{:S(2)}, u32[]{:S(2)}) collective-permute-start(f32[32,8,128]{2,1,0:T(8,128)S(1)} %get-tuple-element.66), channel_id=1, source_target_pairs={{0,8},{8,16},{16,24},{24,0},{1,9},{9,17},{17,25},{25,1},{2,10},{10... | collective-permute-start | bytes 393224 | tf_op jit(solution)/shard_map/ppermute | solution.py:345
  43.9 8.0 %collective-permute-start.8 = (f32[32,8,128]{2,1,0:T(8,128)S(1)}, f32[32,8,128]{2,1,0:T(8,128)S(1)}, u32[]{:S(2)}, u32[]{:S(2)}) collective-permute-start(f32[32,8,128]{2,1,0:T(8,128)S(1)} %get-tuple-element.68), channel_id=1, source_target_pairs={{0,16},{8,24},{16,0},{24,8},{1,17},{9,25},{17,1},{25,9},{2,18},{10... | collective-permute-start | bytes 393224 | tf_op jit(solution)/shard_map/ppermute | solution.py:345
  44.9 7.0 %collective-permute-start.10 = (f32[32,8,128]{2,1,0:T(8,128)S(1)}, f32[32,8,128]{2,1,0:T(8,128)S(1)}, u32[]{:S(2)}, u32[]{:S(2)}) collective-permute-start(f32[32,8,128]{2,1,0:T(8,128)S(1)} %get-tuple-element.70), channel_id=1, source_target_pairs={{0,24},{8,0},{16,8},{24,16},{1,25},{9,1},{17,9},{25,17},{2,26},{10... | collective-permute-start | bytes 393224 | tf_op jit(solution)/shard_map/ppermute | solution.py:345
  47.4 7.4 %collective-permute-start.7 = (f32[32,8,128]{2,1,0:T(8,128)S(1)}, f32[32,8,128]{2,1,0:T(8,128)S(1)}, u32[]{:S(2)}, u32[]{:S(2)}) collective-permute-start(f32[32,8,128]{2,1,0:T(8,128)S(1)} %get-tuple-element.67), channel_id=1, source_target_pairs={{0,8},{8,16},{16,24},{24,0},{1,9},{9,17},{17,25},{25,1},{2,10},{10... | collective-permute-start | bytes 393224 | tf_op jit(solution)/shard_map/ppermute | solution.py:345
  48.8 8.2 %collective-permute-start.9 = (f32[32,8,128]{2,1,0:T(8,128)S(1)}, f32[32,8,128]{2,1,0:T(8,128)S(1)}, u32[]{:S(2)}, u32[]{:S(2)}) collective-permute-start(f32[32,8,128]{2,1,0:T(8,128)S(1)} %get-tuple-element.69), channel_id=1, source_target_pairs={{0,16},{8,24},{16,0},{24,8},{1,17},{9,25},{17,1},{25,9},{2,18},{10... | collective-permute-start | bytes 393224 | tf_op jit(solution)/shard_map/ppermute | solution.py:345
  49.8 7.2 %collective-permute-start.11 = (f32[32,8,128]{2,1,0:T(8,128)S(1)}, f32[32,8,128]{2,1,0:T(8,128)S(1)}, u32[]{:S(2)}, u32[]{:S(2)}) collective-permute-start(f32[32,8,128]{2,1,0:T(8,128)S(1)} %get-tuple-element.71), channel_id=1, source_target_pairs={{0,24},{8,0},{16,8},{24,16},{1,25},{9,1},{17,9},{25,17},{2,26},{10... | collective-permute-start | bytes 393224 | tf_op jit(solution)/shard_map/ppermute | solution.py:345
  57.1 7.6 %collective-permute-start.12 = (f32[64,512]{1,0:T(8,128)S(1)}, f32[64,512]{1,0:T(8,128)S(1)}, u32[]{:S(2)}, u32[]{:S(2)}) collective-permute-start(f32[64,512]{1,0:T(8,128)S(1)} %get-tuple-element.72), channel_id=1, source_target_pairs={{0,7},{1,6},{2,5},{3,4},{4,3},{5,2},{6,1},{7,0},{8,15},{9,14},{10,... | collective-permute-start | bytes 393224 | tf_op jit(solution)/shard_map/ppermute | solution.py:153
  60.2 8.0 %collective-permute-start.13 = (f32[64,512]{1,0:T(8,128)S(1)}, f32[64,512]{1,0:T(8,128)S(1)}, u32[]{:S(2)}, u32[]{:S(2)}) collective-permute-start(f32[64,512]{1,0:T(8,128)S(1)} %get-tuple-element.76), channel_id=1, source_target_pairs={{0,1},{1,0},{2,3},{3,2},{4,5},{5,4},{6,7},{7,6},{8,9},{9,8},{10,11... | collective-permute-start | bytes 393224 | tf_op jit(solution)/shard_map/ppermute | solution.py:153
  60.7 11.0 %collective-permute-start.14 = (f32[64,512]{1,0:T(8,128)S(1)}, f32[64,512]{1,0:T(8,128)S(1)}, u32[]{:S(2)}, u32[]{:S(2)}) collective-permute-start(f32[64,512]{1,0:T(8,128)S(1)} %get-tuple-element.77), channel_id=1, source_target_pairs={{0,2},{1,3},{2,0},{3,1},{4,6},{5,7},{6,4},{7,5},{8,10},{9,11},{10,... | collective-permute-start | bytes 393224 | tf_op jit(solution)/shard_map/ppermute | solution.py:153
  60.7 13.2 %collective-permute-start.15 = (f32[64,512]{1,0:T(8,128)S(1)}, f32[64,512]{1,0:T(8,128)S(1)}, u32[]{:S(2)}, u32[]{:S(2)}) collective-permute-start(f32[64,512]{1,0:T(8,128)S(1)} %get-tuple-element.78), channel_id=1, source_target_pairs={{0,3},{1,2},{2,1},{3,0},{4,7},{5,6},{6,5},{7,4},{8,11},{9,10},{10,... | collective-permute-start | bytes 393224 | tf_op jit(solution)/shard_map/ppermute | solution.py:153
  62.1 11.9 %collective-permute-start.16 = (f32[64,512]{1,0:T(8,128)S(1)}, f32[64,512]{1,0:T(8,128)S(1)}, u32[]{:S(2)}, u32[]{:S(2)}) collective-permute-start(f32[64,512]{1,0:T(8,128)S(1)} %get-tuple-element.79), channel_id=1, source_target_pairs={{0,4},{1,5},{2,6},{3,7},{4,0},{5,1},{6,2},{7,3},{8,12},{9,13},{10,... | collective-permute-start | bytes 393224 | tf_op jit(solution)/shard_map/ppermute | solution.py:153
  64.7 16.1 %collective-permute-start.17 = (f32[64,512]{1,0:T(8,128)S(1)}, f32[64,512]{1,0:T(8,128)S(1)}, u32[]{:S(2)}, u32[]{:S(2)}) collective-permute-start(f32[64,512]{1,0:T(8,128)S(1)} %get-tuple-element.80), channel_id=1, source_target_pairs={{0,5},{1,4},{2,7},{3,6},{4,1},{5,0},{6,3},{7,2},{8,13},{9,12},{10,... | collective-permute-start | bytes 393224 | tf_op jit(solution)/shard_map/ppermute | solution.py:153
  68.2 13.3 %collective-permute-start.18 = (f32[64,512]{1,0:T(8,128)S(1)}, f32[64,512]{1,0:T(8,128)S(1)}, u32[]{:S(2)}, u32[]{:S(2)}) collective-permute-start(f32[64,512]{1,0:T(8,128)S(1)} %get-tuple-element.81), channel_id=1, source_target_pairs={{0,6},{1,7},{2,4},{3,5},{4,2},{5,3},{6,0},{7,1},{8,14},{9,15},{10,... | collective-permute-start | bytes 393224 | tf_op jit(solution)/shard_map/ppermute | solution.py:153
  80.8 0.7 copy-start.2
  81.5 0.6 copy-start.4
  82.1 0.9 copy-start.3
  83.0 0.9 copy-start.5
  85.6 2.1 %collective-permute-start.19 = (f32[384,384]{1,0:T(8,128)S(1)}, f32[384,384]{1,0:T(8,128)S(1)}, u32[]{:S(2)}, u32[]{:S(2)}) collective-permute-start(f32[384,384]{1,0:T(8,128)S(1)} %get-tuple-element.85), channel_id=1, source_target_pairs={{0,1},{1,0},{2,3},{3,2},{4,5},{5,4},{6,7},{7,6},{8,9},{9,8},{10,11... | collective-permute-start | bytes 1769480 | tf_op jit(solution)/shard_map/ppermute | solution.py:400
  85.8 6.0 %collective-permute-start.29 = (f32[384,384]{1,0:T(8,128)S(1)}, f32[384,384]{1,0:T(8,128)S(1)}, u32[]{:S(2)}, u32[]{:S(2)}) collective-permute-start(f32[384,384]{1,0:T(8,128)S(1)} %get-tuple-element.95), channel_id=1, source_target_pairs={{0,1},{1,0},{2,3},{3,2},{4,5},{5,4},{6,7},{7,6},{8,9},{9,8},{10,11... | collective-permute-start | bytes 1769480 | tf_op jit(solution)/shard_map/ppermute | solution.py:400
  87.7 8.1 %collective-permute-start.22 = (f32[4,24,384]{2,1,0:T(8,128)S(1)}, f32[4,24,384]{2,1,0:T(8,128)S(1)}, u32[]{:S(2)}, u32[]{:S(2)}) collective-permute-start(f32[4,24,384]{2,1,0:T(8,128)S(1)} %get-tuple-element.93), channel_id=1, source_target_pairs={{0,24},{8,0},{16,8},{24,16},{1,25},{9,1},{17,9},{25,17},{2,26},{10... | collective-permute-start | bytes 442376 | tf_op jit(solution)/shard_map/ppermute | solution.py:345
  90.0 10.7 %collective-permute-start.21 = (f32[4,24,384]{2,1,0:T(8,128)S(1)}, f32[4,24,384]{2,1,0:T(8,128)}, u32[]{:S(2)}, u32[]{:S(2)}) collective-permute-start(f32[4,24,384]{2,1,0:T(8,128)S(1)} %get-tuple-element.92), channel_id=1, source_target_pairs={{0,16},{8,24},{16,0},{24,8},{1,17},{9,25},{17,1},{25,9},{2,18},{10... | collective-permute-start | bytes 442376 | tf_op jit(solution)/shard_map/ppermute | solution.py:345
  91.0 9.7 %collective-permute-start.20 = (f32[4,24,384]{2,1,0:T(8,128)S(1)}, f32[4,24,384]{2,1,0:T(8,128)}, u32[]{:S(2)}, u32[]{:S(2)}) collective-permute-start(f32[4,24,384]{2,1,0:T(8,128)S(1)} %get-tuple-element.91), channel_id=1, source_target_pairs={{0,8},{8,16},{16,24},{24,0},{1,9},{9,17},{17,25},{25,1},{2,10},{10... | collective-permute-start | bytes 442376 | tf_op jit(solution)/shard_map/ppermute | solution.py:345
  91.9 14.2 %collective-permute-start.32 = (f32[4,24,384]{2,1,0:T(8,128)S(1)}, f32[4,24,384]{2,1,0:T(8,128)S(1)}, u32[]{:S(2)}, u32[]{:S(2)}) collective-permute-start(f32[4,24,384]{2,1,0:T(8,128)S(1)} %get-tuple-element.103), channel_id=1, source_target_pairs={{0,24},{8,0},{16,8},{24,16},{1,25},{9,1},{17,9},{25,17},{2,26},{10... | collective-permute-start | bytes 442376 | tf_op jit(solution)/shard_map/ppermute | solution.py:345
  94.8 11.3 %collective-permute-start.31 = (f32[4,24,384]{2,1,0:T(8,128)S(1)}, f32[4,24,384]{2,1,0:T(8,128)S(1)}, u32[]{:S(2)}, u32[]{:S(2)}) collective-permute-start(f32[4,24,384]{2,1,0:T(8,128)S(1)} %get-tuple-element.102), channel_id=1, source_target_pairs={{0,16},{8,24},{16,0},{24,8},{1,17},{9,25},{17,1},{25,9},{2,18},{10... | collective-permute-start | bytes 442376 | tf_op jit(solution)/shard_map/ppermute | solution.py:345
  95.9 10.3 %collective-permute-start.30 = (f32[4,24,384]{2,1,0:T(8,128)S(1)}, f32[4,24,384]{2,1,0:T(8,128)S(1)}, u32[]{:S(2)}, u32[]{:S(2)}) collective-permute-start(f32[4,24,384]{2,1,0:T(8,128)S(1)} %get-tuple-element.101), channel_id=1, source_target_pairs={{0,8},{8,16},{16,24},{24,0},{1,9},{9,17},{17,25},{25,1},{2,10},{10... | collective-permute-start | bytes 442376 | tf_op jit(solution)/shard_map/ppermute | solution.py:345
  101.7 8.1 %collective-permute-start.25 = (f32[24,384]{1,0:T(8,128)S(1)}, f32[24,384]{1,0:T(8,128)S(1)}, u32[]{:S(2)}, u32[]{:S(2)}) collective-permute-start(f32[24,384]{1,0:T(8,128)S(1)} %get-tuple-element.108), channel_id=1, source_target_pairs={{0,6},{1,7},{2,4},{3,5},{4,2},{5,3},{6,0},{7,1},{8,14},{9,15},{10,... | collective-permute-start | bytes 110600 | tf_op jit(solution)/shard_map/ppermute | solution.py:153
  104.2 6.4 %collective-permute-start.24 = (f32[24,384]{1,0:T(8,128)S(1)}, f32[24,384]{1,0:T(8,128)S(1)}, u32[]{:S(2)}, u32[]{:S(2)}) collective-permute-start(f32[24,384]{1,0:T(8,128)S(1)} %get-tuple-element.109), channel_id=1, source_target_pairs={{0,4},{1,5},{2,6},{3,7},{4,0},{5,1},{6,2},{7,3},{8,12},{9,13},{10,... | collective-permute-start | bytes 110600 | tf_op jit(solution)/shard_map/ppermute | solution.py:153
  106.1 4.6 %collective-permute-start.23 = (f32[24,384]{1,0:T(8,128)S(1)}, f32[24,384]{1,0:T(8,128)S(1)}, u32[]{:S(2)}, u32[]{:S(2)}) collective-permute-start(f32[24,384]{1,0:T(8,128)S(1)} %get-tuple-element.107), channel_id=1, source_target_pairs={{0,2},{1,3},{2,0},{3,1},{4,6},{5,7},{6,4},{7,5},{8,10},{9,11},{10,... | collective-permute-start | bytes 110600 | tf_op jit(solution)/shard_map/ppermute | solution.py:153
  106.2 6.0 %collective-permute-start.35 = (f32[24,384]{1,0:T(8,128)S(1)}, f32[24,384]{1,0:T(8,128)S(1)}, u32[]{:S(2)}, u32[]{:S(2)}) collective-permute-start(f32[24,384]{1,0:T(8,128)S(1)} %get-tuple-element.105), channel_id=1, source_target_pairs={{0,6},{1,7},{2,4},{3,5},{4,2},{5,3},{6,0},{7,1},{8,14},{9,15},{10,... | collective-permute-start | bytes 110600 | tf_op jit(solution)/shard_map/ppermute | solution.py:153
  108.8 6.0 %collective-permute-start.34 = (f32[24,384]{1,0:T(8,128)S(1)}, f32[24,384]{1,0:T(8,128)S(1)}, u32[]{:S(2)}, u32[]{:S(2)}) collective-permute-start(f32[24,384]{1,0:T(8,128)S(1)} %get-tuple-element.106), channel_id=1, source_target_pairs={{0,4},{1,5},{2,6},{3,7},{4,0},{5,1},{6,2},{7,3},{8,12},{9,13},{10,... | collective-permute-start | bytes 110600 | tf_op jit(solution)/shard_map/ppermute | solution.py:153
  109.7 5.0 %collective-permute-start.33 = (f32[24,384]{1,0:T(8,128)S(1)}, f32[24,384]{1,0:T(8,128)S(1)}, u32[]{:S(2)}, u32[]{:S(2)}) collective-permute-start(f32[24,384]{1,0:T(8,128)S(1)} %get-tuple-element.104), channel_id=1, source_target_pairs={{0,2},{1,3},{2,0},{3,1},{4,6},{5,7},{6,4},{7,5},{8,10},{9,11},{10,... | collective-permute-start | bytes 110600 | tf_op jit(solution)/shard_map/ppermute | solution.py:153
  110.7 5.2 %collective-permute-start.26 = (f32[24,384]{1,0:T(8,128)S(1)}, f32[24,384]{1,0:T(8,128)S(1)}, u32[]{:S(2)}, u32[]{:S(2)}) collective-permute-start(f32[24,384]{1,0:T(8,128)S(1)} %fusion.5.refs_0_), channel_id=1, source_target_pairs={{0,8},{8,16},{16,24},{24,0},{1,9},{9,17},{17,25},{25,1},{2,10},{10... | collective-permute-start | bytes 110600 | tf_op jit(solution)/shard_map/ppermute | solution.py:345
  111.0 7.8 %collective-permute-start.27 = (f32[24,384]{1,0:T(8,128)S(1)}, f32[24,384]{1,0:T(8,128)S(1)}, u32[]{:S(2)}, u32[]{:S(2)}) collective-permute-start(f32[24,384]{1,0:T(8,128)S(1)} %fusion.5.refs_0_), channel_id=1, source_target_pairs={{0,16},{8,24},{16,0},{24,8},{1,17},{9,25},{17,1},{25,9},{2,18},{10... | collective-permute-start | bytes 110600 | tf_op jit(solution)/shard_map/ppermute | solution.py:345
  112.2 6.5 %collective-permute-start.28 = (f32[24,384]{1,0:T(8,128)S(1)}, f32[24,384]{1,0:T(8,128)S(1)}, u32[]{:S(2)}, u32[]{:S(2)}) collective-permute-start(f32[24,384]{1,0:T(8,128)S(1)} %fusion.5.refs_0_), channel_id=1, source_target_pairs={{0,24},{8,0},{16,8},{24,16},{1,25},{9,1},{17,9},{25,17},{2,26},{10... | collective-permute-start | bytes 110600 | tf_op jit(solution)/shard_map/ppermute | solution.py:345
  114.8 4.9 %collective-permute-start.36 = (f32[24,384]{1,0:T(8,128)S(1)}, f32[24,384]{1,0:T(8,128)S(1)}, u32[]{:S(2)}, u32[]{:S(2)}) collective-permute-start(f32[24,384]{1,0:T(8,128)S(1)} %fusion.2.refs_4_), channel_id=1, source_target_pairs={{0,8},{8,16},{16,24},{24,0},{1,9},{9,17},{17,25},{25,1},{2,10},{10... | collective-permute-start | bytes 110600 | tf_op jit(solution)/shard_map/ppermute | solution.py:345
  114.8 4.8 %collective-permute-start.37 = (f32[24,384]{1,0:T(8,128)S(1)}, f32[24,384]{1,0:T(8,128)S(1)}, u32[]{:S(2)}, u32[]{:S(2)}) collective-permute-start(f32[24,384]{1,0:T(8,128)S(1)} %fusion.2.refs_4_), channel_id=1, source_target_pairs={{0,16},{8,24},{16,0},{24,8},{1,17},{9,25},{17,1},{25,9},{2,18},{10... | collective-permute-start | bytes 110600 | tf_op jit(solution)/shard_map/ppermute | solution.py:345
  115.9 4.5 %collective-permute-start.38 = (f32[24,384]{1,0:T(8,128)S(1)}, f32[24,384]{1,0:T(8,128)S(1)}, u32[]{:S(2)}, u32[]{:S(2)}) collective-permute-start(f32[24,384]{1,0:T(8,128)S(1)} %fusion.2.refs_4_), channel_id=1, source_target_pairs={{0,24},{8,0},{16,8},{24,16},{1,25},{9,1},{17,9},{25,17},{2,26},{10... | collective-permute-start | bytes 110600 | tf_op jit(solution)/shard_map/ppermute | solution.py:345

commit v9 on v8

--- a/solution.py
+++ b/solution.py
@@ -238,16 +238,25 @@
 
 
 def gram_kernel(band, count, space, chunk, places, *refs):
-    parts, (*outs, hi, lo, wide) = list(refs[: -3 - PARTS]), refs[-3 - PARTS :]
+    parts, (*outs, hi, lo, wide, done) = list(refs[: -4 - PARTS]), refs[-4 - PARTS :]
     own = count // space
     mine = lax.axis_index("band")
-    for offset, subs, apart in places:
+    copies = []
+    for offset, subs, apart in reversed(places):
         size = subs * chunk
-        taken = [parts.pop(0) for _ in range(band)] if apart else parts.pop(0)
+        taken = [parts.pop() for _ in range(band)][::-1] if apart else parts.pop()
         for step in range(band):
             source = partner(mine, band, step, forward=False) if apart else step
             for g in range(space):
-                wide[source, g * own + offset : g * own + offset + size, :] = taken[step][g * size : (g + 1) * size, :]
+                rows = slice(g * own + offset, g * own + offset + size)
+                if apart:
+                    from_ref = taken[step].at[g * size : (g + 1) * size, :]
+                    copies.append(pltpu.make_async_copy(from_ref, wide.at[source, rows, :], done.at[len(copies)]))
+                    copies[-1].start()
+                else:
+                    wide[step, rows, :] = taken[step, g * size : (g + 1) * size, :]
+    for copy in copies:
+        copy.wait()
     for b in range(band):
         top = wide[b].astype(jnp.bfloat16)
         hi[b] = top
@@ -267,9 +276,12 @@
     return pl.pallas_call(
         functools.partial(gram_kernel, band, count, space, chunk, places),
         out_shape=[half] * PARTS + [narrow, narrow],
-        in_specs=[VMEM_SPEC] * len(parts),
+        in_specs=[VMEM_SPEC] + [pl.BlockSpec(memory_space=pl.ANY)] * (len(parts) - 1),
         out_specs=[VMEM_SPEC] * (PARTS + 2),
-        scratch_shapes=[pltpu.VMEM((band, count, cells), jnp.float32)],
+        scratch_shapes=[
+            pltpu.VMEM((band, count, cells), jnp.float32),
+            pltpu.SemaphoreType.DMA((max(1, (len(parts) - 1) * space),)),
+        ],
         compiler_params=pltpu.CompilerParams(vmem_limit_bytes=VMEM_LIMIT),
         cost_estimate=pl.CostEstimate(
             flops=3 * band * band * count * count * cells,
@@ -371,13 +383,14 @@
         vs[:] = [outs[-1]] if len(vs) > 1 else vs
         return [outs[0]] + [rotate(outs[k], "space", k) for k in range(1, space)]
 
-    made = [filtered(c, arrived) for c in range(min(chunks, 2))]
-    made[0], made[-1][0] = lax.optimization_barrier((made[0], made[-1][0]))
+    made = [filtered(c, arrived) for c in range(chunks)]
+    if chunks > 1:
+        made[0], firsts = lax.optimization_barrier((made[0], [m[0] for m in made[1:]]))
+        for m, first in zip(made[1:], firsts):
+            m[0] = first
     head = pack(made[0], space, band, share, chunk, 1, False)[0]
-    head, arrived = lax.optimization_barrier((head, arrived))
     parts = [lax.all_to_all(head, "band", split_axis=0, concat_axis=0, tiled=True)]
     places = [(0, 1, False)]
-    made += [filtered(c, arrived) for c in range(2, chunks)]
     if chunks > 1:
         late = [made[c][k] for k in range(space) for c in range(1, chunks)]
         packed = pack(late, space, band, share, chunk, chunks - 1, True)

time: 121 us -> 125 us (1.033)
  local copies, waits for them, and re-layouts: 3.16 us -> 5.36 us
  Pallas kernels: 12.4 us -> 14 us
    unnamed x12 -> x20, local copies, waits for them, and re-layouts: 3.12 us -> 5.32 us
    pallas_call x1, Pallas kernels: 1.64 us -> 3.26 us  [gram(): pl.pallas_call(functools.partial(gram_kernel, band, count, space, chunk,...]
  transfers between devices with their start and end apart: 41 -> 41, of which waited for: 16 -> 14; matrix products, arithmetic and copies ran while one was open for 1% -> 1% of each run, Pallas kernels for 6% -> 6%
where the time goes in v9:
time: 125 us
  starting transfers between devices  62.7 us (50%)
  waiting for transfers between devices  41.1 us (33%)
  Pallas kernels  14 us (11%)
  local copies, waits for them, and re-layouts  5.36 us (4%)
    ppermute x24, starting transfers between devices, rotate(): return lax.ppermute(x, axis, [(i, (i + step) % size) for i in range(size)])  33 us
    ppermute x24, waiting for transfers between devices, rotate(): return lax.ppermute(x, axis, [(i, (i + step) % size) for i in range(size)])  29.3 us
    ppermute x13, starting transfers between devices, exchange(): return lax.ppermute(x, axis, pairs)  18.9 us
    ppermute x13, waiting for transfers between devices, exchange(): return lax.ppermute(x, axis, pairs)  11.1 us
    unnamed x20, local copies, waits for them, and re-layouts  5.32 us
    all_to_all x1, starting transfers between devices, shards(): lax.all_to_all(orbitals, 'space', split_axis=0, concat_axis=0, tiled=True)  5.31 us
    pallas_call x3, Pallas kernels, run_filter(): pl.pallas_call(functools.partial(filter_kernel, space, layers, tiles, chu...  5.26 us
    all_to_all x1, starting transfers between devices, shards(): lax.all_to_all(head, 'band', split_axis=0, concat_axis=0, tiled=True)  4.98 us
  transfers between devices with their start and end apart: 41, of which 14 were waited for; matrix products, arithmetic and copies ran while one was open for 1% of the time, Pallas kernels for 6%

profile of v9, /device:TPU:0, one launch (start us, length us, event | category | flops | bytes accessed | tf_op | source)
XLA Modules:
  0.0 125.1 jit_solution(14504888608536506899)
XLA Ops:
  0.7 5.3 %all-to-all-start = ((f32[96,2,2048]{2,1,0:T(2,128)}), f32[96,2,2048]{2,1,0:T(2,128)S(1)}, u32[]{:S(2)}, u32[]{:S(2)}) async-start(f32[96,2,2048]{2,1,0:T(2,128)} %param.3), calls=%async_computation | async-start | bytes 3145728 | tf_op jit(solution)/shard_map/all_to_all | solution.py:379
  6.0 2.9 %collective-permute-start = (f32[32,128]{1,0:T(8,128)S(1)}, f32[32,128]{1,0:T(8,128)S(1)}, u32[]{:S(2)}, u32[]{:S(2)}) collective-permute-start(f32[32,128]{1,0:T(8,128)S(1)} %bitcast.55), channel_id=1, source_target_pairs={{0,24},{8,0},{16,8},{24,16},{1,25},{9,1},{17,9},{25,17},{2,26},{10... | collective-permute-start | bytes 49160 | tf_op jit(solution)/shard_map/ppermute | solution.py:357
  8.9 0.6 collective-permute-start.1
  9.4 0.6 collective-permute-start.2
  10.0 15.7 %collective-permute-done.refs_1_ = f32[32,128]{1,0:T(8,128)S(1)} collective-permute-done((f32[32,128]{1,0:T(8,128)S(1)}, f32[32,128]{1,0:T(8,128)S(1)}, u32[]{:S(2)}, u32[]{:S(2)}) %collective-permute-start) | collective-permute-done | bytes 16416 | tf_op jit(solution)/shard_map/ppermute | solution.py:357
  25.7 1.1 collective-permute-done.2.refs_3_
  26.8 1.8 %filter.3 = (f32[32,8,128]{2,1,0:T(8,128)S(1)}, f32[32,8,128]{2,1,0:T(8,128)S(1)}, f32[32,8,128]{2,1,0:T(8,128)S(1)}, f32[32,8,128]{2,1,0:T(8,128)S(1)}, f32[128,128]{1,0:T(8,128)S(1)}) custom-call(f32[3072,128]{1,0:T(8,128)S(1)} %bitcast.48, bf16[512,256]{1,0:T(8,128)(2,1)S(1)} %copy-done, f32[32,128]{1,0:T(8,128)S(1)} %bitcast.58, ...), custom_call_target="tpu_custom_call" | custom-call | flops 6553600 | bytes 1048576 | tf_op jit(solution)/shard_map/filter/pallas_call | solution.py:123
  28.6 0.6 collective-permute-start.3
  29.2 0.6 collective-permute-start.4
  29.8 2.4 %collective-permute-start.5 = (f32[32,8,128]{2,1,0:T(8,128)S(1)}, f32[32,8,128]{2,1,0:T(8,128)S(1)}, u32[]{:S(2)}, u32[]{:S(2)}) collective-permute-start(f32[32,8,128]{2,1,0:T(8,128)S(1)} %get-tuple-element.55), channel_id=1, source_target_pairs={{0,24},{8,0},{16,8},{24,16},{1,25},{9,1},{17,9},{25,17},{2,26},{10... | collective-permute-start | bytes 393224 | tf_op jit(solution)/shard_map/ppermute | solution.py:357
  32.1 1.8 %filter.4 = (f32[32,8,128]{2,1,0:T(8,128)S(1)}, f32[32,8,128]{2,1,0:T(8,128)S(1)}, f32[32,8,128]{2,1,0:T(8,128)S(1)}, f32[32,8,128]{2,1,0:T(8,128)S(1)}) custom-call(f32[3072,128]{1,0:T(8,128)S(1)} %bitcast.49, bf16[512,256]{1,0:T(8,128)(2,1)S(1)} %copy-done, f32[128,128]{1,0:T(8,128)S(1)} %get-tuple-element.56.refs_0_), custom_call_target="tpu_custom_call" | custom-call | flops 6553600 | bytes 1048576 | tf_op jit(solution)/shard_map/filter/pallas_call | solution.py:123
  33.9 0.6 copy-done.8
  34.5 1.8 %filter.5 = (f32[32,8,128]{2,1,0:T(8,128)S(1)}, f32[32,8,128]{2,1,0:T(8,128)S(1)}, f32[32,8,128]{2,1,0:T(8,128)S(1)}, f32[32,8,128]{2,1,0:T(8,128)S(1)}) custom-call(f32[3072,128]{1,0:T(8,128)S(1)} %bitcast.50, bf16[512,256]{1,0:T(8,128)(2,1)S(1)} %copy-done, f32[128,128]{1,0:T(8,128)S(1)} %get-tuple-element.56.refs_0_), custom_call_target="tpu_custom_call" | custom-call | flops 6553600 | bytes 1048576 | tf_op jit(solution)/shard_map/filter/pallas_call | solution.py:123
  36.3 0.9 pack.3
  37.2 5.0 %all-to-all-start.1 = ((f32[8,32,512]{2,1,0:T(8,128)}), f32[8,32,512]{2,1,0:T(8,128)S(1)}, u32[]{:S(2)}, u32[]{:S(2)}) async-start(f32[8,32,512]{2,1,0:T(8,128)} %pack.3), calls=%async_computation.1 | async-start | bytes 1048576 | tf_op jit(solution)/shard_map/all_to_all | solution.py:392
  42.2 1.8 %collective-permute-start.6 = (f32[32,8,128]{2,1,0:T(8,128)S(1)}, f32[32,8,128]{2,1,0:T(8,128)S(1)}, u32[]{:S(2)}, u32[]{:S(2)}) collective-permute-start(f32[32,8,128]{2,1,0:T(8,128)S(1)} %copy-done.9), channel_id=1, source_target_pairs={{0,8},{8,16},{16,24},{24,0},{1,9},{9,17},{17,25},{25,1},{2,10},{10... | collective-permute-start | bytes 393224 | tf_op jit(solution)/shard_map/ppermute | solution.py:357
  44.0 1.2 collective-permute-start.7
  45.2 0.6 collective-permute-start.8
  45.7 1.5 %collective-permute-start.9 = (f32[32,8,128]{2,1,0:T(8,128)S(1)}, f32[32,8,128]{2,1,0:T(8,128)S(1)}, u32[]{:S(2)}, u32[]{:S(2)}) collective-permute-start(f32[32,8,128]{2,1,0:T(8,128)S(1)} %get-tuple-element.64), channel_id=1, source_target_pairs={{0,16},{8,24},{16,0},{24,8},{1,17},{9,25},{17,1},{25,9},{2,18},{10... | collective-permute-start | bytes 393224 | tf_op jit(solution)/shard_map/ppermute | solution.py:357
  47.2 1.7 %collective-permute-start.10 = (f32[32,8,128]{2,1,0:T(8,128)S(1)}, f32[32,8,128]{2,1,0:T(8,128)S(1)}, u32[]{:S(2)}, u32[]{:S(2)}) collective-permute-start(f32[32,8,128]{2,1,0:T(8,128)S(1)} %get-tuple-element.65), channel_id=1, source_target_pairs={{0,24},{8,0},{16,8},{24,16},{1,25},{9,1},{17,9},{25,17},{2,26},{10... | collective-permute-start | bytes 393224 | tf_op jit(solution)/shard_map/ppermute | solution.py:357
  49.0 0.6 collective-permute-done.6.refs_2_.refs_4_
  49.5 1.2 collective-permute-start.11
  50.7 1.6 %collective-permute-done.7.refs_3_.refs_5_ = f32[32,8,128]{2,1,0:T(8,128)S(1)} collective-permute-done((f32[32,8,128]{2,1,0:T(8,128)S(1)}, f32[32,8,128]{2,1,0:T(8,128)S(1)}, u32[]{:S(2)}, u32[]{:S(2)}) %collective-permute-start.7) | collective-permute-done | bytes 131104 | tf_op jit(solution)/shard_map/ppermute | solution.py:357
  52.3 2.4 %collective-permute-done.8.refs_4_.refs_7_ = f32[32,8,128]{2,1,0:T(8,128)S(1)} collective-permute-done((f32[32,8,128]{2,1,0:T(8,128)S(1)}, f32[32,8,128]{2,1,0:T(8,128)S(1)}, u32[]{:S(2)}, u32[]{:S(2)}) %collective-permute-start.8) | collective-permute-done | bytes 131104 | tf_op jit(solution)/shard_map/ppermute | solution.py:357
  54.7 2.7 %collective-permute-done.9.refs_5_.refs_8_ = f32[32,8,128]{2,1,0:T(8,128)S(1)} collective-permute-done((f32[32,8,128]{2,1,0:T(8,128)S(1)}, f32[32,8,128]{2,1,0:T(8,128)S(1)}, u32[]{:S(2)}, u32[]{:S(2)}) %collective-permute-start.9) | collective-permute-done | bytes 131104 | tf_op jit(solution)/shard_map/ppermute | solution.py:357
  57.6 3.1 %collective-permute-start.12 = (f32[64,512]{1,0:T(8,128)S(1)}, f32[64,512]{1,0:T(8,128)S(1)}, u32[]{:S(2)}, u32[]{:S(2)}) collective-permute-start(f32[64,512]{1,0:T(8,128)S(1)} %get-tuple-element.67), channel_id=1, source_target_pairs={{0,7},{1,6},{2,5},{3,4},{4,3},{5,2},{6,1},{7,0},{8,15},{9,14},{10,... | collective-permute-start | bytes 393224 | tf_op jit(solution)/shard_map/ppermute | solution.py:153
  60.7 0.5 collective-permute-start.13
  61.3 1.4 %collective-permute-start.15 = (f32[64,512]{1,0:T(8,128)S(1)}, f32[64,512]{1,0:T(8,128)S(1)}, u32[]{:S(2)}, u32[]{:S(2)}) collective-permute-start(f32[64,512]{1,0:T(8,128)S(1)} %get-tuple-element.76), channel_id=1, source_target_pairs={{0,3},{1,2},{2,1},{3,0},{4,7},{5,6},{6,5},{7,4},{8,11},{9,10},{10,... | collective-permute-start | bytes 393224 | tf_op jit(solution)/shard_map/ppermute | solution.py:153
  62.6 2.6 %collective-permute-done.12.refs_8_ = f32[64,512]{1,0:T(8,128)S(1)} collective-permute-done((f32[64,512]{1,0:T(8,128)S(1)}, f32[64,512]{1,0:T(8,128)S(1)}, u32[]{:S(2)}, u32[]{:S(2)}) %collective-permute-start.12) | collective-permute-done | bytes 131104 | tf_op jit(solution)/shard_map/ppermute | solution.py:153
  65.2 3.5 %collective-permute-start.17 = (f32[64,512]{1,0:T(8,128)S(1)}, f32[64,512]{1,0:T(8,128)S(1)}, u32[]{:S(2)}, u32[]{:S(2)}) collective-permute-start(f32[64,512]{1,0:T(8,128)S(1)} %get-tuple-element.78), channel_id=1, source_target_pairs={{0,5},{1,4},{2,7},{3,6},{4,1},{5,0},{6,3},{7,2},{8,13},{9,12},{10,... | collective-permute-start | bytes 393224 | tf_op jit(solution)/shard_map/ppermute | solution.py:153
  68.7 1.5 %collective-permute-start.18 = (f32[64,512]{1,0:T(8,128)S(1)}, f32[64,512]{1,0:T(8,128)S(1)}, u32[]{:S(2)}, u32[]{:S(2)}) collective-permute-start(f32[64,512]{1,0:T(8,128)S(1)} %get-tuple-element.79), channel_id=1, source_target_pairs={{0,6},{1,7},{2,4},{3,5},{4,2},{5,3},{6,0},{7,1},{8,14},{9,15},{10,... | collective-permute-start | bytes 393224 | tf_op jit(solution)/shard_map/ppermute | solution.py:153
  70.2 2.1 %unpack.1 = f32[3072,128]{1,0:T(8,128)} custom-call(f32[32,8,128]{2,1,0:T(8,128)S(1)} %get-tuple-element.68.refs_0_, f32[32,8,128]{2,1,0:T(8,128)S(1)} %get-tuple-element.59.refs_0_.refs_1_, f32[32,8,128]{2,1,0:T(8,128)S(1)} %get-tuple-element.60.refs_1_.refs_2_, f32[32,8,128]{2,1,0:T(8,128)S(1)} %collective-permute-done.3.refs_3_.refs_1_, ...), custom_call_target="tpu_custom_call" | custom-call | bytes 3145728 | tf_op jit(solution)/shard_map/unpack/pallas_call | solution.py:210
  72.3 2.2 %collective-permute-done.15.refs_4_ = f32[64,512]{1,0:T(8,128)S(1)} collective-permute-done((f32[64,512]{1,0:T(8,128)S(1)}, f32[64,512]{1,0:T(8,128)S(1)}, u32[]{:S(2)}, u32[]{:S(2)}) %collective-permute-start.15) | collective-permute-done | bytes 131104 | tf_op jit(solution)/shard_map/ppermute | solution.py:153
  74.5 0.7 copy-done.2
  75.2 6.1 %collective-permute-done.17.refs_6_ = f32[64,512]{1,0:T(8,128)S(1)} collective-permute-done((f32[64,512]{1,0:T(8,128)S(1)}, f32[64,512]{1,0:T(8,128)S(1)}, u32[]{:S(2)}, u32[]{:S(2)}) %collective-permute-start.17) | collective-permute-done | bytes 131104 | tf_op jit(solution)/shard_map/ppermute | solution.py:153
  81.3 0.6 copy-done.4
  81.9 0.6 copy-done.6
  82.6 0.9 copy-done.3
  83.5 0.9 copy-done.5
  84.4 0.9 copy-done.7
  85.3 3.3 %gram.1 = (f32[384,384]{1,0:T(8,128)S(1)}, f32[384,384]{1,0:T(8,128)S(1)}, bf16[8,96,512]{2,1,0:T(8,128)(2,1)S(1)}, bf16[8,96,512]{2,1,0:T(8,128)(2,1)S(1)}) custom-call(f32[8,32,512]{2,1,0:T(8,128)S(1)} %all-to-all-done.1.refs_0_, f32[64,512]{1,0:T(8,128)S(1)} %get-tuple-element.73.refs_1_, f32[64,512]{1,0:T(8,128)S(1)} %collective-permute-done.13.refs_2_, ...), custom_call_target="tpu_custom_call" | custom-call | flops 905969664 | bytes 2752512 | tf_op jit(solution)/shard_map/gram/pallas_call | solution.py:276
  88.8 0.4 collective-permute-start.29
  89.2 0.8 own_gram.2
  89.9 0.7 collective-permute-done.19
  90.7 3.3 %collective-permute-start.22 = (f32[4,24,384]{2,1,0:T(8,128)S(1)}, f32[4,24,384]{2,1,0:T(8,128)S(1)}, u32[]{:S(2)}, u32[]{:S(2)}) collective-permute-start(f32[4,24,384]{2,1,0:T(8,128)S(1)} %get-tuple-element.91), channel_id=1, source_target_pairs={{0,24},{8,0},{16,8},{24,16},{1,25},{9,1},{17,9},{25,17},{2,26},{10... | collective-permute-start | bytes 442376 | tf_op jit(solution)/shard_map/ppermute | solution.py:357
  94.0 1.0 collective-permute-start.21
  95.0 0.8 own_gram.3
  95.8 3.0 %collective-permute-start.32 = (f32[4,24,384]{2,1,0:T(8,128)S(1)}, f32[4,24,384]{2,1,0:T(8,128)S(1)}, u32[]{:S(2)}, u32[]{:S(2)}) collective-permute-start(f32[4,24,384]{2,1,0:T(8,128)S(1)} %get-tuple-element.101), channel_id=1, source_target_pairs={{0,24},{8,0},{16,8},{24,16},{1,25},{9,1},{17,9},{25,17},{2,26},{10... | collective-permute-start | bytes 442376 | tf_op jit(solution)/shard_map/ppermute | solution.py:357
  98.8 1.0 collective-permute-start.31
  99.9 1.3 %collective-permute-start.30 = (f32[4,24,384]{2,1,0:T(8,128)S(1)}, f32[4,24,384]{2,1,0:T(8,128)S(1)}, u32[]{:S(2)}, u32[]{:S(2)}) collective-permute-start(f32[4,24,384]{2,1,0:T(8,128)S(1)} %get-tuple-element.99), channel_id=1, source_target_pairs={{0,8},{8,16},{16,24},{24,0},{1,9},{9,17},{17,25},{25,1},{2,10},{10... | collective-permute-start | bytes 442376 | tf_op jit(solution)/shard_map/ppermute | solution.py:357
  101.1 3.5 %collective-permute-done.21 = f32[4,24,384]{2,1,0:T(8,128)} collective-permute-done((f32[4,24,384]{2,1,0:T(8,128)S(1)}, f32[4,24,384]{2,1,0:T(8,128)}, u32[]{:S(2)}, u32[]{:S(2)}) %collective-permute-start.21) | collective-permute-done | bytes 147488 | tf_op jit(solution)/shard_map/ppermute | solution.py:357
  104.7 1.0 add_add_fusion.1
  105.7 1.9 %collective-permute-start.25 = (f32[24,384]{1,0:T(8,128)S(1)}, f32[24,384]{1,0:T(8,128)S(1)}, u32[]{:S(2)}, u32[]{:S(2)}) collective-permute-start(f32[24,384]{1,0:T(8,128)S(1)} %get-tuple-element.106), channel_id=1, source_target_pairs={{0,6},{1,7},{2,4},{3,5},{4,2},{5,3},{6,0},{7,1},{8,14},{9,15},{10,... | collective-permute-start | bytes 110600 | tf_op jit(solution)/shard_map/ppermute | solution.py:153
  107.7 2.5 %collective-permute-start.24 = (f32[24,384]{1,0:T(8,128)S(1)}, f32[24,384]{1,0:T(8,128)S(1)}, u32[]{:S(2)}, u32[]{:S(2)}) collective-permute-start(f32[24,384]{1,0:T(8,128)S(1)} %get-tuple-element.107), channel_id=1, source_target_pairs={{0,4},{1,5},{2,6},{3,7},{4,0},{5,1},{6,2},{7,3},{8,12},{9,13},{10,... | collective-permute-start | bytes 110600 | tf_op jit(solution)/shard_map/ppermute | solution.py:153
  110.2 1.9 %collective-permute-start.35 = (f32[24,384]{1,0:T(8,128)S(1)}, f32[24,384]{1,0:T(8,128)S(1)}, u32[]{:S(2)}, u32[]{:S(2)}) collective-permute-start(f32[24,384]{1,0:T(8,128)S(1)} %get-tuple-element.103), channel_id=1, source_target_pairs={{0,6},{1,7},{2,4},{3,5},{4,2},{5,3},{6,0},{7,1},{8,14},{9,15},{10,... | collective-permute-start | bytes 110600 | tf_op jit(solution)/shard_map/ppermute | solution.py:153
  112.2 1.6 %collective-permute-start.34 = (f32[24,384]{1,0:T(8,128)S(1)}, f32[24,384]{1,0:T(8,128)S(1)}, u32[]{:S(2)}, u32[]{:S(2)}) collective-permute-start(f32[24,384]{1,0:T(8,128)S(1)} %get-tuple-element.104), channel_id=1, source_target_pairs={{0,4},{1,5},{2,6},{3,7},{4,0},{5,1},{6,2},{7,3},{8,12},{9,13},{10,... | collective-permute-start | bytes 110600 | tf_op jit(solution)/shard_map/ppermute | solution.py:153
  113.8 0.9 collective-permute-start.33
  115.0 1.0 collective-permute-start.27
  116.1 2.7 %collective-permute-start.28 = (f32[24,384]{1,0:T(8,128)S(1)}, f32[24,384]{1,0:T(8,128)S(1)}, u32[]{:S(2)}, u32[]{:S(2)}) collective-permute-start(f32[24,384]{1,0:T(8,128)S(1)} %fusion.5.refs_0_), channel_id=1, source_target_pairs={{0,24},{8,0},{16,8},{24,16},{1,25},{9,1},{17,9},{25,17},{2,26},{10... | collective-permute-start | bytes 110600 | tf_op jit(solution)/shard_map/ppermute | solution.py:357
  118.8 1.1 collective-permute-start.37
  119.9 2.8 %collective-permute-start.38 = (f32[24,384]{1,0:T(8,128)S(1)}, f32[24,384]{1,0:T(8,128)S(1)}, u32[]{:S(2)}, u32[]{:S(2)}) collective-permute-start(f32[24,384]{1,0:T(8,128)S(1)} %fusion.2.refs_4_), channel_id=1, source_target_pairs={{0,24},{8,0},{16,8},{24,16},{1,25},{9,1},{17,9},{25,17},{2,26},{10... | collective-permute-start | bytes 110600 | tf_op jit(solution)/shard_map/ppermute | solution.py:357
  122.7 0.9 collective-permute-done.36.refs_5_
  123.7 0.7 collective-permute-done.38.refs_7_
  124.4 0.7 place.1
  (56 shorter events, 1.2 us)
Async XLA Ops:
  0.6 26.2 %copy-start = (bf16[512,256]{1,0:T(8,128)(2,1)S(1)}, bf16[512,256]{1,0:T(8,128)(2,1)}, u32[]{:S(2)}) copy-start(bf16[512,256]{1,0:T(8,128)(2,1)} %constant.45.clone.m_ref) | copy-start | bytes 786436
  0.6 5.3 %copy-start.1 = (f32[2,2048]{1,0:T(2,128)S(1)}, f32[2,2048]{1,0:T(2,128)}, u32[]{:S(2)}) copy-start(f32[2,2048]{1,0:T(2,128)} %param.4) | copy-start | bytes 49156
  0.7 26.2 %all-to-all-start = ((f32[96,2,2048]{2,1,0:T(2,128)}), f32[96,2,2048]{2,1,0:T(2,128)S(1)}, u32[]{:S(2)}, u32[]{:S(2)}) async-start(f32[96,2,2048]{2,1,0:T(2,128)} %param.3), calls=%async_computation | async-start | bytes 3145728 | tf_op jit(solution)/shard_map/all_to_all | solution.py:379
  6.0 19.8 %collective-permute-start = (f32[32,128]{1,0:T(8,128)S(1)}, f32[32,128]{1,0:T(8,128)S(1)}, u32[]{:S(2)}, u32[]{:S(2)}) collective-permute-start(f32[32,128]{1,0:T(8,128)S(1)} %bitcast.55), channel_id=1, source_target_pairs={{0,24},{8,0},{16,8},{24,16},{1,25},{9,1},{17,9},{25,17},{2,26},{10... | collective-permute-start | bytes 49160 | tf_op jit(solution)/shard_map/ppermute | solution.py:357
  8.9 16.9 %collective-permute-start.1 = (f32[32,128]{1,0:T(8,128)S(1)}, f32[32,128]{1,0:T(8,128)S(1)}, u32[]{:S(2)}, u32[]{:S(2)}) collective-permute-start(f32[32,128]{1,0:T(8,128)S(1)} %bitcast.56), channel_id=1, source_target_pairs={{0,16},{8,24},{16,0},{24,8},{1,17},{9,25},{17,1},{25,9},{2,18},{10... | collective-permute-start | bytes 49160 | tf_op jit(solution)/shard_map/ppermute | solution.py:357
  9.4 17.4 %collective-permute-start.2 = (f32[32,128]{1,0:T(8,128)S(1)}, f32[32,128]{1,0:T(8,128)S(1)}, u32[]{:S(2)}, u32[]{:S(2)}) collective-permute-start(f32[32,128]{1,0:T(8,128)S(1)} %bitcast.57), channel_id=1, source_target_pairs={{0,8},{8,16},{16,24},{24,0},{1,9},{9,17},{17,25},{25,1},{2,10},{10... | collective-permute-start | bytes 49160 | tf_op jit(solution)/shard_map/ppermute | solution.py:357
  28.6 7.7 %collective-permute-start.3 = (f32[32,8,128]{2,1,0:T(8,128)S(1)}, f32[32,8,128]{2,1,0:T(8,128)S(1)}, u32[]{:S(2)}, u32[]{:S(2)}) collective-permute-start(f32[32,8,128]{2,1,0:T(8,128)S(1)} %get-tuple-element.53), channel_id=1, source_target_pairs={{0,8},{8,16},{16,24},{24,0},{1,9},{9,17},{17,25},{25,1},{2,10},{10... | collective-permute-start | bytes 393224 | tf_op jit(solution)/shard_map/ppermute | solution.py:357
  29.2 7.2 %collective-permute-start.4 = (f32[32,8,128]{2,1,0:T(8,128)S(1)}, f32[32,8,128]{2,1,0:T(8,128)S(1)}, u32[]{:S(2)}, u32[]{:S(2)}) collective-permute-start(f32[32,8,128]{2,1,0:T(8,128)S(1)} %get-tuple-element.54), channel_id=1, source_target_pairs={{0,16},{8,24},{16,0},{24,8},{1,17},{9,25},{17,1},{25,9},{2,18},{10... | collective-permute-start | bytes 393224 | tf_op jit(solution)/shard_map/ppermute | solution.py:357
  29.8 6.6 %collective-permute-start.5 = (f32[32,8,128]{2,1,0:T(8,128)S(1)}, f32[32,8,128]{2,1,0:T(8,128)S(1)}, u32[]{:S(2)}, u32[]{:S(2)}) collective-permute-start(f32[32,8,128]{2,1,0:T(8,128)S(1)} %get-tuple-element.55), channel_id=1, source_target_pairs={{0,24},{8,0},{16,8},{24,16},{1,25},{9,1},{17,9},{25,17},{2,26},{10... | collective-permute-start | bytes 393224 | tf_op jit(solution)/shard_map/ppermute | solution.py:357
  33.9 0.7 copy-start.8
  36.3 5.9 %copy-start.9 = (f32[32,8,128]{2,1,0:T(8,128)S(1)}, f32[32,8,128]{2,1,0:T(8,128)}, u32[]{:S(2)}) copy-start(f32[32,8,128]{2,1,0:T(8,128)} %copy-done.8) | copy-start | bytes 393220
  37.2 45.4 %all-to-all-start.1 = ((f32[8,32,512]{2,1,0:T(8,128)}), f32[8,32,512]{2,1,0:T(8,128)S(1)}, u32[]{:S(2)}, u32[]{:S(2)}) async-start(f32[8,32,512]{2,1,0:T(8,128)} %pack.3), calls=%async_computation.1 | async-start | bytes 1048576 | tf_op jit(solution)/shard_map/all_to_all | solution.py:392
  42.2 7.3 %collective-permute-start.6 = (f32[32,8,128]{2,1,0:T(8,128)S(1)}, f32[32,8,128]{2,1,0:T(8,128)S(1)}, u32[]{:S(2)}, u32[]{:S(2)}) collective-permute-start(f32[32,8,128]{2,1,0:T(8,128)S(1)} %copy-done.9), channel_id=1, source_target_pairs={{0,8},{8,16},{16,24},{24,0},{1,9},{9,17},{17,25},{25,1},{2,10},{10... | collective-permute-start | bytes 393224 | tf_op jit(solution)/shard_map/ppermute | solution.py:357
  44.0 8.3 %collective-permute-start.7 = (f32[32,8,128]{2,1,0:T(8,128)S(1)}, f32[32,8,128]{2,1,0:T(8,128)S(1)}, u32[]{:S(2)}, u32[]{:S(2)}) collective-permute-start(f32[32,8,128]{2,1,0:T(8,128)S(1)} %get-tuple-element.62), channel_id=1, source_target_pairs={{0,8},{8,16},{16,24},{24,0},{1,9},{9,17},{17,25},{25,1},{2,10},{10... | collective-permute-start | bytes 393224 | tf_op jit(solution)/shard_map/ppermute | solution.py:357
  45.2 9.5 %collective-permute-start.8 = (f32[32,8,128]{2,1,0:T(8,128)S(1)}, f32[32,8,128]{2,1,0:T(8,128)S(1)}, u32[]{:S(2)}, u32[]{:S(2)}) collective-permute-start(f32[32,8,128]{2,1,0:T(8,128)S(1)} %get-tuple-element.63), channel_id=1, source_target_pairs={{0,16},{8,24},{16,0},{24,8},{1,17},{9,25},{17,1},{25,9},{2,18},{10... | collective-permute-start | bytes 393224 | tf_op jit(solution)/shard_map/ppermute | solution.py:357
  45.7 11.7 %collective-permute-start.9 = (f32[32,8,128]{2,1,0:T(8,128)S(1)}, f32[32,8,128]{2,1,0:T(8,128)S(1)}, u32[]{:S(2)}, u32[]{:S(2)}) collective-permute-start(f32[32,8,128]{2,1,0:T(8,128)S(1)} %get-tuple-element.64), channel_id=1, source_target_pairs={{0,16},{8,24},{16,0},{24,8},{1,17},{9,25},{17,1},{25,9},{2,18},{10... | collective-permute-start | bytes 393224 | tf_op jit(solution)/shard_map/ppermute | solution.py:357
  47.2 10.2 %collective-permute-start.10 = (f32[32,8,128]{2,1,0:T(8,128)S(1)}, f32[32,8,128]{2,1,0:T(8,128)S(1)}, u32[]{:S(2)}, u32[]{:S(2)}) collective-permute-start(f32[32,8,128]{2,1,0:T(8,128)S(1)} %get-tuple-element.65), channel_id=1, source_target_pairs={{0,24},{8,0},{16,8},{24,16},{1,25},{9,1},{17,9},{25,17},{2,26},{10... | collective-permute-start | bytes 393224 | tf_op jit(solution)/shard_map/ppermute | solution.py:357
  49.5 7.9 %collective-permute-start.11 = (f32[32,8,128]{2,1,0:T(8,128)S(1)}, f32[32,8,128]{2,1,0:T(8,128)S(1)}, u32[]{:S(2)}, u32[]{:S(2)}) collective-permute-start(f32[32,8,128]{2,1,0:T(8,128)S(1)} %get-tuple-element.66), channel_id=1, source_target_pairs={{0,24},{8,0},{16,8},{24,16},{1,25},{9,1},{17,9},{25,17},{2,26},{10... | collective-permute-start | bytes 393224 | tf_op jit(solution)/shard_map/ppermute | solution.py:357
  57.6 7.6 %collective-permute-start.12 = (f32[64,512]{1,0:T(8,128)S(1)}, f32[64,512]{1,0:T(8,128)S(1)}, u32[]{:S(2)}, u32[]{:S(2)}) collective-permute-start(f32[64,512]{1,0:T(8,128)S(1)} %get-tuple-element.67), channel_id=1, source_target_pairs={{0,7},{1,6},{2,5},{3,4},{4,3},{5,2},{6,1},{7,0},{8,15},{9,14},{10,... | collective-permute-start | bytes 393224 | tf_op jit(solution)/shard_map/ppermute | solution.py:153
  60.7 8.0 %collective-permute-start.13 = (f32[64,512]{1,0:T(8,128)S(1)}, f32[64,512]{1,0:T(8,128)S(1)}, u32[]{:S(2)}, u32[]{:S(2)}) collective-permute-start(f32[64,512]{1,0:T(8,128)S(1)} %get-tuple-element.74), channel_id=1, source_target_pairs={{0,1},{1,0},{2,3},{3,2},{4,5},{5,4},{6,7},{7,6},{8,9},{9,8},{10,11... | collective-permute-start | bytes 393224 | tf_op jit(solution)/shard_map/ppermute | solution.py:153
  61.3 11.0 %collective-permute-start.14 = (f32[64,512]{1,0:T(8,128)S(1)}, f32[64,512]{1,0:T(8,128)S(1)}, u32[]{:S(2)}, u32[]{:S(2)}) collective-permute-start(f32[64,512]{1,0:T(8,128)S(1)} %get-tuple-element.75), channel_id=1, source_target_pairs={{0,2},{1,3},{2,0},{3,1},{4,6},{5,7},{6,4},{7,5},{8,10},{9,11},{10,... | collective-permute-start | bytes 393224 | tf_op jit(solution)/shard_map/ppermute | solution.py:153
  61.3 13.2 %collective-permute-start.15 = (f32[64,512]{1,0:T(8,128)S(1)}, f32[64,512]{1,0:T(8,128)S(1)}, u32[]{:S(2)}, u32[]{:S(2)}) collective-permute-start(f32[64,512]{1,0:T(8,128)S(1)} %get-tuple-element.76), channel_id=1, source_target_pairs={{0,3},{1,2},{2,1},{3,0},{4,7},{5,6},{6,5},{7,4},{8,11},{9,10},{10,... | collective-permute-start | bytes 393224 | tf_op jit(solution)/shard_map/ppermute | solution.py:153
  62.6 11.9 %collective-permute-start.16 = (f32[64,512]{1,0:T(8,128)S(1)}, f32[64,512]{1,0:T(8,128)S(1)}, u32[]{:S(2)}, u32[]{:S(2)}) collective-permute-start(f32[64,512]{1,0:T(8,128)S(1)} %get-tuple-element.77), channel_id=1, source_target_pairs={{0,4},{1,5},{2,6},{3,7},{4,0},{5,1},{6,2},{7,3},{8,12},{9,13},{10,... | collective-permute-start | bytes 393224 | tf_op jit(solution)/shard_map/ppermute | solution.py:153
  65.2 16.1 %collective-permute-start.17 = (f32[64,512]{1,0:T(8,128)S(1)}, f32[64,512]{1,0:T(8,128)S(1)}, u32[]{:S(2)}, u32[]{:S(2)}) collective-permute-start(f32[64,512]{1,0:T(8,128)S(1)} %get-tuple-element.78), channel_id=1, source_target_pairs={{0,5},{1,4},{2,7},{3,6},{4,1},{5,0},{6,3},{7,2},{8,13},{9,12},{10,... | collective-permute-start | bytes 393224 | tf_op jit(solution)/shard_map/ppermute | solution.py:153
  68.7 13.2 %collective-permute-start.18 = (f32[64,512]{1,0:T(8,128)S(1)}, f32[64,512]{1,0:T(8,128)S(1)}, u32[]{:S(2)}, u32[]{:S(2)}) collective-permute-start(f32[64,512]{1,0:T(8,128)S(1)} %get-tuple-element.79), channel_id=1, source_target_pairs={{0,6},{1,7},{2,4},{3,5},{4,2},{5,3},{6,0},{7,1},{8,14},{9,15},{10,... | collective-permute-start | bytes 393224 | tf_op jit(solution)/shard_map/ppermute | solution.py:153
  74.5 0.7 copy-start.2
  81.3 0.6 copy-start.4
  81.9 0.6 copy-start.6
  82.6 0.9 copy-start.3
  83.5 0.9 copy-start.5
  84.4 0.9 copy-start.7
  88.6 2.1 %collective-permute-start.19 = (f32[384,384]{1,0:T(8,128)S(1)}, f32[384,384]{1,0:T(8,128)S(1)}, u32[]{:S(2)}, u32[]{:S(2)}) collective-permute-start(f32[384,384]{1,0:T(8,128)S(1)} %get-tuple-element.83), channel_id=1, source_target_pairs={{0,1},{1,0},{2,3},{3,2},{4,5},{5,4},{6,7},{7,6},{8,9},{9,8},{10,11... | collective-permute-start | bytes 1769480 | tf_op jit(solution)/shard_map/ppermute | solution.py:413
  88.8 7.0 %collective-permute-start.29 = (f32[384,384]{1,0:T(8,128)S(1)}, f32[384,384]{1,0:T(8,128)S(1)}, u32[]{:S(2)}, u32[]{:S(2)}) collective-permute-start(f32[384,384]{1,0:T(8,128)S(1)} %get-tuple-element.93), channel_id=1, source_target_pairs={{0,1},{1,0},{2,3},{3,2},{4,5},{5,4},{6,7},{7,6},{8,9},{9,8},{10,11... | collective-permute-start | bytes 1769480 | tf_op jit(solution)/shard_map/ppermute | solution.py:413
  90.7 9.1 %collective-permute-start.22 = (f32[4,24,384]{2,1,0:T(8,128)S(1)}, f32[4,24,384]{2,1,0:T(8,128)S(1)}, u32[]{:S(2)}, u32[]{:S(2)}) collective-permute-start(f32[4,24,384]{2,1,0:T(8,128)S(1)} %get-tuple-element.91), channel_id=1, source_target_pairs={{0,24},{8,0},{16,8},{24,16},{1,25},{9,1},{17,9},{25,17},{2,26},{10... | collective-permute-start | bytes 442376 | tf_op jit(solution)/shard_map/ppermute | solution.py:357
  94.0 10.7 %collective-permute-start.21 = (f32[4,24,384]{2,1,0:T(8,128)S(1)}, f32[4,24,384]{2,1,0:T(8,128)}, u32[]{:S(2)}, u32[]{:S(2)}) collective-permute-start(f32[4,24,384]{2,1,0:T(8,128)S(1)} %get-tuple-element.90), channel_id=1, source_target_pairs={{0,16},{8,24},{16,0},{24,8},{1,17},{9,25},{17,1},{25,9},{2,18},{10... | collective-permute-start | bytes 442376 | tf_op jit(solution)/shard_map/ppermute | solution.py:357
  95.0 9.7 %collective-permute-start.20 = (f32[4,24,384]{2,1,0:T(8,128)S(1)}, f32[4,24,384]{2,1,0:T(8,128)}, u32[]{:S(2)}, u32[]{:S(2)}) collective-permute-start(f32[4,24,384]{2,1,0:T(8,128)S(1)} %get-tuple-element.89), channel_id=1, source_target_pairs={{0,8},{8,16},{16,24},{24,0},{1,9},{9,17},{17,25},{25,1},{2,10},{10... | collective-permute-start | bytes 442376 | tf_op jit(solution)/shard_map/ppermute | solution.py:357
  95.8 14.3 %collective-permute-start.32 = (f32[4,24,384]{2,1,0:T(8,128)S(1)}, f32[4,24,384]{2,1,0:T(8,128)S(1)}, u32[]{:S(2)}, u32[]{:S(2)}) collective-permute-start(f32[4,24,384]{2,1,0:T(8,128)S(1)} %get-tuple-element.101), channel_id=1, source_target_pairs={{0,24},{8,0},{16,8},{24,16},{1,25},{9,1},{17,9},{25,17},{2,26},{10... | collective-permute-start | bytes 442376 | tf_op jit(solution)/shard_map/ppermute | solution.py:357
  98.8 11.3 %collective-permute-start.31 = (f32[4,24,384]{2,1,0:T(8,128)S(1)}, f32[4,24,384]{2,1,0:T(8,128)S(1)}, u32[]{:S(2)}, u32[]{:S(2)}) collective-permute-start(f32[4,24,384]{2,1,0:T(8,128)S(1)} %get-tuple-element.100), channel_id=1, source_target_pairs={{0,16},{8,24},{16,0},{24,8},{1,17},{9,25},{17,1},{25,9},{2,18},{10... | collective-permute-start | bytes 442376 | tf_op jit(solution)/shard_map/ppermute | solution.py:357
  99.9 10.3 %collective-permute-start.30 = (f32[4,24,384]{2,1,0:T(8,128)S(1)}, f32[4,24,384]{2,1,0:T(8,128)S(1)}, u32[]{:S(2)}, u32[]{:S(2)}) collective-permute-start(f32[4,24,384]{2,1,0:T(8,128)S(1)} %get-tuple-element.99), channel_id=1, source_target_pairs={{0,8},{8,16},{16,24},{24,0},{1,9},{9,17},{17,25},{25,1},{2,10},{10... | collective-permute-start | bytes 442376 | tf_op jit(solution)/shard_map/ppermute | solution.py:357
  105.7 8.0 %collective-permute-start.25 = (f32[24,384]{1,0:T(8,128)S(1)}, f32[24,384]{1,0:T(8,128)S(1)}, u32[]{:S(2)}, u32[]{:S(2)}) collective-permute-start(f32[24,384]{1,0:T(8,128)S(1)} %get-tuple-element.106), channel_id=1, source_target_pairs={{0,6},{1,7},{2,4},{3,5},{4,2},{5,3},{6,0},{7,1},{8,14},{9,15},{10,... | collective-permute-start | bytes 110600 | tf_op jit(solution)/shard_map/ppermute | solution.py:153
  107.7 7.0 %collective-permute-start.24 = (f32[24,384]{1,0:T(8,128)S(1)}, f32[24,384]{1,0:T(8,128)S(1)}, u32[]{:S(2)}, u32[]{:S(2)}) collective-permute-start(f32[24,384]{1,0:T(8,128)S(1)} %get-tuple-element.107), channel_id=1, source_target_pairs={{0,4},{1,5},{2,6},{3,7},{4,0},{5,1},{6,2},{7,3},{8,12},{9,13},{10,... | collective-permute-start | bytes 110600 | tf_op jit(solution)/shard_map/ppermute | solution.py:153
  110.1 4.6 %collective-permute-start.23 = (f32[24,384]{1,0:T(8,128)S(1)}, f32[24,384]{1,0:T(8,128)S(1)}, u32[]{:S(2)}, u32[]{:S(2)}) collective-permute-start(f32[24,384]{1,0:T(8,128)S(1)} %get-tuple-element.105), channel_id=1, source_target_pairs={{0,2},{1,3},{2,0},{3,1},{4,6},{5,7},{6,4},{7,5},{8,10},{9,11},{10,... | collective-permute-start | bytes 110600 | tf_op jit(solution)/shard_map/ppermute | solution.py:153
  110.2 5.8 %collective-permute-start.35 = (f32[24,384]{1,0:T(8,128)S(1)}, f32[24,384]{1,0:T(8,128)S(1)}, u32[]{:S(2)}, u32[]{:S(2)}) collective-permute-start(f32[24,384]{1,0:T(8,128)S(1)} %get-tuple-element.103), channel_id=1, source_target_pairs={{0,6},{1,7},{2,4},{3,5},{4,2},{5,3},{6,0},{7,1},{8,14},{9,15},{10,... | collective-permute-start | bytes 110600 | tf_op jit(solution)/shard_map/ppermute | solution.py:153
  112.2 6.6 %collective-permute-start.34 = (f32[24,384]{1,0:T(8,128)S(1)}, f32[24,384]{1,0:T(8,128)S(1)}, u32[]{:S(2)}, u32[]{:S(2)}) collective-permute-start(f32[24,384]{1,0:T(8,128)S(1)} %get-tuple-element.104), channel_id=1, source_target_pairs={{0,4},{1,5},{2,6},{3,7},{4,0},{5,1},{6,2},{7,3},{8,12},{9,13},{10,... | collective-permute-start | bytes 110600 | tf_op jit(solution)/shard_map/ppermute | solution.py:153
  113.8 5.0 %collective-permute-start.33 = (f32[24,384]{1,0:T(8,128)S(1)}, f32[24,384]{1,0:T(8,128)S(1)}, u32[]{:S(2)}, u32[]{:S(2)}) collective-permute-start(f32[24,384]{1,0:T(8,128)S(1)} %get-tuple-element.102), channel_id=1, source_target_pairs={{0,2},{1,3},{2,0},{3,1},{4,6},{5,7},{6,4},{7,5},{8,10},{9,11},{10,... | collective-permute-start | bytes 110600 | tf_op jit(solution)/shard_map/ppermute | solution.py:153
  114.7 5.2 %collective-permute-start.26 = (f32[24,384]{1,0:T(8,128)S(1)}, f32[24,384]{1,0:T(8,128)S(1)}, u32[]{:S(2)}, u32[]{:S(2)}) collective-permute-start(f32[24,384]{1,0:T(8,128)S(1)} %fusion.5.refs_0_), channel_id=1, source_target_pairs={{0,8},{8,16},{16,24},{24,0},{1,9},{9,17},{17,25},{25,1},{2,10},{10... | collective-permute-start | bytes 110600 | tf_op jit(solution)/shard_map/ppermute | solution.py:357
  115.0 7.7 %collective-permute-start.27 = (f32[24,384]{1,0:T(8,128)S(1)}, f32[24,384]{1,0:T(8,128)S(1)}, u32[]{:S(2)}, u32[]{:S(2)}) collective-permute-start(f32[24,384]{1,0:T(8,128)S(1)} %fusion.5.refs_0_), channel_id=1, source_target_pairs={{0,16},{8,24},{16,0},{24,8},{1,17},{9,25},{17,1},{25,9},{2,18},{10... | collective-permute-start | bytes 110600 | tf_op jit(solution)/shard_map/ppermute | solution.py:357
  116.1 6.7 %collective-permute-start.28 = (f32[24,384]{1,0:T(8,128)S(1)}, f32[24,384]{1,0:T(8,128)S(1)}, u32[]{:S(2)}, u32[]{:S(2)}) collective-permute-start(f32[24,384]{1,0:T(8,128)S(1)} %fusion.5.refs_0_), channel_id=1, source_target_pairs={{0,24},{8,0},{16,8},{24,16},{1,25},{9,1},{17,9},{25,17},{2,26},{10... | collective-permute-start | bytes 110600 | tf_op jit(solution)/shard_map/ppermute | solution.py:357
  118.8 4.9 %collective-permute-start.36 = (f32[24,384]{1,0:T(8,128)S(1)}, f32[24,384]{1,0:T(8,128)S(1)}, u32[]{:S(2)}, u32[]{:S(2)}) collective-permute-start(f32[24,384]{1,0:T(8,128)S(1)} %fusion.2.refs_4_), channel_id=1, source_target_pairs={{0,8},{8,16},{16,24},{24,0},{1,9},{9,17},{17,25},{25,1},{2,10},{10... | collective-permute-start | bytes 110600 | tf_op jit(solution)/shard_map/ppermute | solution.py:357
  118.8 4.8 %collective-permute-start.37 = (f32[24,384]{1,0:T(8,128)S(1)}, f32[24,384]{1,0:T(8,128)S(1)}, u32[]{:S(2)}, u32[]{:S(2)}) collective-permute-start(f32[24,384]{1,0:T(8,128)S(1)} %fusion.2.refs_4_), channel_id=1, source_target_pairs={{0,16},{8,24},{16,0},{24,8},{1,17},{9,25},{17,1},{25,9},{2,18},{10... | collective-permute-start | bytes 110600 | tf_op jit(solution)/shard_map/ppermute | solution.py:357
  119.9 4.5 %collective-permute-start.38 = (f32[24,384]{1,0:T(8,128)S(1)}, f32[24,384]{1,0:T(8,128)S(1)}, u32[]{:S(2)}, u32[]{:S(2)}) collective-permute-start(f32[24,384]{1,0:T(8,128)S(1)} %fusion.2.refs_4_), channel_id=1, source_target_pairs={{0,24},{8,0},{16,8},{24,16},{1,25},{9,1},{17,9},{25,17},{2,26},{10... | collective-permute-start | bytes 110600 | tf_op jit(solution)/shard_map/ppermute | solution.py:357

commit v10 on v8

--- a/solution.py
+++ b/solution.py
@@ -153,62 +153,55 @@
     return lax.ppermute(x, axis, pairs)
 
 
-def pack_kernel(space, band, share, chunk, subs, *refs):
-    blocks, outs = refs[: space * subs], refs[space * subs :]
+def pack_kernel(space, band, share, size, *refs):
+    blocks, outs = refs[:space], refs[space:]
     here, mine = lax.axis_index("space"), lax.axis_index("band")
-    for k in range(space):
+    for k, block in enumerate(blocks):
         group = here - k
         group = jnp.where(group < 0, group + space, group)
-        for sub in range(subs):
-            first = pl.multiple_of((group * subs + sub) * chunk, chunk)
-            block = blocks[k * subs + sub]
-            for step in range(band):
-                out = outs[0].at[step] if len(outs) == 1 else outs[step]
-                target = step if len(outs) == 1 else partner(mine, band, step)
-                for q in range(share):
-                    out[pl.ds(first, chunk), q * LANES : (q + 1) * LANES] = block[target * share + q]
-
-
-def pack(blocks, space, band, share, chunk, subs, apart):
-    shape = (space * subs * chunk, share * LANES)
+        first = pl.multiple_of(group * size, size)
+        for step in range(band):
+            out = outs[0].at[step] if len(outs) == 1 else outs[step]
+            target = step if len(outs) == 1 else partner(mine, band, step)
+            for q in range(share):
+                out[pl.ds(first, size), q * LANES : (q + 1) * LANES] = block[target * share + q]
+
+
+def pack(blocks, space, band, share, size, apart):
+    shape = (space * size, share * LANES)
     out_shape = [jax.ShapeDtypeStruct(shape, jnp.float32)] * band
     if not apart:
         out_shape = [jax.ShapeDtypeStruct((band,) + shape, jnp.float32)]
     return pl.pallas_call(
-        functools.partial(pack_kernel, space, band, share, chunk, subs),
+        functools.partial(pack_kernel, space, band, share, size),
         out_shape=out_shape,
-        in_specs=[VMEM_SPEC] * len(blocks),
+        in_specs=[VMEM_SPEC] * space,
         out_specs=[VMEM_SPEC] * len(out_shape),
         compiler_params=pltpu.CompilerParams(vmem_limit_bytes=VMEM_LIMIT),
         cost_estimate=pl.CostEstimate(
-            flops=0, bytes_accessed=8 * band * space * subs * chunk * share * LANES, transcendentals=0
+            flops=0, bytes_accessed=8 * band * space * size * share * LANES, transcendentals=0
         ),
         name="pack",
     )(*blocks)
 
 
-def unpack_kernel(space, rows, chunk, subs_of, *refs):
+def unpack_kernel(space, rows, own, sizes, *refs):
     blocks, out = refs[:-1], refs[-1]
     here = lax.axis_index("space")
-    start = 0
-    taken = 0
-    for subs in subs_of:
-        for k in range(space):
-            group = here - k
-            group = jnp.where(group < 0, group + space, group)
-            for sub in range(subs):
-                block = blocks[taken + k * subs + sub]
-                first = (start + (group * subs + sub) * chunk) * rows
-                for row in range(rows):
-                    out[pl.ds(first + row, chunk, stride=rows), :] = block[row]
-        taken += space * subs
-        start += space * subs * chunk
-
-
-def unpack(blocks, space, rows, chunk, subs_of):
-    count = sum(subs_of) * space * chunk
-    return pl.pallas_call(
-        functools.partial(unpack_kernel, space, rows, chunk, subs_of),
+    for n, block in enumerate(blocks):
+        c, k = divmod(n, space)
+        group = here - k
+        group = jnp.where(group < 0, group + space, group)
+        first = (group * own + sum(sizes[:c])) * rows
+        for row in range(rows):
+            out[pl.ds(first + row, sizes[c], stride=rows), :] = block[row]
+
+
+def unpack(blocks, space, rows, sizes):
+    own = sum(sizes)
+    count = own * space
+    return pl.pallas_call(
+        functools.partial(unpack_kernel, space, rows, own, sizes),
         out_shape=jax.ShapeDtypeStruct((count * rows, LANES), jnp.float32),
         in_specs=[VMEM_SPEC] * len(blocks),
         out_specs=VMEM_SPEC,
@@ -237,12 +230,11 @@
         out[:, columns] = dot(left_hi, top) + (dot(left_hi, rest) + dot(left_lo, top))
 
 
-def gram_kernel(band, count, space, chunk, places, *refs):
+def gram_kernel(band, count, space, places, *refs):
     parts, (*outs, hi, lo, wide) = list(refs[: -3 - PARTS]), refs[-3 - PARTS :]
     own = count // space
     mine = lax.axis_index("band")
-    for offset, subs, apart in places:
-        size = subs * chunk
+    for offset, size, apart in places:
         taken = [parts.pop(0) for _ in range(band)] if apart else parts.pop(0)
         for step in range(band):
             source = partner(mine, band, step, forward=False) if apart else step
@@ -260,12 +252,12 @@
     half_product(band, count, lax.axis_index("band") % 2, hi, lo, first, out)
 
 
-def gram(parts, band, count, space, chunk, places):
+def gram(parts, band, count, space, places):
     cells = parts[0].shape[-1]
     half = jax.ShapeDtypeStruct((band // 2 * count, band * count // PARTS), jnp.float32)
     narrow = jax.ShapeDtypeStruct((band, count, cells), jnp.bfloat16)
     return pl.pallas_call(
-        functools.partial(gram_kernel, band, count, space, chunk, places),
+        functools.partial(gram_kernel, band, count, space, places),
         out_shape=[half] * PARTS + [narrow, narrow],
         in_specs=[VMEM_SPEC] * len(parts),
         out_specs=[VMEM_SPEC] * (PARTS + 2),
@@ -354,8 +346,7 @@
     share = rows // band
     own = count // space
     chunk = max(c for c in range(1, SUBLANES + 1) if own % c == 0)
-    chunks = own // chunk
-
+    sizes = [chunk] if own == chunk else [chunk, own - chunk]
 
     def as_rows(x):
         n = x.shape[0]
@@ -366,29 +357,28 @@
     vs = [own_v] + [rotate(own_v, "space", space - k) for k in range(1, space)]
     arrived = as_rows(lax.all_to_all(orbitals, "space", split_axis=0, concat_axis=0, tiled=True))
 
-    def filtered(c, x):
-        outs = run_filter(x, matrix, vs, c * chunk, space, layers, tiles, chunk)
+    def filtered(offset, size):
+        outs = run_filter(arrived, matrix, vs, offset, space, layers, tiles, size)
         vs[:] = [outs[-1]] if len(vs) > 1 else vs
         return [outs[0]] + [rotate(outs[k], "space", k) for k in range(1, space)]
 
-    made = [filtered(c, arrived) for c in range(min(chunks, 2))]
-    made[0], made[-1][0] = lax.optimization_barrier((made[0], made[-1][0]))
-    head = pack(made[0], space, band, share, chunk, 1, False)[0]
-    head, arrived = lax.optimization_barrier((head, arrived))
-    parts = [lax.all_to_all(head, "band", split_axis=0, concat_axis=0, tiled=True)]
-    places = [(0, 1, False)]
-    made += [filtered(c, arrived) for c in range(2, chunks)]
-    if chunks > 1:
-        late = [made[c][k] for k in range(space) for c in range(1, chunks)]
-        packed = pack(late, space, band, share, chunk, chunks - 1, True)
+    made = [filtered(sum(sizes[:c]), size) for c, size in enumerate(sizes)]
+    if len(made) > 1:
+        made[0], made[1][0] = lax.optimization_barrier((made[0], made[1][0]))
+    head = pack(made[0], space, band, share, sizes[0], False)[0]
+    head = lax.all_to_all(head, "band", split_axis=0, concat_axis=0, tiled=True)
+    parts = [head]
+    places = [(0, sizes[0], False)]
+    if len(made) > 1:
+        packed = pack(made[1], space, band, share, sizes[1], True)
         got = {0: packed[0]}
         for k in reversed(range(1, band)):
             got[k] = exchange(packed[k], "band", k)
         parts += [got[k] for k in range(band)]
-        places.append((chunk, chunks - 1, True))
-    blocks = [made[c][k] for k in range(space) for c in range(chunks)]
-
-    result = unpack(blocks, space, rows, chunk, [chunks])
+        places.append((sizes[0], sizes[1], True))
+        parts[0], made[0][0] = lax.optimization_barrier((parts[0], made[0][0]))
+
+    result = unpack(sum(made, []), space, rows, sizes)
     parts[-1], result = lax.optimization_barrier((parts[-1], result))
     result = result.reshape(count, tiles, layers, LANES).transpose(0, 2, 1, 3).reshape(count, layers, plane)
 
@@ -396,7 +386,7 @@
     pair = lax.axis_index("band") // 2
     scale = 1.0 / (layers * space * plane)
 
-    *others, hi, lo = gram(parts, band, count, space, chunk, places)
+    *others, hi, lo = gram(parts, band, count, space, places)
     others = [lax.ppermute(x, "band", [(i, i ^ 1) for i in range(band)]) for x in others]
     width = band * count // PARTS
     split = (pairs, space, own, width)

time: 121 us -> 122 us (level)
  starting transfers between devices: 61.6 us -> 58.6 us
  waiting for transfers between devices: 42.1 us -> 44.5 us
  Pallas kernels: 12.4 us -> 14 us
    ppermute x24 -> x21, waiting for transfers between devices: 29.3 us -> 33.3 us  [rotate(): return lax.ppermute(x, axis, [(i, (i + step) % size) for i in range(size)])]
    ppermute x24 -> x21, starting transfers between devices: 31.9 us -> 28.3 us  [rotate(): return lax.ppermute(x, axis, [(i, (i + step) % size) for i in range(size)])]
    pallas_call x4, Pallas kernels: 4.68 us -> 6.45 us  [the longest x1 2.61 us: gram(): pl.pallas_call(functools.partial(gram_kernel, band, count, space, places)...]
    ppermute x13, waiting for transfers between devices: 12 us -> 10.4 us  [exchange(): return lax.ppermute(x, axis, pairs)]
    pallas_call x3 -> x2, Pallas kernels: 5.26 us -> 5.08 us  [run_filter(): pl.pallas_call(functools.partial(filter_kernel, space, layers, tiles, chu...]
    unnamed x12 -> x14, local copies, waits for them, and re-layouts: 3.12 us -> 3.13 us
  transfers between devices with their start and end apart: 41 -> 38, of which waited for: 16 -> 13; matrix products, arithmetic and copies ran while one was open for 1% -> 1% of each run, Pallas kernels for 6% -> 7%
where the time goes in v10:
time: 122 us
  starting transfers between devices  58.6 us (48%)
  waiting for transfers between devices  44.5 us (36%)
  Pallas kernels  14 us (11%)
  local copies, waits for them, and re-layouts  3.17 us (3%)
    ppermute x21, waiting for transfers between devices, rotate(): return lax.ppermute(x, axis, [(i, (i + step) % size) for i in range(size)])  33.3 us
    ppermute x21, starting transfers between devices, rotate(): return lax.ppermute(x, axis, [(i, (i + step) % size) for i in range(size)])  28.3 us
    ppermute x13, starting transfers between devices, exchange(): return lax.ppermute(x, axis, pairs)  19.5 us
    ppermute x13, waiting for transfers between devices, exchange(): return lax.ppermute(x, axis, pairs)  10.4 us
    all_to_all x1, starting transfers between devices, shards(): lax.all_to_all(orbitals, 'space', split_axis=0, concat_axis=0, tiled=True)  5.31 us
    pallas_call x2, Pallas kernels, run_filter(): pl.pallas_call(functools.partial(filter_kernel, space, layers, tiles, chu...  5.08 us
    all_to_all x1, starting transfers between devices, shards(): head = lax.all_to_all(head, 'band', split_axis=0, concat_axis=0, tiled=True)  4.99 us
    unnamed x14, local copies, waits for them, and re-layouts  3.13 us
  transfers between devices with their start and end apart: 38, of which 13 were waited for; matrix products, arithmetic and copies ran while one was open for 1% of the time, Pallas kernels for 7%

profile of v10, /device:TPU:0, one launch (start us, length us, event | category | flops | bytes accessed | tf_op | source)
XLA Modules:
  0.0 122.1 jit_solution(2916291966707684930)
XLA Ops:
  0.6 0.0 copy-start
  0.7 5.3 %all-to-all-start = ((f32[96,2,2048]{2,1,0:T(2,128)}), f32[96,2,2048]{2,1,0:T(2,128)S(1)}, u32[]{:S(2)}, u32[]{:S(2)}) async-start(f32[96,2,2048]{2,1,0:T(2,128)} %param.3), calls=%async_computation | async-start | bytes 3145728 | tf_op jit(solution)/shard_map/all_to_all | solution.py:358
  6.0 2.9 %collective-permute-start = (f32[32,128]{1,0:T(8,128)S(1)}, f32[32,128]{1,0:T(8,128)S(1)}, u32[]{:S(2)}, u32[]{:S(2)}) collective-permute-start(f32[32,128]{1,0:T(8,128)S(1)} %bitcast.54), channel_id=1, source_target_pairs={{0,24},{8,0},{16,8},{24,16},{1,25},{9,1},{17,9},{25,17},{2,26},{10... | collective-permute-start | bytes 49160 | tf_op jit(solution)/shard_map/ppermute | solution.py:337
  8.9 0.6 collective-permute-start.1
  9.4 0.6 collective-permute-start.2
  10.0 15.7 %collective-permute-done.refs_1_ = f32[32,128]{1,0:T(8,128)S(1)} collective-permute-done((f32[32,128]{1,0:T(8,128)S(1)}, f32[32,128]{1,0:T(8,128)S(1)}, u32[]{:S(2)}, u32[]{:S(2)}) %collective-permute-start) | collective-permute-done | bytes 16416 | tf_op jit(solution)/shard_map/ppermute | solution.py:337
  25.7 1.1 collective-permute-done.2.refs_3_
  26.8 1.8 %filter.2 = (f32[32,8,128]{2,1,0:T(8,128)S(1)}, f32[32,8,128]{2,1,0:T(8,128)S(1)}, f32[32,8,128]{2,1,0:T(8,128)S(1)}, f32[32,8,128]{2,1,0:T(8,128)S(1)}, f32[128,128]{1,0:T(8,128)S(1)}) custom-call(f32[3072,128]{1,0:T(8,128)S(1)} %bitcast.48, bf16[512,256]{1,0:T(8,128)(2,1)S(1)} %copy-done, f32[32,128]{1,0:T(8,128)S(1)} %bitcast.57, ...), custom_call_target="tpu_custom_call" | custom-call | flops 6553600 | bytes 1048576 | tf_op jit(solution)/shard_map/filter/pallas_call | solution.py:123
  28.6 0.6 collective-permute-start.3
  29.2 0.6 collective-permute-start.4
  29.8 2.4 %collective-permute-start.5 = (f32[32,8,128]{2,1,0:T(8,128)S(1)}, f32[32,8,128]{2,1,0:T(8,128)S(1)}, u32[]{:S(2)}, u32[]{:S(2)}) collective-permute-start(f32[32,8,128]{2,1,0:T(8,128)S(1)} %get-tuple-element.52), channel_id=1, source_target_pairs={{0,24},{8,0},{16,8},{24,16},{1,25},{9,1},{17,9},{25,17},{2,26},{10... | collective-permute-start | bytes 393224 | tf_op jit(solution)/shard_map/ppermute | solution.py:337
  32.1 3.3 %filter.3 = (f32[32,16,128]{2,1,0:T(8,128)S(1)}, f32[32,16,128]{2,1,0:T(8,128)S(1)}, f32[32,16,128]{2,1,0:T(8,128)S(1)}, f32[32,16,128]{2,1,0:T(8,128)S(1)}) custom-call(f32[3072,128]{1,0:T(8,128)S(1)} %bitcast.49, bf16[512,256]{1,0:T(8,128)(2,1)S(1)} %copy-done, f32[128,128]{1,0:T(8,128)S(1)} %get-tuple-element.53.refs_0_), custom_call_target="tpu_custom_call" | custom-call | flops 6553600 | bytes 2097152 | tf_op jit(solution)/shard_map/filter/pallas_call | solution.py:123
  35.5 0.1 collective-permute-done.4.refs_2_
  35.5 0.8 pack.3
  36.4 5.0 %all-to-all-start.1 = ((f32[8,32,512]{2,1,0:T(8,128)}), f32[8,32,512]{2,1,0:T(8,128)S(1)}, u32[]{:S(2)}, u32[]{:S(2)}) async-start(f32[8,32,512]{2,1,0:T(8,128)} %pack.3), calls=%async_computation.1 | async-start | bytes 1048576 | tf_op jit(solution)/shard_map/all_to_all | solution.py:369
  41.4 2.5 %collective-permute-start.6 = (f32[32,16,128]{2,1,0:T(8,128)}, f32[32,16,128]{2,1,0:T(8,128)S(1)}, u32[]{:S(2)}, u32[]{:S(2)}) collective-permute-start(f32[32,16,128]{2,1,0:T(8,128)} %copy-done.2), channel_id=1, source_target_pairs={{0,8},{8,16},{16,24},{24,0},{1,9},{9,17},{17,25},{25,1},{2,10},{10... | collective-permute-start | bytes 786440 | tf_op jit(solution)/shard_map/ppermute | solution.py:337
  43.9 1.0 collective-permute-start.7
  44.9 0.8 collective-permute-start.8
  45.7 6.0 %collective-permute-done.6.refs_1_.refs_5_ = f32[32,16,128]{2,1,0:T(8,128)S(1)} collective-permute-done((f32[32,16,128]{2,1,0:T(8,128)}, f32[32,16,128]{2,1,0:T(8,128)S(1)}, u32[]{:S(2)}, u32[]{:S(2)}) %collective-permute-start.6) | collective-permute-done | bytes 262176 | tf_op jit(solution)/shard_map/ppermute | solution.py:337
  51.8 5.4 %collective-permute-done.7.refs_2_.refs_6_ = f32[32,16,128]{2,1,0:T(8,128)S(1)} collective-permute-done((f32[32,16,128]{2,1,0:T(8,128)S(1)}, f32[32,16,128]{2,1,0:T(8,128)S(1)}, u32[]{:S(2)}, u32[]{:S(2)}) %collective-permute-start.7) | collective-permute-done | bytes 262176 | tf_op jit(solution)/shard_map/ppermute | solution.py:337
  57.2 0.7 pack.2
  57.9 3.1 %collective-permute-start.9 = (f32[64,512]{1,0:T(8,128)S(1)}, f32[64,512]{1,0:T(8,128)S(1)}, u32[]{:S(2)}, u32[]{:S(2)}) collective-permute-start(f32[64,512]{1,0:T(8,128)S(1)} %get-tuple-element.59), channel_id=1, source_target_pairs={{0,7},{1,6},{2,5},{3,4},{4,3},{5,2},{6,1},{7,0},{8,15},{9,14},{10,... | collective-permute-start | bytes 393224 | tf_op jit(solution)/shard_map/ppermute | solution.py:153
  61.0 0.5 collective-permute-start.10
  61.5 1.4 %collective-permute-start.12 = (f32[64,512]{1,0:T(8,128)S(1)}, f32[64,512]{1,0:T(8,128)S(1)}, u32[]{:S(2)}, u32[]{:S(2)}) collective-permute-start(f32[64,512]{1,0:T(8,128)S(1)} %get-tuple-element.70), channel_id=1, source_target_pairs={{0,3},{1,2},{2,1},{3,0},{4,7},{5,6},{6,5},{7,4},{8,11},{9,10},{10,... | collective-permute-start | bytes 393224 | tf_op jit(solution)/shard_map/ppermute | solution.py:153
  62.8 2.6 %collective-permute-done.9.refs_8_ = f32[64,512]{1,0:T(8,128)S(1)} collective-permute-done((f32[64,512]{1,0:T(8,128)S(1)}, f32[64,512]{1,0:T(8,128)S(1)}, u32[]{:S(2)}, u32[]{:S(2)}) %collective-permute-start.9) | collective-permute-done | bytes 131104 | tf_op jit(solution)/shard_map/ppermute | solution.py:153
  65.5 3.5 %collective-permute-start.14 = (f32[64,512]{1,0:T(8,128)S(1)}, f32[64,512]{1,0:T(8,128)}, u32[]{:S(2)}, u32[]{:S(2)}) collective-permute-start(f32[64,512]{1,0:T(8,128)S(1)} %get-tuple-element.72), channel_id=1, source_target_pairs={{0,5},{1,4},{2,7},{3,6},{4,1},{5,0},{6,3},{7,2},{8,13},{9,12},{10,... | collective-permute-start | bytes 393224 | tf_op jit(solution)/shard_map/ppermute | solution.py:153
  69.0 1.5 %collective-permute-start.15 = (f32[64,512]{1,0:T(8,128)S(1)}, f32[64,512]{1,0:T(8,128)}, u32[]{:S(2)}, u32[]{:S(2)}) collective-permute-start(f32[64,512]{1,0:T(8,128)S(1)} %get-tuple-element.73), channel_id=1, source_target_pairs={{0,6},{1,7},{2,4},{3,5},{4,2},{5,3},{6,0},{7,1},{8,14},{9,15},{10,... | collective-permute-start | bytes 393224 | tf_op jit(solution)/shard_map/ppermute | solution.py:153
  70.4 2.3 %unpack.1 = f32[3072,128]{1,0:T(8,128)} custom-call(f32[32,8,128]{2,1,0:T(8,128)S(1)} %get-tuple-element.64.refs_0_, f32[32,8,128]{2,1,0:T(8,128)S(1)} %collective-permute-done.3.refs_1_, f32[32,8,128]{2,1,0:T(8,128)S(1)} %collective-permute-done.4.refs_2_, f32[32,8,128]{2,1,0:T(8,128)S(1)} %collective-permute-done.5.refs_3_, ...), custom_call_target="tpu_custom_call" | custom-call | bytes 3145728 | tf_op jit(solution)/shard_map/unpack/pallas_call | solution.py:203
  72.7 2.0 %collective-permute-done.12.refs_4_ = f32[64,512]{1,0:T(8,128)S(1)} collective-permute-done((f32[64,512]{1,0:T(8,128)S(1)}, f32[64,512]{1,0:T(8,128)S(1)}, u32[]{:S(2)}, u32[]{:S(2)}) %collective-permute-start.12) | collective-permute-done | bytes 131104 | tf_op jit(solution)/shard_map/ppermute | solution.py:153
  74.7 0.7 copy-done.3
  75.4 0.7 copy-done.5
  76.0 5.6 %collective-permute-done.14.refs_6_ = f32[64,512]{1,0:T(8,128)} collective-permute-done((f32[64,512]{1,0:T(8,128)S(1)}, f32[64,512]{1,0:T(8,128)}, u32[]{:S(2)}, u32[]{:S(2)}) %collective-permute-start.14) | collective-permute-done | bytes 131104 | tf_op jit(solution)/shard_map/ppermute | solution.py:153
  81.6 0.9 copy-done.4
  82.5 0.9 copy-done.6
  83.4 2.6 %gram.1 = (f32[384,384]{1,0:T(8,128)S(1)}, f32[384,384]{1,0:T(8,128)S(1)}, bf16[8,96,512]{2,1,0:T(8,128)(2,1)S(1)}, bf16[8,96,512]{2,1,0:T(8,128)(2,1)S(1)}) custom-call(f32[8,32,512]{2,1,0:T(8,128)S(1)} %all-to-all-done.1.refs_0_, f32[64,512]{1,0:T(8,128)S(1)} %get-tuple-element.67.refs_1_, f32[64,512]{1,0:T(8,128)S(1)} %collective-permute-done.10.refs_2_, ...), custom_call_target="tpu_custom_call" | custom-call | flops 905969664 | bytes 2752512 | tf_op jit(solution)/shard_map/gram/pallas_call | solution.py:259
  86.0 0.3 collective-permute-start.16
  86.3 0.3 collective-permute-start.26
  86.6 0.8 own_gram.2
  87.4 0.7 collective-permute-done.16
  88.1 0.1 combine.2
  88.2 2.3 %collective-permute-start.19 = (f32[4,24,384]{2,1,0:T(8,128)S(1)}, f32[4,24,384]{2,1,0:T(8,128)S(1)}, u32[]{:S(2)}, u32[]{:S(2)}) collective-permute-start(f32[4,24,384]{2,1,0:T(8,128)S(1)} %get-tuple-element.85), channel_id=1, source_target_pairs={{0,24},{8,0},{16,8},{24,16},{1,25},{9,1},{17,9},{25,17},{2,26},{10... | collective-permute-start | bytes 442376 | tf_op jit(solution)/shard_map/ppermute | solution.py:337
  90.5 1.0 collective-permute-start.18
  91.5 0.8 own_gram.3
  92.3 0.1 combine.3
  92.4 3.0 %collective-permute-start.29 = (f32[4,24,384]{2,1,0:T(8,128)S(1)}, f32[4,24,384]{2,1,0:T(8,128)S(1)}, u32[]{:S(2)}, u32[]{:S(2)}) collective-permute-start(f32[4,24,384]{2,1,0:T(8,128)S(1)} %get-tuple-element.95), channel_id=1, source_target_pairs={{0,24},{8,0},{16,8},{24,16},{1,25},{9,1},{17,9},{25,17},{2,26},{10... | collective-permute-start | bytes 442376 | tf_op jit(solution)/shard_map/ppermute | solution.py:337
  95.3 1.0 collective-permute-start.28
  96.4 1.3 %collective-permute-start.27 = (f32[4,24,384]{2,1,0:T(8,128)S(1)}, f32[4,24,384]{2,1,0:T(8,128)S(1)}, u32[]{:S(2)}, u32[]{:S(2)}) collective-permute-start(f32[4,24,384]{2,1,0:T(8,128)S(1)} %get-tuple-element.93), channel_id=1, source_target_pairs={{0,8},{8,16},{16,24},{24,0},{1,9},{9,17},{17,25},{25,1},{2,10},{10... | collective-permute-start | bytes 442376 | tf_op jit(solution)/shard_map/ppermute | solution.py:337
  97.6 3.4 %collective-permute-done.18 = f32[4,24,384]{2,1,0:T(8,128)} collective-permute-done((f32[4,24,384]{2,1,0:T(8,128)S(1)}, f32[4,24,384]{2,1,0:T(8,128)}, u32[]{:S(2)}, u32[]{:S(2)}) %collective-permute-start.18) | collective-permute-done | bytes 147488 | tf_op jit(solution)/shard_map/ppermute | solution.py:337
  101.0 1.0 add_add_fusion.1
  102.1 2.6 %collective-permute-start.22 = (f32[24,384]{1,0:T(8,128)S(1)}, f32[24,384]{1,0:T(8,128)S(1)}, u32[]{:S(2)}, u32[]{:S(2)}) collective-permute-start(f32[24,384]{1,0:T(8,128)S(1)} %get-tuple-element.100), channel_id=1, source_target_pairs={{0,6},{1,7},{2,4},{3,5},{4,2},{5,3},{6,0},{7,1},{8,14},{9,15},{10,... | collective-permute-start | bytes 110600 | tf_op jit(solution)/shard_map/ppermute | solution.py:153
  104.6 2.6 %collective-permute-start.21 = (f32[24,384]{1,0:T(8,128)S(1)}, f32[24,384]{1,0:T(8,128)S(1)}, u32[]{:S(2)}, u32[]{:S(2)}) collective-permute-start(f32[24,384]{1,0:T(8,128)S(1)} %get-tuple-element.101), channel_id=1, source_target_pairs={{0,4},{1,5},{2,6},{3,7},{4,0},{5,1},{6,2},{7,3},{8,12},{9,13},{10,... | collective-permute-start | bytes 110600 | tf_op jit(solution)/shard_map/ppermute | solution.py:153
  107.2 1.9 %collective-permute-start.32 = (f32[24,384]{1,0:T(8,128)S(1)}, f32[24,384]{1,0:T(8,128)S(1)}, u32[]{:S(2)}, u32[]{:S(2)}) collective-permute-start(f32[24,384]{1,0:T(8,128)S(1)} %get-tuple-element.97), channel_id=1, source_target_pairs={{0,6},{1,7},{2,4},{3,5},{4,2},{5,3},{6,0},{7,1},{8,14},{9,15},{10,... | collective-permute-start | bytes 110600 | tf_op jit(solution)/shard_map/ppermute | solution.py:153
  109.1 1.7 %collective-permute-start.31 = (f32[24,384]{1,0:T(8,128)S(1)}, f32[24,384]{1,0:T(8,128)S(1)}, u32[]{:S(2)}, u32[]{:S(2)}) collective-permute-start(f32[24,384]{1,0:T(8,128)S(1)} %get-tuple-element.98), channel_id=1, source_target_pairs={{0,4},{1,5},{2,6},{3,7},{4,0},{5,1},{6,2},{7,3},{8,12},{9,13},{10,... | collective-permute-start | bytes 110600 | tf_op jit(solution)/shard_map/ppermute | solution.py:153
  110.8 0.9 collective-permute-start.30
  111.7 0.4 collective-permute-start.23
  112.1 1.0 collective-permute-start.24
  113.2 0.2 collective-permute-done.32
  113.4 2.5 %collective-permute-start.25 = (f32[24,384]{1,0:T(8,128)S(1)}, f32[24,384]{1,0:T(8,128)S(1)}, u32[]{:S(2)}, u32[]{:S(2)}) collective-permute-start(f32[24,384]{1,0:T(8,128)S(1)} %fusion.5.refs_0_), channel_id=1, source_target_pairs={{0,24},{8,0},{16,8},{24,16},{1,25},{9,1},{17,9},{25,17},{2,26},{10... | collective-permute-start | bytes 110600 | tf_op jit(solution)/shard_map/ppermute | solution.py:337
  115.9 0.1 collective-permute-start.33
  115.9 1.0 collective-permute-start.34
  116.9 2.8 %collective-permute-start.35 = (f32[24,384]{1,0:T(8,128)S(1)}, f32[24,384]{1,0:T(8,128)S(1)}, u32[]{:S(2)}, u32[]{:S(2)}) collective-permute-start(f32[24,384]{1,0:T(8,128)S(1)} %fusion.2.refs_4_), channel_id=1, source_target_pairs={{0,24},{8,0},{16,8},{24,16},{1,25},{9,1},{17,9},{25,17},{2,26},{10... | collective-permute-start | bytes 110600 | tf_op jit(solution)/shard_map/ppermute | solution.py:337
  119.8 1.0 collective-permute-done.33.refs_5_
  120.8 0.6 collective-permute-done.35.refs_7_
  121.4 0.7 place.1
  (43 shorter events, 0.2 us)
Async XLA Ops:
  0.6 26.2 %copy-start = (bf16[512,256]{1,0:T(8,128)(2,1)S(1)}, bf16[512,256]{1,0:T(8,128)(2,1)}, u32[]{:S(2)}) copy-start(bf16[512,256]{1,0:T(8,128)(2,1)} %constant.45.clone.m_ref) | copy-start | bytes 786436
  0.6 5.3 %copy-start.1 = (f32[2,2048]{1,0:T(2,128)S(1)}, f32[2,2048]{1,0:T(2,128)}, u32[]{:S(2)}) copy-start(f32[2,2048]{1,0:T(2,128)} %param.4) | copy-start | bytes 49156
  0.7 26.2 %all-to-all-start = ((f32[96,2,2048]{2,1,0:T(2,128)}), f32[96,2,2048]{2,1,0:T(2,128)S(1)}, u32[]{:S(2)}, u32[]{:S(2)}) async-start(f32[96,2,2048]{2,1,0:T(2,128)} %param.3), calls=%async_computation | async-start | bytes 3145728 | tf_op jit(solution)/shard_map/all_to_all | solution.py:358
  6.0 19.8 %collective-permute-start = (f32[32,128]{1,0:T(8,128)S(1)}, f32[32,128]{1,0:T(8,128)S(1)}, u32[]{:S(2)}, u32[]{:S(2)}) collective-permute-start(f32[32,128]{1,0:T(8,128)S(1)} %bitcast.54), channel_id=1, source_target_pairs={{0,24},{8,0},{16,8},{24,16},{1,25},{9,1},{17,9},{25,17},{2,26},{10... | collective-permute-start | bytes 49160 | tf_op jit(solution)/shard_map/ppermute | solution.py:337
  8.9 16.9 %collective-permute-start.1 = (f32[32,128]{1,0:T(8,128)S(1)}, f32[32,128]{1,0:T(8,128)S(1)}, u32[]{:S(2)}, u32[]{:S(2)}) collective-permute-start(f32[32,128]{1,0:T(8,128)S(1)} %bitcast.55), channel_id=1, source_target_pairs={{0,16},{8,24},{16,0},{24,8},{1,17},{9,25},{17,1},{25,9},{2,18},{10... | collective-permute-start | bytes 49160 | tf_op jit(solution)/shard_map/ppermute | solution.py:337
  9.4 17.4 %collective-permute-start.2 = (f32[32,128]{1,0:T(8,128)S(1)}, f32[32,128]{1,0:T(8,128)S(1)}, u32[]{:S(2)}, u32[]{:S(2)}) collective-permute-start(f32[32,128]{1,0:T(8,128)S(1)} %bitcast.56), channel_id=1, source_target_pairs={{0,8},{8,16},{16,24},{24,0},{1,9},{9,17},{17,25},{25,1},{2,10},{10... | collective-permute-start | bytes 49160 | tf_op jit(solution)/shard_map/ppermute | solution.py:337
  28.6 6.9 %collective-permute-start.3 = (f32[32,8,128]{2,1,0:T(8,128)S(1)}, f32[32,8,128]{2,1,0:T(8,128)S(1)}, u32[]{:S(2)}, u32[]{:S(2)}) collective-permute-start(f32[32,8,128]{2,1,0:T(8,128)S(1)} %get-tuple-element.50), channel_id=1, source_target_pairs={{0,8},{8,16},{16,24},{24,0},{1,9},{9,17},{17,25},{25,1},{2,10},{10... | collective-permute-start | bytes 393224 | tf_op jit(solution)/shard_map/ppermute | solution.py:337
  29.2 6.4 %collective-permute-start.4 = (f32[32,8,128]{2,1,0:T(8,128)S(1)}, f32[32,8,128]{2,1,0:T(8,128)S(1)}, u32[]{:S(2)}, u32[]{:S(2)}) collective-permute-start(f32[32,8,128]{2,1,0:T(8,128)S(1)} %get-tuple-element.51), channel_id=1, source_target_pairs={{0,16},{8,24},{16,0},{24,8},{1,17},{9,25},{17,1},{25,9},{2,18},{10... | collective-permute-start | bytes 393224 | tf_op jit(solution)/shard_map/ppermute | solution.py:337
  29.8 5.8 %collective-permute-start.5 = (f32[32,8,128]{2,1,0:T(8,128)S(1)}, f32[32,8,128]{2,1,0:T(8,128)S(1)}, u32[]{:S(2)}, u32[]{:S(2)}) collective-permute-start(f32[32,8,128]{2,1,0:T(8,128)S(1)} %get-tuple-element.52), channel_id=1, source_target_pairs={{0,24},{8,0},{16,8},{24,16},{1,25},{9,1},{17,9},{25,17},{2,26},{10... | collective-permute-start | bytes 393224 | tf_op jit(solution)/shard_map/ppermute | solution.py:337
  35.5 0.9 copy-start.2
  36.4 34.1 %all-to-all-start.1 = ((f32[8,32,512]{2,1,0:T(8,128)}), f32[8,32,512]{2,1,0:T(8,128)S(1)}, u32[]{:S(2)}, u32[]{:S(2)}) async-start(f32[8,32,512]{2,1,0:T(8,128)} %pack.3), calls=%async_computation.1 | async-start | bytes 1048576 | tf_op jit(solution)/shard_map/all_to_all | solution.py:369
  41.4 10.4 %collective-permute-start.6 = (f32[32,16,128]{2,1,0:T(8,128)}, f32[32,16,128]{2,1,0:T(8,128)S(1)}, u32[]{:S(2)}, u32[]{:S(2)}) collective-permute-start(f32[32,16,128]{2,1,0:T(8,128)} %copy-done.2), channel_id=1, source_target_pairs={{0,8},{8,16},{16,24},{24,0},{1,9},{9,17},{17,25},{25,1},{2,10},{10... | collective-permute-start | bytes 786440 | tf_op jit(solution)/shard_map/ppermute | solution.py:337
  43.9 13.2 %collective-permute-start.7 = (f32[32,16,128]{2,1,0:T(8,128)S(1)}, f32[32,16,128]{2,1,0:T(8,128)S(1)}, u32[]{:S(2)}, u32[]{:S(2)}) collective-permute-start(f32[32,16,128]{2,1,0:T(8,128)S(1)} %get-tuple-element.57), channel_id=1, source_target_pairs={{0,16},{8,24},{16,0},{24,8},{1,17},{9,25},{17,1},{25,9},{2,18},{10... | collective-permute-start | bytes 786440 | tf_op jit(solution)/shard_map/ppermute | solution.py:337
  44.9 12.2 %collective-permute-start.8 = (f32[32,16,128]{2,1,0:T(8,128)S(1)}, f32[32,16,128]{2,1,0:T(8,128)S(1)}, u32[]{:S(2)}, u32[]{:S(2)}) collective-permute-start(f32[32,16,128]{2,1,0:T(8,128)S(1)} %get-tuple-element.58), channel_id=1, source_target_pairs={{0,24},{8,0},{16,8},{24,16},{1,25},{9,1},{17,9},{25,17},{2,26},{10... | collective-permute-start | bytes 786440 | tf_op jit(solution)/shard_map/ppermute | solution.py:337
  57.9 7.6 %collective-permute-start.9 = (f32[64,512]{1,0:T(8,128)S(1)}, f32[64,512]{1,0:T(8,128)S(1)}, u32[]{:S(2)}, u32[]{:S(2)}) collective-permute-start(f32[64,512]{1,0:T(8,128)S(1)} %get-tuple-element.59), channel_id=1, source_target_pairs={{0,7},{1,6},{2,5},{3,4},{4,3},{5,2},{6,1},{7,0},{8,15},{9,14},{10,... | collective-permute-start | bytes 393224 | tf_op jit(solution)/shard_map/ppermute | solution.py:153
  61.0 8.0 %collective-permute-start.10 = (f32[64,512]{1,0:T(8,128)S(1)}, f32[64,512]{1,0:T(8,128)S(1)}, u32[]{:S(2)}, u32[]{:S(2)}) collective-permute-start(f32[64,512]{1,0:T(8,128)S(1)} %get-tuple-element.68), channel_id=1, source_target_pairs={{0,1},{1,0},{2,3},{3,2},{4,5},{5,4},{6,7},{7,6},{8,9},{9,8},{10,11... | collective-permute-start | bytes 393224 | tf_op jit(solution)/shard_map/ppermute | solution.py:153
  61.5 11.2 %collective-permute-start.11 = (f32[64,512]{1,0:T(8,128)}, f32[64,512]{1,0:T(8,128)S(1)}, u32[]{:S(2)}, u32[]{:S(2)}) collective-permute-start(f32[64,512]{1,0:T(8,128)} %get-tuple-element.69), channel_id=1, source_target_pairs={{0,2},{1,3},{2,0},{3,1},{4,6},{5,7},{6,4},{7,5},{8,10},{9,11},{10,... | collective-permute-start | bytes 393224 | tf_op jit(solution)/shard_map/ppermute | solution.py:153
  61.5 13.2 %collective-permute-start.12 = (f32[64,512]{1,0:T(8,128)S(1)}, f32[64,512]{1,0:T(8,128)S(1)}, u32[]{:S(2)}, u32[]{:S(2)}) collective-permute-start(f32[64,512]{1,0:T(8,128)S(1)} %get-tuple-element.70), channel_id=1, source_target_pairs={{0,3},{1,2},{2,1},{3,0},{4,7},{5,6},{6,5},{7,4},{8,11},{9,10},{10,... | collective-permute-start | bytes 393224 | tf_op jit(solution)/shard_map/ppermute | solution.py:153
  62.8 12.5 %collective-permute-start.13 = (f32[64,512]{1,0:T(8,128)S(1)}, f32[64,512]{1,0:T(8,128)S(1)}, u32[]{:S(2)}, u32[]{:S(2)}) collective-permute-start(f32[64,512]{1,0:T(8,128)S(1)} %get-tuple-element.71), channel_id=1, source_target_pairs={{0,4},{1,5},{2,6},{3,7},{4,0},{5,1},{6,2},{7,3},{8,12},{9,13},{10,... | collective-permute-start | bytes 393224 | tf_op jit(solution)/shard_map/ppermute | solution.py:153
  65.5 16.1 %collective-permute-start.14 = (f32[64,512]{1,0:T(8,128)S(1)}, f32[64,512]{1,0:T(8,128)}, u32[]{:S(2)}, u32[]{:S(2)}) collective-permute-start(f32[64,512]{1,0:T(8,128)S(1)} %get-tuple-element.72), channel_id=1, source_target_pairs={{0,5},{1,4},{2,7},{3,6},{4,1},{5,0},{6,3},{7,2},{8,13},{9,12},{10,... | collective-permute-start | bytes 393224 | tf_op jit(solution)/shard_map/ppermute | solution.py:153
  69.0 12.6 %collective-permute-start.15 = (f32[64,512]{1,0:T(8,128)S(1)}, f32[64,512]{1,0:T(8,128)}, u32[]{:S(2)}, u32[]{:S(2)}) collective-permute-start(f32[64,512]{1,0:T(8,128)S(1)} %get-tuple-element.73), channel_id=1, source_target_pairs={{0,6},{1,7},{2,4},{3,5},{4,2},{5,3},{6,0},{7,1},{8,14},{9,15},{10,... | collective-permute-start | bytes 393224 | tf_op jit(solution)/shard_map/ppermute | solution.py:153
  74.7 0.7 copy-start.3
  75.4 0.7 copy-start.5
  81.6 0.9 copy-start.4
  82.5 0.9 copy-start.6
  86.0 2.1 %collective-permute-start.16 = (f32[384,384]{1,0:T(8,128)S(1)}, f32[384,384]{1,0:T(8,128)S(1)}, u32[]{:S(2)}, u32[]{:S(2)}) collective-permute-start(f32[384,384]{1,0:T(8,128)S(1)} %get-tuple-element.77), channel_id=1, source_target_pairs={{0,1},{1,0},{2,3},{3,2},{4,5},{5,4},{6,7},{7,6},{8,9},{9,8},{10,11... | collective-permute-start | bytes 1769480 | tf_op jit(solution)/shard_map/ppermute | solution.py:390
  86.3 6.0 %collective-permute-start.26 = (f32[384,384]{1,0:T(8,128)S(1)}, f32[384,384]{1,0:T(8,128)S(1)}, u32[]{:S(2)}, u32[]{:S(2)}) collective-permute-start(f32[384,384]{1,0:T(8,128)S(1)} %get-tuple-element.87), channel_id=1, source_target_pairs={{0,1},{1,0},{2,3},{3,2},{4,5},{5,4},{6,7},{7,6},{8,9},{9,8},{10,11... | collective-permute-start | bytes 1769480 | tf_op jit(solution)/shard_map/ppermute | solution.py:390
  88.2 8.2 %collective-permute-start.19 = (f32[4,24,384]{2,1,0:T(8,128)S(1)}, f32[4,24,384]{2,1,0:T(8,128)S(1)}, u32[]{:S(2)}, u32[]{:S(2)}) collective-permute-start(f32[4,24,384]{2,1,0:T(8,128)S(1)} %get-tuple-element.85), channel_id=1, source_target_pairs={{0,24},{8,0},{16,8},{24,16},{1,25},{9,1},{17,9},{25,17},{2,26},{10... | collective-permute-start | bytes 442376 | tf_op jit(solution)/shard_map/ppermute | solution.py:337
  90.5 10.5 %collective-permute-start.18 = (f32[4,24,384]{2,1,0:T(8,128)S(1)}, f32[4,24,384]{2,1,0:T(8,128)}, u32[]{:S(2)}, u32[]{:S(2)}) collective-permute-start(f32[4,24,384]{2,1,0:T(8,128)S(1)} %get-tuple-element.84), channel_id=1, source_target_pairs={{0,16},{8,24},{16,0},{24,8},{1,17},{9,25},{17,1},{25,9},{2,18},{10... | collective-permute-start | bytes 442376 | tf_op jit(solution)/shard_map/ppermute | solution.py:337
  91.5 9.5 %collective-permute-start.17 = (f32[4,24,384]{2,1,0:T(8,128)S(1)}, f32[4,24,384]{2,1,0:T(8,128)}, u32[]{:S(2)}, u32[]{:S(2)}) collective-permute-start(f32[4,24,384]{2,1,0:T(8,128)S(1)} %get-tuple-element.83), channel_id=1, source_target_pairs={{0,8},{8,16},{16,24},{24,0},{1,9},{9,17},{17,25},{25,1},{2,10},{10... | collective-permute-start | bytes 442376 | tf_op jit(solution)/shard_map/ppermute | solution.py:337
  92.4 14.8 %collective-permute-start.29 = (f32[4,24,384]{2,1,0:T(8,128)S(1)}, f32[4,24,384]{2,1,0:T(8,128)S(1)}, u32[]{:S(2)}, u32[]{:S(2)}) collective-permute-start(f32[4,24,384]{2,1,0:T(8,128)S(1)} %get-tuple-element.95), channel_id=1, source_target_pairs={{0,24},{8,0},{16,8},{24,16},{1,25},{9,1},{17,9},{25,17},{2,26},{10... | collective-permute-start | bytes 442376 | tf_op jit(solution)/shard_map/ppermute | solution.py:337
  95.3 11.8 %collective-permute-start.28 = (f32[4,24,384]{2,1,0:T(8,128)S(1)}, f32[4,24,384]{2,1,0:T(8,128)S(1)}, u32[]{:S(2)}, u32[]{:S(2)}) collective-permute-start(f32[4,24,384]{2,1,0:T(8,128)S(1)} %get-tuple-element.94), channel_id=1, source_target_pairs={{0,16},{8,24},{16,0},{24,8},{1,17},{9,25},{17,1},{25,9},{2,18},{10... | collective-permute-start | bytes 442376 | tf_op jit(solution)/shard_map/ppermute | solution.py:337
  96.4 10.8 %collective-permute-start.27 = (f32[4,24,384]{2,1,0:T(8,128)S(1)}, f32[4,24,384]{2,1,0:T(8,128)S(1)}, u32[]{:S(2)}, u32[]{:S(2)}) collective-permute-start(f32[4,24,384]{2,1,0:T(8,128)S(1)} %get-tuple-element.93), channel_id=1, source_target_pairs={{0,8},{8,16},{16,24},{24,0},{1,9},{9,17},{17,25},{25,1},{2,10},{10... | collective-permute-start | bytes 442376 | tf_op jit(solution)/shard_map/ppermute | solution.py:337
  102.1 8.7 %collective-permute-start.22 = (f32[24,384]{1,0:T(8,128)S(1)}, f32[24,384]{1,0:T(8,128)S(1)}, u32[]{:S(2)}, u32[]{:S(2)}) collective-permute-start(f32[24,384]{1,0:T(8,128)S(1)} %get-tuple-element.100), channel_id=1, source_target_pairs={{0,6},{1,7},{2,4},{3,5},{4,2},{5,3},{6,0},{7,1},{8,14},{9,15},{10,... | collective-permute-start | bytes 110600 | tf_op jit(solution)/shard_map/ppermute | solution.py:153
  104.6 7.1 %collective-permute-start.21 = (f32[24,384]{1,0:T(8,128)S(1)}, f32[24,384]{1,0:T(8,128)S(1)}, u32[]{:S(2)}, u32[]{:S(2)}) collective-permute-start(f32[24,384]{1,0:T(8,128)S(1)} %get-tuple-element.101), channel_id=1, source_target_pairs={{0,4},{1,5},{2,6},{3,7},{4,0},{5,1},{6,2},{7,3},{8,12},{9,13},{10,... | collective-permute-start | bytes 110600 | tf_op jit(solution)/shard_map/ppermute | solution.py:153
  107.2 4.6 %collective-permute-start.20 = (f32[24,384]{1,0:T(8,128)S(1)}, f32[24,384]{1,0:T(8,128)S(1)}, u32[]{:S(2)}, u32[]{:S(2)}) collective-permute-start(f32[24,384]{1,0:T(8,128)S(1)} %get-tuple-element.99), channel_id=1, source_target_pairs={{0,2},{1,3},{2,0},{3,1},{4,6},{5,7},{6,4},{7,5},{8,10},{9,11},{10,... | collective-permute-start | bytes 110600 | tf_op jit(solution)/shard_map/ppermute | solution.py:153
  107.2 6.1 %collective-permute-start.32 = (f32[24,384]{1,0:T(8,128)S(1)}, f32[24,384]{1,0:T(8,128)S(1)}, u32[]{:S(2)}, u32[]{:S(2)}) collective-permute-start(f32[24,384]{1,0:T(8,128)S(1)} %get-tuple-element.97), channel_id=1, source_target_pairs={{0,6},{1,7},{2,4},{3,5},{4,2},{5,3},{6,0},{7,1},{8,14},{9,15},{10,... | collective-permute-start | bytes 110600 | tf_op jit(solution)/shard_map/ppermute | solution.py:153
  109.1 6.7 %collective-permute-start.31 = (f32[24,384]{1,0:T(8,128)S(1)}, f32[24,384]{1,0:T(8,128)S(1)}, u32[]{:S(2)}, u32[]{:S(2)}) collective-permute-start(f32[24,384]{1,0:T(8,128)S(1)} %get-tuple-element.98), channel_id=1, source_target_pairs={{0,4},{1,5},{2,6},{3,7},{4,0},{5,1},{6,2},{7,3},{8,12},{9,13},{10,... | collective-permute-start | bytes 110600 | tf_op jit(solution)/shard_map/ppermute | solution.py:153
  110.8 5.1 %collective-permute-start.30 = (f32[24,384]{1,0:T(8,128)S(1)}, f32[24,384]{1,0:T(8,128)S(1)}, u32[]{:S(2)}, u32[]{:S(2)}) collective-permute-start(f32[24,384]{1,0:T(8,128)S(1)} %get-tuple-element.96), channel_id=1, source_target_pairs={{0,2},{1,3},{2,0},{3,1},{4,6},{5,7},{6,4},{7,5},{8,10},{9,11},{10,... | collective-permute-start | bytes 110600 | tf_op jit(solution)/shard_map/ppermute | solution.py:153
  111.7 5.2 %collective-permute-start.23 = (f32[24,384]{1,0:T(8,128)S(1)}, f32[24,384]{1,0:T(8,128)S(1)}, u32[]{:S(2)}, u32[]{:S(2)}) collective-permute-start(f32[24,384]{1,0:T(8,128)S(1)} %fusion.5.refs_0_), channel_id=1, source_target_pairs={{0,8},{8,16},{16,24},{24,0},{1,9},{9,17},{17,25},{25,1},{2,10},{10... | collective-permute-start | bytes 110600 | tf_op jit(solution)/shard_map/ppermute | solution.py:337
  112.1 7.6 %collective-permute-start.24 = (f32[24,384]{1,0:T(8,128)S(1)}, f32[24,384]{1,0:T(8,128)S(1)}, u32[]{:S(2)}, u32[]{:S(2)}) collective-permute-start(f32[24,384]{1,0:T(8,128)S(1)} %fusion.5.refs_0_), channel_id=1, source_target_pairs={{0,16},{8,24},{16,0},{24,8},{1,17},{9,25},{17,1},{25,9},{2,18},{10... | collective-permute-start | bytes 110600 | tf_op jit(solution)/shard_map/ppermute | solution.py:337
  113.4 6.4 %collective-permute-start.25 = (f32[24,384]{1,0:T(8,128)S(1)}, f32[24,384]{1,0:T(8,128)S(1)}, u32[]{:S(2)}, u32[]{:S(2)}) collective-permute-start(f32[24,384]{1,0:T(8,128)S(1)} %fusion.5.refs_0_), channel_id=1, source_target_pairs={{0,24},{8,0},{16,8},{24,16},{1,25},{9,1},{17,9},{25,17},{2,26},{10... | collective-permute-start | bytes 110600 | tf_op jit(solution)/shard_map/ppermute | solution.py:337
  115.9 4.9 %collective-permute-start.33 = (f32[24,384]{1,0:T(8,128)S(1)}, f32[24,384]{1,0:T(8,128)S(1)}, u32[]{:S(2)}, u32[]{:S(2)}) collective-permute-start(f32[24,384]{1,0:T(8,128)S(1)} %fusion.2.refs_4_), channel_id=1, source_target_pairs={{0,8},{8,16},{16,24},{24,0},{1,9},{9,17},{17,25},{25,1},{2,10},{10... | collective-permute-start | bytes 110600 | tf_op jit(solution)/shard_map/ppermute | solution.py:337
  115.9 4.8 %collective-permute-start.34 = (f32[24,384]{1,0:T(8,128)S(1)}, f32[24,384]{1,0:T(8,128)S(1)}, u32[]{:S(2)}, u32[]{:S(2)}) collective-permute-start(f32[24,384]{1,0:T(8,128)S(1)} %fusion.2.refs_4_), channel_id=1, source_target_pairs={{0,16},{8,24},{16,0},{24,8},{1,17},{9,25},{17,1},{25,9},{2,18},{10... | collective-permute-start | bytes 110600 | tf_op jit(solution)/shard_map/ppermute | solution.py:337
  116.9 4.5 %collective-permute-start.35 = (f32[24,384]{1,0:T(8,128)S(1)}, f32[24,384]{1,0:T(8,128)S(1)}, u32[]{:S(2)}, u32[]{:S(2)}) collective-permute-start(f32[24,384]{1,0:T(8,128)S(1)} %fusion.2.refs_4_), channel_id=1, source_target_pairs={{0,24},{8,0},{16,8},{24,16},{1,25},{9,1},{17,9},{25,17},{2,26},{10... | collective-permute-start | bytes 110600 | tf_op jit(solution)/shard_map/ppermute | solution.py:337

commit v11 on v10

--- a/solution.py
+++ b/solution.py
@@ -33,19 +33,24 @@
     return matrix.astype(ml_dtypes.bfloat16)
 
 
-def filter_kernel(space, layers, tiles, chunk, pitch, offset, x_ref, m_ref, *refs):
+def filter_kernel(space, layers, tiles, chunk, pitch, x_ref, m_ref, *refs):
     f0, f1, coef, mm, hi, lo = refs[-6:]
     rows = tiles * layers
-    if len(refs) == 2 * space + 7:
-        joined = refs[2 * space]
+    here = lax.axis_index("space")
+
+    def slab_of(s):
+        slab = here + s
+        return jnp.where(slab >= space, slab - space, slab)
+
+    if pitch > chunk:
+        out_refs, joined = refs[:space], refs[space]
         for s in range(space):
-            joined[s * rows : (s + 1) * rows, :] = refs[s][...]
-        out_refs = refs[space : 2 * space]
+            first = pl.multiple_of((slab_of(s) * pitch + chunk) * rows, rows)
+            joined[s * rows : (s + 1) * rows, :] = x_ref[pl.ds(first, rows), :]
     else:
         joined, out_refs = refs[0], refs[1 : 1 + space]
     planes = space * layers
     quads, height, wide = f0.shape
-    here = lax.axis_index("space")
 
     def put(f, j, v):
         f[j] = v
@@ -60,9 +65,7 @@
             for p in range(planes):
                 s, l = divmod(p, layers)
                 row = (2 * j + half) * layers + l
-                slab = here + s
-                slab = jnp.where(slab >= space, slab - space, slab)
-                column.append(x_ref[pl.ds((slab * pitch + offset) * rows + row, chunk, stride=rows), :])
+                column.append(x_ref[pl.ds(slab_of(s) * (pitch * rows) + row, chunk, stride=rows), :])
                 w = joined[s * rows + row : s * rows + row + 1, :]
                 coef[j, p * chunk : (p + 1) * chunk, half * LANES : (half + 1) * LANES] = jnp.broadcast_to(
                     0.5 * w - 1.125, (chunk, LANES)
@@ -112,18 +115,18 @@
 VMEM_SPEC = pl.BlockSpec(memory_space=pltpu.VMEM)
 
 
-def run_filter(x, matrix, vs, offset, space, layers, tiles, chunk):
+def run_filter(x, matrix, joined, space, layers, tiles, chunk):
     rows = tiles * layers
     planes = space * layers
     pitch = x.shape[0] // (space * rows)
     shape = (tiles // 2, planes * chunk, 2 * LANES)
     out_shape = [jax.ShapeDtypeStruct((rows, chunk, LANES), jnp.float32)] * space
-    if len(vs) > 1:
+    if not joined:
         out_shape.append(jax.ShapeDtypeStruct((space * rows, LANES), jnp.float32))
     return pl.pallas_call(
-        functools.partial(filter_kernel, space, layers, tiles, chunk, pitch, offset),
+        functools.partial(filter_kernel, space, layers, tiles, chunk, pitch),
         out_shape=out_shape,
-        in_specs=[VMEM_SPEC] * (2 + len(vs)),
+        in_specs=[VMEM_SPEC] * (2 + len(joined)),
         out_specs=[VMEM_SPEC] * len(out_shape),
         scratch_shapes=[pltpu.VMEM(shape, jnp.float32)] * 4 + [pltpu.VMEM(shape, jnp.bfloat16)] * 2,
         compiler_params=pltpu.CompilerParams(vmem_limit_bytes=VMEM_LIMIT),
@@ -133,7 +136,7 @@
             transcendentals=0,
         ),
         name="filter",
-    )(x, matrix, *vs)
+    )(x, matrix, *joined)
 
 
 def partner(index, size, k, forward=True):
@@ -353,18 +356,23 @@
         return x.reshape(n, layers, tiles, LANES).transpose(0, 2, 1, 3).reshape(n * rows, LANES)
 
     matrix = jnp.asarray(plane_matrix())
-    own_v = as_rows(potential[None])
-    vs = [own_v] + [rotate(own_v, "space", space - k) for k in range(1, space)]
-    arrived = as_rows(lax.all_to_all(orbitals, "space", split_axis=0, concat_axis=0, tiled=True))
-
-    def filtered(offset, size):
-        outs = run_filter(arrived, matrix, vs, offset, space, layers, tiles, size)
-        vs[:] = [outs[-1]] if len(vs) > 1 else vs
-        return [outs[0]] + [rotate(outs[k], "space", k) for k in range(1, space)]
-
-    made = [filtered(sum(sizes[:c]), size) for c, size in enumerate(sizes)]
-    if len(made) > 1:
-        made[0], made[1][0] = lax.optimization_barrier((made[0], made[1][0]))
+    def over_space(x):
+        x = x.reshape((-1,) + x.shape[2:])
+        return lax.all_to_all(x, "space", split_axis=0, concat_axis=0, tiled=True)
+
+    by_group = orbitals.reshape(space, own, layers, plane)
+    slab_v = jnp.broadcast_to(potential[None, None], (space, 1, layers, plane))
+    arrived = [over_space(jnp.concatenate([by_group[:, :chunk], slab_v], axis=1))]
+    if len(sizes) > 1:
+        arrived[0], late = lax.optimization_barrier((arrived[0], by_group[:, chunk:]))
+        arrived.append(over_space(late))
+
+    joined = []
+    made = []
+    for size, x in zip(sizes, arrived):
+        outs = run_filter(as_rows(x), matrix, joined, space, layers, tiles, size)
+        joined = joined or [outs[-1]]
+        made.append([outs[0]] + [rotate(outs[k], "space", k) for k in range(1, space)])
     head = pack(made[0], space, band, share, sizes[0], False)[0]
     head = lax.all_to_all(head, "band", split_axis=0, concat_axis=0, tiled=True)
     parts = [head]

time: 122 us -> 127 us (1.041)
  waiting for transfers between devices: 44.5 us -> 46.7 us
    all_to_all x1 -> x2, waiting for transfers between devices: 0.01 us -> 7.68 us  [over_space(): return lax.all_to_all(x, 'space', split_axis=0, concat_axis=0, tiled=True)]
    ppermute x21 -> x18, waiting for transfers between devices: 33.3 us -> 26.7 us  [rotate(): return lax.ppermute(x, axis, [(i, (i + step) % size) for i in range(size)])]
    all_to_all x1 -> x2, starting transfers between devices: 5.31 us -> 8.68 us  [over_space(): return lax.all_to_all(x, 'space', split_axis=0, concat_axis=0, tiled=True)]
    unnamed x14 -> x4, local copies, waits for them, and re-layouts: 3.13 us -> 0.01 us
    slice x0 -> x2, local copies, waits for them, and re-layouts: none -> 2.24 us  [the longest x1 1.2 us: shards(): by_group[:, :chunk]]
    ppermute x21 -> x18, starting transfers between devices: 28.3 us -> 26.3 us  [rotate(): return lax.ppermute(x, axis, [(i, (i + step) % size) for i in range(size)])]
  transfers between devices with their start and end apart: 38 -> 36, of which waited for: 13 -> 12; matrix products, arithmetic and copies ran while one was open for 1% -> 2% of each run, Pallas kernels for 7% -> 8%
where the time goes in v11:
time: 127 us
  starting transfers between devices  59.8 us (47%)
  waiting for transfers between devices  46.7 us (37%)
  Pallas kernels  14 us (11%)
  local copies, waits for them, and re-layouts  3.02 us (2%)
  other arithmetic  2.32 us (2%)
    ppermute x18, waiting for transfers between devices, rotate(): return lax.ppermute(x, axis, [(i, (i + step) % size) for i in range(size)])  26.7 us
    ppermute x18, starting transfers between devices, rotate(): return lax.ppermute(x, axis, [(i, (i + step) % size) for i in range(size)])  26.3 us
    ppermute x13, starting transfers between devices, exchange(): return lax.ppermute(x, axis, pairs)  19.3 us
    ppermute x13, waiting for transfers between devices, exchange(): return lax.ppermute(x, axis, pairs)  11.6 us
    all_to_all x2, starting transfers between devices, over_space(): return lax.all_to_all(x, 'space', split_axis=0, concat_axis=0, tiled=True)  8.68 us
    all_to_all x2, waiting for transfers between devices, over_space(): return lax.all_to_all(x, 'space', split_axis=0, concat_axis=0, tiled=True)  7.68 us
    pallas_call x2, Pallas kernels, run_filter(): pl.pallas_call(functools.partial(filter_kernel, space, layers, tiles, chu...  5.08 us
    all_to_all x1, starting transfers between devices, shards(): head = lax.all_to_all(head, 'band', split_axis=0, concat_axis=0, tiled=True)  4.89 us
  transfers between devices with their start and end apart: 36, of which 12 were waited for; matrix products, arithmetic and copies ran while one was open for 2% of the time, Pallas kernels for 8%

profile of v11, /device:TPU:0, one launch (start us, length us, event | category | flops | bytes accessed | tf_op | source)
XLA Modules:
  0.0 126.7 jit_solution(4891896035064715174)
XLA Ops:
  0.6 1.2 slice.8
  1.8 0.7 broadcast_in_dim.2
  2.6 1.2 pad_maximum_fusion
  3.7 5.2 %all-to-all-start = ((f32[36,2,2048]{2,1,0:T(2,128)}), f32[36,2,2048]{2,1,0:T(2,128)S(1)}, u32[]{:S(2)}, u32[]{:S(2)}) async-start(f32[36,2,2048]{2,1,0:T(2,128)} %bitcast.1), calls=%async_computation | async-start | bytes 1179648 | tf_op jit(solution)/shard_map/all_to_all | solution.py:361
  8.9 1.0 slice.9
  10.0 7.7 %all-to-all-done = f32[36,2,2048]{2,1,0:T(2,128)S(1)} async-done(((f32[36,2,2048]{2,1,0:T(2,128)}), f32[36,2,2048]{2,1,0:T(2,128)S(1)}, u32[]{:S(2)}, u32[]{:S(2)}) %all-to-all-start) | async-done | bytes 589856 | tf_op jit(solution)/shard_map/all_to_all | solution.py:361
  17.6 3.5 %all-to-all-start.1 = ((f32[64,2,2048]{2,1,0:T(2,128)}), f32[64,2,2048]{2,1,0:T(2,128)S(1)}, u32[]{:S(2)}, u32[]{:S(2)}) async-start(f32[64,2,2048]{2,1,0:T(2,128)} %bitcast.2), calls=%async_computation.1 | async-start | bytes 2097152 | tf_op jit(solution)/shard_map/all_to_all | solution.py:361
  21.2 1.8 %filter.2 = (f32[32,8,128]{2,1,0:T(8,128)S(1)}, f32[32,8,128]{2,1,0:T(8,128)S(1)}, f32[32,8,128]{2,1,0:T(8,128)S(1)}, f32[32,8,128]{2,1,0:T(8,128)S(1)}, f32[128,128]{1,0:T(8,128)S(1)}) custom-call(f32[1152,128]{1,0:T(8,128)S(1)} %bitcast.52, bf16[512,256]{1,0:T(8,128)(2,1)S(1)} %copy-done), custom_call_target="tpu_custom_call" | custom-call | flops 6553600 | bytes 1048576 | tf_op jit(solution)/shard_map/filter/pallas_call | solution.py:126
  22.9 2.0 %collective-permute-start.4 = (f32[32,8,128]{2,1,0:T(8,128)S(1)}, f32[32,8,128]{2,1,0:T(8,128)S(1)}, u32[]{:S(2)}, u32[]{:S(2)}) collective-permute-start(f32[32,8,128]{2,1,0:T(8,128)S(1)} %get-tuple-element.55), channel_id=1, source_target_pairs={{0,8},{8,16},{16,24},{24,0},{1,9},{9,17},{17,25},{25,1},{2,10},{10... | collective-permute-start | bytes 393224 | tf_op jit(solution)/shard_map/ppermute | solution.py:340
  25.0 1.5 %collective-permute-start.5 = (f32[32,8,128]{2,1,0:T(8,128)S(1)}, f32[32,8,128]{2,1,0:T(8,128)S(1)}, u32[]{:S(2)}, u32[]{:S(2)}) collective-permute-start(f32[32,8,128]{2,1,0:T(8,128)S(1)} %get-tuple-element.56), channel_id=1, source_target_pairs={{0,16},{8,24},{16,0},{24,8},{1,17},{9,25},{17,1},{25,9},{2,18},{10... | collective-permute-start | bytes 393224 | tf_op jit(solution)/shard_map/ppermute | solution.py:340
  26.4 1.5 %collective-permute-start.6 = (f32[32,8,128]{2,1,0:T(8,128)S(1)}, f32[32,8,128]{2,1,0:T(8,128)S(1)}, u32[]{:S(2)}, u32[]{:S(2)}) collective-permute-start(f32[32,8,128]{2,1,0:T(8,128)S(1)} %get-tuple-element.57), channel_id=1, source_target_pairs={{0,24},{8,0},{16,8},{24,16},{1,25},{9,1},{17,9},{25,17},{2,26},{10... | collective-permute-start | bytes 393224 | tf_op jit(solution)/shard_map/ppermute | solution.py:340
  27.9 11.3 %collective-permute-done.4.refs_1_ = f32[32,8,128]{2,1,0:T(8,128)S(1)} collective-permute-done((f32[32,8,128]{2,1,0:T(8,128)S(1)}, f32[32,8,128]{2,1,0:T(8,128)S(1)}, u32[]{:S(2)}, u32[]{:S(2)}) %collective-permute-start.4) | collective-permute-done | bytes 131104 | tf_op jit(solution)/shard_map/ppermute | solution.py:340
  39.2 0.4 collective-permute-done.5.refs_2_
  39.5 0.0 collective-permute-done.6.refs_3_
  39.6 0.9 pack.3
  40.4 4.9 %all-to-all-start.2 = ((f32[8,32,512]{2,1,0:T(8,128)}), f32[8,32,512]{2,1,0:T(8,128)S(1)}, u32[]{:S(2)}, u32[]{:S(2)}) async-start(f32[8,32,512]{2,1,0:T(8,128)} %pack.3), calls=%async_computation.2 | async-start | bytes 1048576 | tf_op jit(solution)/shard_map/all_to_all | solution.py:377
  45.3 3.3 %filter.3 = (f32[32,16,128]{2,1,0:T(8,128)S(1)}, f32[32,16,128]{2,1,0:T(8,128)S(1)}, f32[32,16,128]{2,1,0:T(8,128)S(1)}, f32[32,16,128]{2,1,0:T(8,128)S(1)}) custom-call(f32[2048,128]{1,0:T(8,128)S(1)} %bitcast.51, bf16[512,256]{1,0:T(8,128)(2,1)S(1)} %copy-done, f32[128,128]{1,0:T(8,128)S(1)} %get-tuple-element.48.refs_0_), custom_call_target="tpu_custom_call" | custom-call | flops 6553600 | bytes 2097152 | tf_op jit(solution)/shard_map/filter/pallas_call | solution.py:126
  48.7 1.5 %collective-permute-start = (f32[32,16,128]{2,1,0:T(8,128)S(1)}, f32[32,16,128]{2,1,0:T(8,128)S(1)}, u32[]{:S(2)}, u32[]{:S(2)}) collective-permute-start(f32[32,16,128]{2,1,0:T(8,128)S(1)} %get-tuple-element.50), channel_id=1, source_target_pairs={{0,8},{8,16},{16,24},{24,0},{1,9},{9,17},{17,25},{25,1},{2,10},{10... | collective-permute-start | bytes 786440 | tf_op jit(solution)/shard_map/ppermute | solution.py:340
  50.2 0.5 collective-permute-start.1
  50.7 2.4 %collective-permute-start.2 = (f32[32,16,128]{2,1,0:T(8,128)S(1)}, f32[32,16,128]{2,1,0:T(8,128)S(1)}, u32[]{:S(2)}, u32[]{:S(2)}) collective-permute-start(f32[32,16,128]{2,1,0:T(8,128)S(1)} %get-tuple-element.52), channel_id=1, source_target_pairs={{0,24},{8,0},{16,8},{24,16},{1,25},{9,1},{17,9},{25,17},{2,26},{10... | collective-permute-start | bytes 786440 | tf_op jit(solution)/shard_map/ppermute | solution.py:340
  53.1 5.7 %collective-permute-done.refs_1_.refs_5_ = f32[32,16,128]{2,1,0:T(8,128)S(1)} collective-permute-done((f32[32,16,128]{2,1,0:T(8,128)S(1)}, f32[32,16,128]{2,1,0:T(8,128)S(1)}, u32[]{:S(2)}, u32[]{:S(2)}) %collective-permute-start) | collective-permute-done | bytes 262176 | tf_op jit(solution)/shard_map/ppermute | solution.py:340
  58.8 5.2 %collective-permute-done.1.refs_2_.refs_6_ = f32[32,16,128]{2,1,0:T(8,128)S(1)} collective-permute-done((f32[32,16,128]{2,1,0:T(8,128)S(1)}, f32[32,16,128]{2,1,0:T(8,128)S(1)}, u32[]{:S(2)}, u32[]{:S(2)}) %collective-permute-start.1) | collective-permute-done | bytes 262176 | tf_op jit(solution)/shard_map/ppermute | solution.py:340
  63.9 0.0 collective-permute-done.2.refs_3_.refs_7_
  64.0 0.7 pack.2
  64.7 3.0 %collective-permute-start.3 = (f32[64,512]{1,0:T(8,128)S(1)}, f32[64,512]{1,0:T(8,128)S(1)}, u32[]{:S(2)}, u32[]{:S(2)}) collective-permute-start(f32[64,512]{1,0:T(8,128)S(1)} %get-tuple-element.53), channel_id=1, source_target_pairs={{0,7},{1,6},{2,5},{3,4},{4,3},{5,2},{6,1},{7,0},{8,15},{9,14},{10,... | collective-permute-start | bytes 393224 | tf_op jit(solution)/shard_map/ppermute | solution.py:156
  67.8 0.5 collective-permute-start.7
  68.3 0.0 collective-permute-start.8
  68.3 1.4 %collective-permute-start.9 = (f32[64,512]{1,0:T(8,128)S(1)}, f32[64,512]{1,0:T(8,128)S(1)}, u32[]{:S(2)}, u32[]{:S(2)}) collective-permute-start(f32[64,512]{1,0:T(8,128)S(1)} %get-tuple-element.64), channel_id=1, source_target_pairs={{0,3},{1,2},{2,1},{3,0},{4,7},{5,6},{6,5},{7,4},{8,11},{9,10},{10,... | collective-permute-start | bytes 393224 | tf_op jit(solution)/shard_map/ppermute | solution.py:156
  69.7 2.6 %collective-permute-done.3.refs_8_ = f32[64,512]{1,0:T(8,128)S(1)} collective-permute-done((f32[64,512]{1,0:T(8,128)S(1)}, f32[64,512]{1,0:T(8,128)S(1)}, u32[]{:S(2)}, u32[]{:S(2)}) %collective-permute-start.3) | collective-permute-done | bytes 131104 | tf_op jit(solution)/shard_map/ppermute | solution.py:156
  72.3 3.5 %collective-permute-start.11 = (f32[64,512]{1,0:T(8,128)S(1)}, f32[64,512]{1,0:T(8,128)}, u32[]{:S(2)}, u32[]{:S(2)}) collective-permute-start(f32[64,512]{1,0:T(8,128)S(1)} %get-tuple-element.66), channel_id=1, source_target_pairs={{0,5},{1,4},{2,7},{3,6},{4,1},{5,0},{6,3},{7,2},{8,13},{9,12},{10,... | collective-permute-start | bytes 393224 | tf_op jit(solution)/shard_map/ppermute | solution.py:156
  75.8 1.5 %collective-permute-start.12 = (f32[64,512]{1,0:T(8,128)S(1)}, f32[64,512]{1,0:T(8,128)}, u32[]{:S(2)}, u32[]{:S(2)}) collective-permute-start(f32[64,512]{1,0:T(8,128)S(1)} %get-tuple-element.67), channel_id=1, source_target_pairs={{0,6},{1,7},{2,4},{3,5},{4,2},{5,3},{6,0},{7,1},{8,14},{9,15},{10,... | collective-permute-start | bytes 393224 | tf_op jit(solution)/shard_map/ppermute | solution.py:156
  77.2 0.0 all-to-all-done.2.refs_0_
  77.2 2.3 %unpack.1 = f32[3072,128]{1,0:T(8,128)} custom-call(f32[32,8,128]{2,1,0:T(8,128)S(1)} %get-tuple-element.58.refs_0_, f32[32,8,128]{2,1,0:T(8,128)S(1)} %collective-permute-done.4.refs_1_, f32[32,8,128]{2,1,0:T(8,128)S(1)} %collective-permute-done.5.refs_2_, f32[32,8,128]{2,1,0:T(8,128)S(1)} %collective-permute-done.6.refs_3_, ...), custom_call_target="tpu_custom_call" | custom-call | bytes 3145728 | tf_op jit(solution)/shard_map/unpack/pallas_call | solution.py:206
  79.5 2.0 %collective-permute-done.9.refs_4_ = f32[64,512]{1,0:T(8,128)S(1)} collective-permute-done((f32[64,512]{1,0:T(8,128)S(1)}, f32[64,512]{1,0:T(8,128)S(1)}, u32[]{:S(2)}, u32[]{:S(2)}) %collective-permute-start.9) | collective-permute-done | bytes 131104 | tf_op jit(solution)/shard_map/ppermute | solution.py:156
  81.5 6.9 %collective-permute-done.11.refs_6_ = f32[64,512]{1,0:T(8,128)} collective-permute-done((f32[64,512]{1,0:T(8,128)S(1)}, f32[64,512]{1,0:T(8,128)}, u32[]{:S(2)}, u32[]{:S(2)}) %collective-permute-start.11) | collective-permute-done | bytes 131104 | tf_op jit(solution)/shard_map/ppermute | solution.py:156
  88.5 2.6 %gram.1 = (f32[384,384]{1,0:T(8,128)S(1)}, f32[384,384]{1,0:T(8,128)S(1)}, bf16[8,96,512]{2,1,0:T(8,128)(2,1)S(1)}, bf16[8,96,512]{2,1,0:T(8,128)(2,1)S(1)}) custom-call(f32[8,32,512]{2,1,0:T(8,128)S(1)} %all-to-all-done.2.refs_0_, f32[64,512]{1,0:T(8,128)S(1)} %get-tuple-element.61.refs_1_, f32[64,512]{1,0:T(8,128)S(1)} %collective-permute-done.7.refs_2_, ...), custom_call_target="tpu_custom_call" | custom-call | flops 905969664 | bytes 2752512 | tf_op jit(solution)/shard_map/gram/pallas_call | solution.py:262
  91.1 0.2 collective-permute-start.13
  91.3 0.4 collective-permute-start.23
  91.7 0.8 own_gram.2
  92.5 0.7 collective-permute-done.13
  93.2 0.1 combine.2
  93.2 1.7 %collective-permute-start.16 = (f32[4,24,384]{2,1,0:T(8,128)S(1)}, f32[4,24,384]{2,1,0:T(8,128)}, u32[]{:S(2)}, u32[]{:S(2)}) collective-permute-start(f32[4,24,384]{2,1,0:T(8,128)S(1)} %get-tuple-element.79), channel_id=1, source_target_pairs={{0,24},{8,0},{16,8},{24,16},{1,25},{9,1},{17,9},{25,17},{2,26},{10... | collective-permute-start | bytes 442376 | tf_op jit(solution)/shard_map/ppermute | solution.py:340
  94.9 1.5 %collective-permute-start.15 = (f32[4,24,384]{2,1,0:T(8,128)S(1)}, f32[4,24,384]{2,1,0:T(8,128)}, u32[]{:S(2)}, u32[]{:S(2)}) collective-permute-start(f32[4,24,384]{2,1,0:T(8,128)S(1)} %get-tuple-element.78), channel_id=1, source_target_pairs={{0,16},{8,24},{16,0},{24,8},{1,17},{9,25},{17,1},{25,9},{2,18},{10... | collective-permute-start | bytes 442376 | tf_op jit(solution)/shard_map/ppermute | solution.py:340
  96.4 0.8 own_gram.3
  97.2 0.1 combine.3
  97.3 3.0 %collective-permute-start.26 = (f32[4,24,384]{2,1,0:T(8,128)S(1)}, f32[4,24,384]{2,1,0:T(8,128)S(1)}, u32[]{:S(2)}, u32[]{:S(2)}) collective-permute-start(f32[4,24,384]{2,1,0:T(8,128)S(1)} %get-tuple-element.89), channel_id=1, source_target_pairs={{0,24},{8,0},{16,8},{24,16},{1,25},{9,1},{17,9},{25,17},{2,26},{10... | collective-permute-start | bytes 442376 | tf_op jit(solution)/shard_map/ppermute | solution.py:340
  100.3 0.6 collective-permute-start.25
  100.8 1.9 %collective-permute-start.24 = (f32[4,24,384]{2,1,0:T(8,128)S(1)}, f32[4,24,384]{2,1,0:T(8,128)S(1)}, u32[]{:S(2)}, u32[]{:S(2)}) collective-permute-start(f32[4,24,384]{2,1,0:T(8,128)S(1)} %get-tuple-element.87), channel_id=1, source_target_pairs={{0,8},{8,16},{16,24},{24,0},{1,9},{9,17},{17,25},{25,1},{2,10},{10... | collective-permute-start | bytes 442376 | tf_op jit(solution)/shard_map/ppermute | solution.py:340
  102.7 1.9 %collective-permute-done.15 = f32[4,24,384]{2,1,0:T(8,128)} collective-permute-done((f32[4,24,384]{2,1,0:T(8,128)S(1)}, f32[4,24,384]{2,1,0:T(8,128)}, u32[]{:S(2)}, u32[]{:S(2)}) %collective-permute-start.15) | collective-permute-done | bytes 147488 | tf_op jit(solution)/shard_map/ppermute | solution.py:340
  104.6 1.1 add_add_fusion.1
  105.7 2.5 %collective-permute-start.19 = (f32[24,384]{1,0:T(8,128)S(1)}, f32[24,384]{1,0:T(8,128)S(1)}, u32[]{:S(2)}, u32[]{:S(2)}) collective-permute-start(f32[24,384]{1,0:T(8,128)S(1)} %get-tuple-element.94), channel_id=1, source_target_pairs={{0,6},{1,7},{2,4},{3,5},{4,2},{5,3},{6,0},{7,1},{8,14},{9,15},{10,... | collective-permute-start | bytes 110600 | tf_op jit(solution)/shard_map/ppermute | solution.py:156
  108.2 2.5 %collective-permute-start.18 = (f32[24,384]{1,0:T(8,128)S(1)}, f32[24,384]{1,0:T(8,128)S(1)}, u32[]{:S(2)}, u32[]{:S(2)}) collective-permute-start(f32[24,384]{1,0:T(8,128)S(1)} %get-tuple-element.95), channel_id=1, source_target_pairs={{0,4},{1,5},{2,6},{3,7},{4,0},{5,1},{6,2},{7,3},{8,12},{9,13},{10,... | collective-permute-start | bytes 110600 | tf_op jit(solution)/shard_map/ppermute | solution.py:156
  110.8 2.0 %collective-permute-start.29 = (f32[24,384]{1,0:T(8,128)S(1)}, f32[24,384]{1,0:T(8,128)S(1)}, u32[]{:S(2)}, u32[]{:S(2)}) collective-permute-start(f32[24,384]{1,0:T(8,128)S(1)} %get-tuple-element.91), channel_id=1, source_target_pairs={{0,6},{1,7},{2,4},{3,5},{4,2},{5,3},{6,0},{7,1},{8,14},{9,15},{10,... | collective-permute-start | bytes 110600 | tf_op jit(solution)/shard_map/ppermute | solution.py:156
  112.7 2.4 %collective-permute-start.28 = (f32[24,384]{1,0:T(8,128)S(1)}, f32[24,384]{1,0:T(8,128)S(1)}, u32[]{:S(2)}, u32[]{:S(2)}) collective-permute-start(f32[24,384]{1,0:T(8,128)S(1)} %get-tuple-element.92), channel_id=1, source_target_pairs={{0,4},{1,5},{2,6},{3,7},{4,0},{5,1},{6,2},{7,3},{8,12},{9,13},{10,... | collective-permute-start | bytes 110600 | tf_op jit(solution)/shard_map/ppermute | solution.py:156
  115.2 0.0 collective-permute-start.27
  115.2 1.9 %collective-permute-start.20 = (f32[24,384]{1,0:T(8,128)S(1)}, f32[24,384]{1,0:T(8,128)S(1)}, u32[]{:S(2)}, u32[]{:S(2)}) collective-permute-start(f32[24,384]{1,0:T(8,128)S(1)} %fusion.5.refs_0_), channel_id=1, source_target_pairs={{0,8},{8,16},{16,24},{24,0},{1,9},{9,17},{17,25},{25,1},{2,10},{10... | collective-permute-start | bytes 110600 | tf_op jit(solution)/shard_map/ppermute | solution.py:340
  117.1 0.6 collective-permute-start.21
  117.7 2.7 %collective-permute-start.22 = (f32[24,384]{1,0:T(8,128)S(1)}, f32[24,384]{1,0:T(8,128)S(1)}, u32[]{:S(2)}, u32[]{:S(2)}) collective-permute-start(f32[24,384]{1,0:T(8,128)S(1)} %fusion.5.refs_0_), channel_id=1, source_target_pairs={{0,24},{8,0},{16,8},{24,16},{1,25},{9,1},{17,9},{25,17},{2,26},{10... | collective-permute-start | bytes 110600 | tf_op jit(solution)/shard_map/ppermute | solution.py:340
  120.4 0.1 collective-permute-start.30
  120.5 0.8 collective-permute-start.31
  121.3 2.4 %collective-permute-start.32 = (f32[24,384]{1,0:T(8,128)S(1)}, f32[24,384]{1,0:T(8,128)S(1)}, u32[]{:S(2)}, u32[]{:S(2)}) collective-permute-start(f32[24,384]{1,0:T(8,128)S(1)} %fusion.2.refs_4_), channel_id=1, source_target_pairs={{0,24},{8,0},{16,8},{24,16},{1,25},{9,1},{17,9},{25,17},{2,26},{10... | collective-permute-start | bytes 110600 | tf_op jit(solution)/shard_map/ppermute | solution.py:340
  123.6 1.7 %collective-permute-done.30.refs_5_ = f32[24,384]{1,0:T(8,128)S(1)} collective-permute-done((f32[24,384]{1,0:T(8,128)S(1)}, f32[24,384]{1,0:T(8,128)S(1)}, u32[]{:S(2)}, u32[]{:S(2)}) %collective-permute-start.30) | collective-permute-done | bytes 36896 | tf_op jit(solution)/shard_map/ppermute | solution.py:340
  125.3 0.6 collective-permute-done.32.refs_7_
  125.9 0.7 place.1
  (33 shorter events, 0.2 us)
Async XLA Ops:
  0.6 8.3 %copy-start.1 = (f32[96,2,2048]{2,1,0:T(2,128)S(1)}, f32[96,2,2048]{2,1,0:T(2,128)}, u32[]{:S(2)}) copy-start(f32[96,2,2048]{2,1,0:T(2,128)} %param.3) | copy-start | bytes 4718596
  3.7 13.9 %all-to-all-start = ((f32[36,2,2048]{2,1,0:T(2,128)}), f32[36,2,2048]{2,1,0:T(2,128)S(1)}, u32[]{:S(2)}, u32[]{:S(2)}) async-start(f32[36,2,2048]{2,1,0:T(2,128)} %bitcast.1), calls=%async_computation | async-start | bytes 1179648 | tf_op jit(solution)/shard_map/all_to_all | solution.py:361
  10.0 11.2 %copy-start = (bf16[512,256]{1,0:T(8,128)(2,1)S(1)}, bf16[512,256]{1,0:T(8,128)(2,1)}, u32[]{:S(2)}) copy-start(bf16[512,256]{1,0:T(8,128)(2,1)} %constant.45.clone.m_ref) | copy-start | bytes 786436
  17.6 22.8 %all-to-all-start.1 = ((f32[64,2,2048]{2,1,0:T(2,128)}), f32[64,2,2048]{2,1,0:T(2,128)S(1)}, u32[]{:S(2)}, u32[]{:S(2)}) async-start(f32[64,2,2048]{2,1,0:T(2,128)} %bitcast.2), calls=%async_computation.1 | async-start | bytes 2097152 | tf_op jit(solution)/shard_map/all_to_all | solution.py:361
  22.9 16.2 %collective-permute-start.4 = (f32[32,8,128]{2,1,0:T(8,128)S(1)}, f32[32,8,128]{2,1,0:T(8,128)S(1)}, u32[]{:S(2)}, u32[]{:S(2)}) collective-permute-start(f32[32,8,128]{2,1,0:T(8,128)S(1)} %get-tuple-element.55), channel_id=1, source_target_pairs={{0,8},{8,16},{16,24},{24,0},{1,9},{9,17},{17,25},{25,1},{2,10},{10... | collective-permute-start | bytes 393224 | tf_op jit(solution)/shard_map/ppermute | solution.py:340
  25.0 14.6 %collective-permute-start.5 = (f32[32,8,128]{2,1,0:T(8,128)S(1)}, f32[32,8,128]{2,1,0:T(8,128)S(1)}, u32[]{:S(2)}, u32[]{:S(2)}) collective-permute-start(f32[32,8,128]{2,1,0:T(8,128)S(1)} %get-tuple-element.56), channel_id=1, source_target_pairs={{0,16},{8,24},{16,0},{24,8},{1,17},{9,25},{17,1},{25,9},{2,18},{10... | collective-permute-start | bytes 393224 | tf_op jit(solution)/shard_map/ppermute | solution.py:340
  26.4 13.1 %collective-permute-start.6 = (f32[32,8,128]{2,1,0:T(8,128)S(1)}, f32[32,8,128]{2,1,0:T(8,128)S(1)}, u32[]{:S(2)}, u32[]{:S(2)}) collective-permute-start(f32[32,8,128]{2,1,0:T(8,128)S(1)} %get-tuple-element.57), channel_id=1, source_target_pairs={{0,24},{8,0},{16,8},{24,16},{1,25},{9,1},{17,9},{25,17},{2,26},{10... | collective-permute-start | bytes 393224 | tf_op jit(solution)/shard_map/ppermute | solution.py:340
  40.4 36.8 %all-to-all-start.2 = ((f32[8,32,512]{2,1,0:T(8,128)}), f32[8,32,512]{2,1,0:T(8,128)S(1)}, u32[]{:S(2)}, u32[]{:S(2)}) async-start(f32[8,32,512]{2,1,0:T(8,128)} %pack.3), calls=%async_computation.2 | async-start | bytes 1048576 | tf_op jit(solution)/shard_map/all_to_all | solution.py:377
  48.7 10.1 %collective-permute-start = (f32[32,16,128]{2,1,0:T(8,128)S(1)}, f32[32,16,128]{2,1,0:T(8,128)S(1)}, u32[]{:S(2)}, u32[]{:S(2)}) collective-permute-start(f32[32,16,128]{2,1,0:T(8,128)S(1)} %get-tuple-element.50), channel_id=1, source_target_pairs={{0,8},{8,16},{16,24},{24,0},{1,9},{9,17},{17,25},{25,1},{2,10},{10... | collective-permute-start | bytes 786440 | tf_op jit(solution)/shard_map/ppermute | solution.py:340
  50.2 13.8 %collective-permute-start.1 = (f32[32,16,128]{2,1,0:T(8,128)S(1)}, f32[32,16,128]{2,1,0:T(8,128)S(1)}, u32[]{:S(2)}, u32[]{:S(2)}) collective-permute-start(f32[32,16,128]{2,1,0:T(8,128)S(1)} %get-tuple-element.51), channel_id=1, source_target_pairs={{0,16},{8,24},{16,0},{24,8},{1,17},{9,25},{17,1},{25,9},{2,18},{10... | collective-permute-start | bytes 786440 | tf_op jit(solution)/shard_map/ppermute | solution.py:340
  50.7 13.3 %collective-permute-start.2 = (f32[32,16,128]{2,1,0:T(8,128)S(1)}, f32[32,16,128]{2,1,0:T(8,128)S(1)}, u32[]{:S(2)}, u32[]{:S(2)}) collective-permute-start(f32[32,16,128]{2,1,0:T(8,128)S(1)} %get-tuple-element.52), channel_id=1, source_target_pairs={{0,24},{8,0},{16,8},{24,16},{1,25},{9,1},{17,9},{25,17},{2,26},{10... | collective-permute-start | bytes 786440 | tf_op jit(solution)/shard_map/ppermute | solution.py:340
  64.7 7.6 %collective-permute-start.3 = (f32[64,512]{1,0:T(8,128)S(1)}, f32[64,512]{1,0:T(8,128)S(1)}, u32[]{:S(2)}, u32[]{:S(2)}) collective-permute-start(f32[64,512]{1,0:T(8,128)S(1)} %get-tuple-element.53), channel_id=1, source_target_pairs={{0,7},{1,6},{2,5},{3,4},{4,3},{5,2},{6,1},{7,0},{8,15},{9,14},{10,... | collective-permute-start | bytes 393224 | tf_op jit(solution)/shard_map/ppermute | solution.py:156
  67.8 8.0 %collective-permute-start.7 = (f32[64,512]{1,0:T(8,128)S(1)}, f32[64,512]{1,0:T(8,128)S(1)}, u32[]{:S(2)}, u32[]{:S(2)}) collective-permute-start(f32[64,512]{1,0:T(8,128)S(1)} %get-tuple-element.62), channel_id=1, source_target_pairs={{0,1},{1,0},{2,3},{3,2},{4,5},{5,4},{6,7},{7,6},{8,9},{9,8},{10,11... | collective-permute-start | bytes 393224 | tf_op jit(solution)/shard_map/ppermute | solution.py:156
  68.3 11.2 %collective-permute-start.8 = (f32[64,512]{1,0:T(8,128)}, f32[64,512]{1,0:T(8,128)S(1)}, u32[]{:S(2)}, u32[]{:S(2)}) collective-permute-start(f32[64,512]{1,0:T(8,128)} %get-tuple-element.63), channel_id=1, source_target_pairs={{0,2},{1,3},{2,0},{3,1},{4,6},{5,7},{6,4},{7,5},{8,10},{9,11},{10,... | collective-permute-start | bytes 393224 | tf_op jit(solution)/shard_map/ppermute | solution.py:156
  68.3 13.2 %collective-permute-start.9 = (f32[64,512]{1,0:T(8,128)S(1)}, f32[64,512]{1,0:T(8,128)S(1)}, u32[]{:S(2)}, u32[]{:S(2)}) collective-permute-start(f32[64,512]{1,0:T(8,128)S(1)} %get-tuple-element.64), channel_id=1, source_target_pairs={{0,3},{1,2},{2,1},{3,0},{4,7},{5,6},{6,5},{7,4},{8,11},{9,10},{10,... | collective-permute-start | bytes 393224 | tf_op jit(solution)/shard_map/ppermute | solution.py:156
  69.7 11.9 %collective-permute-start.10 = (f32[64,512]{1,0:T(8,128)S(1)}, f32[64,512]{1,0:T(8,128)S(1)}, u32[]{:S(2)}, u32[]{:S(2)}) collective-permute-start(f32[64,512]{1,0:T(8,128)S(1)} %get-tuple-element.65), channel_id=1, source_target_pairs={{0,4},{1,5},{2,6},{3,7},{4,0},{5,1},{6,2},{7,3},{8,12},{9,13},{10,... | collective-permute-start | bytes 393224 | tf_op jit(solution)/shard_map/ppermute | solution.py:156
  72.3 16.2 %collective-permute-start.11 = (f32[64,512]{1,0:T(8,128)S(1)}, f32[64,512]{1,0:T(8,128)}, u32[]{:S(2)}, u32[]{:S(2)}) collective-permute-start(f32[64,512]{1,0:T(8,128)S(1)} %get-tuple-element.66), channel_id=1, source_target_pairs={{0,5},{1,4},{2,7},{3,6},{4,1},{5,0},{6,3},{7,2},{8,13},{9,12},{10,... | collective-permute-start | bytes 393224 | tf_op jit(solution)/shard_map/ppermute | solution.py:156
  75.8 12.7 %collective-permute-start.12 = (f32[64,512]{1,0:T(8,128)S(1)}, f32[64,512]{1,0:T(8,128)}, u32[]{:S(2)}, u32[]{:S(2)}) collective-permute-start(f32[64,512]{1,0:T(8,128)S(1)} %get-tuple-element.67), channel_id=1, source_target_pairs={{0,6},{1,7},{2,4},{3,5},{4,2},{5,3},{6,0},{7,1},{8,14},{9,15},{10,... | collective-permute-start | bytes 393224 | tf_op jit(solution)/shard_map/ppermute | solution.py:156
  91.1 2.1 %collective-permute-start.13 = (f32[384,384]{1,0:T(8,128)S(1)}, f32[384,384]{1,0:T(8,128)S(1)}, u32[]{:S(2)}, u32[]{:S(2)}) collective-permute-start(f32[384,384]{1,0:T(8,128)S(1)} %get-tuple-element.71), channel_id=1, source_target_pairs={{0,1},{1,0},{2,3},{3,2},{4,5},{5,4},{6,7},{7,6},{8,9},{9,8},{10,11... | collective-permute-start | bytes 1769480 | tf_op jit(solution)/shard_map/ppermute | solution.py:398
  91.3 5.9 %collective-permute-start.23 = (f32[384,384]{1,0:T(8,128)S(1)}, f32[384,384]{1,0:T(8,128)S(1)}, u32[]{:S(2)}, u32[]{:S(2)}) collective-permute-start(f32[384,384]{1,0:T(8,128)S(1)} %get-tuple-element.81), channel_id=1, source_target_pairs={{0,1},{1,0},{2,3},{3,2},{4,5},{5,4},{6,7},{7,6},{8,9},{9,8},{10,11... | collective-permute-start | bytes 1769480 | tf_op jit(solution)/shard_map/ppermute | solution.py:398
  93.2 7.6 %collective-permute-start.16 = (f32[4,24,384]{2,1,0:T(8,128)S(1)}, f32[4,24,384]{2,1,0:T(8,128)}, u32[]{:S(2)}, u32[]{:S(2)}) collective-permute-start(f32[4,24,384]{2,1,0:T(8,128)S(1)} %get-tuple-element.79), channel_id=1, source_target_pairs={{0,24},{8,0},{16,8},{24,16},{1,25},{9,1},{17,9},{25,17},{2,26},{10... | collective-permute-start | bytes 442376 | tf_op jit(solution)/shard_map/ppermute | solution.py:340
  94.9 9.6 %collective-permute-start.15 = (f32[4,24,384]{2,1,0:T(8,128)S(1)}, f32[4,24,384]{2,1,0:T(8,128)}, u32[]{:S(2)}, u32[]{:S(2)}) collective-permute-start(f32[4,24,384]{2,1,0:T(8,128)S(1)} %get-tuple-element.78), channel_id=1, source_target_pairs={{0,16},{8,24},{16,0},{24,8},{1,17},{9,25},{17,1},{25,9},{2,18},{10... | collective-permute-start | bytes 442376 | tf_op jit(solution)/shard_map/ppermute | solution.py:340
  96.4 8.2 %collective-permute-start.14 = (f32[4,24,384]{2,1,0:T(8,128)S(1)}, f32[4,24,384]{2,1,0:T(8,128)}, u32[]{:S(2)}, u32[]{:S(2)}) collective-permute-start(f32[4,24,384]{2,1,0:T(8,128)S(1)} %get-tuple-element.77), channel_id=1, source_target_pairs={{0,8},{8,16},{16,24},{24,0},{1,9},{9,17},{17,25},{25,1},{2,10},{10... | collective-permute-start | bytes 442376 | tf_op jit(solution)/shard_map/ppermute | solution.py:340
  97.3 13.4 %collective-permute-start.26 = (f32[4,24,384]{2,1,0:T(8,128)S(1)}, f32[4,24,384]{2,1,0:T(8,128)S(1)}, u32[]{:S(2)}, u32[]{:S(2)}) collective-permute-start(f32[4,24,384]{2,1,0:T(8,128)S(1)} %get-tuple-element.89), channel_id=1, source_target_pairs={{0,24},{8,0},{16,8},{24,16},{1,25},{9,1},{17,9},{25,17},{2,26},{10... | collective-permute-start | bytes 442376 | tf_op jit(solution)/shard_map/ppermute | solution.py:340
  100.3 10.4 %collective-permute-start.25 = (f32[4,24,384]{2,1,0:T(8,128)S(1)}, f32[4,24,384]{2,1,0:T(8,128)S(1)}, u32[]{:S(2)}, u32[]{:S(2)}) collective-permute-start(f32[4,24,384]{2,1,0:T(8,128)S(1)} %get-tuple-element.88), channel_id=1, source_target_pairs={{0,16},{8,24},{16,0},{24,8},{1,17},{9,25},{17,1},{25,9},{2,18},{10... | collective-permute-start | bytes 442376 | tf_op jit(solution)/shard_map/ppermute | solution.py:340
  100.8 9.9 %collective-permute-start.24 = (f32[4,24,384]{2,1,0:T(8,128)S(1)}, f32[4,24,384]{2,1,0:T(8,128)S(1)}, u32[]{:S(2)}, u32[]{:S(2)}) collective-permute-start(f32[4,24,384]{2,1,0:T(8,128)S(1)} %get-tuple-element.87), channel_id=1, source_target_pairs={{0,8},{8,16},{16,24},{24,0},{1,9},{9,17},{17,25},{25,1},{2,10},{10... | collective-permute-start | bytes 442376 | tf_op jit(solution)/shard_map/ppermute | solution.py:340
  105.7 9.5 %collective-permute-start.19 = (f32[24,384]{1,0:T(8,128)S(1)}, f32[24,384]{1,0:T(8,128)S(1)}, u32[]{:S(2)}, u32[]{:S(2)}) collective-permute-start(f32[24,384]{1,0:T(8,128)S(1)} %get-tuple-element.94), channel_id=1, source_target_pairs={{0,6},{1,7},{2,4},{3,5},{4,2},{5,3},{6,0},{7,1},{8,14},{9,15},{10,... | collective-permute-start | bytes 110600 | tf_op jit(solution)/shard_map/ppermute | solution.py:156
  108.2 7.0 %collective-permute-start.18 = (f32[24,384]{1,0:T(8,128)S(1)}, f32[24,384]{1,0:T(8,128)S(1)}, u32[]{:S(2)}, u32[]{:S(2)}) collective-permute-start(f32[24,384]{1,0:T(8,128)S(1)} %get-tuple-element.95), channel_id=1, source_target_pairs={{0,4},{1,5},{2,6},{3,7},{4,0},{5,1},{6,2},{7,3},{8,12},{9,13},{10,... | collective-permute-start | bytes 110600 | tf_op jit(solution)/shard_map/ppermute | solution.py:156
  110.7 4.6 %collective-permute-start.17 = (f32[24,384]{1,0:T(8,128)S(1)}, f32[24,384]{1,0:T(8,128)S(1)}, u32[]{:S(2)}, u32[]{:S(2)}) collective-permute-start(f32[24,384]{1,0:T(8,128)S(1)} %get-tuple-element.93), channel_id=1, source_target_pairs={{0,2},{1,3},{2,0},{3,1},{4,6},{5,7},{6,4},{7,5},{8,10},{9,11},{10,... | collective-permute-start | bytes 110600 | tf_op jit(solution)/shard_map/ppermute | solution.py:156
  110.8 6.9 %collective-permute-start.29 = (f32[24,384]{1,0:T(8,128)S(1)}, f32[24,384]{1,0:T(8,128)S(1)}, u32[]{:S(2)}, u32[]{:S(2)}) collective-permute-start(f32[24,384]{1,0:T(8,128)S(1)} %get-tuple-element.91), channel_id=1, source_target_pairs={{0,6},{1,7},{2,4},{3,5},{4,2},{5,3},{6,0},{7,1},{8,14},{9,15},{10,... | collective-permute-start | bytes 110600 | tf_op jit(solution)/shard_map/ppermute | solution.py:156
  112.7 7.7 %collective-permute-start.28 = (f32[24,384]{1,0:T(8,128)S(1)}, f32[24,384]{1,0:T(8,128)S(1)}, u32[]{:S(2)}, u32[]{:S(2)}) collective-permute-start(f32[24,384]{1,0:T(8,128)S(1)} %get-tuple-element.92), channel_id=1, source_target_pairs={{0,4},{1,5},{2,6},{3,7},{4,0},{5,1},{6,2},{7,3},{8,12},{9,13},{10,... | collective-permute-start | bytes 110600 | tf_op jit(solution)/shard_map/ppermute | solution.py:156
  115.2 5.2 %collective-permute-start.27 = (f32[24,384]{1,0:T(8,128)S(1)}, f32[24,384]{1,0:T(8,128)S(1)}, u32[]{:S(2)}, u32[]{:S(2)}) collective-permute-start(f32[24,384]{1,0:T(8,128)S(1)} %get-tuple-element.90), channel_id=1, source_target_pairs={{0,2},{1,3},{2,0},{3,1},{4,6},{5,7},{6,4},{7,5},{8,10},{9,11},{10,... | collective-permute-start | bytes 110600 | tf_op jit(solution)/shard_map/ppermute | solution.py:156
  115.2 6.0 %collective-permute-start.20 = (f32[24,384]{1,0:T(8,128)S(1)}, f32[24,384]{1,0:T(8,128)S(1)}, u32[]{:S(2)}, u32[]{:S(2)}) collective-permute-start(f32[24,384]{1,0:T(8,128)S(1)} %fusion.5.refs_0_), channel_id=1, source_target_pairs={{0,8},{8,16},{16,24},{24,0},{1,9},{9,17},{17,25},{25,1},{2,10},{10... | collective-permute-start | bytes 110600 | tf_op jit(solution)/shard_map/ppermute | solution.py:340
  117.1 6.5 %collective-permute-start.21 = (f32[24,384]{1,0:T(8,128)S(1)}, f32[24,384]{1,0:T(8,128)S(1)}, u32[]{:S(2)}, u32[]{:S(2)}) collective-permute-start(f32[24,384]{1,0:T(8,128)S(1)} %fusion.5.refs_0_), channel_id=1, source_target_pairs={{0,16},{8,24},{16,0},{24,8},{1,17},{9,25},{17,1},{25,9},{2,18},{10... | collective-permute-start | bytes 110600 | tf_op jit(solution)/shard_map/ppermute | solution.py:340
  117.7 6.0 %collective-permute-start.22 = (f32[24,384]{1,0:T(8,128)S(1)}, f32[24,384]{1,0:T(8,128)S(1)}, u32[]{:S(2)}, u32[]{:S(2)}) collective-permute-start(f32[24,384]{1,0:T(8,128)S(1)} %fusion.5.refs_0_), channel_id=1, source_target_pairs={{0,24},{8,0},{16,8},{24,16},{1,25},{9,1},{17,9},{25,17},{2,26},{10... | collective-permute-start | bytes 110600 | tf_op jit(solution)/shard_map/ppermute | solution.py:340
  120.4 4.9 %collective-permute-start.30 = (f32[24,384]{1,0:T(8,128)S(1)}, f32[24,384]{1,0:T(8,128)S(1)}, u32[]{:S(2)}, u32[]{:S(2)}) collective-permute-start(f32[24,384]{1,0:T(8,128)S(1)} %fusion.2.refs_4_), channel_id=1, source_target_pairs={{0,8},{8,16},{16,24},{24,0},{1,9},{9,17},{17,25},{25,1},{2,10},{10... | collective-permute-start | bytes 110600 | tf_op jit(solution)/shard_map/ppermute | solution.py:340
  120.5 4.8 %collective-permute-start.31 = (f32[24,384]{1,0:T(8,128)S(1)}, f32[24,384]{1,0:T(8,128)S(1)}, u32[]{:S(2)}, u32[]{:S(2)}) collective-permute-start(f32[24,384]{1,0:T(8,128)S(1)} %fusion.2.refs_4_), channel_id=1, source_target_pairs={{0,16},{8,24},{16,0},{24,8},{1,17},{9,25},{17,1},{25,9},{2,18},{10... | collective-permute-start | bytes 110600 | tf_op jit(solution)/shard_map/ppermute | solution.py:340
  121.3 4.7 %collective-permute-start.32 = (f32[24,384]{1,0:T(8,128)S(1)}, f32[24,384]{1,0:T(8,128)S(1)}, u32[]{:S(2)}, u32[]{:S(2)}) collective-permute-start(f32[24,384]{1,0:T(8,128)S(1)} %fusion.2.refs_4_), channel_id=1, source_target_pairs={{0,24},{8,0},{16,8},{24,16},{1,25},{9,1},{17,9},{25,17},{2,26},{10... | collective-permute-start | bytes 110600 | tf_op jit(solution)/shard_map/ppermute | solution.py:340
